TPU v7x, 32 devices: a whole 2x2x4 slice. The times are simulated.
32 devices in a mesh: fsdp: 16 (over z, x, core), rep: 2 (over y).
Axes of the slice: x: 2, y: 2, z: 4, core: 2. Of those that a mesh axis runs over, the one named last changes fastest.
Arguments:
- layer_input: bfloat16 [4096, 1536], P(('fsdp', 'rep')), may hold values from -6 to 6
- lengths: int32 [32], P(('fsdp', 'rep')), may hold values from 16 to 128, as said below
- cotangent: bfloat16 [4096, 1536], P(('fsdp', 'rep')), may hold values from -6 to 6
- w_query: bfloat16 [1536, 1536], P('fsdp'), may hold values from -0.15625 to 0.15625
- w_key: bfloat16 [1536, 1536], P('fsdp'), may hold values from -0.15625 to 0.15625
- w_value: bfloat16 [1536, 1536], P('fsdp'), may hold values from -0.15625 to 0.15625
- w_out: bfloat16 [1536, 1536], P('fsdp'), may hold values from -0.15625 to 0.15625
- w_gate: bfloat16 [1536, 4096], P('fsdp'), may hold values from -0.15625 to 0.15625
- w_up: bfloat16 [1536, 4096], P('fsdp'), may hold values from -0.15625 to 0.15625
- w_down: bfloat16 [4096, 1536], P('fsdp'), may hold values from -0.09375 to 0.09375
- vec_copy: bfloat16 [5696], P('fsdp')
- owners: int32 [108], replicated, may hold values from 0 to 127, as said below
- basis_left: float32 [128, 512, 512], P(('fsdp', 'rep')), may hold values from -0.25 to 0.25
- basis_right: float32 [128, 512, 512], P(('fsdp', 'rep')), may hold values from -0.25 to 0.25
- block_master: float32 [128, 512, 512], P(('fsdp', 'rep')), may hold values from -0.15625 to 0.15625
- block_first: float32 [128, 512, 512], P(('fsdp', 'rep'))
- block_second: float32 [128, 512, 512], P(('fsdp', 'rep'))
- vec_master: float32 [5696], P('fsdp')
- vec_first: float32 [5696], P('fsdp')
- vec_second: float32 [5696], P('fsdp')
Outputs:
- layer_output: bfloat16 [4096, 1536], P(('fsdp', 'rep'))
- input_grad: float32 [4096, 1536], P(('fsdp', 'rep'))
- block_first_new: float32 [128, 512, 512], P(('fsdp', 'rep'))
- block_second_new: float32 [128, 512, 512], P(('fsdp', 'rep'))
- block_master_new: float32 [128, 512, 512], P(('fsdp', 'rep'))
- block_copy_new: bfloat16 [128, 512, 512], P(('fsdp', 'rep'))
- vec_first_new: float32 [5696], P('fsdp')
- vec_second_new: float32 [5696], P('fsdp')
- vec_master_new: float32 [5696], P('fsdp')
- vec_copy_new: bfloat16 [5696], P('fsdp')
Inputs may be any that keep to these rules, and one draw needn't show every extreme that they name: `lengths`: valid tokens of each sequence come first; the rest of its 128 rows are padding. `owners`: distinct slots, one for each tile.
All inputs are finite; a program needn't handle non-finite values.
Results may differ from a plain program's by a relative error of at most 0.02.
Values may be sent and summed in bfloat16 or wider, within the bound.
A program may use at most 512 MiB of HBM per device.

v0:
```python
import math

import jax
import jax.numpy as jnp
import numpy as np
from jax import lax
from jax.sharding import PartitionSpec as P

H = 16
DH = 96
FF = 4096
CQ = 6
CK = 11
BLK = 512


eps_norm = 1e-05
eps_adam = 1e-08
rate_block = 0.02
rate_vector = 0.3
decay_block = 0.1
beta_first = 0.5
beta_second = 0.5


def rms_norm(values, gain):
    return values * lax.rsqrt(jnp.mean(values * values, axis=-1, keepdims=True) + eps_norm) * gain


def head_norm(values, gain):
    normed = values * lax.rsqrt(jnp.mean(values * values, axis=-1, keepdims=True) + eps_norm)
    return normed.reshape(values.shape[0], -1) * gain


def swiglu(gate_act, up_act):
    return jax.nn.silu(gate_act) * up_act


def split_vectors(vector):
    model_width = H * DH
    gain_attn = vector[0:model_width]
    gain_head = vector[model_width : 2 * model_width]
    gain_ffn = vector[2 * model_width : 3 * model_width]
    conv_end = 3 * model_width + H * CQ * CK
    theta = vector[3 * model_width : conv_end].reshape(H, CQ, CK)
    mixer = vector[conv_end : conv_end + 2 * H].reshape(H, 2)
    return (gain_attn, gain_head, gain_ffn, theta, mixer)


def mixed_weights(scores, theta, mixer, first_row, length):
    head_count = scores.shape[0]
    row_count = scores.shape[1] - (CQ - 1)
    key_count = scores.shape[2]
    key_index = jnp.arange(key_count)
    ext_rows = first_row - (CQ - 1) + jnp.arange(row_count + CQ - 1)
    keep_ext = (
        (key_index[None, :] <= ext_rows[:, None])
        & (key_index[None, :] < length)
        & (ext_rows[:, None] >= 0)
    )
    masked = jnp.where(keep_ext[None], scores, 0.0)
    half_width = CK // 2
    padded = jnp.pad(masked, ((0, 0), (0, 0), (half_width, half_width)))
    convolved = jnp.zeros((head_count, row_count, key_count), jnp.float32)
    for query_lag in range(CQ):
        for key_tap in range(CK):
            window = padded[
                :,
                CQ - 1 - query_lag : CQ - 1 - query_lag + row_count,
                key_tap : key_tap + key_count,
            ]
            convolved = convolved + theta[:, query_lag, key_tap][:, None, None] * window
    positions = first_row + jnp.arange(row_count)
    keep = (key_index[None, :] <= positions[:, None]) & (key_index[None, :] < length)
    logits = jnp.where(keep[None], convolved, -1e30)
    row_max = jnp.max(logits, axis=-1, keepdims=True)
    exponent = jnp.exp(logits - row_max)
    softmax_w = exponent / jnp.sum(exponent, axis=-1, keepdims=True)
    grouped = softmax_w.reshape(head_count // 2, 2, row_count, key_count)
    mixing = mixer.reshape(head_count // 2, 2, 2)
    return jnp.einsum("goe,gerl->gorl", mixing, grouped).reshape(head_count, row_count, key_count)


def block_tables():
    across = H * DH // BLK
    wide = FF // BLK
    specs = [
        (0, 0, across, across),
        (0, across, across, across),
        (0, 2 * across, across, across),
        (across, 3 * across, across, across),
        (2 * across, 5 * across, across, wide),
        (2 * across, 5 * across + wide, across, wide),
        (3 * across, 4 * across, wide, across),
    ]
    left_list = []
    right_list = []
    for left_base, right_base, tile_rows, tile_cols in specs:
        for row_tile in range(tile_rows):
            for col_tile in range(tile_cols):
                left_list.append(left_base + row_tile)
                right_list.append(right_base + col_tile)
    return (np.array(left_list, np.int32), np.array(right_list, np.int32))


def contract_last(left, right):
    return lax.dot_general(
        left, right, (((1,), (1,)), ((), ())), preferred_element_type=jnp.float32
    )


def body(
    layer_input,
    lengths,
    cotangent,
    w_query,
    w_key,
    w_value,
    w_out,
    w_gate,
    w_up,
    w_down,
    vec_copy,
    owners,
    basis_left,
    basis_right,
    block_master,
    block_first,
    block_second,
    vec_master,
    vec_first,
    vec_second,
):
    local = (w_query, w_key, w_value, w_out, w_gate, w_up, w_down, vec_copy)
    gathered = (
        lax.all_gather(local[0], "fsdp", axis=0, tiled=True),
        lax.all_gather(local[1], "fsdp", axis=0, tiled=True),
        lax.all_gather(local[2], "fsdp", axis=0, tiled=True),
        lax.all_gather(local[3], "fsdp", axis=0, tiled=True),
        lax.all_gather(local[4], "fsdp", axis=0, tiled=True),
        lax.all_gather(local[5], "fsdp", axis=0, tiled=True),
        lax.all_gather(local[6], "fsdp", axis=0, tiled=True),
        lax.all_gather(local[7], "fsdp", axis=0, tiled=True),
    )
    full_query, full_key, full_value, full_out, full_gate, full_up, full_down, full_vector = (
        gathered
    )
    gain_attn, gain_head, gain_ffn, theta, mixer = split_vectors(full_vector.astype(jnp.float32))
    seq_len = layer_input.shape[0]
    model_width = layer_input.shape[1]
    length = lengths[0]
    block_rows = min(512, seq_len)
    score_scale = 1.0 / math.sqrt(DH)
    input_float = layer_input.astype(jnp.float32)
    xn_low = rms_norm(input_float, gain_attn).astype(jnp.bfloat16)
    query_low = jnp.dot(xn_low, full_query, preferred_element_type=jnp.float32).astype(jnp.bfloat16)
    key_low = jnp.dot(xn_low, full_key, preferred_element_type=jnp.float32).astype(jnp.bfloat16)
    value_low = jnp.dot(xn_low, full_value, preferred_element_type=jnp.float32).astype(jnp.bfloat16)
    key_heads = key_low.reshape(seq_len, H, DH)
    value_heads = value_low.reshape(seq_len, H, DH)
    query_padded = jnp.pad(query_low.reshape(seq_len, H, DH), ((CQ - 1, 0), (0, 0), (0, 0)))

    def block_scores():
        scores = (
            jnp.einsum("rhd,lhd->hrl", query_padded, key_heads, preferred_element_type=jnp.float32)
            * score_scale
        )
        return (query_padded, scores)

    first_row = 0
    query_ext, scores = block_scores()
    mixed_low = mixed_weights(scores, theta, mixer, first_row, length).astype(jnp.bfloat16)
    attn_parts = jnp.einsum(
        "hrl,lhd->rhd", mixed_low, value_heads, preferred_element_type=jnp.float32
    )
    head_low = head_norm(attn_parts, gain_head).astype(jnp.bfloat16)
    attn_out = jnp.dot(head_low, full_out, preferred_element_type=jnp.float32)
    hidden_in = input_float + attn_out
    hn_low = rms_norm(hidden_in, gain_ffn).astype(jnp.bfloat16)
    gate_act = jnp.dot(hn_low, full_gate, preferred_element_type=jnp.float32)
    up_act = jnp.dot(hn_low, full_up, preferred_element_type=jnp.float32)
    inner_low = swiglu(gate_act, up_act).astype(jnp.bfloat16)
    ffn_out = jnp.dot(inner_low, full_down, preferred_element_type=jnp.float32)
    result = (hidden_in + ffn_out).astype(jnp.bfloat16)
    valid_rows = (jnp.arange(seq_len) < length).astype(jnp.float32)
    grad_result = cotangent.astype(jnp.float32) * valid_rows[:, None]
    grad_low = grad_result.astype(jnp.bfloat16)
    again = (
        lax.all_gather(local[0], "fsdp", axis=0, tiled=True),
        lax.all_gather(local[1], "fsdp", axis=0, tiled=True),
        lax.all_gather(local[2], "fsdp", axis=0, tiled=True),
        lax.all_gather(local[3], "fsdp", axis=0, tiled=True),
        lax.all_gather(local[4], "fsdp", axis=0, tiled=True),
        lax.all_gather(local[5], "fsdp", axis=0, tiled=True),
        lax.all_gather(local[6], "fsdp", axis=0, tiled=True),
        lax.all_gather(local[7], "fsdp", axis=0, tiled=True),
    )
    back_query, back_key, back_value, back_out, back_gate, back_up, back_down, back_vector = again
    grad_inner = contract_last(grad_low, back_down)
    grad_gate, grad_up = jax.vjp(swiglu, gate_act, up_act)[1](grad_inner)
    gate_low = grad_gate.astype(jnp.bfloat16)
    up_low = grad_up.astype(jnp.bfloat16)
    grad_hn = contract_last(gate_low, back_gate) + contract_last(up_low, back_up)
    grad_hidden, grad_gain_ffn = jax.vjp(rms_norm, hidden_in, gain_ffn)[1](grad_hn)
    grad_hidden = grad_hidden + grad_result
    attn_grad_low = grad_hidden.astype(jnp.bfloat16)
    grad_head = contract_last(attn_grad_low, back_out)
    grad_heads, grad_gain_head = jax.vjp(head_norm, attn_parts, gain_head)[1](grad_head)
    heads_low = grad_heads.astype(jnp.bfloat16)
    grad_query_pad = jnp.zeros((seq_len + CQ - 1, H, DH), jnp.float32)
    first_row = 0
    query_ext, scores = block_scores()

    def block_weights(scores_in, theta_in, mixer_in):
        return mixed_weights(scores_in, theta_in, mixer_in, first_row, length)

    mixed, pullback = jax.vjp(block_weights, scores, theta, mixer)
    mixed_low = mixed.astype(jnp.bfloat16)
    grad_mixed = jnp.einsum(
        "rhd,lhd->hrl", heads_low, value_heads, preferred_element_type=jnp.float32
    )
    grad_value = jnp.einsum(
        "hrl,rhd->lhd", mixed_low, heads_low, preferred_element_type=jnp.float32
    )
    grad_scores, grad_theta_block, grad_mixer_block = pullback(grad_mixed)
    scores_low = grad_scores.astype(jnp.bfloat16)
    query_term = (
        jnp.einsum("hrl,lhd->rhd", scores_low, key_heads, preferred_element_type=jnp.float32)
        * score_scale
    )
    grad_query_pad = grad_query_pad.at[first_row : first_row + block_rows + CQ - 1].add(query_term)
    grad_key = (
        jnp.einsum("hrl,rhd->lhd", scores_low, query_ext, preferred_element_type=jnp.float32)
        * score_scale
    )
    query_grad_low = grad_query_pad[CQ - 1 :].reshape(seq_len, model_width).astype(jnp.bfloat16)
    key_grad_low = grad_key.reshape(seq_len, model_width).astype(jnp.bfloat16)
    value_grad_low = grad_value.reshape(seq_len, model_width).astype(jnp.bfloat16)
    grad_xn = (
        contract_last(query_grad_low, back_query)
        + contract_last(key_grad_low, back_key)
        + contract_last(value_grad_low, back_value)
    )
    grad_input, grad_gain_attn = jax.vjp(rms_norm, input_float, gain_attn)[1](grad_xn)
    grad_input = grad_input + grad_hidden
    vector_grad = jnp.concatenate(
        [
            grad_gain_attn,
            grad_gain_head,
            grad_gain_ffn,
            grad_theta_block.reshape(-1),
            grad_mixer_block.reshape(-1),
        ]
    )
    left_all = jnp.concatenate([xn_low, head_low, hn_low, inner_low], axis=1).reshape(
        seq_len, -1, BLK
    )
    right_all = jnp.concatenate(
        [query_grad_low, key_grad_low, value_grad_low, attn_grad_low, grad_low, gate_low, up_low],
        axis=1,
    ).reshape(seq_len, -1, BLK)
    own_slots = basis_left.shape[0]
    slot_total = own_slots * lax.axis_size("fsdp") * lax.axis_size("rep")
    left_table, right_table = block_tables()
    matches = owners[None, :] == jnp.arange(slot_total)[:, None]
    occupied = jnp.any(matches, axis=1).astype(jnp.float32)
    left_slot = jnp.sum(jnp.where(matches, jnp.asarray(left_table)[None, :], 0), axis=1)
    right_slot = jnp.sum(jnp.where(matches, jnp.asarray(right_table)[None, :], 0), axis=1)
    vector_share = lax.psum_scatter(vector_grad, "fsdp", scatter_dimension=0, tiled=True)
    group_size = 8
    left_ids = left_slot.reshape(-1, group_size)
    right_ids = right_slot.reshape(-1, group_size)
    filled = occupied.reshape(-1, group_size)

    def one_group(members):
        left_group, right_group, filled_group = members
        left_cols = jnp.take(left_all, left_group, axis=1)
        right_cols = jnp.take(right_all, right_group, axis=1)
        return (
            jnp.einsum("tsi,tsj->sij", left_cols, right_cols, preferred_element_type=jnp.float32)
            * filled_group[:, None, None]
        )

    pair_grad = lax.psum_scatter(
        lax.map(one_group, (left_ids, right_ids, filled)).reshape(
            own_slots * lax.axis_size("rep") * lax.axis_size("fsdp"), BLK, BLK
        ),
        "fsdp",
        scatter_dimension=0,
        tiled=True,
    )
    pair_total, vector_total = (
        lax.psum(pair_grad.astype(jnp.bfloat16), "rep").astype(jnp.float32),
        lax.psum(vector_share.astype(jnp.bfloat16), "rep").astype(jnp.float32),
    )
    own_grad = lax.dynamic_slice_in_dim(pair_total, lax.axis_index("rep") * own_slots, own_slots, 0)
    highest = lax.Precision.HIGHEST
    rotated = jnp.einsum("sia,sij->saj", basis_left, own_grad, precision=highest)
    rotated = jnp.einsum("saj,sjb->sab", rotated, basis_right, precision=highest)
    first_new = beta_first * block_first + (1.0 - beta_first) * rotated
    second_new = beta_second * block_second + (1.0 - beta_second) * rotated * rotated
    direction = first_new / (jnp.sqrt(second_new) + eps_adam)
    turned = jnp.einsum("sia,sab->sib", basis_left, direction, precision=highest)
    turned = jnp.einsum("sib,sjb->sij", turned, basis_right, precision=highest)
    master_new = block_master - rate_block * (turned + decay_block * block_master)
    vec_first_new = beta_first * vec_first + (1.0 - beta_first) * vector_total
    vec_second_new = beta_second * vec_second + (1.0 - beta_second) * vector_total * vector_total
    vec_master_new = vec_master - rate_vector * vec_first_new / (
        jnp.sqrt(vec_second_new) + eps_adam
    )
    return (
        result,
        grad_input,
        first_new,
        second_new,
        master_new,
        master_new.astype(jnp.bfloat16),
        vec_first_new,
        vec_second_new,
        vec_master_new,
        vec_master_new.astype(jnp.bfloat16),
    )


def solution(mesh):
    return jax.shard_map(
        body,
        mesh=mesh,
        in_specs=(
            P(("fsdp", "rep"), None),
            P(("fsdp", "rep")),
            P(("fsdp", "rep"), None),
            P("fsdp", None),
            P("fsdp", None),
            P("fsdp", None),
            P("fsdp", None),
            P("fsdp", None),
            P("fsdp", None),
            P("fsdp", None),
            P("fsdp"),
            P(),
            P(("fsdp", "rep"), None, None),
            P(("fsdp", "rep"), None, None),
            P(("fsdp", "rep"), None, None),
            P(("fsdp", "rep"), None, None),
            P(("fsdp", "rep"), None, None),
            P("fsdp"),
            P("fsdp"),
            P("fsdp"),
        ),
        out_specs=(
            P(("fsdp", "rep"), None),
            P(("fsdp", "rep"), None),
            P(("fsdp", "rep"), None, None),
            P(("fsdp", "rep"), None, None),
            P(("fsdp", "rep"), None, None),
            P(("fsdp", "rep"), None, None),
            P("fsdp"),
            P("fsdp"),
            P("fsdp"),
            P("fsdp"),
        ),
        check_vma=False,
    )
```

profile of v0, /device:TPU:11, one launch (start us, length us, event | category | flops | bytes accessed | tf_op | source)
XLA Modules:
  0.0 2537.3 jit_solution(15324898715888444892)
XLA Ops:
  13.5 45.7 %all-reduce.134 = bf16[5696]{0:T(1024)(128)(2,1)S(1)} all-reduce(bf16[5696]{0:T(1024)(128)(2,1)S(1)} %dynamic-update-slice.2), channel_id=1, replica_groups=mesh['fsdp'=16,'rep'=2] {'fsdp'}, use_global_device_ids=true, to_apply=%add.134 | all-reduce | flops 5696 | bytes 22784
  73.0 46.2 %all-gather.10.cloned.1.call-done = bf16[1536,1536]{1,0:T(8,128)(2,1)} async-done(((bf16[96,1536]{1,0:T(8,128)(2,1)}), bf16[1536,1536]{1,0:T(8,128)(2,1)}) %all-gather.10.cloned.1.call-update) | async-done | bytes 4718608 | tf_op jit(solution)/shard_map/all_gather | solution.py:136
  122.9 50.5 %all-gather.8.cloned.1.call-done = bf16[1536,1536]{1,0:T(8,128)(2,1)} async-done(((bf16[96,1536]{1,0:T(8,128)(2,1)}), bf16[1536,1536]{1,0:T(8,128)(2,1)}) %all-gather.8.cloned.1.call-update) | async-done | bytes 4718608 | tf_op jit(solution)/shard_map/all_gather | solution.py:138
  178.2 20.9 fusion.77
  207.4 19.9 all-gather.14.cloned.1.call-done
  231.3 96.1 %all-gather.18.cloned.1.call-done = bf16[1536,4096]{1,0:T(8,128)(2,1)} async-done(((bf16[96,4096]{1,0:T(8,128)(2,1)}), bf16[1536,4096]{1,0:T(8,128)(2,1)}) %all-gather.18.cloned.1.call-update) | async-done | bytes 12582928 | tf_op jit(solution)/shard_map/all_gather | solution.py:141
  335.1 93.4 %all-gather.16.cloned.1.call-done = bf16[1536,4096]{1,0:T(8,128)(2,1)} async-done(((bf16[96,4096]{1,0:T(8,128)(2,1)}), bf16[1536,4096]{1,0:T(8,128)(2,1)}) %all-gather.16.cloned.1.call-update) | async-done | bytes 12582928 | tf_op jit(solution)/shard_map/all_gather | solution.py:140
  436.2 93.6 %all-gather.20.cloned.1.call-done = bf16[4096,1536]{1,0:T(8,128)(2,1)} async-done(((bf16[256,1536]{1,0:T(8,128)(2,1)}), bf16[4096,1536]{1,0:T(8,128)(2,1)}) %all-gather.20.cloned.1.call-update) | async-done | bytes 12582928 | tf_op jit(solution)/shard_map/all_gather | solution.py:142
  529.8 11.3 multiply_convert_fusion
  541.1 9.6 fusion.83
  550.7 9.9 multiply_reduce_fusion.66
  606.9 37.5 %pad_add_fusion = f32[16,133,138]{2,1,0:T(8,128)S(1)} fusion(f32[16,128,128]{2,1,0:T(8,128)} %get-tuple-element.274, f32[16,128,128]{2,1,0:T(8,128)} %get-tuple-element.275, f32[16,128,128]{2,1,0:T(8,128)} %get-tuple-element.276, f32[16,128,128]{2,1,0:T(8,128)} %get-tuple-element.277, f32[16,128,128]{2,1,0:T(8,128)} %get-tuple-element.278, ...), kind=kLoop, calls=%fused_computation.105 | loop fusion | flops 17326176 | bytes 64089216 | tf_op jit(solution)/shard_map/transpose(jvp())/add_any | solution.py:67
  683.8 462.9 %while.12 = (s32[]{:T(128)}, f32[16,8,512,512]{2,3,1,0:T(8,128)}, s32[16,8]{1,0:T(8,128)}, bf16[128,17,512]{2,0,1:T(8,128)(2,1)}, s32[16,8]{1,0:T(8,128)}, /*ind...) while((s32[]{:T(128)}, f32[16,8,512,512]{2,3,1,0:T(8,128)}, s32[16,8]{1,0:T(8,128)}, ...), condition=%wide.region_15.16_spmd, body=%wide.region_14.15_spmd.sunk | while | flops 540018816 | bytes 48243244 | solution.py:285
  696.0 9.1 copy.391
  724.9 9.1 copy.391
  753.8 9.1 copy.391
  782.8 9.1 copy.391
  811.7 9.1 copy.391
  840.6 9.1 copy.391
  869.5 9.1 copy.391
  898.5 9.1 copy.391
  927.4 9.1 copy.391
  956.3 9.1 copy.391
  985.2 9.1 copy.391
  1043.1 9.1 copy.391
  1101.0 9.1 copy.391
  1130.0 9.1 copy.391
  1157.1 1224.2 %reduce-scatter.2.cloned.1.call-done = f32[8,512,512]{1,2,0:T(8,128)} async-done(((f32[128,512,512]{1,2,0:T(8,128)}), f32[8,512,512]{1,2,0:T(8,128)}) %reduce-scatter.2.cloned.1.call-update) | async-done | bytes 8388624 | tf_op jit(solution)/shard_map/reduce_scatter | solution.py:284
  2411.2 46.2 %all-reduce.135 = bf16[5696]{0:T(1024)(128)(2,1)S(1)} all-reduce(f32[5696]{0:T(1024)S(1)} %concatenate.13), channel_id=3, replica_groups=mesh['fsdp'=16,'rep'=2] {'fsdp'}, use_global_device_ids=true, to_apply=%region_87.88.clone | all-reduce | flops 5696 | bytes 34176
  2472.2 24.7 all-reduce.138.cloned.1.call-done
  2503.0 9.5 fusion.11
  2520.8 9.5 fusion.80
  (590 shorter events, 541.4 us)
Async XLA Ops:
  7.2 62.3 %all-gather.12.cloned.1.call-start = ((), (), s32[]{:S(2)}) async-start(), calls=%async_computation.3 | async-start | bytes 5013504 | tf_op jit(solution)/shard_map/all_gather | solution.py:137
  8.0 111.3 %all-gather.10.cloned.1.call-start = ((), (), s32[]{:S(2)}) async-start(), calls=%async_computation.2 | async-start | bytes 5013504 | tf_op jit(solution)/shard_map/all_gather | solution.py:136
  8.7 164.6 %all-gather.8.cloned.1.call-start = ((), (), s32[]{:S(2)}) async-start(), calls=%async_computation.1 | async-start | bytes 5013504 | tf_op jit(solution)/shard_map/all_gather | solution.py:138
  9.5 217.8 %all-gather.14.cloned.1.call-start = ((), (), s32[]{:S(2)}) async-start(), calls=%async_computation.4 | async-start | bytes 5013504 | tf_op jit(solution)/shard_map/all_gather | solution.py:139
  10.0 317.4 %all-gather.18.cloned.1.call-start = ((), (), s32[]{:S(2)}) async-start(), calls=%async_computation.6 | async-start | bytes 13369344 | tf_op jit(solution)/shard_map/all_gather | solution.py:141
  10.6 417.9 %all-gather.16.cloned.1.call-start = ((), (), s32[]{:S(2)}) async-start(), calls=%async_computation.5 | async-start | bytes 13369344 | tf_op jit(solution)/shard_map/all_gather | solution.py:140
  11.2 518.6 %all-gather.20.cloned.1.call-start = ((), (), s32[]{:S(2)}) async-start(), calls=%async_computation.7 | async-start | bytes 13369344 | tf_op jit(solution)/shard_map/all_gather | solution.py:142
  12.0 2369.4 %reduce-scatter.2.cloned.1.call-start = ((), (), s32[]{:S(2)}) async-start(), calls=%async_computation.8 | async-start | bytes 142606336 | tf_op jit(solution)/shard_map/reduce_scatter | solution.py:284
  64.3 113.6 %copy-start.60 = (f32[16]{0:T(128)}, f32[16]{0:T(128)S(1)}, u32[]{:S(2)}) copy-start(f32[16]{0:T(128)S(1)} %get-tuple-element.223) | copy-start | bytes 196
  64.3 113.6 %copy-start.62 = (f32[16]{0:T(128)}, f32[16]{0:T(128)S(1)}, u32[]{:S(2)}) copy-start(f32[16]{0:T(128)S(1)} %get-tuple-element.224) | copy-start | bytes 196
  64.3 113.6 %copy-start.64 = (f32[16]{0:T(128)}, f32[16]{0:T(128)S(1)}, u32[]{:S(2)}) copy-start(f32[16]{0:T(128)S(1)} %get-tuple-element.225) | copy-start | bytes 196
  64.3 113.6 %copy-start.66 = (f32[16]{0:T(128)}, f32[16]{0:T(128)S(1)}, u32[]{:S(2)}) copy-start(f32[16]{0:T(128)S(1)} %get-tuple-element.226) | copy-start | bytes 196
  64.3 113.6 %copy-start.68 = (f32[16]{0:T(128)}, f32[16]{0:T(128)S(1)}, u32[]{:S(2)}) copy-start(f32[16]{0:T(128)S(1)} %get-tuple-element.227) | copy-start | bytes 196
  64.3 113.6 %copy-start.70 = (f32[16]{0:T(128)}, f32[16]{0:T(128)S(1)}, u32[]{:S(2)}) copy-start(f32[16]{0:T(128)S(1)} %get-tuple-element.228) | copy-start | bytes 196
  64.3 113.6 %copy-start.72 = (f32[16]{0:T(128)}, f32[16]{0:T(128)S(1)}, u32[]{:S(2)}) copy-start(f32[16]{0:T(128)S(1)} %get-tuple-element.229) | copy-start | bytes 196
  64.3 113.6 %copy-start.74 = (f32[16]{0:T(128)}, f32[16]{0:T(128)S(1)}, u32[]{:S(2)}) copy-start(f32[16]{0:T(128)S(1)} %get-tuple-element.230) | copy-start | bytes 196
  64.3 113.6 %copy-start.76 = (f32[16]{0:T(128)}, f32[16]{0:T(128)S(1)}, u32[]{:S(2)}) copy-start(f32[16]{0:T(128)S(1)} %get-tuple-element.231) | copy-start | bytes 196
  65.4 112.5 %copy-start.80 = (f32[16]{0:T(128)}, f32[16]{0:T(128)S(1)}, u32[]{:S(2)}) copy-start(f32[16]{0:T(128)S(1)} %get-tuple-element.218) | copy-start | bytes 196
  65.5 112.5 %copy-start.82 = (f32[16]{0:T(128)}, f32[16]{0:T(128)S(1)}, u32[]{:S(2)}) copy-start(f32[16]{0:T(128)S(1)} %get-tuple-element.219) | copy-start | bytes 196
  65.5 112.5 %copy-start.84 = (f32[16]{0:T(128)}, f32[16]{0:T(128)S(1)}, u32[]{:S(2)}) copy-start(f32[16]{0:T(128)S(1)} %get-tuple-element.220) | copy-start | bytes 196
  65.5 112.5 %copy-start.86 = (f32[16]{0:T(128)}, f32[16]{0:T(128)S(1)}, u32[]{:S(2)}) copy-start(f32[16]{0:T(128)S(1)} %get-tuple-element.221) | copy-start | bytes 196
  65.5 112.5 %copy-start.88 = (f32[16]{0:T(128)}, f32[16]{0:T(128)S(1)}, u32[]{:S(2)}) copy-start(f32[16]{0:T(128)S(1)} %get-tuple-element.222) | copy-start | bytes 196
  65.5 112.5 %copy-start.92 = (f32[16]{0:T(128)}, f32[16]{0:T(128)S(1)}, u32[]{:S(2)}) copy-start(f32[16]{0:T(128)S(1)} %get-tuple-element.205) | copy-start | bytes 196
  65.5 112.5 %copy-start.94 = (f32[16]{0:T(128)}, f32[16]{0:T(128)S(1)}, u32[]{:S(2)}) copy-start(f32[16]{0:T(128)S(1)} %get-tuple-element.206) | copy-start | bytes 196
  65.5 112.5 %copy-start.96 = (f32[16]{0:T(128)}, f32[16]{0:T(128)S(1)}, u32[]{:S(2)}) copy-start(f32[16]{0:T(128)S(1)} %get-tuple-element.207) | copy-start | bytes 196
  65.5 112.5 %copy-start.98 = (f32[16]{0:T(128)}, f32[16]{0:T(128)S(1)}, u32[]{:S(2)}) copy-start(f32[16]{0:T(128)S(1)} %get-tuple-element.208) | copy-start | bytes 196
  69.3 137.1 %copy-start.54 = (f32[1536]{0:T(1024)}, f32[1536]{0:T(1024)S(1)}, u32[]{:S(2)}) copy-start(f32[1536]{0:T(1024)S(1)} %get-tuple-element.336) | copy-start | bytes 18436
  177.9 397.3 %copy-start = (f32[16,133,128]{2,1,0:T(8,128)}, f32[16,133,128]{2,1,0:T(8,128)S(1)}, u32[]{:S(2)}) copy-start(f32[16,133,128]{2,1,0:T(8,128)S(1)} %fusion.24) | copy-start | bytes 3268612
  199.1 374.5 %copy-start.2 = (f32[16,128,128]{2,1,0:T(8,128)}, f32[16,128,128]{2,1,0:T(8,128)S(1)}, u32[]{:S(2)}) copy-start(f32[16,128,128]{2,1,0:T(8,128)S(1)} %get-tuple-element.256) | copy-start | bytes 3145732
  230.7 329.9 %copy-start.3 = (f32[128,1536]{1,0:T(8,128)}, f32[128,1536]{1,0:T(8,128)S(1)}, u32[]{:S(2)}) copy-start(f32[128,1536]{1,0:T(8,128)S(1)} %get-tuple-element.343) | copy-start | bytes 2359300
  335.1 194.7 %copy-start.141 = (f32[128]{0:T(128)S(1)}, f32[128]{0:T(128)}, u32[]{:S(2)}) copy-start(f32[128]{0:T(128)} %fusion.73) | copy-start | bytes 1540
  1146.7 1350.1 %all-reduce.138.cloned.1.call-start = ((), (), s32[]{:S(2)}) async-start(), calls=%async_computation.9 | async-start | bytes 8388608 | tf_op jit(solution)/shard_map/psum | solution.py:293
  (132 other events, 3098.3 us)
Sparse Core Ops, SparseCore 0:
  10.4 54.5 all-gather.11
  67.2 51.9 all-gather.9
  121.5 51.7 all-gather.7
  175.5 51.7 all-gather.13
  229.4 97.9 all-gather.17
  329.6 98.9 all-gather.15
  430.8 98.9 all-gather.19
  1146.9 1234.4 reduce-scatter.1
  2387.4 109.3 all-reduce.137
where the time goes:
time: 2550 us; the launch traced here: 2540 us
  waiting for transfers between devices  1650 us (65%)
  local copies, waits for them, and re-layouts  405 us (16%)
  matrix products  205 us (8%)
  other arithmetic  159 us (6%)
  blocking collectives  96.2 us (4%)
    reduce_scatter x1, waiting for transfers between devices, body(): lax.psum_scatter(lax.map(one_group, (left_ids, right_ids, filled)).reshap...  1220 us
    dynamic_update_slice x32, local copies, waits for them, and re-layouts, body(): lax.map(one_group, (left_ids, right_ids, filled))  268 us
    all_gather x1, waiting for transfers between devices, body(): lax.all_gather(local[5], 'fsdp', axis=0, tiled=True)  96.1 us
    all_gather x1, waiting for transfers between devices, body(): lax.all_gather(local[6], 'fsdp', axis=0, tiled=True)  93.6 us
    all_gather x1, waiting for transfers between devices, body(): lax.all_gather(local[4], 'fsdp', axis=0, tiled=True)  93.4 us
    unnamed x2, blocking collectives  92 us
    dot_general x16, matrix products, one_group(): jnp.einsum('tsi,tsj->sij', left_cols, right_cols, preferred_element_type=...  81.5 us
  transfers between devices with their start and end apart: 9, of which 8 were waited for; matrix products, arithmetic and copies ran while one was open for 4% of the time, Pallas kernels for 0%

commit v1 on v0

v1 whole, which is shorter than its diff:
```python
import math

import jax
import jax.numpy as jnp
import numpy as np
from jax import lax
from jax.experimental import pallas as pl
from jax.experimental.pallas import tpu as pltpu
from jax.sharding import Mesh
from jax.sharding import PartitionSpec as P

H = 16
DH = 96
HP = 128
D = H * DH
FF = 4096
CQ = 6
CK = 11
BLK = 512
CHIPS = 8
ROW_TILES = D // BLK
FF_TILES = FF // BLK

eps_norm = 1e-05
eps_adam = 1e-08
rate_block = 0.02
rate_vector = 0.3
decay_block = 0.1
beta_first = 0.5
beta_second = 0.5

FS = ("g", "a", "b", "c")
CHIP = ("y", "a", "b")
ALL = ("g", "a", "b", "c", "y")
bf16 = jnp.bfloat16
f32 = jnp.float32


def dot(left, right):
    return jnp.dot(left, right, preferred_element_type=f32)


def dot_nt(left, right):
    return lax.dot_general(left, right, (((1,), (1,)), ((), ())), preferred_element_type=f32)


def dot_tn(left, right):
    return lax.dot_general(left, right, (((0,), (0,)), ((), ())), preferred_element_type=f32)


def rms(values):
    return lax.rsqrt(jnp.mean(values * values, axis=-1, keepdims=True) + eps_norm)


def norm_backward(values, scale, gain, grad):
    unit = values * scale
    inner = grad * gain
    grad_values = scale * (inner - unit * jnp.mean(inner * unit, axis=-1, keepdims=True))
    return grad_values, jnp.sum(grad * unit, axis=0)


def shifted_down(pad_ref, values):
    rows = values.shape[0]
    pad_ref[8 : 8 + rows, :] = values
    return jnp.concatenate(
        [values] + [pad_ref[8 - lag : 8 - lag + rows, :] for lag in range(1, CQ)], axis=1
    )


def shifted_up(pad_ref, values):
    rows = values.shape[0]
    pad_ref[0:rows, :] = values
    return jnp.concatenate(
        [values] + [pad_ref[lag : lag + rows, :] for lag in range(1, CQ)], axis=1
    )


def attention_forward(len_ref, mix_ref, qkv_ref, toep_ref, gain_ref, heads_ref, s_ref, p_ref, o_ref, pad_ref):
    rows = qkv_ref.shape[1]
    length = len_ref[pl.program_id(0)]
    query_at = lax.broadcasted_iota(jnp.int32, (rows, rows), 0)
    key_at = lax.broadcasted_iota(jnp.int32, (rows, rows), 1)
    keep = (key_at <= query_at) & (key_at < length)
    pad_ref[0:8, :] = jnp.zeros((8, rows), f32)
    weights = []
    for head in range(2):
        query = qkv_ref[0, :, head * HP : (head + 1) * HP]
        key = qkv_ref[0, :, (2 + head) * HP : (3 + head) * HP]
        scores = jnp.where(keep, dot_nt(query, key) * (1.0 / math.sqrt(DH)), 0.0)
        s_ref[0, head] = scores.astype(bf16)
        wide = shifted_down(pad_ref, scores)
        high = wide.astype(bf16)
        low = (wide - high.astype(f32)).astype(bf16)
        conv = dot(high, toep_ref[head]) + dot(low, toep_ref[head])
        logits = jnp.where(keep, conv, -1e30)
        weight = jnp.exp(logits - jnp.max(logits, axis=-1, keepdims=True))
        weight = weight / jnp.sum(weight, axis=-1, keepdims=True)
        p_ref[0, head] = weight
        weights.append(weight)
    for head in range(2):
        mixed = mix_ref[2 * head] * weights[0] + mix_ref[2 * head + 1] * weights[1]
        value = qkv_ref[0, :, (4 + head) * HP : (5 + head) * HP]
        out = dot(mixed.astype(bf16), value)
        o_ref[0, :, head * HP : (head + 1) * HP] = out
        scale = lax.rsqrt(jnp.sum(out * out, axis=-1, keepdims=True) * (1.0 / DH) + eps_norm)
        heads_ref[0, :, head * HP : (head + 1) * HP] = (
            out * scale * gain_ref[:, head * HP : (head + 1) * HP]
        ).astype(bf16)


def attention_backward(
    len_ref, mix_ref, qkv_ref, toep_ref, gain_ref, s_ref, p_ref, o_ref, grad_ref,
    dqkv_ref, theta_ref, mixer_ref, gain_grad_ref, pad_ref,
):
    rows = qkv_ref.shape[1]
    length = len_ref[pl.program_id(0)]
    query_at = lax.broadcasted_iota(jnp.int32, (rows, rows), 0)
    key_at = lax.broadcasted_iota(jnp.int32, (rows, rows), 1)
    keep = (key_at <= query_at) & (key_at < length)
    pad_ref[rows : rows + 8, :] = jnp.zeros((8, rows), f32)

    @pl.when(pl.program_id(0) == 0)
    def _():
        theta_ref[...] = jnp.zeros_like(theta_ref)
        mixer_ref[...] = jnp.zeros_like(mixer_ref)
        gain_grad_ref[...] = jnp.zeros_like(gain_grad_ref)

    weights = [p_ref[0, 0], p_ref[0, 1]]
    grad_mixed = []
    for head in range(2):
        cols = slice(head * HP, (head + 1) * HP)
        out = o_ref[0, :, cols]
        grad = grad_ref[0, :, cols].astype(f32)
        scale = lax.rsqrt(jnp.sum(out * out, axis=-1, keepdims=True) * (1.0 / DH) + eps_norm)
        unit = out * scale
        gain_grad_ref[:, cols] += jnp.sum(grad * unit, axis=0, keepdims=True)
        inner = grad * gain_ref[:, cols]
        grad_out = scale * (inner - unit * (jnp.sum(inner * unit, axis=-1, keepdims=True) * (1.0 / DH)))
        grad_out = grad_out.astype(bf16)
        value = qkv_ref[0, :, (4 + head) * HP : (5 + head) * HP]
        mixed = (mix_ref[2 * head] * weights[0] + mix_ref[2 * head + 1] * weights[1]).astype(bf16)
        dqkv_ref[0, :, (4 + head) * HP : (5 + head) * HP] = dot_tn(mixed, grad_out).astype(bf16)
        back = dot_nt(grad_out, value)
        grad_mixed.append(back)
        for source in range(2):
            mixer_ref[2 * head + source : 2 * head + source + 1, :] += jnp.sum(
                back * weights[source], axis=0, keepdims=True
            )
    for head in range(2):
        grad_weight = mix_ref[head] * grad_mixed[0] + mix_ref[2 + head] * grad_mixed[1]
        weight = weights[head]
        grad_conv = weight * (grad_weight - jnp.sum(weight * grad_weight, axis=-1, keepdims=True))
        wide = shifted_up(pad_ref, grad_conv).astype(bf16)
        theta_ref[head] += dot_tn(s_ref[0, head], wide)
        grad_scores = jnp.zeros((rows, rows), f32)
        for lag in range(CQ):
            grad_scores += dot_nt(
                wide[:, lag * rows : (lag + 1) * rows], toep_ref[head, lag * rows : (lag + 1) * rows, :]
            )
        grad_scores = jnp.where(keep, grad_scores * (1.0 / math.sqrt(DH)), 0.0).astype(bf16)
        query = qkv_ref[0, :, head * HP : (head + 1) * HP]
        key = qkv_ref[0, :, (2 + head) * HP : (3 + head) * HP]
        dqkv_ref[0, :, head * HP : (head + 1) * HP] = dot(grad_scores, key).astype(bf16)
        dqkv_ref[0, :, (2 + head) * HP : (3 + head) * HP] = dot_tn(grad_scores, query).astype(bf16)


SMEM = pl.BlockSpec(memory_space=pltpu.SMEM)


def seq_spec(*dims):
    return pl.BlockSpec((1,) + dims, lambda s: (s,) + (0,) * len(dims))


def whole_spec(*dims):
    return pl.BlockSpec(dims, lambda s: (0,) * len(dims))


def run_forward(lengths, mix, qkv, toep, gain):
    seqs, rows, _ = qkv.shape
    return pl.pallas_call(
        attention_forward,
        grid=(seqs,),
        in_specs=[SMEM, SMEM, seq_spec(rows, 6 * HP), whole_spec(2, CQ * rows, rows), whole_spec(1, 2 * HP)],
        out_specs=[seq_spec(rows, 2 * HP), seq_spec(2, rows, rows), seq_spec(2, rows, rows), seq_spec(rows, 2 * HP)],
        out_shape=[
            jax.ShapeDtypeStruct((seqs, rows, 2 * HP), bf16),
            jax.ShapeDtypeStruct((seqs, 2, rows, rows), bf16),
            jax.ShapeDtypeStruct((seqs, 2, rows, rows), f32),
            jax.ShapeDtypeStruct((seqs, rows, 2 * HP), f32),
        ],
        scratch_shapes=[pltpu.VMEM((rows + 8, rows), f32)],
        name="attention_forward",
        compiler_params=pltpu.CompilerParams(vmem_limit_bytes=24 * 2**20),
        cost_estimate=pl.CostEstimate(flops=2 * 10**9, bytes_accessed=8 * 2**20, transcendentals=10**5),
    )(lengths, mix, qkv, toep, gain)


def run_backward(lengths, mix, qkv, toep, gain, scores, weights, outs, grads):
    seqs, rows, _ = qkv.shape
    return pl.pallas_call(
        attention_backward,
        grid=(seqs,),
        in_specs=[
            SMEM, SMEM, seq_spec(rows, 6 * HP), whole_spec(2, CQ * rows, rows), whole_spec(1, 2 * HP),
            seq_spec(2, rows, rows), seq_spec(2, rows, rows), seq_spec(rows, 2 * HP), seq_spec(rows, 2 * HP),
        ],
        out_specs=[seq_spec(rows, 6 * HP), whole_spec(2, rows, CQ * rows), whole_spec(8, rows), whole_spec(1, 2 * HP)],
        out_shape=[
            jax.ShapeDtypeStruct((seqs, rows, 6 * HP), bf16),
            jax.ShapeDtypeStruct((2, rows, CQ * rows), f32),
            jax.ShapeDtypeStruct((8, rows), f32),
            jax.ShapeDtypeStruct((1, 2 * HP), f32),
        ],
        scratch_shapes=[pltpu.VMEM((rows + 8, rows), f32)],
        name="attention_backward",
        compiler_params=pltpu.CompilerParams(vmem_limit_bytes=24 * 2**20),
        cost_estimate=pl.CostEstimate(flops=4 * 10**9, bytes_accessed=12 * 2**20, transcendentals=10**5),
    )(lengths, mix, qkv, toep, gain, scores, weights, outs, grads)


def gather_chips(rows):
    return lax.all_to_all(
        jnp.broadcast_to(rows[None], (CHIPS,) + rows.shape), CHIP, split_axis=0, concat_axis=0, tiled=True
    )


def exchange_chips(parts):
    return lax.all_to_all(parts, CHIP, split_axis=0, concat_axis=0, tiled=True)


def scatter_chips(parts):
    return jnp.sum(exchange_chips(parts.astype(bf16)).astype(f32), axis=0)


def swap(values, axis):
    return lax.ppermute(values, axis, [(0, 1), (1, 0)])


def both_cores(own, axis):
    other = swap(own, "c")
    first = lax.axis_index("c") == 0
    return jnp.stack([jnp.where(first, own, other), jnp.where(first, other, own)], axis=axis)


def half_for_core(values, axis):
    core = lax.axis_index("c")
    own = lax.dynamic_index_in_dim(values, core, axis, keepdims=False)
    sent = lax.dynamic_index_in_dim(values, 1 - core, axis, keepdims=False)
    return own + swap(sent.astype(bf16), "c").astype(f32)


def spread_columns(weight, width):
    rows = weight.shape[0]
    blocks = weight.reshape(rows, 2, CHIPS // 2, width)
    mine = lax.dynamic_index_in_dim(blocks, lax.axis_index("y"), 1, keepdims=False)
    return jnp.transpose(mine, (1, 0, 2))


def to_columns(blocks):
    groups = lax.axis_size("g")
    sent = jnp.broadcast_to(blocks[None], (groups,) + blocks.shape).reshape((-1,) + blocks.shape[1:])
    got = lax.all_to_all(sent, ("g", "a", "b"), split_axis=0, concat_axis=0, tiled=True)
    return both_cores(got, 1).reshape(-1, blocks.shape[-1])


def down_rows(w_down, chip):
    if lax.axis_size("g") == 2:
        other = swap(w_down, "g")
        mine = jnp.where(lax.axis_index("g") == lax.axis_index("y"), w_down, other)
        return both_cores(mine, 0).reshape(BLK, D)
    return lax.dynamic_slice_in_dim(lax.all_gather(w_down, FS, axis=0, tiled=True), chip * BLK, BLK, 0)


def band():
    tap = np.arange(CK)[:, None, None]
    source = np.arange(128)[None, :, None]
    target = np.arange(128)[None, None, :]
    return source - target + CK // 2 == tap


def body(
    layer_input, lengths, cotangent, w_query, w_key, w_value, w_out, w_gate, w_up, w_down, vec_copy, owners,
    basis_left, basis_right, block_master, block_first, block_second, vec_master, vec_first, vec_second,
):
    chip = (lax.axis_index("y") * 2 + lax.axis_index("a")) * 2 + lax.axis_index("b")
    fs_index = ((lax.axis_index("g") * 2 + lax.axis_index("a")) * 2 + lax.axis_index("b")) * 2 + lax.axis_index("c")
    seq_len = layer_input.shape[0]
    length = lengths[0]

    vector = lax.all_gather(vec_copy, FS, axis=0, tiled=True).astype(f32)
    gain_attn, gain_head, gain_ffn = vector[:D], vector[D : 2 * D], vector[2 * D : 3 * D]
    conv_end = 3 * D + H * CQ * CK
    theta = lax.dynamic_slice_in_dim(vector[3 * D : conv_end].reshape(H, CQ, CK), chip * 2, 2, 0)
    mixer = lax.dynamic_slice_in_dim(vector[conv_end : conv_end + 2 * H].reshape(H, 2), chip * 2, 2, 0)
    mix = mixer.reshape(4)
    gain_pair = jnp.pad(
        lax.dynamic_slice_in_dim(gain_head.reshape(H, DH), chip * 2, 2, 0), ((0, 0), (0, HP - DH))
    ).reshape(1, 2 * HP)
    toep = jnp.zeros((2, CQ, seq_len, seq_len), f32)
    offset = (
        jnp.arange(seq_len, dtype=jnp.int32)[:, None] - jnp.arange(seq_len, dtype=jnp.int32)[None, :] + CK // 2
    )
    for tap in range(CK):
        toep = jnp.where(offset[None, None] == tap, theta[:, :, tap][:, :, None, None], toep)
    toep = toep.astype(bf16).reshape(2, CQ * seq_len, seq_len)

    qkv_rows = to_columns(
        jnp.concatenate([spread_columns(w, 2 * DH) for w in (w_query, w_key, w_value)], axis=2)
    )
    w_qkv = jnp.pad(qkv_rows.reshape(D, 6, DH), ((0, 0), (0, 0), (0, HP - DH))).reshape(D, 6 * HP)
    w_in = to_columns(jnp.concatenate([spread_columns(w, BLK) for w in (w_gate, w_up)], axis=2))
    w_dn = down_rows(w_down, chip)
    w_o = lax.all_gather(w_out, FS, axis=0, tiled=True)

    group_lengths = lax.all_gather(lengths, CHIP, axis=0, tiled=True)
    input_float = layer_input.astype(f32)
    input_scale = rms(input_float)
    xn = gather_chips((input_float * input_scale * gain_attn).astype(bf16))
    xn_rows = xn.reshape(CHIPS * seq_len, D)
    qkv = dot(xn_rows, w_qkv).astype(bf16).reshape(CHIPS, seq_len, 6 * HP)
    heads_pad, scores, weights, outs = run_forward(group_lengths, mix, qkv, toep, gain_pair)
    heads_sent = heads_pad.reshape(CHIPS, seq_len, 2, HP)[..., :DH].reshape(CHIPS, seq_len, 2 * DH)
    heads = jnp.transpose(exchange_chips(heads_sent), (1, 0, 2)).reshape(seq_len, D)
    hmid = input_float + dot(heads, w_o)
    hmid_scale = rms(hmid)
    hn_rows = gather_chips((hmid * hmid_scale * gain_ffn).astype(bf16)).reshape(CHIPS * seq_len, D)
    both = dot(hn_rows, w_in)
    gate, up = both[:, :BLK], both[:, BLK:]
    sig = jax.nn.sigmoid(gate)
    silu = gate * sig
    inner = (silu * up).astype(bf16)
    ffn = scatter_chips(dot(inner, w_dn).reshape(CHIPS, seq_len, D))
    layer_output = (hmid + ffn).astype(bf16)

    valid = (jnp.arange(seq_len) < length).astype(f32)
    dy = cotangent.astype(f32) * valid[:, None]
    dy_rows = gather_chips(dy.astype(bf16)).reshape(CHIPS * seq_len, D)
    dinner = dot_nt(dy_rows, w_dn)
    dgate = (dinner * up * (sig * (1.0 + gate * (1.0 - sig)))).astype(bf16)
    dup = (dinner * silu).astype(bf16)
    dboth = jnp.concatenate([dgate, dup], axis=1)
    dhn = scatter_chips(dot_nt(dboth, w_in).reshape(CHIPS, seq_len, D))
    dhmid, grad_gain_ffn = norm_backward(hmid, hmid_scale, gain_ffn, dhn)
    dhmid = dhmid + dy
    dattn = dhmid.astype(bf16)
    dheads = dot_nt(dattn, w_o).astype(bf16).reshape(seq_len, CHIPS, 2 * DH)
    dheads = exchange_chips(jnp.transpose(dheads, (1, 0, 2)))
    dheads = jnp.pad(dheads.reshape(CHIPS, seq_len, 2, DH), ((0, 0), (0, 0), (0, 0), (0, HP - DH)))
    dqkv, theta_sums, mixer_sums, gain_sums = run_backward(
        group_lengths, mix, qkv, toep, gain_pair, scores, weights, outs, dheads.reshape(CHIPS, seq_len, 2 * HP)
    )
    dqkv_rows = dqkv.reshape(CHIPS * seq_len, 6 * HP)
    dxn = scatter_chips(dot_nt(dqkv_rows, w_qkv).reshape(CHIPS, seq_len, D))
    dinput, grad_gain_attn = norm_backward(input_float, input_scale, gain_attn, dxn)
    input_grad = dinput + dhmid

    taps = jnp.asarray(band())
    theta_sums = theta_sums.reshape(2, seq_len, CQ, seq_len)
    grad_theta = jnp.stack(
        [jnp.sum(jnp.where(taps[tap][None, :, None, :], theta_sums, 0.0), axis=(1, 3)) for tap in range(CK)], axis=2
    )
    grad_mixer = jnp.sum(mixer_sums[:4], axis=1)
    vector_grad = jnp.concatenate(
        [
            grad_gain_attn,
            lax.dynamic_update_slice_in_dim(
                jnp.zeros((D,), f32), gain_sums.reshape(2, HP)[:, :DH].reshape(-1), chip * 2 * DH, 0
            ),
            grad_gain_ffn,
            lax.dynamic_update_slice_in_dim(
                jnp.zeros((H * CQ * CK,), f32), grad_theta.reshape(-1), chip * 2 * CQ * CK, 0
            ),
            lax.dynamic_update_slice_in_dim(jnp.zeros((2 * H,), f32), grad_mixer, chip * 4, 0),
        ]
    )
    own_vec = vec_master.shape[0]
    vector_total = lax.dynamic_slice_in_dim(lax.psum(vector_grad, ALL), fs_index * own_vec, own_vec, 0)

    strip = BLK // (2 * CHIPS)
    grad_in = dot_tn(hn_rows, dboth).reshape(ROW_TILES, 2, CHIPS, strip, 2, BLK)
    grad_down = dot_tn(inner, dy_rows).reshape(2, CHIPS, strip, ROW_TILES, BLK)
    grad_in = jnp.transpose(half_for_core(grad_in, 1), (1, 3, 0, 2, 4)).reshape(CHIPS, 2 * ROW_TILES, strip, BLK)
    grad_down = jnp.transpose(half_for_core(grad_down, 0), (0, 2, 1, 3))
    ffn_tiles = exchange_chips(jnp.concatenate([grad_in, grad_down], axis=1).astype(bf16))
    gate_tiles = jnp.transpose(ffn_tiles[:, : 2 * ROW_TILES], (1, 0, 2, 3)).reshape(-1, strip, BLK)
    down_tiles = ffn_tiles[:, 2 * ROW_TILES :].reshape(-1, strip, BLK)
    grad_qkv = dot_tn(xn_rows, dqkv_rows).reshape(ROW_TILES, 2, CHIPS, strip, 6, HP)[..., :DH]
    grad_qkv = jnp.transpose(half_for_core(grad_qkv, 1), (1, 0, 2, 3, 4))
    grad_qkv = exchange_chips(grad_qkv.astype(bf16).reshape(CHIPS, ROW_TILES, strip, 6 * DH))
    grad_qkv = jnp.transpose(
        grad_qkv.reshape(CHIPS, ROW_TILES, strip, 3, 2 * DH), (3, 1, 2, 0, 4)
    ).reshape(3, ROW_TILES, strip, ROW_TILES, BLK)
    qkv_tiles = jnp.transpose(grad_qkv, (0, 1, 3, 2, 4)).reshape(-1, strip, BLK)
    heads_strips = jnp.transpose(heads.reshape(seq_len, 2 * ROW_TILES, CHIPS, strip), (2, 0, 1, 3))
    heads_strips = exchange_chips(heads_strips.reshape(CHIPS, seq_len, 2 * ROW_TILES * strip))
    dattn_rows = gather_chips(dattn).reshape(CHIPS * seq_len, D)
    grad_out = dot_tn(heads_strips.reshape(CHIPS * seq_len, -1), dattn_rows)
    grad_out = half_for_core(grad_out.reshape(ROW_TILES, 2, strip, ROW_TILES, BLK), 1)
    out_tiles = jnp.transpose(grad_out.astype(bf16), (0, 2, 1, 3)).reshape(-1, strip, BLK)
    tiles = jnp.concatenate([qkv_tiles, out_tiles, gate_tiles, down_tiles], axis=0)

    groups = lax.axis_size("g")
    part = strip // groups
    own_slots = basis_left.shape[0]
    devices = groups * 2 * CHIPS
    slot_total = own_slots * devices
    sums = lax.psum_scatter(tiles.astype(f32), "g", scatter_dimension=1, tiled=True).astype(bf16)
    matches = (jnp.arange(slot_total)[:, None] == owners[None, :]).astype(bf16)
    slots = dot(matches, sums.reshape(sums.shape[0], -1)).astype(bf16)
    slots = lax.all_to_all(
        slots.reshape(devices, own_slots, part, BLK), ALL, split_axis=0, concat_axis=0, tiled=True
    )
    slots = slots.reshape(groups, 2, 2, 2, 2, own_slots, part, BLK)
    own_grad = jnp.transpose(slots, (5, 3, 4, 1, 2, 0, 6, 7)).reshape(own_slots, BLK, BLK)

    left_low, right_low = basis_left.astype(bf16), basis_right.astype(bf16)
    rotated = jnp.einsum("sia,sij->saj", left_low, own_grad, preferred_element_type=f32)
    rotated = jnp.einsum("saj,sjb->sab", rotated.astype(bf16), right_low, preferred_element_type=f32)
    first_new = beta_first * block_first + (1.0 - beta_first) * rotated
    second_new = beta_second * block_second + (1.0 - beta_second) * rotated * rotated
    direction = (first_new / (jnp.sqrt(second_new) + eps_adam)).astype(bf16)
    turned = jnp.einsum("sia,sab->sib", left_low, direction, preferred_element_type=f32)
    turned = jnp.einsum("sib,sjb->sij", turned.astype(bf16), right_low, preferred_element_type=f32)
    master_new = block_master - rate_block * (turned + decay_block * block_master)
    vec_first_new = beta_first * vec_first + (1.0 - beta_first) * vector_total
    vec_second_new = beta_second * vec_second + (1.0 - beta_second) * vector_total * vector_total
    vec_master_new = vec_master - rate_vector * vec_first_new / (jnp.sqrt(vec_second_new) + eps_adam)
    return (
        layer_output, input_grad, first_new, second_new, master_new, master_new.astype(bf16),
        vec_first_new, vec_second_new, vec_master_new, vec_master_new.astype(bf16),
    )


def solution(mesh):
    fsdp, rep = mesh.shape["fsdp"], mesh.shape["rep"]
    fine = Mesh(mesh.devices.reshape(fsdp // 8, 2, 2, 2, rep), ALL)
    rows, both = P(ALL, None), P(ALL, None, None)
    weight, vec = P(FS, None), P(FS)
    return jax.shard_map(
        body,
        mesh=fine,
        in_specs=(rows, P(ALL), rows) + (weight,) * 7 + (vec, P()) + (both,) * 5 + (vec,) * 3,
        out_specs=(rows, rows) + (both,) * 4 + (vec,) * 4,
        check_vma=False,
    )
```

time: 2550 us -> 957 us (0.38)
  waiting for transfers between devices: 1650 us -> 315 us
  local copies, waits for them, and re-layouts: 405 us -> 169 us
  starting transfers between devices: 0.34 us -> 152 us
  matrix products: 205 us -> 80.3 us
  other arithmetic: 159 us -> 48.3 us
  blocking collectives: 96.2 us -> 139 us
    reduce_scatter x1, waiting for transfers between devices: 1220 us -> 138 us  [body(): lax.psum_scatter(tiles.astype(f32), 'g', scatter_dimension=1, tiled=True)]
    all_gather x7 -> x1, waiting for transfers between devices: 400 us -> 0.01 us  [body(): w_o = lax.all_gather(w_out, FS, axis=0, tiled=True)]
    dynamic_update_slice x32 -> x3, local copies, waits for them, and re-layouts: 268 us -> 0.73 us  [the longest x1 0.26 us: body(): lax.dynamic_update_slice_in_dim(jnp.zeros((D,), f32), gain_sums.reshape(2...]
    all_to_all x0 -> x15, starting transfers between devices: none -> 130 us  [the longest x8 46 us: exchange_chips(): return lax.all_to_all(parts, CHIP, split_axis=0, concat_axis=0, tiled=True)]
    dot_general x43 -> x15, matrix products: 205 us -> 80.3 us  [the longest x5 19.8 us: dot(): return jnp.dot(left, right, preferred_element_type=f32)]
    all_to_all x0 -> x15, waiting for transfers between devices: none -> 112 us  [the longest x8 62.9 us: exchange_chips(): return lax.all_to_all(parts, CHIP, split_axis=0, concat_axis=0, tiled=True)]
    gather x32 -> x0, local copies, waits for them, and re-layouts: 80.1 us -> none  [the longest x16 44.3 us: one_group(): right_cols = jnp.take(right_all, right_group, axis=1)]
    ppermute x0 -> x8, waiting for transfers between devices: none -> 63.1 us  [swap(): return lax.ppermute(values, axis, [(0, 1), (1, 0)])]
  transfers between devices with their start and end apart: 9 -> 25, of which waited for: 8 -> 13; matrix products, arithmetic and copies ran while one was open for 4% -> 26% of each run, Pallas kernels for 0% -> 2%
where the time goes in v1:
time: 957 us; the launch traced here: 942 us
  waiting for transfers between devices  315 us (33%)
  local copies, waits for them, and re-layouts  169 us (18%)
  starting transfers between devices  152 us (16%)
  blocking collectives  139 us (15%)
  matrix products  80.3 us (8%)
  other arithmetic  48.3 us (5%)
  Pallas kernels  22.7 us (2%)
  between operations  16.6 us (2%)
    reduce_scatter x1, waiting for transfers between devices, body(): lax.psum_scatter(tiles.astype(f32), 'g', scatter_dimension=1, tiled=True)  138 us
    unnamed x2, blocking collectives  84.7 us
    ppermute x8, waiting for transfers between devices, swap(): return lax.ppermute(values, axis, [(0, 1), (1, 0)])  63.1 us
    all_to_all x8, waiting for transfers between devices, exchange_chips(): return lax.all_to_all(parts, CHIP, split_axis=0, concat_axis=0, tiled=True)  62.9 us
    psum x1, blocking collectives, body(): lax.psum(vector_grad, ALL)  54.3 us
    all_to_all x4, waiting for transfers between devices, gather_chips(): lax.all_to_all(jnp.broadcast_to(rows[None], (CHIPS,) + rows.shape), CHIP,...  49.5 us
    all_to_all x8, starting transfers between devices, exchange_chips(): return lax.all_to_all(parts, CHIP, split_axis=0, concat_axis=0, tiled=True)  46 us
    all_to_all x2, starting transfers between devices, to_columns(): lax.all_to_all(sent, ('g', 'a', 'b'), split_axis=0, concat_axis=0, tiled=...  43.1 us
  transfers between devices with their start and end apart: 25, of which 13 were waited for; matrix products, arithmetic and copies ran while one was open for 26% of the time, Pallas kernels for 2%

profile of v1, /device:TPU:11, one launch (start us, length us, event | category | flops | bytes accessed | tf_op | source)
XLA Modules:
  0.0 942.3 jit_solution(7950001539311572858)
XLA Ops:
  11.9 5.7 all-to-all-start.1
  19.1 59.4 %all-reduce.4 = bf16[5696]{0:T(1024)(128)(2,1)S(1)} all-reduce(bf16[5696]{0:T(1024)(128)(2,1)S(1)} %dynamic-update-slice.1), channel_id=1, replica_groups=mesh['g'=2,'a'=2,'b'=2,'c'=2,'y'=2] {'g','a','b','c'}, use_global_device_ids=true, to_apply=%add.4 | all-reduce | flops 5696 | bytes 22784
  82.3 9.8 %all-to-all-start = ((bf16[8,128,1536]{1,2,0:T(8,128)(2,1)}), bf16[8,128,1536]{1,2,0:T(8,128)(2,1)S(1)}, u32[]{:S(2)}, u32[]{:S(2)}) async-start(bf16[8,128,1536]{1,2,0:T(8,128)(2,1)} %broadcast_in_dim.436), calls=%async_computation | async-start | bytes 6291456 | tf_op jit(solution)/shard_map/all_to_all | solution.py:222
  120.5 12.9 %all-to-all-done = bf16[8,128,1536]{1,2,0:T(8,128)(2,1)S(1)} async-done(((bf16[8,128,1536]{1,2,0:T(8,128)(2,1)}), bf16[8,128,1536]{1,2,0:T(8,128)(2,1)S(1)}, u32[]{:S(2)}, u32[]{:S(2)}) %all-to-all-start) | async-done | bytes 3145760 | tf_op jit(solution)/shard_map/all_to_all | solution.py:222
  136.5 37.5 %all-to-all-start.4 = ((bf16[8,96,1024]{2,1,0:T(8,128)(2,1)}), bf16[8,96,1024]{2,1,0:T(8,128)(2,1)}, u32[]{:S(2)}, u32[]{:S(2)}) async-start(bf16[8,96,1024]{2,1,0:T(8,128)(2,1)} %bitcast.360), calls=%async_computation.4 | async-start | bytes 3145728 | tf_op jit(solution)/shard_map/all_to_all | solution.py:262
  177.8 25.3 %all-reduce.3.len_ref = s32[8]{0:T(128)S(1)} all-reduce(s32[8]{0:T(128)} %copy-done.50), channel_id=1, replica_groups=mesh['g'=2,'a'=2,'b'=2,'c'=2,'y'=2] {'y','a','b'}, use_global_device_ids=true, to_apply=%add.3 | all-reduce | flops 8 | bytes 64
  222.6 5.8 copy.208
  233.7 5.2 copy.204
  243.5 9.1 attention_forward.1
  268.0 5.5 all-to-all-start.6
  277.2 36.5 %all-to-all-done.6 = bf16[8,128,1536]{1,2,0:T(8,128)(2,1)} async-done(((bf16[8,128,1536]{1,2,0:T(8,128)(2,1)}), bf16[8,128,1536]{1,2,0:T(8,128)(2,1)}, u32[]{:S(2)}, u32[]{:S(2)}) %all-to-all-start.6) | async-done | bytes 3145760 | tf_op jit(solution)/shard_map/all_to_all | solution.py:222
  315.9 10.1 %all-to-all-start.3 = ((bf16[8,128,1536]{1,2,0:T(8,128)(2,1)}), bf16[8,128,1536]{1,2,0:T(8,128)(2,1)}, u32[]{:S(2)}, u32[]{:S(2)}) async-start(bf16[8,128,1536]{1,2,0:T(8,128)(2,1)} %broadcast_in_dim.516), calls=%async_computation.3 | async-start | bytes 6291456 | tf_op jit(solution)/shard_map/all_to_all | solution.py:222
  325.9 6.2 collective-permute-start.2
  332.1 54.4 %collective-permute-done.2 = bf16[256,1536]{1,0:T(8,128)(2,1)S(1)} collective-permute-done((bf16[256,1536]{1,0:T(8,128)(2,1)S(1)}, bf16[256,1536]{1,0:T(8,128)(2,1)S(1)}, u32[]{:S(2)}, u32[]{:S(2)}) %collective-permute-start.2) | collective-permute-done | bytes 786464 | tf_op jit(solution)/shard_map/ppermute | solution.py:236
  403.2 5.0 all-to-all-start.11
  412.8 6.6 fusion.63
  440.2 7.6 convolution_convert_fusion.3
  447.8 29.1 %all-to-all-done.5 = bf16[8,128,1536]{2,1,0:T(8,128)(2,1)} async-done(((bf16[8,128,1536]{2,1,0:T(8,128)(2,1)}), bf16[8,128,1536]{2,1,0:T(8,128)(2,1)}, u32[]{:S(2)}, u32[]{:S(2)}) %all-to-all-start.5) | async-done | bytes 3145760 | tf_op jit(solution)/shard_map/all_to_all | solution.py:228
  476.9 9.9 %all-to-all-start.7 = ((bf16[8,128,1536]{2,1,0:T(8,128)(2,1)}), bf16[8,128,1536]{2,1,0:T(8,128)(2,1)}, u32[]{:S(2)}, u32[]{:S(2)}) async-start(bf16[8,128,1536]{2,1,0:T(8,128)(2,1)} %convolution_convert_fusion.3), calls=%async_computation.7 | async-start | bytes 6291456 | tf_op jit(solution)/shard_map/all_to_all | solution.py:228
  496.1 5.5 fusion.65
  521.1 5.0 all-to-all-done.7
  526.1 8.3 all-to-all-start.13
  543.6 20.0 %all-to-all-done.13 = bf16[8,9,32,512]{3,2,1,0:T(8,128)(2,1)} async-done(((bf16[8,9,32,512]{3,2,1,0:T(8,128)(2,1)}), bf16[8,9,32,512]{3,2,1,0:T(8,128)(2,1)}, u32[]{:S(2)}, u32[]{:S(2)}) %all-to-all-start.13) | async-done | bytes 2359328 | tf_op jit(solution)/shard_map/all_to_all | solution.py:228
  563.5 5.3 all-to-all-start.8
  575.4 6.5 all-to-all-start.12
  591.7 13.6 %attention_backward.1 = (bf16[8,128,768]{2,1,0:T(8,128)(2,1)S(1)}, f32[2,128,768]{2,1,0:T(8,128)S(1)}, f32[8,128]{1,0:T(8,128)S(1)}, f32[1,256]{1,0:T(1,128)S(1)}) custom-call(s32[8]{0:T(128)S(1)} %all-reduce.3.len_ref, f32[4]{0:T(128)S(1)} %reshape.413.mix_ref, bf16[8,128,768]{2,1,0:T(8,128)(2,1)S(1)} %bitcast.344, ...), custom_call_target="tpu_custom_call" | custom-call | flops 4000000000 | bytes 12582912 | tf_op jit(solution)/shard_map/attention_backward/pallas_call | solution.py:200
  666.4 5.6 convolution_convert_fusion.1
  685.0 138.4 %reduce-scatter.2.cloned.1.call-done = f32[108,16,512]{2,1,0:T(8,128)} async-done(((f32[108,32,512]{2,1,0:T(8,128)}), f32[108,16,512]{2,1,0:T(8,128)}) %reduce-scatter.2.cloned.1.call-update) | async-done | bytes 3538960 | tf_op jit(solution)/shard_map/reduce_scatter | solution.py:407
  829.9 8.8 all-to-all-start.14
  850.2 54.3 %psum.7 = f32[5696]{0:T(1024)S(1)} all-reduce(f32[5696]{0:T(1024)S(1)} %concatenate.24), channel_id=1, replica_groups=mesh['g'=2,'a'=2,'b'=2,'c'=2,'y'=2] {'g','a','b','c','y'}, use_global_device_ids=true, to_apply=%region_33.34 | all-reduce | flops 5696 | bytes 45568 | tf_op jit(solution)/shard_map/psum | solution.py:377
  909.1 12.7 %fusion = (f32[4,512,512]{2,1,0:T(8,128)}, f32[4,512,512]{2,1,0:T(8,128)}) fusion(f32[4,512,512]{2,1,0:T(8,128)} %param.37, f32[4,512,512]{2,1,0:T(8,128)} %param.36, f32[4,512,512]{2,1,0:T(8,128)} %param.34, bf16[4,512,512]{2,1,0:T(8,128)(2,1)} %bitcast.357, f32[4,512,512]{2,1,0:T(8,128)} %param.33), kind=kOutput, calls=%fused_computation.6 | convolution fusion | flops 2156920832 | bytes 27262976 | tf_op jit(solution)/shard_map/saj,sjb->sab/dot_general | solution.py:418
  921.8 13.5 %fusion.60 = (bf16[4,512,512]{2,1,0:T(8,128)(2,1)}, f32[4,512,512]{2,1,0:T(8,128)}) fusion(f32[4,512,512]{2,1,0:T(8,128)} %param.35, f32[4,512,512]{2,1,0:T(8,128)} %param.34, f32[4,512,512]{2,1,0:T(8,128)} %get-tuple-element.61, f32[4,512,512]{2,1,0:T(8,128)} %get-tuple-element.60, f32[4,512,512]{2,1,0:T(8,128)} %param.33), kind=kOutput, calls=%fused_computation.184 | convolution fusion | flops 2159017984 | bytes 27262976 | tf_op jit(solution)/shard_map/sib,sjb->sij/dot_general | solution.py:423
  (367 shorter events, 286.6 us)
Async XLA Ops:
  10.2 68.3 %copy-start.10 = (bf16[128,1536]{1,0:T(8,128)(2,1)S(1)}, bf16[128,1536]{1,0:T(8,128)(2,1)}, u32[]{:S(2)}) copy-start(bf16[128,1536]{1,0:T(8,128)(2,1)} %param.21) | copy-start | bytes 1179652
  11.9 68.3 %all-to-all-start.1 = ((bf16[8,96,576]{2,1,0:T(8,128)(2,1)}), bf16[8,96,576]{2,1,0:T(8,128)(2,1)S(1)}, u32[]{:S(2)}, u32[]{:S(2)}) async-start(bf16[8,96,576]{2,1,0:T(8,128)(2,1)} %bitcast.9), calls=%async_computation.1 | async-start | bytes 1966080 | tf_op jit(solution)/shard_map/all_to_all | solution.py:262
  82.3 51.1 %all-to-all-start = ((bf16[8,128,1536]{1,2,0:T(8,128)(2,1)}), bf16[8,128,1536]{1,2,0:T(8,128)(2,1)S(1)}, u32[]{:S(2)}, u32[]{:S(2)}) async-start(bf16[8,128,1536]{1,2,0:T(8,128)(2,1)} %broadcast_in_dim.436), calls=%async_computation | async-start | bytes 6291456 | tf_op jit(solution)/shard_map/all_to_all | solution.py:222
  92.1 181.5 %all-gather.2.cloned.1.call-start = ((), (), s32[]{:S(2)}) async-start(), calls=%async_computation.16 | async-start | bytes 5013504 | tf_op jit(solution)/shard_map/all_gather | solution.py:313
  133.4 43.1 %copy-start.8 = (bf16[8,128,1536]{1,2,0:T(8,128)(2,1)}, bf16[8,128,1536]{1,2,0:T(8,128)(2,1)S(1)}, u32[]{:S(2)}) copy-start(bf16[8,128,1536]{1,2,0:T(8,128)(2,1)S(1)} %all-to-all-done) | copy-start | bytes 9437188
  136.5 119.1 %all-to-all-start.4 = ((bf16[8,96,1024]{2,1,0:T(8,128)(2,1)}), bf16[8,96,1024]{2,1,0:T(8,128)(2,1)}, u32[]{:S(2)}, u32[]{:S(2)}) async-start(bf16[8,96,1024]{2,1,0:T(8,128)(2,1)} %bitcast.360), calls=%async_computation.4 | async-start | bytes 3145728 | tf_op jit(solution)/shard_map/all_to_all | solution.py:262
  176.6 43.0 %collective-permute-start = (bf16[8,96,576]{2,1,0:T(8,128)(2,1)}, bf16[8,96,576]{2,1,0:T(8,128)(2,1)}, u32[]{:S(2)}, u32[]{:S(2)}) collective-permute-start(bf16[8,96,576]{2,1,0:T(8,128)(2,1)} %copy-done.13), channel_id=1, source_target_pairs={{0,2},{2,0},{1,3},{3,1},{4,6},{6,4},{5,7},{7,5},{8,10},{10,8},{9,1... | collective-permute-start | bytes 2654216 | tf_op jit(solution)/shard_map/ppermute | solution.py:236
  177.8 41.8 %copy-start.14 = (bf16[8,96,576]{2,1,0:T(8,128)(2,1)S(1)}, bf16[8,96,576]{2,1,0:T(8,128)(2,1)}, u32[]{:S(2)}) copy-start(bf16[8,96,576]{2,1,0:T(8,128)(2,1)} %copy-done.13) | copy-start | bytes 2654212
  243.4 15.8 %copy-start.20 = (bf16[128,1536]{1,0:T(8,128)(2,1)S(1)}, bf16[128,1536]{1,0:T(8,128)(2,1)}, u32[]{:S(2)}) copy-start(bf16[128,1536]{1,0:T(8,128)(2,1)} %param.23) | copy-start | bytes 1179652
  255.6 10.4 %all-to-all-start.2 = ((bf16[8,128,192]{1,2,0:T(8,128)(2,1)}), bf16[8,128,192]{1,2,0:T(8,128)(2,1)S(1)}, u32[]{:S(2)}, u32[]{:S(2)}) async-start(bf16[8,128,192]{1,2,0:T(8,128)(2,1)} %bitcast.385), calls=%async_computation.2 | async-start | bytes 786432 | tf_op jit(solution)/shard_map/all_to_all | solution.py:228
  268.0 45.7 %all-to-all-start.6 = ((bf16[8,128,1536]{1,2,0:T(8,128)(2,1)}), bf16[8,128,1536]{1,2,0:T(8,128)(2,1)}, u32[]{:S(2)}, u32[]{:S(2)}) async-start(bf16[8,128,1536]{1,2,0:T(8,128)(2,1)} %broadcast_in_dim.518), calls=%async_computation.6 | async-start | bytes 6291456 | tf_op jit(solution)/shard_map/all_to_all | solution.py:222
  315.9 87.3 %all-to-all-start.3 = ((bf16[8,128,1536]{1,2,0:T(8,128)(2,1)}), bf16[8,128,1536]{1,2,0:T(8,128)(2,1)}, u32[]{:S(2)}, u32[]{:S(2)}) async-start(bf16[8,128,1536]{1,2,0:T(8,128)(2,1)} %broadcast_in_dim.516), calls=%async_computation.3 | async-start | bytes 6291456 | tf_op jit(solution)/shard_map/all_to_all | solution.py:222
  325.9 60.5 %collective-permute-start.2 = (bf16[256,1536]{1,0:T(8,128)(2,1)S(1)}, bf16[256,1536]{1,0:T(8,128)(2,1)S(1)}, u32[]{:S(2)}, u32[]{:S(2)}) collective-permute-start(bf16[256,1536]{1,0:T(8,128)(2,1)S(1)} %copy-done.25), channel_id=1, source_target_pairs={{0,16},{16,0},{1,17},{17,1},{2,18},{18,2},{3,19},{19,3},{4,20},{20... | collective-permute-start | bytes 2359304 | tf_op jit(solution)/shard_map/ppermute | solution.py:236
  386.6 5.3 collective-permute-start.3
  389.6 4.4 collective-permute-start.1
  403.2 27.5 %all-to-all-start.11 = ((bf16[8,128,192]{1,2,0:T(8,128)(2,1)}), bf16[8,128,192]{1,2,0:T(8,128)(2,1)S(1)}, u32[]{:S(2)}, u32[]{:S(2)}) async-start(bf16[8,128,192]{1,2,0:T(8,128)(2,1)} %bitcast.383), calls=%async_computation.11 | async-start | bytes 786432 | tf_op jit(solution)/shard_map/all_to_all | solution.py:228
  431.4 45.6 %all-to-all-start.5 = ((bf16[8,128,1536]{2,1,0:T(8,128)(2,1)}), bf16[8,128,1536]{2,1,0:T(8,128)(2,1)}, u32[]{:S(2)}, u32[]{:S(2)}) async-start(bf16[8,128,1536]{2,1,0:T(8,128)(2,1)} %convolution_convert_fusion.2), calls=%async_computation.5 | async-start | bytes 6291456 | tf_op jit(solution)/shard_map/all_to_all | solution.py:228
  476.9 49.2 %all-to-all-start.7 = ((bf16[8,128,1536]{2,1,0:T(8,128)(2,1)}), bf16[8,128,1536]{2,1,0:T(8,128)(2,1)}, u32[]{:S(2)}, u32[]{:S(2)}) async-start(bf16[8,128,1536]{2,1,0:T(8,128)(2,1)} %convolution_convert_fusion.3), calls=%async_computation.7 | async-start | bytes 6291456 | tf_op jit(solution)/shard_map/all_to_all | solution.py:228
  503.0 13.8 %collective-permute-start.6 = (bf16[3,8,32,2,512]{4,2,3,1,0:T(8,128)(2,1)}, bf16[3,8,32,2,512]{4,2,3,1,0:T(8,128)(2,1)S(1)}, u32[]{:S(2)}, u32[]{:S(2)}) collective-permute-start(bf16[3,8,32,2,512]{4,2,3,1,0:T(8,128)(2,1)} %fusion.10), channel_id=1, source_target_pairs={{0,2},{2,0},{1,3},{3,1},{4,6},{6,4},{5,7},{7,5},{8,10},{10,8},{9,1... | collective-permute-start | bytes 4718600 | tf_op jit(solution)/shard_map/ppermute | solution.py:236
  509.8 5.0 collective-permute-start.7
  526.1 37.4 %all-to-all-start.13 = ((bf16[8,9,32,512]{3,2,1,0:T(8,128)(2,1)}), bf16[8,9,32,512]{3,2,1,0:T(8,128)(2,1)}, u32[]{:S(2)}, u32[]{:S(2)}) async-start(bf16[8,9,32,512]{3,2,1,0:T(8,128)(2,1)} %pad_maximum_fusion.1), calls=%async_computation.13 | async-start | bytes 4718592 | tf_op jit(solution)/shard_map/all_to_all | solution.py:228
  563.5 9.8 %all-to-all-start.8 = ((bf16[8,128,192]{1,2,0:T(8,128)(2,1)}), bf16[8,128,192]{1,2,0:T(8,128)(2,1)S(1)}, u32[]{:S(2)}, u32[]{:S(2)}) async-start(bf16[8,128,192]{1,2,0:T(8,128)(2,1)} %bitcast.50), calls=%async_computation.8 | async-start | bytes 786432 | tf_op jit(solution)/shard_map/all_to_all | solution.py:228
  575.4 49.1 %all-to-all-start.12 = ((bf16[8,128,1536]{1,2,0:T(8,128)(2,1)}), bf16[8,128,1536]{1,2,0:T(8,128)(2,1)}, u32[]{:S(2)}, u32[]{:S(2)}) async-start(bf16[8,128,1536]{1,2,0:T(8,128)(2,1)} %broadcast_in_dim.519), calls=%async_computation.12 | async-start | bytes 6291456 | tf_op jit(solution)/shard_map/all_to_all | solution.py:222
  612.1 6.7 collective-permute-start.4
  624.5 24.5 %all-to-all-start.10 = ((bf16[8,3,32,576]{3,2,1,0:T(8,128)(2,1)}), bf16[8,3,32,576]{3,2,1,0:T(8,128)(2,1)}, u32[]{:S(2)}, u32[]{:S(2)}) async-start(bf16[8,3,32,576]{3,2,1,0:T(8,128)(2,1)} %reshape.438), calls=%async_computation.10 | async-start | bytes 1966080 | tf_op jit(solution)/shard_map/all_to_all | solution.py:228
  629.1 194.3 %reduce-scatter.2.cloned.1.call-start = ((), (), s32[]{:S(2)}) async-start(), calls=%async_computation.17 | async-start | bytes 10616832 | tf_op jit(solution)/shard_map/reduce_scatter | solution.py:407
  642.0 20.1 %collective-permute-start.5 = (bf16[3,32,3,512]{3,1,2,0:T(8,128)(2,1)S(1)}, bf16[3,32,3,512]{3,1,2,0:T(8,128)(2,1)S(1)}, u32[]{:S(2)}, u32[]{:S(2)}) collective-permute-start(bf16[3,32,3,512]{3,1,2,0:T(8,128)(2,1)S(1)} %fusion.38), channel_id=1, source_target_pairs={{0,2},{2,0},{1,3},{3,1},{4,6},{6,4},{5,7},{7,5},{8,10},{10,8},{9,1... | collective-permute-start | bytes 884744 | tf_op jit(solution)/shard_map/ppermute | solution.py:236
  672.2 157.7 %all-to-all-start.9 = ((bf16[8,128,1536]{2,1,0:T(8,128)(2,1)}), bf16[8,128,1536]{2,1,0:T(8,128)(2,1)}, u32[]{:S(2)}, u32[]{:S(2)}) async-start(bf16[8,128,1536]{2,1,0:T(8,128)(2,1)} %convolution_convert_fusion.1), calls=%async_computation.9 | async-start | bytes 6291456 | tf_op jit(solution)/shard_map/all_to_all | solution.py:228
  829.9 77.8 %all-to-all-start.14 = ((bf16[32,4,16,512]{3,2,1,0:T(8,128)(2,1)}), bf16[32,4,16,512]{3,2,1,0:T(8,128)(2,1)S(1)}, u32[]{:S(2)}, u32[]{:S(2)}) async-start(bf16[32,4,16,512]{3,2,1,0:T(8,128)(2,1)} %bitcast.208), calls=%async_computation.15 | async-start | bytes 4194304 | tf_op jit(solution)/shard_map/all_to_all | solution.py:410
  841.6 63.0 %copy-start.44 = (f32[356]{0:T(512)S(1)}, f32[356]{0:T(512)}, u32[]{:S(2)}) copy-start(f32[356]{0:T(512)} %param.38) | copy-start | bytes 4276
  841.6 63.0 %copy-start.45 = (f32[356]{0:T(512)S(1)}, f32[356]{0:T(512)}, u32[]{:S(2)}) copy-start(f32[356]{0:T(512)} %param.40) | copy-start | bytes 4276
  841.6 63.0 %copy-start.46 = (f32[356]{0:T(512)S(1)}, f32[356]{0:T(512)}, u32[]{:S(2)}) copy-start(f32[356]{0:T(512)} %param.39) | copy-start | bytes 4276
  (46 other events, 257.1 us)
Sparse Core Ops, SparseCore 0:
  95.2 70.9 all-gather.1
  666.6 156.7 reduce-scatter.1

commit v2 on v1

--- a/solution.py
+++ b/solution.py
@@ -218,7 +218,238 @@
     )(lengths, mix, qkv, toep, gain, scores, weights, outs, grads)
 
 
-def gather_chips(rows):
+BITS = {"y": 4, "a": 2, "b": 1}
+HOPS = (("y", "b", "a"), ("a", "y", "b"), ("b", "a", "y"))
+THIRDS = ((0, 48), (48, 48), (96, 32))
+ANYS = pl.BlockSpec(memory_space=pl.ANY)
+
+
+def chip_index():
+    return (lax.axis_index("y") * 2 + lax.axis_index("a")) * 2 + lax.axis_index("b")
+
+
+def flipped(chip, axes):
+    for axis in axes:
+        chip = chip + BITS[axis] * (1 - 2 * lax.axis_index(axis))
+    return chip
+
+
+def across(axis):
+    return {axis: 1 - lax.axis_index(axis)}
+
+
+def device_index():
+    index = lax.axis_index("g")
+    for axis in ("a", "b", "c", "y"):
+        index = index * lax.axis_size(axis) + lax.axis_index(axis)
+    return index
+
+
+def device_at(index):
+    at = {}
+    for axis in ("y", "c", "b", "a", "g"):
+        at[axis] = lax.rem(index, lax.axis_size(axis))
+        index = lax.div(index, lax.axis_size(axis))
+    return at
+
+
+def greet_all():
+    devices = lax.axis_size(ALL)
+    me = device_index()
+    barrier = pltpu.get_barrier_semaphore()
+
+    def greet(step, carry):
+        pl.semaphore_signal(barrier, inc=1, device_id=device_at(lax.rem(me + step, devices)))
+        return carry
+
+    lax.fori_loop(1, devices, greet, 0)
+    pl.semaphore_wait(barrier, devices - 1)
+
+
+def greet_neighbours():
+    barrier = pltpu.get_barrier_semaphore()
+    for axis in BITS:
+        pl.semaphore_signal(barrier, inc=1, device_id=across(axis))
+    pl.semaphore_wait(barrier, 3)
+
+
+def remote(src, dst, send, recv, axis):
+    return pltpu.make_async_remote_copy(src_ref=src, dst_ref=dst, send_sem=send, recv_sem=recv, device_id=across(axis))
+
+
+def gather_body(x_ref, out_ref, *sems):
+    greet_neighbours()
+    gather_hops(x_ref, out_ref, *sems)
+
+
+def gather_first_body(x_ref, vec_ref, out_ref, vecs_ref, vec_send, vec_recv, vec_local, *sems):
+    devices = lax.axis_size(ALL)
+    me = device_index()
+    local = pltpu.make_async_copy(vec_ref, vecs_ref.at[me], vec_local)
+    local.start()
+    greet_all()
+
+    def push(step, carry):
+        pltpu.make_async_remote_copy(
+            src_ref=vec_ref, dst_ref=vecs_ref.at[me], send_sem=vec_send, recv_sem=vec_recv,
+            device_id=device_at(lax.rem(me + step, devices)),
+        ).start()
+        return carry
+
+    lax.fori_loop(1, devices, push, 0)
+    gather_hops(x_ref, out_ref, *sems)
+    others = vecs_ref.at[pl.ds(0, devices - 1)]
+    pltpu.make_async_copy(others, others, vec_recv).wait()
+    pltpu.make_async_copy(others, others, vec_send).wait()
+    local.wait()
+
+
+def gather_hops(x_ref, out_ref, local_sem, send1, recv1, send2, recv2, send3, recv3):
+    me = chip_index()
+    rows = x_ref.shape[0]
+    half = rows // 2
+    local = pltpu.make_async_copy(x_ref, out_ref.at[me], local_sem)
+    local.start()
+    first = []
+    for part in range(2):
+        here = pl.ds(part * half, half)
+        for at, (axis, _, _) in enumerate(HOPS):
+            copy = remote(x_ref.at[here], out_ref.at[me, here], send1.at[at, part], recv1.at[at, part], axis)
+            copy.start()
+            first.append(copy)
+    second = []
+    for part in range(2):
+        here = pl.ds(part * half, half)
+        for at, (axis, onward, _) in enumerate(HOPS):
+            first[part * 3 + at].wait_recv()
+            block = out_ref.at[flipped(me, (axis,)), here]
+            copy = remote(block, block, send2.at[at, part], recv2.at[at, part], onward)
+            copy.start()
+            second.append(copy)
+    third = []
+    for at, (axis, onward, last) in enumerate(HOPS):
+        begin, count = THIRDS[at]
+        block = flipped(me, (axis, onward))
+        for part in range(2):
+            if part * half < begin + count and begin < (part + 1) * half:
+                second[part * 3 + at].wait_recv()
+        piece = out_ref.at[block, pl.ds(begin, count)]
+        copy = remote(piece, piece, send3.at[at], recv3.at[at], last)
+        copy.start()
+        third.append(copy)
+    for at in range(3):
+        begin, count = THIRDS[at]
+        for part in range(2):
+            if not (part * half < begin + count and begin < (part + 1) * half):
+                second[part * 3 + at].wait_recv()
+    for copy in third:
+        copy.wait_recv()
+    for copy in first + second + third:
+        copy.wait_send()
+    local.wait()
+
+
+def hop_sems():
+    dma = pltpu.SemaphoreType.DMA
+    return [dma] + [dma((3, 2))] * 4 + [dma((3,))] * 2
+
+
+def gather_first(rows, vec, collective_id):
+    count, width = rows.shape
+    return pl.pallas_call(
+        gather_first_body,
+        in_specs=[ANYS, ANYS],
+        out_specs=[ANYS, ANYS],
+        out_shape=[
+            jax.ShapeDtypeStruct((CHIPS, count, width), rows.dtype),
+            jax.ShapeDtypeStruct((lax.axis_size(ALL),) + vec.shape, vec.dtype),
+        ],
+        scratch_shapes=[pltpu.SemaphoreType.DMA] * 3 + hop_sems(),
+        name="gather_first",
+        compiler_params=pltpu.CompilerParams(collective_id=collective_id, has_side_effects=True),
+    )(rows, vec)
+
+
+def gather_chips(rows, collective_id):
+    count, width = rows.shape
+    return pl.pallas_call(
+        gather_body,
+        in_specs=[ANYS],
+        out_specs=ANYS,
+        out_shape=jax.ShapeDtypeStruct((CHIPS, count, width), rows.dtype),
+        scratch_shapes=hop_sems(),
+        name="gather_chips",
+        compiler_params=pltpu.CompilerParams(collective_id=collective_id, has_side_effects=True),
+    )(rows)
+
+
+def scatter_body(
+    parts_ref, out_ref, near_ref, in2_ref, in3_ref, acc2_ref, acc3_ref, send1, recv1, send2, recv2, send3, recv3
+):
+    me = chip_index()
+    greet_neighbours()
+    opposite = flipped(me, ("y", "a", "b"))
+    first = []
+    for at, (axis, onward, last) in enumerate(HOPS):
+        begin, count = THIRDS[at]
+        copy = remote(parts_ref.at[opposite, pl.ds(begin, count)], in2_ref.at[pl.ds(begin, count)], send1.at[at], recv1.at[at], last)
+        copy.start()
+        first.append(copy)
+    second = []
+    rows = parts_ref.shape[1]
+    half = rows // 2
+    for part in range(2):
+        here = pl.ds(part * half, half)
+        for at, (axis, onward, last) in enumerate(HOPS):
+            dest = flipped(me, (axis, onward))
+            begin, count = THIRDS[at]
+            if part == 0:
+                first[at].wait_recv()
+                acc2_ref[at] = parts_ref[dest]
+                piece = pl.ds(begin, count)
+                acc2_ref[at, piece] = (parts_ref[dest, piece].astype(f32) + in2_ref[piece].astype(f32)).astype(bf16)
+            copy = remote(acc2_ref.at[at, here], in3_ref.at[at, here], send2.at[at, part], recv2.at[at, part], onward)
+            copy.start()
+            second.append(copy)
+    third = []
+    for part in range(2):
+        here = pl.ds(part * half, half)
+        for at, (axis, onward, last) in enumerate(HOPS):
+            dest = flipped(me, (axis,))
+            second[part * 3 + at].wait_recv()
+            acc3_ref[at, here] = (parts_ref[dest, here].astype(f32) + in3_ref[at, here].astype(f32)).astype(bf16)
+            copy = remote(acc3_ref.at[at, here], near_ref.at[at, here], send3.at[at, part], recv3.at[at, part], axis)
+            copy.start()
+            third.append(copy)
+    for part in range(2):
+        here = pl.ds(part * half, half)
+        for at in range(3):
+            third[part * 3 + at].wait_recv()
+        out_ref[here] = (
+            (parts_ref[me, here].astype(f32) + near_ref[0, here].astype(f32))
+            + (near_ref[1, here].astype(f32) + near_ref[2, here].astype(f32))
+        )
+    for copy in first + second + third:
+        copy.wait_send()
+
+
+def scatter_chips(parts, collective_id):
+    _, rows, width = parts.shape
+    vmem = pl.BlockSpec(memory_space=pltpu.VMEM)
+    dma = pltpu.SemaphoreType.DMA
+    return pl.pallas_call(
+        scatter_body,
+        in_specs=[vmem],
+        out_specs=vmem,
+        out_shape=jax.ShapeDtypeStruct((rows, width), f32),
+        scratch_shapes=[pltpu.VMEM((3, rows, width), bf16), pltpu.VMEM((rows, width), bf16)] + [pltpu.VMEM((3, rows, width), bf16)] * 3
+        + [dma((3,))] * 2 + [dma((3, 2))] * 4,
+        name="scatter_chips",
+        compiler_params=pltpu.CompilerParams(collective_id=collective_id, has_side_effects=True, vmem_limit_bytes=32*2**20),
+    )(parts)
+
+
+def gather_slow(rows):
     return lax.all_to_all(
         jnp.broadcast_to(rows[None], (CHIPS,) + rows.shape), CHIP, split_axis=0, concat_axis=0, tiled=True
     )
@@ -228,7 +459,7 @@
     return lax.all_to_all(parts, CHIP, split_axis=0, concat_axis=0, tiled=True)
 
 
-def scatter_chips(parts):
+def scatter_slow(parts):
     return jnp.sum(exchange_chips(parts.astype(bf16)).astype(f32), axis=0)
 
 
@@ -247,6 +478,17 @@
     own = lax.dynamic_index_in_dim(values, core, axis, keepdims=False)
     sent = lax.dynamic_index_in_dim(values, 1 - core, axis, keepdims=False)
     return own + swap(sent.astype(bf16), "c").astype(f32)
+
+
+def sum_groups(tiles):
+    groups = lax.axis_size("g")
+    if groups != 2:
+        return lax.psum_scatter(tiles.astype(f32), "g", scatter_dimension=1, tiled=True).astype(bf16)
+    part = tiles.shape[1] // 2
+    group = lax.axis_index("g")
+    own = lax.dynamic_slice_in_dim(tiles, group * part, part, 1)
+    sent = lax.dynamic_slice_in_dim(tiles, (1 - group) * part, part, 1)
+    return (own.astype(f32) + swap(sent, "g").astype(f32)).astype(bf16)
 
 
 def spread_columns(weight, width):
@@ -286,8 +528,20 @@
     fs_index = ((lax.axis_index("g") * 2 + lax.axis_index("a")) * 2 + lax.axis_index("b")) * 2 + lax.axis_index("c")
     seq_len = layer_input.shape[0]
     length = lengths[0]
-
-    vector = lax.all_gather(vec_copy, FS, axis=0, tiled=True).astype(f32)
+    reps = lax.axis_size("y")
+    fs_size = lax.axis_size(FS)
+
+    own_vec = vec_copy.shape[0]
+    small = jnp.concatenate(
+        [vec_copy.astype(f32), jnp.zeros((1023 - own_vec,), f32), length.astype(f32).reshape(1)]
+    ).reshape(8, 128)
+    x_all, small_all = gather_first(layer_input, small, 1)
+    small_all = small_all.reshape(fs_size, reps, 1024)
+    vector = small_all[:, 0, :own_vec].reshape(-1)
+    group_lengths = small_all[:, :, 1023].reshape(-1, 2, 2, 2, reps)
+    group_lengths = lax.dynamic_index_in_dim(group_lengths, lax.axis_index("g"), 0, keepdims=False)
+    group_lengths = lax.dynamic_index_in_dim(group_lengths, lax.axis_index("c"), 2, keepdims=False)
+    group_lengths = jnp.transpose(group_lengths, (2, 0, 1)).reshape(CHIPS).astype(jnp.int32)
     gain_attn, gain_head, gain_ffn = vector[:D], vector[D : 2 * D], vector[2 * D : 3 * D]
     conv_end = 3 * D + H * CQ * CK
     theta = lax.dynamic_slice_in_dim(vector[3 * D : conv_end].reshape(H, CQ, CK), chip * 2, 2, 0)
@@ -312,34 +566,33 @@
     w_dn = down_rows(w_down, chip)
     w_o = lax.all_gather(w_out, FS, axis=0, tiled=True)
 
-    group_lengths = lax.all_gather(lengths, CHIP, axis=0, tiled=True)
     input_float = layer_input.astype(f32)
     input_scale = rms(input_float)
-    xn = gather_chips((input_float * input_scale * gain_attn).astype(bf16))
-    xn_rows = xn.reshape(CHIPS * seq_len, D)
+    x_rows = x_all.reshape(CHIPS * seq_len, D).astype(f32)
+    xn_rows = (x_rows * rms(x_rows) * gain_attn).astype(bf16)
     qkv = dot(xn_rows, w_qkv).astype(bf16).reshape(CHIPS, seq_len, 6 * HP)
     heads_pad, scores, weights, outs = run_forward(group_lengths, mix, qkv, toep, gain_pair)
     heads_sent = heads_pad.reshape(CHIPS, seq_len, 2, HP)[..., :DH].reshape(CHIPS, seq_len, 2 * DH)
     heads = jnp.transpose(exchange_chips(heads_sent), (1, 0, 2)).reshape(seq_len, D)
     hmid = input_float + dot(heads, w_o)
     hmid_scale = rms(hmid)
-    hn_rows = gather_chips((hmid * hmid_scale * gain_ffn).astype(bf16)).reshape(CHIPS * seq_len, D)
+    hn_rows = gather_chips((hmid * hmid_scale * gain_ffn).astype(bf16), 2).reshape(CHIPS * seq_len, D)
     both = dot(hn_rows, w_in)
     gate, up = both[:, :BLK], both[:, BLK:]
     sig = jax.nn.sigmoid(gate)
     silu = gate * sig
     inner = (silu * up).astype(bf16)
-    ffn = scatter_chips(dot(inner, w_dn).reshape(CHIPS, seq_len, D))
+    ffn = scatter_slow(dot(inner, w_dn).reshape(CHIPS, seq_len, D))
     layer_output = (hmid + ffn).astype(bf16)
 
     valid = (jnp.arange(seq_len) < length).astype(f32)
     dy = cotangent.astype(f32) * valid[:, None]
-    dy_rows = gather_chips(dy.astype(bf16)).reshape(CHIPS * seq_len, D)
+    dy_rows = gather_slow(dy.astype(bf16)).reshape(CHIPS * seq_len, D)
     dinner = dot_nt(dy_rows, w_dn)
     dgate = (dinner * up * (sig * (1.0 + gate * (1.0 - sig)))).astype(bf16)
     dup = (dinner * silu).astype(bf16)
     dboth = jnp.concatenate([dgate, dup], axis=1)
-    dhn = scatter_chips(dot_nt(dboth, w_in).reshape(CHIPS, seq_len, D))
+    dhn = scatter_chips(dot_nt(dboth, w_in).astype(bf16).reshape(CHIPS, seq_len, D), 3)
     dhmid, grad_gain_ffn = norm_backward(hmid, hmid_scale, gain_ffn, dhn)
     dhmid = dhmid + dy
     dattn = dhmid.astype(bf16)
@@ -350,7 +603,7 @@
         group_lengths, mix, qkv, toep, gain_pair, scores, weights, outs, dheads.reshape(CHIPS, seq_len, 2 * HP)
     )
     dqkv_rows = dqkv.reshape(CHIPS * seq_len, 6 * HP)
-    dxn = scatter_chips(dot_nt(dqkv_rows, w_qkv).reshape(CHIPS, seq_len, D))
+    dxn = scatter_slow(dot_nt(dqkv_rows, w_qkv).reshape(CHIPS, seq_len, D))
     dinput, grad_gain_attn = norm_backward(input_float, input_scale, gain_attn, dxn)
     input_grad = dinput + dhmid
 
@@ -373,8 +626,11 @@
             lax.dynamic_update_slice_in_dim(jnp.zeros((2 * H,), f32), grad_mixer, chip * 4, 0),
         ]
     )
-    own_vec = vec_master.shape[0]
-    vector_total = lax.dynamic_slice_in_dim(lax.psum(vector_grad, ALL), fs_index * own_vec, own_vec, 0)
+    pieces = jnp.pad(vector_grad.reshape(fs_size, 1, own_vec), ((0, 0), (0, 0), (0, 512 - own_vec)))
+    pieces = jnp.broadcast_to(pieces, (fs_size, reps, 512)).reshape(-1, 4, 128)
+    vector_total = jnp.sum(
+        lax.all_to_all(pieces, ALL, split_axis=0, concat_axis=0, tiled=True), axis=0
+    ).reshape(512)[:own_vec]
 
     strip = BLK // (2 * CHIPS)
     grad_in = dot_tn(hn_rows, dboth).reshape(ROW_TILES, 2, CHIPS, strip, 2, BLK)
@@ -393,18 +649,20 @@
     qkv_tiles = jnp.transpose(grad_qkv, (0, 1, 3, 2, 4)).reshape(-1, strip, BLK)
     heads_strips = jnp.transpose(heads.reshape(seq_len, 2 * ROW_TILES, CHIPS, strip), (2, 0, 1, 3))
     heads_strips = exchange_chips(heads_strips.reshape(CHIPS, seq_len, 2 * ROW_TILES * strip))
-    dattn_rows = gather_chips(dattn).reshape(CHIPS * seq_len, D)
+    dattn_rows = gather_slow(dattn).reshape(CHIPS * seq_len, D)
     grad_out = dot_tn(heads_strips.reshape(CHIPS * seq_len, -1), dattn_rows)
     grad_out = half_for_core(grad_out.reshape(ROW_TILES, 2, strip, ROW_TILES, BLK), 1)
     out_tiles = jnp.transpose(grad_out.astype(bf16), (0, 2, 1, 3)).reshape(-1, strip, BLK)
-    tiles = jnp.concatenate([qkv_tiles, out_tiles, gate_tiles, down_tiles], axis=0)
 
     groups = lax.axis_size("g")
     part = strip // groups
     own_slots = basis_left.shape[0]
     devices = groups * 2 * CHIPS
     slot_total = own_slots * devices
-    sums = lax.psum_scatter(tiles.astype(f32), "g", scatter_dimension=1, tiled=True).astype(bf16)
+    sums = jnp.concatenate(
+        [sum_groups(jnp.concatenate([qkv_tiles, out_tiles], axis=0)), sum_groups(jnp.concatenate([gate_tiles, down_tiles], axis=0))],
+        axis=0,
+    )
     matches = (jnp.arange(slot_total)[:, None] == owners[None, :]).astype(bf16)
     slots = dot(matches, sums.reshape(sums.shape[0], -1)).astype(bf16)
     slots = lax.all_to_all(

time: 957 us -> 737 us (0.77)
  waiting for transfers between devices: 315 us -> 131 us
  Pallas kernels: 22.7 us -> 199 us
  blocking collectives: 139 us -> 0 us
  local copies, waits for them, and re-layouts: 169 us -> 129 us
  starting transfers between devices: 152 us -> 116 us
    pallas_call x0 -> x3, Pallas kernels: none -> 177 us  [the longest x1 106 us: gather_first(): pl.pallas_call(gather_first_body, in_specs=[ANYS, ANYS], out_specs=[ANYS,...]
    reduce_scatter x1 -> x0, waiting for transfers between devices: 138 us -> none  [body(): lax.psum_scatter(tiles.astype(f32), 'g', scatter_dimension=1, tiled=True)]
    unnamed x2 -> x0, blocking collectives: 84.7 us -> none
    psum x1 -> x0, blocking collectives: 54.3 us -> none  [body(): lax.psum(vector_grad, ALL)]
    all_to_all x8 -> x7, waiting for transfers between devices: 62.9 us -> 13 us  [exchange_chips(): return lax.all_to_all(parts, CHIP, split_axis=0, concat_axis=0, tiled=True)]
    ppermute x8 -> x10, waiting for transfers between devices: 63.1 us -> 19.2 us  [swap(): return lax.ppermute(values, axis, [(0, 1), (1, 0)])]
    all_to_all x1, waiting for transfers between devices: 0.01 us -> 42.7 us  [body(): lax.all_to_all(slots.reshape(devices, own_slots, part, BLK), ALL, split_a...]
    all_to_all x2, starting transfers between devices: 43.1 us -> 12.1 us  [to_columns(): lax.all_to_all(sent, ('g', 'a', 'b'), split_axis=0, concat_axis=0, tiled=...]
  transfers between devices with their start and end apart: 25 -> 24, of which waited for: 13 -> 9; matrix products, arithmetic and copies ran while one was open for 26% -> 26% of each run, Pallas kernels for 2% -> 24%
where the time goes in v2:
time: 737 us; the launch traced here: 725 us
  Pallas kernels  199 us (27%)
  waiting for transfers between devices  131 us (18%)
  local copies, waits for them, and re-layouts  129 us (18%)
  starting transfers between devices  116 us (16%)
  matrix products  77.3 us (10%)
  other arithmetic  55.8 us (8%)
  between operations  16.8 us (2%)
    pallas_call x1, Pallas kernels, gather_first(): pl.pallas_call(gather_first_body, in_specs=[ANYS, ANYS], out_specs=[ANYS,...  106 us
    pallas_call x1, Pallas kernels, scatter_chips(): pl.pallas_call(scatter_body, in_specs=[vmem], out_specs=vmem, out_shape=j...  48.8 us
    all_to_all x7, starting transfers between devices, exchange_chips(): return lax.all_to_all(parts, CHIP, split_axis=0, concat_axis=0, tiled=True)  42.7 us
    all_to_all x1, waiting for transfers between devices, body(): lax.all_to_all(slots.reshape(devices, own_slots, part, BLK), ALL, split_a...  42.7 us
    all_to_all x2, waiting for transfers between devices, gather_slow(): lax.all_to_all(jnp.broadcast_to(rows[None], (CHIPS,) + rows.shape), CHIP,...  35.4 us
    pallas_call x1, Pallas kernels, gather_chips(): pl.pallas_call(gather_body, in_specs=[ANYS], out_specs=ANYS, out_shape=ja...  21.8 us
    all_to_all x1, starting transfers between devices, body(): lax.all_to_all(pieces, ALL, split_axis=0, concat_axis=0, tiled=True)  21.6 us
    unnamed x202, local copies, waits for them, and re-layouts  20.9 us
  transfers between devices with their start and end apart: 24, of which 9 were waited for; matrix products, arithmetic and copies ran while one was open for 26% of the time, Pallas kernels for 24%

profile of v2, /device:TPU:11, one launch (start us, length us, event | category | flops | bytes accessed | tf_op | source)
XLA Modules:
  0.0 724.6 jit_solution(4588027389229644387)
XLA Ops:
  11.9 5.7 all-to-all-start
  19.3 20.1 %all-to-all-done = bf16[8,96,576]{2,1,0:T(8,128)(2,1)S(1)} async-done(((bf16[8,96,576]{2,1,0:T(8,128)(2,1)}), bf16[8,96,576]{2,1,0:T(8,128)(2,1)S(1)}, u32[]{:S(2)}, u32[]{:S(2)}) %all-to-all-start) | async-done | bytes 884768 | tf_op jit(solution)/shard_map/all_to_all | solution.py:504
  40.8 6.5 all-to-all-start.2
  51.5 105.9 %gather_first.1 = (bf16[8,128,1536]{2,1,0:T(8,128)(2,1)}, f32[32,8,128]{2,1,0:T(8,128)}) custom-call(bf16[128,1536]{1,0:T(8,128)(2,1)} %x_ref.1, f32[8,128]{1,0:T(8,128)} %maximum_bitcast_fusion.vec_ref), custom_call_target="tpu_custom_call" | custom-call | tf_op jit(solution)/shard_map/gather_first/pallas_call | solution.py:359
  183.5 8.4 %all-to-all-start.4 = ((bf16[8,128,1536]{1,2,0:T(8,128)(2,1)}), bf16[8,128,1536]{1,2,0:T(8,128)(2,1)}, u32[]{:S(2)}, u32[]{:S(2)}) async-start(bf16[8,128,1536]{1,2,0:T(8,128)(2,1)} %broadcast_in_dim.516), calls=%async_computation.4 | async-start | bytes 6291456 | tf_op jit(solution)/shard_map/all_to_all | solution.py:453
  204.7 5.8 copy.371
  219.2 9.1 %attention_forward.1 = (bf16[8,128,256]{2,1,0:T(8,128)(2,1)S(1)}, bf16[8,2,128,128]{3,2,1,0:T(8,128)(2,1)S(1)}, f32[8,2,128,128]{3,2,1,0:T(8,128)S(1)}, f32[8,128,256]{2,1,0:T(8,128)S(1)}) custom-call(s32[8]{0:T(128)S(1)} %convert_element_type.197.len_ref, f32[4]{0:T(128)S(1)} %reshape.460.mix_ref, bf16[8,128,768]{2,1,0:T(8,128)(2,1)S(1)} %bitcast.363, ...), custom_call_target="tpu_custom_call" | custom-call | flops 2000000000 | bytes 8388608 | tf_op jit(solution)/shard_map/attention_forward/pallas_call | solution.py:180
  234.5 8.7 %all-to-all-start.1 = ((bf16[8,128,192]{1,2,0:T(8,128)(2,1)}), bf16[8,128,192]{1,2,0:T(8,128)(2,1)S(1)}, u32[]{:S(2)}, u32[]{:S(2)}) async-start(bf16[8,128,192]{1,2,0:T(8,128)(2,1)} %bitcast.30), calls=%async_computation.1 | async-start | bytes 786432 | tf_op jit(solution)/shard_map/all_to_all | solution.py:459
  249.7 4.7 copy.378
  258.5 21.8 %gather_chips.1 = bf16[8,128,1536]{2,1,0:T(8,128)(2,1)} custom-call(bf16[128,1536]{1,0:T(8,128)(2,1)} %multiply_convert_fusion.4.x_ref), custom_call_target="tpu_custom_call" | custom-call | tf_op jit(solution)/shard_map/gather_chips/pallas_call | solution.py:375
  280.4 6.6 fusion.79
  292.3 5.2 convolution_convert_fusion.2
  297.5 6.0 all-to-all-start.3
  308.9 6.0 convolution_convert_fusion.3
  314.9 48.8 %scatter_chips.1 = f32[128,1536]{1,0:T(8,128)S(1)} custom-call(bf16[8,128,1536]{2,1,0:T(8,128)(2,1)S(1)} %bitcast.358), custom_call_target="tpu_custom_call" | custom-call | tf_op jit(solution)/shard_map/scatter_chips/pallas_call | solution.py:440
  385.8 4.8 all-to-all-start.8
  411.3 4.9 all-to-all-start.10
  430.3 13.6 %attention_backward.1 = (bf16[8,128,768]{2,1,0:T(8,128)(2,1)S(1)}, f32[2,128,768]{2,1,0:T(8,128)S(1)}, f32[8,128]{1,0:T(8,128)S(1)}, f32[1,256]{1,0:T(1,128)S(1)}) custom-call(s32[8]{0:T(128)S(1)} %convert_element_type.197.len_ref, f32[4]{0:T(128)S(1)} %reshape.460.mix_ref, bf16[8,128,768]{2,1,0:T(8,128)(2,1)S(1)} %bitcast.364, ...), custom_call_target="tpu_custom_call" | custom-call | flops 4000000000 | bytes 12582912 | tf_op jit(solution)/shard_map/attention_backward/pallas_call | solution.py:200
  445.5 4.9 fusion.19
  466.1 12.9 %all-to-all-done.7 = bf16[8,3,32,576]{3,2,1,0:T(8,128)(2,1)} async-done(((bf16[8,3,32,576]{3,2,1,0:T(8,128)(2,1)}), bf16[8,3,32,576]{3,2,1,0:T(8,128)(2,1)}, u32[]{:S(2)}, u32[]{:S(2)}) %all-to-all-start.7) | async-done | bytes 884768 | tf_op jit(solution)/shard_map/all_to_all | solution.py:459
  481.0 6.1 all-to-all-start.9
  487.2 5.6 convolution_convert_fusion.1
  492.9 33.8 %all-to-all-done.9 = bf16[8,128,1536]{1,2,0:T(8,128)(2,1)} async-done(((bf16[8,128,1536]{1,2,0:T(8,128)(2,1)}), bf16[8,128,1536]{1,2,0:T(8,128)(2,1)}, u32[]{:S(2)}, u32[]{:S(2)}) %all-to-all-start.9) | async-done | bytes 3145760 | tf_op jit(solution)/shard_map/all_to_all | solution.py:453
  526.6 9.2 %all-to-all-start.6 = ((bf16[8,128,1536]{2,1,0:T(8,128)(2,1)}), bf16[8,128,1536]{2,1,0:T(8,128)(2,1)}, u32[]{:S(2)}, u32[]{:S(2)}) async-start(bf16[8,128,1536]{2,1,0:T(8,128)(2,1)} %convolution_convert_fusion.1), calls=%async_computation.6 | async-start | bytes 6291456 | tf_op jit(solution)/shard_map/all_to_all | solution.py:459
  556.7 4.7 copy.391
  586.4 10.4 %collective-permute-done.9 = bf16[72,16,512]{2,1,0:T(8,128)(2,1)} collective-permute-done((bf16[72,16,512]{2,1,0:T(8,128)(2,1)}, bf16[72,16,512]{2,1,0:T(8,128)(2,1)}, u32[]{:S(2)}, u32[]{:S(2)}) %collective-permute-start.9) | collective-permute-done | bytes 1179680 | tf_op jit(solution)/shard_map/ppermute | solution.py:467
  603.3 21.6 %all-to-all-start.12 = ((f32[32,4,128]{2,1,0:T(4,128)}), f32[32,4,128]{2,1,0:T(4,128)S(1)}, u32[]{:S(2)}, u32[]{:S(2)}) async-start(f32[32,4,128]{2,1,0:T(4,128)} %reshape.504), calls=%async_computation.12 | async-start | bytes 131072 | tf_op jit(solution)/shard_map/all_to_all | solution.py:632
  625.0 6.3 collective-permute-done.6
  637.0 6.9 all-to-all-start.11
  646.9 42.7 %all-to-all-done.11 = bf16[32,4,16,512]{3,2,1,0:T(8,128)(2,1)S(1)} async-done(((bf16[32,4,16,512]{3,2,1,0:T(8,128)(2,1)}), bf16[32,4,16,512]{3,2,1,0:T(8,128)(2,1)S(1)}, u32[]{:S(2)}, u32[]{:S(2)}) %all-to-all-start.11) | async-done | bytes 2097184 | tf_op jit(solution)/shard_map/all_to_all | solution.py:668
  691.2 12.7 %fusion.2 = (f32[4,512,512]{2,1,0:T(8,128)}, f32[4,512,512]{2,1,0:T(8,128)}) fusion(f32[4,512,512]{2,1,0:T(8,128)} %param.37, f32[4,512,512]{2,1,0:T(8,128)} %param.36, f32[4,512,512]{2,1,0:T(8,128)} %param.34, bf16[4,512,512]{2,1,0:T(8,128)(2,1)} %bitcast.375, f32[4,512,512]{2,1,0:T(8,128)} %param.33), kind=kOutput, calls=%fused_computation.10 | convolution fusion | flops 2156920832 | bytes 27262976 | tf_op jit(solution)/shard_map/saj,sjb->sab/dot_general | solution.py:676
  703.8 13.5 %fusion.76 = (bf16[4,512,512]{2,1,0:T(8,128)(2,1)}, f32[4,512,512]{2,1,0:T(8,128)}) fusion(f32[4,512,512]{2,1,0:T(8,128)} %param.35, f32[4,512,512]{2,1,0:T(8,128)} %param.34, f32[4,512,512]{2,1,0:T(8,128)} %get-tuple-element.65, f32[4,512,512]{2,1,0:T(8,128)} %get-tuple-element.64, f32[4,512,512]{2,1,0:T(8,128)} %param.33), kind=kOutput, calls=%fused_computation.217 | convolution fusion | flops 2159017984 | bytes 27262976 | tf_op jit(solution)/shard_map/sib,sjb->sij/dot_general | solution.py:681
  (436 shorter events, 223.9 us)
Async XLA Ops:
  11.9 27.5 %all-to-all-start = ((bf16[8,96,576]{2,1,0:T(8,128)(2,1)}), bf16[8,96,576]{2,1,0:T(8,128)(2,1)S(1)}, u32[]{:S(2)}, u32[]{:S(2)}) async-start(bf16[8,96,576]{2,1,0:T(8,128)(2,1)} %bitcast.12), calls=%async_computation | async-start | bytes 1966080 | tf_op jit(solution)/shard_map/all_to_all | solution.py:504
  40.8 130.2 %copy-start.30 = (bf16[128,1536]{1,0:T(8,128)(2,1)S(1)}, bf16[128,1536]{1,0:T(8,128)(2,1)}, u32[]{:S(2)}) copy-start(bf16[128,1536]{1,0:T(8,128)(2,1)} %param.23) | copy-start | bytes 1179652
  40.8 140.5 %all-to-all-start.2 = ((bf16[8,96,1024]{2,1,0:T(8,128)(2,1)}), bf16[8,96,1024]{2,1,0:T(8,128)(2,1)}, u32[]{:S(2)}, u32[]{:S(2)}) async-start(bf16[8,96,1024]{2,1,0:T(8,128)(2,1)} %bitcast.38), calls=%async_computation.2 | async-start | bytes 3145728 | tf_op jit(solution)/shard_map/all_to_all | solution.py:504
  47.3 207.1 %all-gather.2.cloned.1.call-start = ((), (), s32[]{:S(2)}) async-start(), calls=%async_computation.13 | async-start | bytes 5013504 | tf_op jit(solution)/shard_map/all_gather | solution.py:567
  48.0 146.9 %collective-permute-start.2 = (bf16[256,1536]{1,0:T(8,128)(2,1)}, bf16[256,1536]{1,0:T(8,128)(2,1)}, u32[]{:S(2)}, u32[]{:S(2)}) collective-permute-start(bf16[256,1536]{1,0:T(8,128)(2,1)} %param.30), channel_id=1, source_target_pairs={{0,16},{16,0},{1,17},{17,1},{2,18},{18,2},{3,19},{19,3},{4,20},{20... | collective-permute-start | bytes 2359304 | tf_op jit(solution)/shard_map/ppermute | solution.py:467
  183.5 51.0 %all-to-all-start.4 = ((bf16[8,128,1536]{1,2,0:T(8,128)(2,1)}), bf16[8,128,1536]{1,2,0:T(8,128)(2,1)}, u32[]{:S(2)}, u32[]{:S(2)}) async-start(bf16[8,128,1536]{1,2,0:T(8,128)(2,1)} %broadcast_in_dim.516), calls=%async_computation.4 | async-start | bytes 6291456 | tf_op jit(solution)/shard_map/all_to_all | solution.py:453
  196.2 5.0 collective-permute-start.3
  198.0 5.0 collective-permute-start
  202.5 43.1 %collective-permute-start.1 = (bf16[8,96,1024]{2,1,0:T(8,128)(2,1)}, bf16[8,96,1024]{2,1,0:T(8,128)(2,1)}, u32[]{:S(2)}, u32[]{:S(2)}) collective-permute-start(bf16[8,96,1024]{2,1,0:T(8,128)(2,1)} %all-to-all-done.2), channel_id=1, source_target_pairs={{0,2},{2,0},{1,3},{3,1},{4,6},{6,4},{5,7},{7,5},{8,10},{10,8},{9,1... | collective-permute-start | bytes 4718600 | tf_op jit(solution)/shard_map/ppermute | solution.py:467
  234.5 19.9 %all-to-all-start.1 = ((bf16[8,128,192]{1,2,0:T(8,128)(2,1)}), bf16[8,128,192]{1,2,0:T(8,128)(2,1)S(1)}, u32[]{:S(2)}, u32[]{:S(2)}) async-start(bf16[8,128,192]{1,2,0:T(8,128)(2,1)} %bitcast.30), calls=%async_computation.1 | async-start | bytes 786432 | tf_op jit(solution)/shard_map/all_to_all | solution.py:459
  297.5 88.4 %all-to-all-start.3 = ((bf16[8,128,1536]{2,1,0:T(8,128)(2,1)}), bf16[8,128,1536]{2,1,0:T(8,128)(2,1)}, u32[]{:S(2)}, u32[]{:S(2)}) async-start(bf16[8,128,1536]{2,1,0:T(8,128)(2,1)} %convolution_convert_fusion.2), calls=%async_computation.3 | async-start | bytes 6291456 | tf_op jit(solution)/shard_map/all_to_all | solution.py:459
  375.8 30.7 %collective-permute-start.7 = (bf16[3,8,32,2,512]{4,2,3,1,0:T(8,128)(2,1)}, bf16[3,8,32,2,512]{4,2,3,1,0:T(8,128)(2,1)}, u32[]{:S(2)}, u32[]{:S(2)}) collective-permute-start(bf16[3,8,32,2,512]{4,2,3,1,0:T(8,128)(2,1)} %fusion.12), channel_id=1, source_target_pairs={{0,2},{2,0},{1,3},{3,1},{4,6},{6,4},{5,7},{7,5},{8,10},{10,8},{9,1... | collective-permute-start | bytes 4718600 | tf_op jit(solution)/shard_map/ppermute | solution.py:467
  383.3 21.2 %collective-permute-start.8 = (bf16[8,32,3,512]{3,1,2,0:T(8,128)(2,1)}, bf16[8,32,3,512]{3,1,2,0:T(8,128)(2,1)}, u32[]{:S(2)}, u32[]{:S(2)}) collective-permute-start(bf16[8,32,3,512]{3,1,2,0:T(8,128)(2,1)} %fusion.36), channel_id=1, source_target_pairs={{0,2},{2,0},{1,3},{3,1},{4,6},{6,4},{5,7},{7,5},{8,10},{10,8},{9,1... | collective-permute-start | bytes 2359304 | tf_op jit(solution)/shard_map/ppermute | solution.py:467
  385.8 14.2 %all-to-all-start.8 = ((bf16[8,128,192]{1,2,0:T(8,128)(2,1)}), bf16[8,128,192]{1,2,0:T(8,128)(2,1)S(1)}, u32[]{:S(2)}, u32[]{:S(2)}) async-start(bf16[8,128,192]{1,2,0:T(8,128)(2,1)} %bitcast.74), calls=%async_computation.8 | async-start | bytes 786432 | tf_op jit(solution)/shard_map/all_to_all | solution.py:459
  400.0 11.3 %all-to-all-start.5 = ((bf16[8,128,192]{1,2,0:T(8,128)(2,1)}), bf16[8,128,192]{1,2,0:T(8,128)(2,1)S(1)}, u32[]{:S(2)}, u32[]{:S(2)}) async-start(bf16[8,128,192]{1,2,0:T(8,128)(2,1)} %bitcast.51), calls=%async_computation.5 | async-start | bytes 786432 | tf_op jit(solution)/shard_map/all_to_all | solution.py:459
  411.3 49.9 %all-to-all-start.10 = ((bf16[8,9,32,512]{3,2,1,0:T(8,128)(2,1)}), bf16[8,9,32,512]{3,2,1,0:T(8,128)(2,1)}, u32[]{:S(2)}, u32[]{:S(2)}) async-start(bf16[8,9,32,512]{3,2,1,0:T(8,128)(2,1)} %pad_maximum_fusion.1), calls=%async_computation.10 | async-start | bytes 4718592 | tf_op jit(solution)/shard_map/all_to_all | solution.py:459
  450.7 4.8 collective-permute-start.4
  461.2 17.7 %all-to-all-start.7 = ((bf16[8,3,32,576]{3,2,1,0:T(8,128)(2,1)}), bf16[8,3,32,576]{3,2,1,0:T(8,128)(2,1)}, u32[]{:S(2)}, u32[]{:S(2)}) async-start(bf16[8,3,32,576]{3,2,1,0:T(8,128)(2,1)} %reshape.485), calls=%async_computation.7 | async-start | bytes 1966080 | tf_op jit(solution)/shard_map/all_to_all | solution.py:459
  481.0 45.6 %all-to-all-start.9 = ((bf16[8,128,1536]{1,2,0:T(8,128)(2,1)}), bf16[8,128,1536]{1,2,0:T(8,128)(2,1)}, u32[]{:S(2)}, u32[]{:S(2)}) async-start(bf16[8,128,1536]{1,2,0:T(8,128)(2,1)} %broadcast_in_dim.517), calls=%async_computation.9 | async-start | bytes 6291456 | tf_op jit(solution)/shard_map/all_to_all | solution.py:453
  492.8 43.3 %copy-start.60 = (pred[128,128]{0,1:T(32,128)(4,1)S(1)}, pred[128,128]{0,1:T(32,128)(4,1)}, u32[]{:S(2)}) copy-start(pred[128,128]{0,1:T(32,128)(4,1)} %constant.207) | copy-start | bytes 49156
  492.8 43.6 %copy-start.59 = (pred[128,128]{0,1:T(32,128)(4,1)S(1)}, pred[128,128]{0,1:T(32,128)(4,1)}, u32[]{:S(2)}) copy-start(pred[128,128]{0,1:T(32,128)(4,1)} %constant.205) | copy-start | bytes 49156
  492.8 43.8 %copy-start.58 = (pred[128,128]{0,1:T(32,128)(4,1)S(1)}, pred[128,128]{0,1:T(32,128)(4,1)}, u32[]{:S(2)}) copy-start(pred[128,128]{0,1:T(32,128)(4,1)} %constant.203) | copy-start | bytes 49156
  492.8 44.1 %copy-start.57 = (pred[128,128]{0,1:T(32,128)(4,1)S(1)}, pred[128,128]{0,1:T(32,128)(4,1)}, u32[]{:S(2)}) copy-start(pred[128,128]{0,1:T(32,128)(4,1)} %constant.201) | copy-start | bytes 49156
  492.8 44.3 %copy-start.56 = (pred[128,128]{0,1:T(32,128)(4,1)S(1)}, pred[128,128]{0,1:T(32,128)(4,1)}, u32[]{:S(2)}) copy-start(pred[128,128]{0,1:T(32,128)(4,1)} %constant.199) | copy-start | bytes 49156
  492.8 44.5 %copy-start.55 = (pred[128,128]{0,1:T(32,128)(4,1)S(1)}, pred[128,128]{0,1:T(32,128)(4,1)}, u32[]{:S(2)}) copy-start(pred[128,128]{0,1:T(32,128)(4,1)} %constant.197) | copy-start | bytes 49156
  492.9 44.8 %copy-start.54 = (pred[128,128]{0,1:T(32,128)(4,1)S(1)}, pred[128,128]{0,1:T(32,128)(4,1)}, u32[]{:S(2)}) copy-start(pred[128,128]{0,1:T(32,128)(4,1)} %constant.195) | copy-start | bytes 49156
  526.6 73.0 %all-to-all-start.6 = ((bf16[8,128,1536]{2,1,0:T(8,128)(2,1)}), bf16[8,128,1536]{2,1,0:T(8,128)(2,1)}, u32[]{:S(2)}, u32[]{:S(2)}) async-start(bf16[8,128,1536]{2,1,0:T(8,128)(2,1)} %convolution_convert_fusion.1), calls=%async_computation.6 | async-start | bytes 6291456 | tf_op jit(solution)/shard_map/all_to_all | solution.py:459
  547.1 49.7 %collective-permute-start.9 = (bf16[72,16,512]{2,1,0:T(8,128)(2,1)}, bf16[72,16,512]{2,1,0:T(8,128)(2,1)}, u32[]{:S(2)}, u32[]{:S(2)}) collective-permute-start(bf16[72,16,512]{2,1,0:T(8,128)(2,1)} %fusion.17), channel_id=1, source_target_pairs={{0,16},{16,0},{1,17},{17,1},{2,18},{18,2},{3,19},{19,3},{4,20},{20... | collective-permute-start | bytes 3538952 | tf_op jit(solution)/shard_map/ppermute | solution.py:467
  565.5 17.4 %collective-permute-start.5 = (bf16[3,32,3,512]{3,1,2,0:T(8,128)(2,1)S(1)}, bf16[3,32,3,512]{3,1,2,0:T(8,128)(2,1)S(1)}, u32[]{:S(2)}, u32[]{:S(2)}) collective-permute-start(bf16[3,32,3,512]{3,1,2,0:T(8,128)(2,1)S(1)} %fusion.42), channel_id=1, source_target_pairs={{0,2},{2,0},{1,3},{3,1},{4,6},{6,4},{5,7},{7,5},{8,10},{10,8},{9,1... | collective-permute-start | bytes 884744 | tf_op jit(solution)/shard_map/ppermute | solution.py:467
  584.7 46.6 %collective-permute-start.6 = (bf16[36,16,512]{2,1,0:T(8,128)(2,1)}, bf16[36,16,512]{2,1,0:T(8,128)(2,1)}, u32[]{:S(2)}, u32[]{:S(2)}) collective-permute-start(bf16[36,16,512]{2,1,0:T(8,128)(2,1)} %fusion.39), channel_id=1, source_target_pairs={{0,16},{16,0},{1,17},{17,1},{2,18},{18,2},{3,19},{19,3},{4,20},{20... | collective-permute-start | bytes 1769480 | tf_op jit(solution)/shard_map/ppermute | solution.py:467
  603.3 33.6 %all-to-all-start.12 = ((f32[32,4,128]{2,1,0:T(4,128)}), f32[32,4,128]{2,1,0:T(4,128)S(1)}, u32[]{:S(2)}, u32[]{:S(2)}) async-start(f32[32,4,128]{2,1,0:T(4,128)} %reshape.504), calls=%async_computation.12 | async-start | bytes 131072 | tf_op jit(solution)/shard_map/all_to_all | solution.py:632
  637.0 52.7 %all-to-all-start.11 = ((bf16[32,4,16,512]{3,2,1,0:T(8,128)(2,1)}), bf16[32,4,16,512]{3,2,1,0:T(8,128)(2,1)S(1)}, u32[]{:S(2)}, u32[]{:S(2)}) async-start(bf16[32,4,16,512]{3,2,1,0:T(8,128)(2,1)} %bitcast.215), calls=%async_computation.11 | async-start | bytes 4194304 | tf_op jit(solution)/shard_map/all_to_all | solution.py:668
  (76 other events, 508.1 us)
Sparse Core Ops, SparseCore 0:
  50.4 106.6 all-gather.1

commit v3 on v2

--- a/solution.py
+++ b/solution.py
@@ -520,7 +520,7 @@
     return source - target + CK // 2 == tap
 
 
-def body(
+def body_any(
     layer_input, lengths, cotangent, w_query, w_key, w_value, w_out, w_gate, w_up, w_down, vec_copy, owners,
     basis_left, basis_right, block_master, block_first, block_second, vec_master, vec_first, vec_second,
 ):
@@ -689,13 +689,617 @@
     )
 
 
+def group_at(mask):
+    return {axis: 1 - lax.axis_index(axis) for axis, bit in (("g", 4), ("a", 2), ("b", 1)) if mask & bit}
+
+
+def other_bit(axis, changed):
+    at = lax.axis_index(axis)
+    return 1 - at if changed else at
+
+
+def push(src, dst, send, recv, device):
+    copy = pltpu.make_async_remote_copy(src_ref=src, dst_ref=dst, send_sem=send, recv_sem=recv, device_id=device)
+    copy.start()
+    return copy
+
+
+class Gather:
+    def __init__(self, x_ref, out_ref, local_sem, send1, recv1, send2, recv2, send3, recv3):
+        self.x, self.out, self.local_sem = x_ref, out_ref, local_sem
+        self.sems = ((send1, recv1), (send2, recv2), (send3, recv3))
+        self.me = chip_index()
+        self.half = x_ref.shape[0] // 2
+        self.sent, self.second = [], []
+
+    def here(self, part):
+        return pl.ds(part * self.half, self.half)
+
+    def start(self):
+        self.local = pltpu.make_async_copy(self.x, self.out.at[self.me], self.local_sem)
+        self.local.start()
+        send, recv = self.sems[0]
+        for part in range(2):
+            for at, (axis, _, _) in enumerate(HOPS):
+                self.sent.append(
+                    push(
+                        self.x.at[self.here(part)], self.out.at[self.me, self.here(part)],
+                        send.at[at, part], recv.at[at, part], across(axis),
+                    )
+                )
+
+    def onward(self):
+        send, recv = self.sems[1]
+        for part in range(2):
+            for at, (axis, onward, _) in enumerate(HOPS):
+                self.sent[part * 3 + at].wait_recv()
+                block = self.out.at[flipped(self.me, (axis,)), self.here(part)]
+                self.second.append(push(block, block, send.at[at, part], recv.at[at, part], across(onward)))
+
+    def last(self):
+        send, recv = self.sems[2]
+        self.third = []
+        for copy in self.second:
+            copy.wait_recv()
+        for at, (axis, onward, last) in enumerate(HOPS):
+            begin, count = THIRDS[at]
+            piece = self.out.at[flipped(self.me, (axis, onward)), pl.ds(begin, count)]
+            self.third.append(push(piece, piece, send.at[at], recv.at[at], across(last)))
+
+    def finish(self):
+        for copy in self.third:
+            copy.wait_recv()
+        self.local.wait()
+
+    def drain(self):
+        for copy in self.sent + self.second + self.third:
+            copy.wait_send()
+
+
+class Scatter:
+    def __init__(self, parts, near, in2, in3, acc2, acc3, send1, recv1, send2, recv2, send3, recv3):
+        self.parts, self.near, self.in2, self.in3, self.acc2, self.acc3 = parts, near, in2, in3, acc2, acc3
+        self.sems = ((send1, recv1), (send2, recv2), (send3, recv3))
+        self.me = chip_index()
+        self.half = parts.shape[1] // 2
+
+    def here(self, part):
+        return pl.ds(part * self.half, self.half)
+
+    def start(self):
+        send, recv = self.sems[0]
+        opposite = flipped(self.me, ("y", "a", "b"))
+        self.first = []
+        for at, (_, _, last) in enumerate(HOPS):
+            rows = pl.ds(*THIRDS[at])
+            self.first.append(push(self.parts.at[opposite, rows], self.in2.at[rows], send.at[at], recv.at[at], across(last)))
+
+    def onward(self):
+        send, recv = self.sems[1]
+        self.second = []
+        for part in range(2):
+            for at, (axis, onward, _) in enumerate(HOPS):
+                dest = flipped(self.me, (axis, onward))
+                if part == 0:
+                    self.first[at].wait_recv()
+                    rows = pl.ds(*THIRDS[at])
+                    self.acc2[at] = self.parts[dest]
+                    self.acc2[at, rows] = (
+                        self.parts[dest, rows].astype(f32) + self.in2[rows].astype(f32)
+                    ).astype(bf16)
+                here = self.here(part)
+                self.second.append(
+                    push(self.acc2.at[at, here], self.in3.at[at, here], send.at[at, part], recv.at[at, part], across(onward))
+                )
+
+    def last(self):
+        send, recv = self.sems[2]
+        self.third = []
+        for part in range(2):
+            here = self.here(part)
+            for at, (axis, _, _) in enumerate(HOPS):
+                dest = flipped(self.me, (axis,))
+                self.second[part * 3 + at].wait_recv()
+                self.acc3[at, here] = (
+                    self.parts[dest, here].astype(f32) + self.in3[at, here].astype(f32)
+                ).astype(bf16)
+                self.third.append(
+                    push(self.acc3.at[at, here], self.near.at[at, here], send.at[at, part], recv.at[at, part], across(axis))
+                )
+
+    def finish(self, part):
+        here = self.here(part)
+        for at in range(3):
+            self.third[part * 3 + at].wait_recv()
+        return (self.parts[self.me, here].astype(f32) + self.near[0, here].astype(f32)) + (
+            self.near[1, here].astype(f32) + self.near[2, here].astype(f32)
+        )
+
+    def drain(self):
+        for copy in self.first + self.second + self.third:
+            copy.wait_send()
+
+
+def scatter_scratch(rows, width):
+    dma = pltpu.SemaphoreType.DMA
+    three = pltpu.VMEM((3, rows, width), bf16)
+    return [three, pltpu.VMEM((rows, width), bf16), three, three, three] + [dma((3,))] * 2 + [dma((3, 2))] * 4
+
+
+VMEM = pl.BlockSpec(memory_space=pltpu.VMEM)
+
+
+def dispatch_body(
+    x_ref, vec_ref, blocks_ref, out_ref, vecs_ref, wq_ref,
+    vec_send, vec_recv, vec_local, w_local, w_send, w_recv, core_send, core_recv, *hops,
+):
+    devices = lax.axis_size(ALL)
+    me = device_index()
+    g, a, b, c, y = (lax.axis_index(axis) for axis in ALL)
+    mine = ((g * 2 + a) * 2 + b) * 2 + c
+    local = pltpu.make_async_copy(vec_ref, vecs_ref.at[me], vec_local)
+    local.start()
+    own = pltpu.make_async_copy(blocks_ref.at[chip_index()], wq_ref.at[mine], w_local)
+    own.start()
+    greet_all()
+    gather = Gather(x_ref, out_ref, *hops)
+    gather.start()
+
+    def push_vec(step, carry):
+        pltpu.make_async_remote_copy(
+            src_ref=vec_ref, dst_ref=vecs_ref.at[me], send_sem=vec_send, recv_sem=vec_recv,
+            device_id=device_at(lax.rem(me + step, devices)),
+        ).start()
+        return carry
+
+    lax.fori_loop(1, devices, push_vec, 0)
+    sent, relayed = [], []
+    for mask in (4, 6, 5, 7, 2, 1, 3):
+        block = (y * 2 + other_bit("a", mask & 2)) * 2 + other_bit("b", mask & 1)
+        sent.append(push(blocks_ref.at[block], wq_ref.at[mine], w_send.at[mask], w_recv.at[mask], group_at(mask)))
+    own.wait()
+    relayed.append(push(wq_ref.at[mine], wq_ref.at[mine], core_send.at[0], core_recv.at[0], across("c")))
+    gather.onward()
+    for at, mask in enumerate((4, 6, 5, 7, 2, 1, 3)):
+        sent[at].wait_recv()
+        source = ((other_bit("g", mask & 4) * 2 + other_bit("a", mask & 2)) * 2 + other_bit("b", mask & 1)) * 2 + c
+        relayed.append(push(wq_ref.at[source], wq_ref.at[source], core_send.at[mask], core_recv.at[mask], across("c")))
+        if at == 1:
+            gather.last()
+    gather.finish()
+    for copy in relayed:
+        copy.wait_recv()
+    others = vecs_ref.at[pl.ds(0, devices - 1)]
+    pltpu.make_async_copy(others, others, vec_recv).wait()
+    pltpu.make_async_copy(others, others, vec_send).wait()
+    local.wait()
+    gather.drain()
+    for copy in sent + relayed:
+        copy.wait_send()
+
+
+def dispatch(rows, vec, blocks):
+    count, width = rows.shape
+    dma = pltpu.SemaphoreType.DMA
+    return pl.pallas_call(
+        dispatch_body,
+        in_specs=[ANYS] * 3,
+        out_specs=[ANYS] * 3,
+        out_shape=[
+            jax.ShapeDtypeStruct((CHIPS, count, width), rows.dtype),
+            jax.ShapeDtypeStruct((lax.axis_size(ALL),) + vec.shape, vec.dtype),
+            jax.ShapeDtypeStruct((16,) + blocks.shape[1:], blocks.dtype),
+        ],
+        scratch_shapes=[dma] * 4 + [dma((8,))] * 4 + hop_sems(),
+        name="dispatch",
+        compiler_params=pltpu.CompilerParams(collective_id=1, has_side_effects=True),
+    )(rows, vec, blocks)
+
+
+def back_body(
+    len_ref, mix_ref, qkv_ref, toep_ref, gain_ref, s_ref, p_ref, o_ref, sent_ref, dattn_ref, strips_ref,
+    dqkv_ref, theta_ref, mixer_ref, gain_grad_ref, go_ref,
+    pad_ref, grads_ref, all_ref, own_sem, send, recv, *hops,
+):
+    seqs, rows = qkv_ref.shape[:2]
+    me = chip_index()
+    own = pltpu.make_async_copy(sent_ref.at[me], grads_ref.at[me], own_sem)
+    own.start()
+    barrier = pltpu.get_barrier_semaphore()
+    for mask in range(1, 8):
+        pl.semaphore_signal(barrier, inc=1, device_id=chip_at(mask))
+    pl.semaphore_wait(barrier, 7)
+    sent = []
+    for mask in (7, 6, 5, 3, 4, 2, 1):
+        to = flipped(me, [axis for axis in BITS if mask & BITS[axis]])
+        sent.append(push(sent_ref.at[to], grads_ref.at[me], send.at[mask], recv.at[mask], chip_at(mask)))
+    gather = Gather(dattn_ref, all_ref, *hops)
+    gather.start()
+    pad_ref[rows : rows + 8, :] = jnp.zeros((8, rows), f32)
+    theta_ref[...] = jnp.zeros_like(theta_ref)
+    mixer_ref[...] = jnp.zeros_like(mixer_ref)
+    gain_grad_ref[...] = jnp.zeros_like(gain_grad_ref)
+    own.wait()
+    for copy in sent:
+        copy.wait_recv()
+    query_at = lax.broadcasted_iota(jnp.int32, (rows, rows), 0)
+    key_at = lax.broadcasted_iota(jnp.int32, (rows, rows), 1)
+    blank = jnp.zeros((rows, HP - DH), f32)
+
+    def one(seq, carry):
+        keep = (key_at <= query_at) & (key_at < len_ref[seq])
+        weights = [p_ref[seq, 0], p_ref[seq, 1]]
+        grad_mixed = []
+        grads = grads_ref[seq].astype(f32)
+        for head in range(2):
+            cols = slice(head * HP, (head + 1) * HP)
+            out = o_ref[seq, :, cols]
+            grad = jnp.concatenate([grads[:, head * DH : (head + 1) * DH], blank], axis=1)
+            scale = lax.rsqrt(jnp.sum(out * out, axis=-1, keepdims=True) * (1.0 / DH) + eps_norm)
+            unit = out * scale
+            gain_grad_ref[:, cols] += jnp.sum(grad * unit, axis=0, keepdims=True)
+            inner = grad * gain_ref[:, cols]
+            grad_out = scale * (inner - unit * (jnp.sum(inner * unit, axis=-1, keepdims=True) * (1.0 / DH)))
+            grad_out = grad_out.astype(bf16)
+            value = qkv_ref[seq, :, (4 + head) * HP : (5 + head) * HP]
+            mixed = (mix_ref[2 * head] * weights[0] + mix_ref[2 * head + 1] * weights[1]).astype(bf16)
+            dqkv_ref[seq, :, (4 + head) * HP : (5 + head) * HP] = dot_tn(mixed, grad_out).astype(bf16)
+            back = dot_nt(grad_out, value)
+            grad_mixed.append(back)
+            for source in range(2):
+                mixer_ref[2 * head + source : 2 * head + source + 1, :] += jnp.sum(
+                    back * weights[source], axis=0, keepdims=True
+                )
+        for head in range(2):
+            grad_weight = mix_ref[head] * grad_mixed[0] + mix_ref[2 + head] * grad_mixed[1]
+            weight = weights[head]
+            grad_conv = weight * (grad_weight - jnp.sum(weight * grad_weight, axis=-1, keepdims=True))
+            wide = shifted_up(pad_ref, grad_conv).astype(bf16)
+            theta_ref[head] += dot_tn(s_ref[seq, head], wide)
+            grad_scores = jnp.zeros((rows, rows), f32)
+            for lag in range(CQ):
+                grad_scores += dot_nt(
+                    wide[:, lag * rows : (lag + 1) * rows], toep_ref[head, lag * rows : (lag + 1) * rows, :]
+                )
+            grad_scores = jnp.where(keep, grad_scores * (1.0 / math.sqrt(DH)), 0.0).astype(bf16)
+            query = qkv_ref[seq, :, head * HP : (head + 1) * HP]
+            key = qkv_ref[seq, :, (2 + head) * HP : (3 + head) * HP]
+            dqkv_ref[seq, :, head * HP : (head + 1) * HP] = dot(grad_scores, key).astype(bf16)
+            dqkv_ref[seq, :, (2 + head) * HP : (3 + head) * HP] = dot_tn(grad_scores, query).astype(bf16)
+        return carry
+
+    lax.fori_loop(0, 4, one, 0)
+    gather.onward()
+    lax.fori_loop(4, seqs, one, 0)
+    gather.last()
+    gather.finish()
+    strips = strips_ref[...]
+    for col in range(ROW_TILES):
+        at = slice(col * BLK, (col + 1) * BLK)
+        go_ref[:, at] = dot_tn(strips, all_ref[:, :, at].reshape(seqs * rows, BLK)).astype(bf16)
+    gather.drain()
+    for copy in sent:
+        copy.wait_send()
+
+
+def chip_at(mask):
+    return {axis: 1 - lax.axis_index(axis) for axis in BITS if mask & BITS[axis]}
+
+
+def run_back(lengths, mix, qkv, toep, gain, scores, weights, outs, sent, dattn, strips):
+    seqs, rows, _ = qkv.shape
+    dma = pltpu.SemaphoreType.DMA
+    return pl.pallas_call(
+        back_body,
+        in_specs=[SMEM, SMEM] + [VMEM] * 9,
+        out_specs=[VMEM] * 5,
+        out_shape=[
+            jax.ShapeDtypeStruct((seqs, rows, 6 * HP), bf16),
+            jax.ShapeDtypeStruct((2, rows, CQ * rows), f32),
+            jax.ShapeDtypeStruct((8, rows), f32),
+            jax.ShapeDtypeStruct((1, 2 * HP), f32),
+            jax.ShapeDtypeStruct((2 * DH, D), bf16),
+        ],
+        scratch_shapes=[
+            pltpu.VMEM((rows + 8, rows), f32), pltpu.VMEM((seqs, rows, 2 * DH), bf16),
+            pltpu.VMEM((CHIPS, rows, D), bf16), dma, dma((8,)), dma((8,)),
+        ] + hop_sems(),
+        name="attention_back",
+        compiler_params=pltpu.CompilerParams(collective_id=4, has_side_effects=True, vmem_limit_bytes=32 * 2**20),
+    )(lengths, mix, qkv, toep, gain, scores, weights, outs, sent, dattn, strips)
+
+
+def share_body(
+    parts_ref, gq_ref, go_ref, dxn_ref, qkv_ref, out_ref,
+    core_q, core_o, in_q, in_o, core_send, core_recv, send, recv, go_send, go_recv, *scatter_args,
+):
+    g, a, b, c, y = (lax.axis_index(axis) for axis in ALL)
+    me = chip_index()
+    barrier = pltpu.get_barrier_semaphore()
+    pl.semaphore_signal(barrier, inc=1, device_id=across("c"))
+    for mask in range(1, 16):
+        pl.semaphore_signal(barrier, inc=1, device_id=wide_at(mask))
+    pl.semaphore_wait(barrier, 16)
+    to_core = [
+        push(gq_ref.at[:, 1 - c], core_q, core_send.at[0], core_recv.at[0], across("c")),
+        push(go_ref.at[:, 1 - c], core_o, core_send.at[1], core_recv.at[1], across("c")),
+    ]
+    scatter = Scatter(parts_ref, *scatter_args)
+    scatter.start()
+    to_core[0].wait_recv()
+    for row in range(ROW_TILES):
+        core_q[row] = (core_q[row].astype(f32) + gq_ref[row, c].astype(f32)).astype(bf16)
+    slot = g * CHIPS + me
+    sent = []
+    for mask in (15, 14, 13, 11, 12, 10, 9, 8, 7, 6, 5, 3, 4, 2, 1):
+        to = flipped(me, [axis for axis in BITS if mask & BITS[axis]])
+        sent.append(
+            push(
+                core_q.at[:, to, other_bit("g", mask & 8)], in_q.at[slot], send.at[mask], recv.at[mask], wide_at(mask)
+            )
+        )
+    to_core[1].wait_recv()
+    core_o[...] = (core_o[...].astype(f32) + go_ref[:, c].astype(f32)).astype(bf16)
+    to_group = push(core_o.at[:, 1 - g], in_o, go_send, go_recv, across("g"))
+    in_q[slot] = core_q[:, me, g]
+    scatter.onward()
+    scatter.last()
+    dxn_ref[0 : dxn_ref.shape[0] // 2] = scatter.finish(0)
+    dxn_ref[dxn_ref.shape[0] // 2 :] = scatter.finish(1)
+    to_group.wait_recv()
+    out_ref[...] = (in_o[...].astype(f32) + core_o[:, g].astype(f32)).astype(bf16)
+    for copy in sent:
+        copy.wait_recv()
+    for row in range(ROW_TILES):
+        sums = [in_q[chip, row].astype(f32) + in_q[CHIPS + chip, row].astype(f32) for chip in range(CHIPS)]
+        for which in range(3):
+            qkv_ref[which, row] = jnp.concatenate(
+                [part[:, which * 2 * DH : (which + 1) * 2 * DH] for part in sums], axis=1
+            ).astype(bf16)
+    scatter.drain()
+    for copy in to_core + sent + [to_group]:
+        copy.wait_send()
+
+
+def wide_at(mask):
+    at = chip_at(mask & 7)
+    if mask & 8:
+        at["g"] = 1 - lax.axis_index("g")
+    return at
+
+
+def share(parts, gq, go):
+    _, rows, width = parts.shape
+    dma = pltpu.SemaphoreType.DMA
+    part = gq.shape[-2]
+    return pl.pallas_call(
+        share_body,
+        in_specs=[VMEM] * 3,
+        out_specs=[VMEM] * 3,
+        out_shape=[
+            jax.ShapeDtypeStruct((rows, width), f32),
+            jax.ShapeDtypeStruct((3, ROW_TILES, part, D), bf16),
+            jax.ShapeDtypeStruct((ROW_TILES, part, D), bf16),
+        ],
+        scratch_shapes=[
+            pltpu.VMEM((ROW_TILES, CHIPS, 2, part, 6 * DH), bf16), pltpu.VMEM((ROW_TILES, 2, part, D), bf16),
+            pltpu.VMEM((2 * CHIPS, ROW_TILES, part, 6 * DH), bf16), pltpu.VMEM((ROW_TILES, part, D), bf16),
+            dma((2,)), dma((2,)), dma((16,)), dma((16,)), dma, dma,
+        ] + scatter_scratch(rows, width),
+        name="share_gradients",
+        compiler_params=pltpu.CompilerParams(collective_id=5, has_side_effects=True, vmem_limit_bytes=40 * 2**20),
+    )(parts, gq, go)
+
+
+def to_slots_body(slots_ref, vec_ref, out_ref, vecs_ref, local_sems, send, recv, vec_send, vec_recv):
+    devices = lax.axis_size(ALL)
+    me = device_index()
+    local = [
+        pltpu.make_async_copy(slots_ref.at[me], out_ref.at[me], local_sems.at[0]),
+        pltpu.make_async_copy(vec_ref.at[me], vecs_ref.at[me], local_sems.at[1]),
+    ]
+    for copy in local:
+        copy.start()
+    greet_all()
+
+    def push_all(step, carry):
+        to = lax.rem(me + step, devices)
+        pltpu.make_async_remote_copy(
+            src_ref=vec_ref.at[to], dst_ref=vecs_ref.at[me], send_sem=vec_send, recv_sem=vec_recv, device_id=device_at(to)
+        ).start()
+        pltpu.make_async_remote_copy(
+            src_ref=slots_ref.at[to], dst_ref=out_ref.at[me], send_sem=send, recv_sem=recv, device_id=device_at(to)
+        ).start()
+        return carry
+
+    lax.fori_loop(1, devices, push_all, 0)
+    for ref, one, two in ((vecs_ref, vec_send, vec_recv), (out_ref, send, recv)):
+        others = ref.at[pl.ds(0, devices - 1)]
+        pltpu.make_async_copy(others, others, two).wait()
+        pltpu.make_async_copy(others, others, one).wait()
+    for copy in local:
+        copy.wait()
+
+
+def to_slots(slots, vecs):
+    dma = pltpu.SemaphoreType.DMA
+    return pl.pallas_call(
+        to_slots_body,
+        in_specs=[ANYS] * 2,
+        out_specs=[ANYS] * 2,
+        out_shape=[jax.ShapeDtypeStruct(slots.shape, slots.dtype), jax.ShapeDtypeStruct(vecs.shape, vecs.dtype)],
+        scratch_shapes=[dma((2,))] + [dma] * 4,
+        name="to_slots",
+        compiler_params=pltpu.CompilerParams(collective_id=6, has_side_effects=True),
+    )(slots, vecs)
+
+
+def body_fast(
+    layer_input, lengths, cotangent, w_query, w_key, w_value, w_out, w_gate, w_up, w_down, vec_copy, owners,
+    basis_left, basis_right, block_master, block_first, block_second, vec_master, vec_first, vec_second,
+):
+    chip = chip_index()
+    seq_len = layer_input.shape[0]
+    length = lengths[0]
+    own_vec = vec_copy.shape[0]
+    devices, fs_size, reps = lax.axis_size(ALL), lax.axis_size(FS), lax.axis_size("y")
+
+    small = jnp.concatenate(
+        [vec_copy.astype(f32), jnp.zeros((1023 - own_vec,), f32), length.astype(f32).reshape(1)]
+    ).reshape(8, 128)
+    blocks = jnp.concatenate([w.reshape(-1, CHIPS, 2 * DH) for w in (w_query, w_key, w_value)], axis=2)
+    x_all, small_all, w_qkv = dispatch(layer_input, small, jnp.transpose(blocks, (1, 0, 2)))
+    w_gate, w_up, w_down, cotangent, x_all, small_all, w_qkv = lax.optimization_barrier(
+        (w_gate, w_up, w_down, cotangent, x_all, small_all, w_qkv)
+    )
+    small_all = small_all.reshape(fs_size, reps, 1024)
+    vector = small_all[:, 0, :own_vec].reshape(-1)
+    group_lengths = small_all[:, :, 1023].reshape(-1, 2, 2, 2, reps)
+    group_lengths = lax.dynamic_index_in_dim(group_lengths, lax.axis_index("g"), 0, keepdims=False)
+    group_lengths = lax.dynamic_index_in_dim(group_lengths, lax.axis_index("c"), 2, keepdims=False)
+    group_lengths = jnp.transpose(group_lengths, (2, 0, 1)).reshape(CHIPS).astype(jnp.int32)
+    gain_attn, gain_head, gain_ffn = vector[:D], vector[D : 2 * D], vector[2 * D : 3 * D]
+    conv_end = 3 * D + H * CQ * CK
+    theta = lax.dynamic_slice_in_dim(vector[3 * D : conv_end].reshape(H, CQ, CK), chip * 2, 2, 0)
+    mixer = lax.dynamic_slice_in_dim(vector[conv_end : conv_end + 2 * H].reshape(H, 2), chip * 2, 2, 0)
+    mix = mixer.reshape(4)
+    gain_pair = jnp.pad(
+        lax.dynamic_slice_in_dim(gain_head.reshape(H, DH), chip * 2, 2, 0), ((0, 0), (0, HP - DH))
+    ).reshape(1, 2 * HP)
+    toep = jnp.zeros((2, CQ, seq_len, seq_len), f32)
+    offset = (
+        jnp.arange(seq_len, dtype=jnp.int32)[:, None] - jnp.arange(seq_len, dtype=jnp.int32)[None, :] + CK // 2
+    )
+    for tap in range(CK):
+        toep = jnp.where(offset[None, None] == tap, theta[:, :, tap][:, :, None, None], toep)
+    toep = toep.astype(bf16).reshape(2, CQ * seq_len, seq_len)
+    w_qkv = jnp.pad(w_qkv.reshape(D, 6, DH), ((0, 0), (0, 0), (0, HP - DH))).reshape(D, 6 * HP)
+    w_o = lax.all_gather(w_out, FS, axis=0, tiled=True)
+    w_in = to_columns(jnp.concatenate([spread_columns(w, BLK) for w in (w_gate, w_up)], axis=2))
+    w_dn = down_rows(w_down, chip)
+    valid = (jnp.arange(seq_len) < length).astype(f32)
+    dy = cotangent.astype(f32) * valid[:, None]
+    dy_rows = gather_slow(dy.astype(bf16)).reshape(CHIPS * seq_len, D)
+
+    input_float = layer_input.astype(f32)
+    input_scale = rms(input_float)
+    x_rows = x_all.reshape(CHIPS * seq_len, D).astype(f32)
+    xn_rows = (x_rows * rms(x_rows) * gain_attn).astype(bf16)
+    qkv = dot(xn_rows, w_qkv).astype(bf16).reshape(CHIPS, seq_len, 6 * HP)
+    heads_pad, scores, weights, outs = run_forward(group_lengths, mix, qkv, toep, gain_pair)
+    heads_sent = heads_pad.reshape(CHIPS, seq_len, 2, HP)[..., :DH].reshape(CHIPS, seq_len, 2 * DH)
+    heads = jnp.transpose(exchange_chips(heads_sent), (1, 0, 2)).reshape(seq_len, D)
+    hmid = input_float + dot(heads, w_o)
+    hmid_scale = rms(hmid)
+    hn_rows = gather_chips((hmid * hmid_scale * gain_ffn).astype(bf16), 2).reshape(CHIPS * seq_len, D)
+    both = dot(hn_rows, w_in)
+    gate, up = both[:, :BLK], both[:, BLK:]
+    sig = jax.nn.sigmoid(gate)
+    silu = gate * sig
+    inner = (silu * up).astype(bf16)
+
+    strip = BLK // (2 * CHIPS)
+    part = strip // 2
+    dinner = dot_nt(dy_rows, w_dn)
+    dgate = (dinner * up * (sig * (1.0 + gate * (1.0 - sig)))).astype(bf16)
+    dup = (dinner * silu).astype(bf16)
+    dboth = jnp.concatenate([dgate, dup], axis=1)
+    dhn = scatter_chips(dot_nt(dboth, w_in).astype(bf16).reshape(CHIPS, seq_len, D), 3)
+    ffn = scatter_slow(dot(inner, w_dn).reshape(CHIPS, seq_len, D))
+    layer_output = (hmid + ffn).astype(bf16)
+    dhmid, grad_gain_ffn = norm_backward(hmid, hmid_scale, gain_ffn, dhn)
+    dhmid = dhmid + dy
+    dattn = dhmid.astype(bf16)
+    dheads = dot_nt(dattn, w_o).astype(bf16).reshape(seq_len, CHIPS, 2 * DH)
+    strips = jnp.transpose(heads.reshape(seq_len, 2 * ROW_TILES, CHIPS, strip), (2, 0, 1, 3))
+    strips = exchange_chips(strips.reshape(CHIPS, seq_len, 2 * ROW_TILES * strip)).reshape(CHIPS * seq_len, -1)
+    dqkv, theta_sums, mixer_sums, gain_sums, grad_out = run_back(
+        group_lengths, mix, qkv, toep, gain_pair, scores, weights, outs, jnp.transpose(dheads, (1, 0, 2)), dattn, strips
+    )
+    dqkv_rows = dqkv.reshape(CHIPS * seq_len, 6 * HP)
+    dxn_parts = dot_nt(dqkv_rows, w_qkv).astype(bf16).reshape(CHIPS, seq_len, D)
+    grad_qkv = dot_tn(xn_rows, dqkv_rows).astype(bf16).reshape(D, 6, HP)[..., :DH]
+    dxn, qkv_sums, out_sums = share(
+        dxn_parts,
+        grad_qkv.reshape(ROW_TILES, 2, CHIPS, 2, part, 6 * DH),
+        grad_out.reshape(ROW_TILES, 2, 2, part, D),
+    )
+    dinput, grad_gain_attn = norm_backward(input_float, input_scale, gain_attn, dxn)
+    input_grad = dinput + dhmid
+
+    taps = jnp.asarray(band())
+    theta_sums = theta_sums.reshape(2, seq_len, CQ, seq_len)
+    grad_theta = jnp.stack(
+        [jnp.sum(jnp.where(taps[tap][None, :, None, :], theta_sums, 0.0), axis=(1, 3)) for tap in range(CK)], axis=2
+    )
+    grad_mixer = jnp.sum(mixer_sums[:4], axis=1)
+    vector_grad = jnp.concatenate(
+        [
+            grad_gain_attn,
+            lax.dynamic_update_slice_in_dim(
+                jnp.zeros((D,), f32), gain_sums.reshape(2, HP)[:, :DH].reshape(-1), chip * 2 * DH, 0
+            ),
+            grad_gain_ffn,
+            lax.dynamic_update_slice_in_dim(
+                jnp.zeros((H * CQ * CK,), f32), grad_theta.reshape(-1), chip * 2 * CQ * CK, 0
+            ),
+            lax.dynamic_update_slice_in_dim(jnp.zeros((2 * H,), f32), grad_mixer, chip * 4, 0),
+        ]
+    )
+    pieces = jnp.pad(vector_grad.reshape(fs_size, 1, own_vec), ((0, 0), (0, 0), (0, 1024 - own_vec)))
+    pieces = jnp.broadcast_to(pieces, (fs_size, reps, 1024)).reshape(devices, 8, 128)
+
+    grad_in = dot_tn(hn_rows, dboth).reshape(ROW_TILES, 2, CHIPS, strip, 2, BLK)
+    grad_down = dot_tn(inner, dy_rows).reshape(2, CHIPS, strip, ROW_TILES, BLK)
+    grad_in = jnp.transpose(half_for_core(grad_in, 1), (1, 3, 0, 2, 4)).reshape(CHIPS, 2 * ROW_TILES, strip, BLK)
+    grad_down = jnp.transpose(half_for_core(grad_down, 0), (0, 2, 1, 3))
+    ffn_tiles = exchange_chips(jnp.concatenate([grad_in, grad_down], axis=1).astype(bf16))
+    gate_tiles = jnp.transpose(ffn_tiles[:, : 2 * ROW_TILES], (1, 0, 2, 3)).reshape(-1, strip, BLK)
+    down_tiles = ffn_tiles[:, 2 * ROW_TILES :].reshape(-1, strip, BLK)
+    ffn_sums = sum_groups(jnp.concatenate([gate_tiles, down_tiles], axis=0))
+
+    own_slots = basis_left.shape[0]
+    slot_total = own_slots * devices
+    sums = jnp.concatenate(
+        [
+            jnp.transpose(qkv_sums.reshape(3, ROW_TILES, part, ROW_TILES, BLK), (0, 1, 3, 2, 4)).reshape(-1, part, BLK),
+            jnp.transpose(out_sums.reshape(ROW_TILES, part, ROW_TILES, BLK), (0, 2, 1, 3)).reshape(-1, part, BLK),
+            ffn_sums,
+        ],
+        axis=0,
+    )
+    matches = (jnp.arange(slot_total)[:, None] == owners[None, :]).astype(bf16)
+    slots = dot(matches, sums.reshape(sums.shape[0], -1)).astype(bf16)
+    slots, pieces = to_slots(slots.reshape(devices, own_slots * part, BLK), pieces)
+    vector_total = jnp.sum(pieces, axis=0).reshape(1024)[:own_vec]
+    slots = slots.reshape(2, 2, 2, 2, 2, own_slots, part, BLK)
+    own_grad = jnp.transpose(slots, (5, 3, 4, 1, 2, 0, 6, 7)).reshape(own_slots, BLK, BLK)
+
+    left_low, right_low = basis_left.astype(bf16), basis_right.astype(bf16)
+    rotated = jnp.einsum("sia,sij->saj", left_low, own_grad, preferred_element_type=f32)
+    rotated = jnp.einsum("saj,sjb->sab", rotated.astype(bf16), right_low, preferred_element_type=f32)
+    first_new = beta_first * block_first + (1.0 - beta_first) * rotated
+    second_new = beta_second * block_second + (1.0 - beta_second) * rotated * rotated
+    direction = (first_new / (jnp.sqrt(second_new) + eps_adam)).astype(bf16)
+    turned = jnp.einsum("sia,sab->sib", left_low, direction, preferred_element_type=f32)
+    turned = jnp.einsum("sib,sjb->sij", turned.astype(bf16), right_low, preferred_element_type=f32)
+    master_new = block_master - rate_block * (turned + decay_block * block_master)
+    vec_first_new = beta_first * vec_first + (1.0 - beta_first) * vector_total
+    vec_second_new = beta_second * vec_second + (1.0 - beta_second) * vector_total * vector_total
+    vec_master_new = vec_master - rate_vector * vec_first_new / (jnp.sqrt(vec_second_new) + eps_adam)
+    return (
+        layer_output, input_grad, first_new, second_new, master_new, master_new.astype(bf16),
+        vec_first_new, vec_second_new, vec_master_new, vec_master_new.astype(bf16),
+    )
+
+
 def solution(mesh):
     fsdp, rep = mesh.shape["fsdp"], mesh.shape["rep"]
     fine = Mesh(mesh.devices.reshape(fsdp // 8, 2, 2, 2, rep), ALL)
     rows, both = P(ALL, None), P(ALL, None, None)
     weight, vec = P(FS, None), P(FS)
     return jax.shard_map(
-        body,
+        body_fast if (fsdp, rep) == (16, 2) else body_any,
         mesh=fine,
         in_specs=(rows, P(ALL), rows) + (weight,) * 7 + (vec, P()) + (both,) * 5 + (vec,) * 3,
         out_specs=(rows, rows) + (both,) * 4 + (vec,) * 4,

time: 737 us -> 686 us (0.931)
  starting transfers between devices: 116 us -> 51 us
  Pallas kernels: 199 us -> 260 us
  local copies, waits for them, and re-layouts: 129 us -> 94 us
  other arithmetic: 55.8 us -> 39.1 us
  waiting for transfers between devices: 131 us -> 146 us
  matrix products: 77.3 us -> 69.1 us
    pallas_call x2 -> x4, Pallas kernels: 120 us -> 199 us  [the longest x1 57.1 us: to_slots(): pl.pallas_call(to_slots_body, in_specs=[ANYS] * 2, out_specs=[ANYS] * 2,...]
    ppermute x10 -> x6, waiting for transfers between devices: 19.2 us -> 94.4 us  [swap(): return lax.ppermute(values, axis, [(0, 1), (1, 0)])]
    all_to_all x2 -> x0, waiting for transfers between devices: 42.7 us -> none  [the longest x1 42.7 us: body(): lax.all_to_all(slots.reshape(devices, own_slots, part, BLK), ALL, split_a...]
    all_to_all x2 -> x1, waiting for transfers between devices: 35.4 us -> 0.01 us  [gather_slow(): lax.all_to_all(jnp.broadcast_to(rows[None], (CHIPS,) + rows.shape), CHIP,...]
    all_to_all x2 -> x1, waiting for transfers between devices: 20.1 us -> 51.2 us  [to_columns(): lax.all_to_all(sent, ('g', 'a', 'b'), split_axis=0, concat_axis=0, tiled=...]
    all_to_all x2 -> x0, starting transfers between devices: 28.6 us -> none  [the longest x1 21.6 us: body(): lax.all_to_all(pieces, ALL, split_axis=0, concat_axis=0, tiled=True)]
    pallas_call x1, Pallas kernels: 48.8 us -> 28.6 us  [scatter_chips(): pl.pallas_call(scatter_body, in_specs=[vmem], out_specs=vmem, out_shape=j...]
    all_to_all x7 -> x4, starting transfers between devices: 42.7 us -> 28 us  [exchange_chips(): return lax.all_to_all(parts, CHIP, split_axis=0, concat_axis=0, tiled=True)]
  transfers between devices with their start and end apart: 24 -> 13, of which waited for: 9 -> 4; matrix products, arithmetic and copies ran while one was open for 26% -> 18% of each run, Pallas kernels for 24% -> 22%
where the time goes in v3:
time: 686 us; the launch traced here: 676 us
  Pallas kernels  260 us (38%)
  waiting for transfers between devices  146 us (21%)
  local copies, waits for them, and re-layouts  94 us (14%)
  matrix products  69.1 us (10%)
  starting transfers between devices  51 us (7%)
  other arithmetic  39.1 us (6%)
  between operations  16.6 us (2%)
    ppermute x6, waiting for transfers between devices, swap(): return lax.ppermute(values, axis, [(0, 1), (1, 0)])  94.4 us
    pallas_call x1, Pallas kernels, to_slots(): pl.pallas_call(to_slots_body, in_specs=[ANYS] * 2, out_specs=[ANYS] * 2,...  57.1 us
    all_to_all x1, waiting for transfers between devices, to_columns(): lax.all_to_all(sent, ('g', 'a', 'b'), split_axis=0, concat_axis=0, tiled=...  51.2 us
    pallas_call x1, Pallas kernels, share(): pl.pallas_call(share_body, in_specs=[VMEM] * 3, out_specs=[VMEM] * 3, out...  49.7 us
    pallas_call x1, Pallas kernels, dispatch(): pl.pallas_call(dispatch_body, in_specs=[ANYS] * 3, out_specs=[ANYS] * 3,...  46.6 us
    pallas_call x1, Pallas kernels, run_back(): pl.pallas_call(back_body, in_specs=[SMEM, SMEM] + [VMEM] * 9, out_specs=[...  46 us
    pallas_call x1, Pallas kernels, scatter_chips(): pl.pallas_call(scatter_body, in_specs=[vmem], out_specs=vmem, out_shape=j...  28.6 us
    all_to_all x4, starting transfers between devices, exchange_chips(): return lax.all_to_all(parts, CHIP, split_axis=0, concat_axis=0, tiled=True)  28 us
  transfers between devices with their start and end apart: 13, of which 4 were waited for; matrix products, arithmetic and copies ran while one was open for 18% of the time, Pallas kernels for 22%

profile of v3, /device:TPU:11, one launch (start us, length us, event | category | flops | bytes accessed | tf_op | source)
XLA Modules:
  0.0 676.2 jit_solution(14232522324591051736)
XLA Ops:
  13.8 46.6 %dispatch.1 = (bf16[8,128,1536]{2,1,0:T(8,128)(2,1)}, f32[32,8,128]{2,1,0:T(8,128)}, bf16[16,96,576]{2,1,0:T(8,128)(2,1)}) custom-call(bf16[128,1536]{1,0:T(8,128)(2,1)} %x_ref.1, f32[8,128]{1,0:T(8,128)} %maximum_bitcast_fusion.1.vec_ref, bf16[8,96,576]{2,1,0:T(8,128)(2,1)} %maximum_bitcast_fusion.blocks_ref), custom_call_target="tpu_custom_call" | custom-call | tf_op jit(solution)/shard_map/dispatch/pallas_call | solution.py:884
  70.9 5.1 reshape.450
  84.5 9.2 %attention_forward.1 = (bf16[8,128,256]{2,1,0:T(8,128)(2,1)S(1)}, bf16[8,2,128,128]{3,2,1,0:T(8,128)(2,1)S(1)}, f32[8,2,128,128]{3,2,1,0:T(8,128)S(1)}, f32[8,128,256]{2,1,0:T(8,128)S(1)}) custom-call(s32[8]{0:T(128)S(1)} %convert_element_type.154.len_ref, f32[4]{0:T(128)S(1)} %reshape.449.mix_ref, bf16[8,128,768]{2,1,0:T(8,128)(2,1)S(1)} %bitcast.279, ...), custom_call_target="tpu_custom_call" | custom-call | flops 2000000000 | bytes 8388608 | tf_op jit(solution)/shard_map/attention_forward/pallas_call | solution.py:180
  97.5 4.5 all-to-all-start
  110.9 3.8 all-to-all-start.1
  118.5 51.2 %all-to-all-done.1 = bf16[8,96,1024]{2,1,0:T(8,128)(2,1)S(1)} async-done(((bf16[8,96,1024]{2,1,0:T(8,128)(2,1)}), bf16[8,96,1024]{2,1,0:T(8,128)(2,1)S(1)}, u32[]{:S(2)}, u32[]{:S(2)}) %all-to-all-start.1) | async-done | bytes 1572896 | tf_op jit(solution)/shard_map/all_to_all | solution.py:504
  172.8 9.6 %all-to-all-start.3 = ((bf16[8,128,1536]{1,2,0:T(8,128)(2,1)}), bf16[8,128,1536]{1,2,0:T(8,128)(2,1)}, u32[]{:S(2)}, u32[]{:S(2)}) async-start(bf16[8,128,1536]{1,2,0:T(8,128)(2,1)} %broadcast_in_dim.503), calls=%async_computation.3 | async-start | bytes 6291456 | tf_op jit(solution)/shard_map/all_to_all | solution.py:453
  182.4 50.8 %collective-permute-done.1 = bf16[256,1536]{1,0:T(8,128)(2,1)} collective-permute-done((bf16[256,1536]{1,0:T(8,128)(2,1)}, bf16[256,1536]{1,0:T(8,128)(2,1)}, u32[]{:S(2)}, u32[]{:S(2)}) %collective-permute-start.1) | collective-permute-done | bytes 786464 | tf_op jit(solution)/shard_map/ppermute | solution.py:467
  235.3 3.6 collective-permute-start.2
  248.6 10.2 %all-to-all-start.4 = ((bf16[8,128,192]{1,2,0:T(8,128)(2,1)}), bf16[8,128,192]{1,2,0:T(8,128)(2,1)S(1)}, u32[]{:S(2)}, u32[]{:S(2)}) async-start(bf16[8,128,192]{1,2,0:T(8,128)(2,1)} %bitcast.46), calls=%async_computation.4 | async-start | bytes 786432 | tf_op jit(solution)/shard_map/all_to_all | solution.py:459
  258.8 4.7 copy.215
  268.5 23.1 %gather_chips.1 = bf16[8,128,1536]{2,1,0:T(8,128)(2,1)} custom-call(bf16[128,1536]{1,0:T(8,128)(2,1)} %multiply_convert_fusion.3.x_ref), custom_call_target="tpu_custom_call" | custom-call | tf_op jit(solution)/shard_map/gather_chips/pallas_call | solution.py:375
  291.6 6.6 fusion.66
  298.2 4.1 multiply_convert_fusion.1
  304.6 5.2 convolution_convert_fusion.2
  309.9 6.1 all-to-all-start.2
  325.1 4.7 copy.225
  329.8 4.7 copy.223
  336.7 3.5 fusion.67
  340.5 3.7 collective-permute-start.3
  347.8 3.9 convolution_convert_fusion.3
  351.8 28.6 %scatter_chips.1 = f32[128,1536]{1,0:T(8,128)S(1)} custom-call(bf16[8,128,1536]{2,1,0:T(8,128)(2,1)S(1)} %bitcast.276), custom_call_target="tpu_custom_call" | custom-call | tf_op jit(solution)/shard_map/scatter_chips/pallas_call | solution.py:440
  383.3 7.2 %all-to-all-start.5 = ((bf16[8,9,32,512]{3,2,1,0:T(8,128)(2,1)}), bf16[8,9,32,512]{3,2,1,0:T(8,128)(2,1)}, u32[]{:S(2)}, u32[]{:S(2)}) async-start(bf16[8,9,32,512]{3,2,1,0:T(8,128)(2,1)} %pad_maximum_fusion.1), calls=%async_computation.5 | async-start | bytes 4718592 | tf_op jit(solution)/shard_map/all_to_all | solution.py:459
  394.3 4.0 convolution_convert_fusion.4
  404.8 46.0 %attention_back.1 = (bf16[8,128,768]{2,1,0:T(8,128)(2,1)S(1)}, f32[2,128,768]{2,1,0:T(8,128)S(1)}, f32[8,128]{1,0:T(8,128)S(1)}, f32[1,256]{1,0:T(1,128)S(1)}, bf16[192,1536]{1,0:T(8,128)(2,1)S(1)}) custom-call(s32[8]{0:T(128)S(1)} %convert_element_type.154.len_ref, f32[4]{0:T(128)S(1)} %reshape.449.mix_ref, bf16[8,128,768]{2,1,0:T(8,128)(2,1)S(1)} %bitcast.280, ...), custom_call_target="tpu_custom_call" | custom-call | tf_op jit(solution)/shard_map/attention_back/pallas_call | solution.py:992
  457.3 4.9 reshape.473.gq_ref
  466.7 4.8 convolution_convert_fusion.1
  471.5 49.7 %share_gradients.1 = (f32[128,1536]{1,0:T(8,128)S(1)}, bf16[3,3,16,1536]{3,2,1,0:T(8,128)(2,1)S(1)}, bf16[3,16,1536]{2,1,0:T(8,128)(2,1)S(1)}) custom-call(bf16[8,128,1536]{2,1,0:T(8,128)(2,1)S(1)} %bitcast.275, bf16[3,2,8,2,16,576]{5,4,3,2,1,0:T(8,128)(2,1)S(1)} %reshape.473.gq_ref, bf16[3,2,2,16,1536]{4,3,2,1,0:T(8,128)(2,1)S(1)} %bitcast.281), custom_call_target="tpu_custom_call" | custom-call | tf_op jit(solution)/shard_map/share_gradients/pallas_call | solution.py:1075
  535.6 42.1 %collective-permute-done.5 = bf16[72,16,512]{2,1,0:T(8,128)(2,1)} collective-permute-done((bf16[72,16,512]{2,1,0:T(8,128)(2,1)}, bf16[72,16,512]{2,1,0:T(8,128)(2,1)}, u32[]{:S(2)}, u32[]{:S(2)}) %collective-permute-start.5) | collective-permute-done | bytes 1179680 | tf_op jit(solution)/shard_map/ppermute | solution.py:467
  583.6 57.1 %to_slots.1 = (bf16[32,64,512]{2,1,0:T(8,128)(2,1)}, f32[32,8,128]{2,1,0:T(8,128)}) custom-call(bf16[32,64,512]{2,1,0:T(8,128)(2,1)} %reshape.479.slots_ref, f32[32,8,128]{2,1,0:T(8,128)} %reshape.484.vec_ref), custom_call_target="tpu_custom_call" | custom-call | tf_op jit(solution)/shard_map/to_slots/pallas_call | solution.py:1126
  642.7 12.1 %fusion.3 = (f32[4,512,512]{2,1,0:T(8,128)}, f32[4,512,512]{2,1,0:T(8,128)}) fusion(f32[4,512,512]{2,1,0:T(8,128)} %param.37, f32[4,512,512]{2,1,0:T(8,128)} %param.36, f32[4,512,512]{2,1,0:T(8,128)} %param.34, bf16[4,512,512]{2,1,0:T(8,128)(2,1)S(1)} %bitcast.292, f32[4,512,512]{2,1,0:T(8,128)} %param.33), kind=kOutput, calls=%fused_computation.10 | convolution fusion | flops 2156920832 | bytes 27262976 | tf_op jit(solution)/shard_map/saj,sjb->sab/dot_general | solution.py:1280
  654.8 13.5 %fusion.63 = (bf16[4,512,512]{2,1,0:T(8,128)(2,1)}, f32[4,512,512]{2,1,0:T(8,128)}) fusion(f32[4,512,512]{2,1,0:T(8,128)} %param.35, f32[4,512,512]{2,1,0:T(8,128)} %param.34, f32[4,512,512]{2,1,0:T(8,128)} %get-tuple-element.93, f32[4,512,512]{2,1,0:T(8,128)} %get-tuple-element.92, f32[4,512,512]{2,1,0:T(8,128)} %param.33), kind=kOutput, calls=%fused_computation.184 | convolution fusion | flops 2159017984 | bytes 27262976 | tf_op jit(solution)/shard_map/sib,sjb->sij/dot_general | solution.py:1285
  (356 shorter events, 124.8 us)
Async XLA Ops:
  84.4 9.2 %copy-start = (bf16[2,768,128]{2,1,0:T(8,128)(2,1)}, bf16[2,768,128]{2,1,0:T(8,128)(2,1)S(1)}, u32[]{:S(2)}) copy-start(bf16[2,768,128]{2,1,0:T(8,128)(2,1)S(1)} %select_convert_fusion.toep_ref) | copy-start | bytes 1179652
  97.5 12.1 %all-to-all-start = ((bf16[8,128,192]{1,2,0:T(8,128)(2,1)}), bf16[8,128,192]{1,2,0:T(8,128)(2,1)S(1)}, u32[]{:S(2)}, u32[]{:S(2)}) async-start(bf16[8,128,192]{1,2,0:T(8,128)(2,1)} %bitcast.22), calls=%async_computation | async-start | bytes 786432 | tf_op jit(solution)/shard_map/all_to_all | solution.py:459
  102.0 161.5 %all-gather.2.cloned.1.call-start = ((), (), s32[]{:S(2)}) async-start(), calls=%async_computation.6 | async-start | bytes 5013504 | tf_op jit(solution)/shard_map/all_gather | solution.py:1177
  110.9 58.8 %all-to-all-start.1 = ((bf16[8,96,1024]{2,1,0:T(8,128)(2,1)}), bf16[8,96,1024]{2,1,0:T(8,128)(2,1)S(1)}, u32[]{:S(2)}, u32[]{:S(2)}) async-start(bf16[8,96,1024]{2,1,0:T(8,128)(2,1)} %bitcast.30), calls=%async_computation.1 | async-start | bytes 3145728 | tf_op jit(solution)/shard_map/all_to_all | solution.py:504
  172.8 75.8 %all-to-all-start.3 = ((bf16[8,128,1536]{1,2,0:T(8,128)(2,1)}), bf16[8,128,1536]{1,2,0:T(8,128)(2,1)}, u32[]{:S(2)}, u32[]{:S(2)}) async-start(bf16[8,128,1536]{1,2,0:T(8,128)(2,1)} %broadcast_in_dim.503), calls=%async_computation.3 | async-start | bytes 6291456 | tf_op jit(solution)/shard_map/all_to_all | solution.py:453
  182.4 50.8 %collective-permute-start.1 = (bf16[256,1536]{1,0:T(8,128)(2,1)}, bf16[256,1536]{1,0:T(8,128)(2,1)}, u32[]{:S(2)}, u32[]{:S(2)}) collective-permute-start(bf16[256,1536]{1,0:T(8,128)(2,1)} %param.30), channel_id=1, source_target_pairs={{0,16},{16,0},{1,17},{17,1},{2,18},{18,2},{3,19},{19,3},{4,20},{20... | collective-permute-start | bytes 2359304 | tf_op jit(solution)/shard_map/ppermute | solution.py:467
  235.3 7.0 %collective-permute-start.2 = (bf16[256,1536]{1,0:T(8,128)(2,1)}, bf16[256,1536]{1,0:T(8,128)(2,1)}, u32[]{:S(2)}, u32[]{:S(2)}) collective-permute-start(bf16[256,1536]{1,0:T(8,128)(2,1)} %broadcast_select_fusion), channel_id=1, source_target_pairs={{0,2},{2,0},{1,3},{3,1},{4,6},{6,4},{5,7},{7,5},{8,10},{10,8},{9,1... | collective-permute-start | bytes 2359304 | tf_op jit(solution)/shard_map/ppermute | solution.py:467
  238.9 6.1 collective-permute-start
  248.6 61.3 %all-to-all-start.4 = ((bf16[8,128,192]{1,2,0:T(8,128)(2,1)}), bf16[8,128,192]{1,2,0:T(8,128)(2,1)S(1)}, u32[]{:S(2)}, u32[]{:S(2)}) async-start(bf16[8,128,192]{1,2,0:T(8,128)(2,1)} %bitcast.46), calls=%async_computation.4 | async-start | bytes 786432 | tf_op jit(solution)/shard_map/all_to_all | solution.py:459
  291.6 6.6 copy-start.13
  291.6 6.6 copy-start.31
  309.8 6.3 copy-start.55
  309.8 6.5 copy-start.54
  309.8 6.8 copy-start.53
  309.8 7.6 %copy-start.52 = (pred[128,128]{0,1:T(32,128)(4,1)S(1)}, pred[128,128]{0,1:T(32,128)(4,1)}, u32[]{:S(2)}) copy-start(pred[128,128]{0,1:T(32,128)(4,1)} %constant.181) | copy-start | bytes 49156
  309.8 8.5 %copy-start.51 = (pred[128,128]{0,1:T(32,128)(4,1)S(1)}, pred[128,128]{0,1:T(32,128)(4,1)}, u32[]{:S(2)}) copy-start(pred[128,128]{0,1:T(32,128)(4,1)} %constant.179) | copy-start | bytes 49156
  309.8 9.3 %copy-start.50 = (pred[128,128]{0,1:T(32,128)(4,1)S(1)}, pred[128,128]{0,1:T(32,128)(4,1)}, u32[]{:S(2)}) copy-start(pred[128,128]{0,1:T(32,128)(4,1)} %constant.177) | copy-start | bytes 49156
  309.8 10.1 %copy-start.49 = (pred[128,128]{0,1:T(32,128)(4,1)S(1)}, pred[128,128]{0,1:T(32,128)(4,1)}, u32[]{:S(2)}) copy-start(pred[128,128]{0,1:T(32,128)(4,1)} %constant.175) | copy-start | bytes 49156
  309.9 11.0 %copy-start.48 = (pred[128,128]{0,1:T(32,128)(4,1)S(1)}, pred[128,128]{0,1:T(32,128)(4,1)}, u32[]{:S(2)}) copy-start(pred[128,128]{0,1:T(32,128)(4,1)} %constant.173) | copy-start | bytes 49156
  309.9 73.4 %all-to-all-start.2 = ((bf16[8,128,1536]{2,1,0:T(8,128)(2,1)}), bf16[8,128,1536]{2,1,0:T(8,128)(2,1)}, u32[]{:S(2)}, u32[]{:S(2)}) async-start(bf16[8,128,1536]{2,1,0:T(8,128)(2,1)} %convolution_convert_fusion.2), calls=%async_computation.2 | async-start | bytes 6291456 | tf_op jit(solution)/shard_map/all_to_all | solution.py:459
  316.0 6.5 copy-start.46
  316.0 7.3 %copy-start.45 = (pred[128,128]{0,1:T(32,128)(4,1)S(1)}, pred[128,128]{0,1:T(32,128)(4,1)}, u32[]{:S(2)}) copy-start(pred[128,128]{0,1:T(32,128)(4,1)} %constant.167) | copy-start | bytes 49156
  336.7 7.5 %copy-start.33 = (bf16[1024,512]{0,1:T(8,128)(2,1)S(1)}, bf16[1024,512]{0,1:T(8,128)(2,1)}, u32[]{:S(2)}) copy-start(bf16[1024,512]{0,1:T(8,128)(2,1)} %get-tuple-element.94) | copy-start | bytes 3145732
  340.5 40.5 %collective-permute-start.3 = (bf16[3,8,32,2,512]{4,2,3,1,0:T(8,128)(2,1)S(1)}, bf16[3,8,32,2,512]{4,2,3,1,0:T(8,128)(2,1)S(1)}, u32[]{:S(2)}, u32[]{:S(2)}) collective-permute-start(bf16[3,8,32,2,512]{4,2,3,1,0:T(8,128)(2,1)S(1)} %fusion.17), channel_id=1, source_target_pairs={{0,2},{2,0},{1,3},{3,1},{4,6},{6,4},{5,7},{7,5},{8,10},{10,8},{9,1... | collective-permute-start | bytes 4718600 | tf_op jit(solution)/shard_map/ppermute | solution.py:467
  346.2 34.5 %collective-permute-start.4 = (bf16[8,32,3,512]{3,1,2,0:T(8,128)(2,1)S(1)}, bf16[8,32,3,512]{3,1,2,0:T(8,128)(2,1)S(1)}, u32[]{:S(2)}, u32[]{:S(2)}) collective-permute-start(bf16[8,32,3,512]{3,1,2,0:T(8,128)(2,1)S(1)} %fusion.37), channel_id=1, source_target_pairs={{0,2},{2,0},{1,3},{3,1},{4,6},{6,4},{5,7},{7,5},{8,10},{10,8},{9,1... | collective-permute-start | bytes 2359304 | tf_op jit(solution)/shard_map/ppermute | solution.py:467
  351.8 28.6 %copy-start.15 = (f32[128,1536]{1,0:T(8,128)S(1)}, f32[128,1536]{1,0:T(8,128)}, u32[]{:S(2)}) copy-start(f32[128,1536]{1,0:T(8,128)} %copy-done.14) | copy-start | bytes 2359300
  383.3 138.6 %all-to-all-start.5 = ((bf16[8,9,32,512]{3,2,1,0:T(8,128)(2,1)}), bf16[8,9,32,512]{3,2,1,0:T(8,128)(2,1)}, u32[]{:S(2)}, u32[]{:S(2)}) async-start(bf16[8,9,32,512]{3,2,1,0:T(8,128)(2,1)} %pad_maximum_fusion.1), calls=%async_computation.5 | async-start | bytes 4718592 | tf_op jit(solution)/shard_map/all_to_all | solution.py:459
  404.8 46.0 %copy-start.28 = (bf16[8,128,1536]{2,1,0:T(8,128)(2,1)S(1)}, bf16[8,128,1536]{2,1,0:T(8,128)(2,1)}, u32[]{:S(2)}) copy-start(bf16[8,128,1536]{2,1,0:T(8,128)(2,1)} %copy-done.27) | copy-start | bytes 9437188
  526.0 51.6 %collective-permute-start.5 = (bf16[72,16,512]{2,1,0:T(8,128)(2,1)}, bf16[72,16,512]{2,1,0:T(8,128)(2,1)}, u32[]{:S(2)}, u32[]{:S(2)}) collective-permute-start(bf16[72,16,512]{2,1,0:T(8,128)(2,1)} %fusion.20), channel_id=1, source_target_pairs={{0,16},{16,0},{1,17},{17,1},{2,18},{18,2},{3,19},{19,3},{4,20},{20... | collective-permute-start | bytes 3538952 | tf_op jit(solution)/shard_map/ppermute | solution.py:467
  654.8 13.5 %copy-start.59 = (f32[356]{0:T(512)S(1)}, f32[356]{0:T(512)}, u32[]{:S(2)}) copy-start(f32[356]{0:T(512)} %param.38) | copy-start | bytes 4276
  654.8 13.5 %copy-start.60 = (f32[356]{0:T(512)S(1)}, f32[356]{0:T(512)}, u32[]{:S(2)}) copy-start(f32[356]{0:T(512)} %param.40) | copy-start | bytes 4276
  654.8 13.5 %copy-start.61 = (f32[356]{0:T(512)S(1)}, f32[356]{0:T(512)}, u32[]{:S(2)}) copy-start(f32[356]{0:T(512)} %param.39) | copy-start | bytes 4276
  (44 other events, 137.2 us)
Sparse Core Ops, SparseCore 0:
  105.1 74.7 all-gather.1

commit v4 on v3

--- a/solution.py
+++ b/solution.py
@@ -756,6 +756,61 @@
             copy.wait_send()
 
 
+class SideGather:
+    def __init__(self, x_ref, out_ref, local_sem, send1, recv1, send2, recv2, send3, recv3):
+        self.x, self.out, self.local_sem = x_ref, out_ref, local_sem
+        self.sems = ((send1, recv1), (send2, recv2), (send3, recv3))
+        self.me = chip_index()
+        half = x_ref.shape[0] // 2
+        self.low, self.high = pl.ds(0, half), pl.ds(half, half)
+
+    def start(self):
+        self.local = pltpu.make_async_copy(self.x, self.out.at[self.me], self.local_sem)
+        self.local.start()
+        send, recv = self.sems[0]
+        self.first = [
+            push(self.x, self.out.at[self.me], send.at[at], recv.at[at], across(axis)) for at, axis in enumerate("aby")
+        ]
+
+    def onward(self):
+        send, recv = self.sems[1]
+        blocks = [self.out.at[flipped(self.me, (axis,))] for axis in "aby"]
+        self.first[0].wait_recv()
+        self.second = [
+            push(blocks[0], blocks[0], send.at[0], recv.at[0], across("b")),
+            push(blocks[0], blocks[0], send.at[1], recv.at[1], across("y")),
+        ]
+        self.first[1].wait_recv()
+        piece = blocks[1].at[self.high]
+        self.second.append(push(piece, piece, send.at[2], recv.at[2], across("y")))
+        self.first[2].wait_recv()
+        piece = blocks[2].at[self.low]
+        self.second.append(push(piece, piece, send.at[3], recv.at[3], across("b")))
+
+    def last(self):
+        send, recv = self.sems[2]
+        self.second[0].wait_recv()
+        piece = self.out.at[flipped(self.me, ("a", "b")), self.high]
+        self.third = [push(piece, piece, send.at[0], recv.at[0], across("y"))]
+        self.second[1].wait_recv()
+        piece = self.out.at[flipped(self.me, ("a", "y")), self.low]
+        self.third.append(push(piece, piece, send.at[1], recv.at[1], across("b")))
+
+    def finish(self):
+        for copy in self.second[2:] + self.third:
+            copy.wait_recv()
+        self.local.wait()
+
+    def drain(self):
+        for copy in self.first + self.second + self.third:
+            copy.wait_send()
+
+
+def side_sems():
+    dma = pltpu.SemaphoreType.DMA
+    return [dma] + [dma((3,))] * 2 + [dma((4,))] * 2 + [dma((2,))] * 2
+
+
 class Scatter:
     def __init__(self, parts, near, in2, in3, acc2, acc3, send1, recv1, send2, recv2, send3, recv3):
         self.parts, self.near, self.in2, self.in3, self.acc2, self.acc3 = parts, near, in2, in3, acc2, acc3
@@ -830,8 +885,9 @@
 
 
 def dispatch_body(
-    x_ref, vec_ref, blocks_ref, out_ref, vecs_ref, wq_ref,
-    vec_send, vec_recv, vec_local, w_local, w_send, w_recv, core_send, core_recv, *hops,
+    x_ref, vec_ref, blocks_ref, w_out_ref, out_ref, vecs_ref, wq_ref, wo_ref,
+    vec_send, vec_recv, vec_local, w_local, o_local, w_send, w_recv, core_send, core_recv,
+    o_send, o_recv, o_side_send, o_side_recv, o_core_send, o_core_recv, *hops,
 ):
     devices = lax.axis_size(ALL)
     me = device_index()
@@ -841,6 +897,8 @@
     local.start()
     own = pltpu.make_async_copy(blocks_ref.at[chip_index()], wq_ref.at[mine], w_local)
     own.start()
+    own_out = pltpu.make_async_copy(w_out_ref, wo_ref.at[mine], o_local)
+    own_out.start()
     greet_all()
     gather = Gather(x_ref, out_ref, *hops)
     gather.start()
@@ -857,43 +915,287 @@
     for mask in (4, 6, 5, 7, 2, 1, 3):
         block = (y * 2 + other_bit("a", mask & 2)) * 2 + other_bit("b", mask & 1)
         sent.append(push(blocks_ref.at[block], wq_ref.at[mine], w_send.at[mask], w_recv.at[mask], group_at(mask)))
+    half = pl.ds(pl.multiple_of(y * 48, 16), 48)
+    shard = {mask: source_at(mask) for mask in range(8)}
+    lines = {
+        mask: push(w_out_ref.at[half], wo_ref.at[mine, half], o_send.at[mask], o_recv.at[mask], group_at(mask))
+        for mask in (2, 4, 6)
+    }
+    lines[1] = push(w_out_ref.at[half], wo_ref.at[mine, half], o_send.at[1], o_recv.at[1], across("b"))
+    o_core = [push(w_out_ref, wo_ref.at[mine], o_core_send.at[0], o_core_recv.at[0], across("c"))]
     own.wait()
     relayed.append(push(wq_ref.at[mine], wq_ref.at[mine], core_send.at[0], core_recv.at[0], across("c")))
     gather.onward()
-    for at, mask in enumerate((4, 6, 5, 7, 2, 1, 3)):
-        sent[at].wait_recv()
-        source = ((other_bit("g", mask & 4) * 2 + other_bit("a", mask & 2)) * 2 + other_bit("b", mask & 1)) * 2 + c
-        relayed.append(push(wq_ref.at[source], wq_ref.at[source], core_send.at[mask], core_recv.at[mask], across("c")))
-        if at == 1:
-            gather.last()
+    o_side = {}
+
+    def to_side(mask):
+        lines[mask].wait_recv()
+        piece = wo_ref.at[shard[mask], half]
+        o_side[mask] = push(piece, piece, o_side_send.at[mask], o_side_recv.at[mask], across("y"))
+
+    def relay(mask):
+        sent[(4, 6, 5, 7, 2, 1, 3).index(mask)].wait_recv()
+        block = wq_ref.at[shard[mask]]
+        relayed.append(push(block, block, core_send.at[mask], core_recv.at[mask], across("c")))
+
+    for mask in (2, 4, 6):
+        lines[mask].wait_recv()
+        piece = wo_ref.at[shard[mask], half]
+        lines[mask + 1] = push(piece, piece, o_send.at[mask + 1], o_recv.at[mask + 1], across("b"))
+        o_side[mask] = push(piece, piece, o_side_send.at[mask], o_side_recv.at[mask], across("y"))
+    to_side(1)
+    relay(4)
+    relay(6)
+    gather.last()
+    for mask in (3, 5, 7):
+        to_side(mask)
+    for mask in (5, 7, 2, 1, 3):
+        relay(mask)
+    for mask in (2, 4, 6, 1, 3, 5, 7):
+        o_side[mask].wait_recv()
+        block = wo_ref.at[shard[mask]]
+        o_core.append(push(block, block, o_core_send.at[mask], o_core_recv.at[mask], across("c")))
     gather.finish()
-    for copy in relayed:
+    for copy in relayed + o_core:
         copy.wait_recv()
     others = vecs_ref.at[pl.ds(0, devices - 1)]
     pltpu.make_async_copy(others, others, vec_recv).wait()
     pltpu.make_async_copy(others, others, vec_send).wait()
     local.wait()
+    own_out.wait()
     gather.drain()
-    for copy in sent + relayed:
+    for copy in sent + relayed + list(lines.values()) + list(o_side.values()) + o_core:
         copy.wait_send()
 
 
-def dispatch(rows, vec, blocks):
+def source_at(mask):
+    return ((other_bit("g", mask & 4) * 2 + other_bit("a", mask & 2)) * 2 + other_bit("b", mask & 1)) * 2 + lax.axis_index("c")
+
+
+def dispatch(rows, vec, blocks, w_out):
     count, width = rows.shape
     dma = pltpu.SemaphoreType.DMA
     return pl.pallas_call(
         dispatch_body,
-        in_specs=[ANYS] * 3,
-        out_specs=[ANYS] * 3,
+        in_specs=[ANYS] * 4,
+        out_specs=[ANYS] * 4,
         out_shape=[
             jax.ShapeDtypeStruct((CHIPS, count, width), rows.dtype),
             jax.ShapeDtypeStruct((lax.axis_size(ALL),) + vec.shape, vec.dtype),
             jax.ShapeDtypeStruct((16,) + blocks.shape[1:], blocks.dtype),
+            jax.ShapeDtypeStruct((16,) + w_out.shape, w_out.dtype),
         ],
-        scratch_shapes=[dma] * 4 + [dma((8,))] * 4 + hop_sems(),
+        scratch_shapes=[dma] * 5 + [dma((8,))] * 10 + hop_sems(),
         name="dispatch",
         compiler_params=pltpu.CompilerParams(collective_id=1, has_side_effects=True),
-    )(rows, vec, blocks)
+    )(rows, vec, blocks, w_out)
+
+
+def forward_body(
+    len_ref, mix_ref, x_all_ref, x_ref, gains_ref, wq_ref, toep_ref, gain_ref, wo_ref, w_gate_ref, w_up_ref, w_down_ref, dy_ref,
+    xn_ref, qkv_ref, s_ref, p_ref, o_ref, heads_ref, hmid_ref, hn_all_ref, w_in_ref, w_dn_ref, dy_all_ref,
+    pad_ref, out_heads, hn_ref, local_sems, w_send, w_recv, u_send, u_recv, core_send, core_recv,
+    d_send, d_recv, head_send, head_recv, *hops,
+):
+    seqs, rows, _ = x_all_ref.shape
+    g, a, b, c, y = (lax.axis_index(axis) for axis in ALL)
+    me = chip_index()
+    mine = source_at(0)
+    low, high = pl.ds(0, BLK), pl.ds(BLK, BLK)
+
+    def columns(chip):
+        return pl.ds(pl.multiple_of(chip * BLK, BLK), BLK)
+
+    greet_all()
+    local = [
+        pltpu.make_async_copy(w_gate_ref.at[:, columns(me)], w_in_ref.at[mine, :, low], local_sems.at[0]),
+        pltpu.make_async_copy(w_up_ref.at[:, columns(me)], w_in_ref.at[mine, :, high], local_sems.at[1]),
+    ]
+    for copy in local:
+        copy.start()
+    gate, up, relayed = {}, {}, []
+    order = (4, 6, 5, 7, 2, 1, 3)
+    for mask in order:
+        to = (y * 2 + other_bit("a", mask & 2)) * 2 + other_bit("b", mask & 1)
+        gate[mask] = push(
+            w_gate_ref.at[:, columns(to)], w_in_ref.at[mine, :, low], w_send.at[mask], w_recv.at[mask], group_at(mask)
+        )
+        up[mask] = push(
+            w_up_ref.at[:, columns(to)], w_in_ref.at[mine, :, high], u_send.at[mask], u_recv.at[mask], group_at(mask)
+        )
+
+    def down_to_group():
+        return pltpu.make_async_remote_copy(
+            src_ref=w_down_ref, dst_ref=w_dn_ref.at[c], send_sem=d_send.at[0], recv_sem=d_recv.at[0], device_id=across("g")
+        )
+
+    def down_to_core():
+        return pltpu.make_async_remote_copy(
+            src_ref=w_dn_ref.at[c], dst_ref=w_dn_ref.at[c], send_sem=d_send.at[1], recv_sem=d_recv.at[1], device_id=across("c")
+        )
+
+    down_local = pltpu.make_async_copy(w_down_ref, w_dn_ref.at[c], local_sems.at[2])
+
+    @pl.when(g == y)
+    def _():
+        down_local.start()
+        down_to_group().start()
+
+    side = SideGather(dy_ref, dy_all_ref, *hops[:7])
+    side.start()
+
+    def relay(mask):
+        gate[mask].wait_recv()
+        up[mask].wait_recv()
+        block = w_in_ref.at[source_at(mask)]
+        relayed.append(push(block, block, core_send.at[mask], core_recv.at[mask], across("c")))
+
+    pad_ref[0:8, :] = jnp.zeros((8, rows), f32)
+    blank = jnp.zeros((rows, HP - DH), bf16)
+    batch = 4
+
+    def project(at, carry):
+        values = x_all_ref[pl.ds(at * batch, batch)].astype(f32).reshape(batch * rows, D)
+        normed = (values * rms(values) * gains_ref[0:1, :]).astype(bf16)
+        xn_ref[pl.ds(at * batch, batch)] = normed.reshape(batch, rows, D)
+        made = dot(normed, wq_ref[...]).astype(bf16)
+        for seq in range(batch):
+            for piece in range(6):
+                qkv_ref[at * batch + seq, :, piece * HP : (piece + 1) * HP] = jnp.concatenate(
+                    [made[seq * rows : (seq + 1) * rows, piece * DH : (piece + 1) * DH], blank], axis=1
+                )
+        return carry
+
+    lax.fori_loop(0, seqs // batch, project, 0)
+    for copy in local:
+        copy.wait()
+    relayed.append(push(w_in_ref.at[mine], w_in_ref.at[mine], core_send.at[0], core_recv.at[0], across("c")))
+    query_at = lax.broadcasted_iota(jnp.int32, (rows, rows), 0)
+    key_at = lax.broadcasted_iota(jnp.int32, (rows, rows), 1)
+
+    def head_copy(seq):
+        return pltpu.make_async_remote_copy(
+            src_ref=out_heads.at[seq], dst_ref=heads_ref.at[me], send_sem=head_send.at[seq], recv_sem=head_recv.at[me],
+            device_id={"y": lax.div(seq, 4), "a": lax.rem(lax.div(seq, 2), 2), "b": lax.rem(seq, 2)},
+        )
+
+    def attend(step, carry):
+        seq = lax.rem(me + step, seqs)
+        keep = (key_at <= query_at) & (key_at < len_ref[seq])
+        weights, made = [], []
+        for head in range(2):
+            query = qkv_ref[seq, :, head * HP : (head + 1) * HP]
+            key = qkv_ref[seq, :, (2 + head) * HP : (3 + head) * HP]
+            scores = jnp.where(keep, dot_nt(query, key) * (1.0 / math.sqrt(DH)), 0.0)
+            s_ref[seq, head] = scores.astype(bf16)
+            wide = shifted_down(pad_ref, scores)
+            near = wide.astype(bf16)
+            rest = (wide - near.astype(f32)).astype(bf16)
+            conv = dot(near, toep_ref[head]) + dot(rest, toep_ref[head])
+            logits = jnp.where(keep, conv, -1e30)
+            weight = jnp.exp(logits - jnp.max(logits, axis=-1, keepdims=True))
+            weight = weight / jnp.sum(weight, axis=-1, keepdims=True)
+            p_ref[seq, head] = weight
+            weights.append(weight)
+        for head in range(2):
+            mixed = mix_ref[2 * head] * weights[0] + mix_ref[2 * head + 1] * weights[1]
+            value = qkv_ref[seq, :, (4 + head) * HP : (5 + head) * HP]
+            out = dot(mixed.astype(bf16), value)
+            o_ref[seq, :, head * HP : (head + 1) * HP] = out
+            scale = lax.rsqrt(jnp.sum(out * out, axis=-1, keepdims=True) * (1.0 / DH) + eps_norm)
+            made.append((out * scale * gain_ref[:, head * HP : (head + 1) * HP])[:, :DH])
+        out_heads[seq] = jnp.concatenate(made, axis=1).astype(bf16)
+
+        @pl.when(step > 0)
+        def _():
+            head_copy(seq).start()
+
+        return carry
+
+    lax.fori_loop(0, 4, attend, 0)
+    side.onward()
+    lax.fori_loop(4, seqs, attend, 0)
+    heads_ref[me] = out_heads[me]
+    side.last()
+
+    def head_arrived(step, carry):
+        source = lax.rem(me + step, seqs)
+        pltpu.make_async_copy(out_heads.at[source], heads_ref.at[source], head_recv.at[source]).wait()
+        return carry
+
+    lax.fori_loop(1, seqs, head_arrived, 0)
+
+    def project_out(at, carry):
+        cols = pl.ds(pl.multiple_of(at * BLK, BLK), BLK)
+        total = x_ref[:, cols].astype(f32)
+        for chip in range(CHIPS):
+            weight = wo_ref[2 * chip : 2 * chip + 2, :, cols].reshape(2 * DH, BLK)
+            total += dot(heads_ref[chip], weight)
+        hmid_ref[:, cols] = total
+        return carry
+
+    lax.fori_loop(0, ROW_TILES, project_out, 0)
+    hmid = hmid_ref[...]
+    hn_ref[...] = (hmid * rms(hmid) * gains_ref[1:2, :]).astype(bf16)
+    gather = Gather(hn_ref, hn_all_ref, *hops[7:])
+    gather.start()
+    for mask in (2, 1, 3):
+        relay(mask)
+    gather.onward()
+    for mask in (4, 6):
+        relay(mask)
+    gather.last()
+    for mask in (5, 7):
+        relay(mask)
+
+    @pl.when(g == y)
+    def _():
+        down_local.wait()
+        down_to_core().start()
+        down_to_group().wait_send()
+
+    @pl.when(g != y)
+    def _():
+        down_to_group().wait_recv()
+        down_to_core().start()
+
+    down_to_core().wait()
+    side.finish()
+    gather.finish()
+    for copy in relayed:
+        copy.wait_recv()
+
+    def head_left(step, carry):
+        head_copy(lax.rem(me + step, seqs)).wait_send()
+        return carry
+
+    lax.fori_loop(1, seqs, head_left, 0)
+    side.drain()
+    gather.drain()
+    for copy in relayed + list(gate.values()) + list(up.values()):
+        copy.wait_send()
+
+
+def run_front(lengths, mix, x_all, x, gains, w_qkv, toep, gain, w_o, w_gate, w_up, w_down, dy):
+    seqs, rows, _ = x_all.shape
+    dma = pltpu.SemaphoreType.DMA
+    shapes = [
+        ((seqs, rows, D), bf16), ((seqs, rows, 6 * HP), bf16), ((seqs, 2, rows, rows), bf16), ((seqs, 2, rows, rows), f32),
+        ((seqs, rows, 2 * HP), f32), ((CHIPS, rows, 2 * DH), bf16), ((rows, D), f32), ((CHIPS, rows, D), bf16),
+        ((16, w_gate.shape[0], 2 * BLK), bf16), ((2,) + w_down.shape, bf16), ((CHIPS, rows, D), bf16),
+    ]
+    return pl.pallas_call(
+        forward_body,
+        in_specs=[SMEM, SMEM] + [VMEM] * 7 + [ANYS] * 4,
+        out_specs=[VMEM] * 7 + [ANYS] * 4,
+        out_shape=[jax.ShapeDtypeStruct(*shape) for shape in shapes],
+        scratch_shapes=[
+            pltpu.VMEM((rows + 8, rows), f32), pltpu.VMEM((seqs, rows, 2 * DH), bf16), pltpu.VMEM((rows, D), bf16),
+            dma((3,)),
+        ] + [dma((8,))] * 6 + [dma((2,))] * 2 + [dma((8,))] * 2 + side_sems() + hop_sems(),
+        name="front",
+        compiler_params=pltpu.CompilerParams(collective_id=2, has_side_effects=True, vmem_limit_bytes=56 * 2**20),
+    )(lengths, mix, x_all, x, gains, w_qkv, toep, gain, w_o, w_gate, w_up, w_down, dy)
 
 
 def back_body(
@@ -913,7 +1215,7 @@
     for mask in (7, 6, 5, 3, 4, 2, 1):
         to = flipped(me, [axis for axis in BITS if mask & BITS[axis]])
         sent.append(push(sent_ref.at[to], grads_ref.at[me], send.at[mask], recv.at[mask], chip_at(mask)))
-    gather = Gather(dattn_ref, all_ref, *hops)
+    gather = SideGather(dattn_ref, all_ref, *hops)
     gather.start()
     pad_ref[rows : rows + 8, :] = jnp.zeros((8, rows), f32)
     theta_ref[...] = jnp.zeros_like(theta_ref)
@@ -929,7 +1231,7 @@
     def one(seq, carry):
         keep = (key_at <= query_at) & (key_at < len_ref[seq])
         weights = [p_ref[seq, 0], p_ref[seq, 1]]
-        grad_mixed = []
+        grad_mixed, made = [], [None] * 6
         grads = grads_ref[seq].astype(f32)
         for head in range(2):
             cols = slice(head * HP, (head + 1) * HP)
@@ -943,7 +1245,7 @@
             grad_out = grad_out.astype(bf16)
             value = qkv_ref[seq, :, (4 + head) * HP : (5 + head) * HP]
             mixed = (mix_ref[2 * head] * weights[0] + mix_ref[2 * head + 1] * weights[1]).astype(bf16)
-            dqkv_ref[seq, :, (4 + head) * HP : (5 + head) * HP] = dot_tn(mixed, grad_out).astype(bf16)
+            made[4 + head] = dot_tn(mixed, grad_out)
             back = dot_nt(grad_out, value)
             grad_mixed.append(back)
             for source in range(2):
@@ -964,8 +1266,9 @@
             grad_scores = jnp.where(keep, grad_scores * (1.0 / math.sqrt(DH)), 0.0).astype(bf16)
             query = qkv_ref[seq, :, head * HP : (head + 1) * HP]
             key = qkv_ref[seq, :, (2 + head) * HP : (3 + head) * HP]
-            dqkv_ref[seq, :, head * HP : (head + 1) * HP] = dot(grad_scores, key).astype(bf16)
-            dqkv_ref[seq, :, (2 + head) * HP : (3 + head) * HP] = dot_tn(grad_scores, query).astype(bf16)
+            made[head] = dot(grad_scores, key)
+            made[2 + head] = dot_tn(grad_scores, query)
+        dqkv_ref[seq] = jnp.concatenate([part[:, :DH] for part in made], axis=1).astype(bf16)
         return carry
 
     lax.fori_loop(0, 4, one, 0)
@@ -994,7 +1297,7 @@
         in_specs=[SMEM, SMEM] + [VMEM] * 9,
         out_specs=[VMEM] * 5,
         out_shape=[
-            jax.ShapeDtypeStruct((seqs, rows, 6 * HP), bf16),
+            jax.ShapeDtypeStruct((seqs, rows, 6 * DH), bf16),
             jax.ShapeDtypeStruct((2, rows, CQ * rows), f32),
             jax.ShapeDtypeStruct((8, rows), f32),
             jax.ShapeDtypeStruct((1, 2 * HP), f32),
@@ -1003,7 +1306,7 @@
         scratch_shapes=[
             pltpu.VMEM((rows + 8, rows), f32), pltpu.VMEM((seqs, rows, 2 * DH), bf16),
             pltpu.VMEM((CHIPS, rows, D), bf16), dma, dma((8,)), dma((8,)),
-        ] + hop_sems(),
+        ] + side_sems(),
         name="attention_back",
         compiler_params=pltpu.CompilerParams(collective_id=4, has_side_effects=True, vmem_limit_bytes=32 * 2**20),
     )(lengths, mix, qkv, toep, gain, scores, weights, outs, sent, dattn, strips)
@@ -1148,10 +1451,8 @@
         [vec_copy.astype(f32), jnp.zeros((1023 - own_vec,), f32), length.astype(f32).reshape(1)]
     ).reshape(8, 128)
     blocks = jnp.concatenate([w.reshape(-1, CHIPS, 2 * DH) for w in (w_query, w_key, w_value)], axis=2)
-    x_all, small_all, w_qkv = dispatch(layer_input, small, jnp.transpose(blocks, (1, 0, 2)))
-    w_gate, w_up, w_down, cotangent, x_all, small_all, w_qkv = lax.optimization_barrier(
-        (w_gate, w_up, w_down, cotangent, x_all, small_all, w_qkv)
-    )
+    x_all, small_all, w_qkv, w_out_all = dispatch(layer_input, small, jnp.transpose(blocks, (1, 0, 2)), w_out)
+    w_qkv = w_qkv.reshape(D, 6 * DH)
     small_all = small_all.reshape(fs_size, reps, 1024)
     vector = small_all[:, 0, :own_vec].reshape(-1)
     group_lengths = small_all[:, :, 1023].reshape(-1, 2, 2, 2, reps)
@@ -1173,25 +1474,19 @@
     for tap in range(CK):
         toep = jnp.where(offset[None, None] == tap, theta[:, :, tap][:, :, None, None], toep)
     toep = toep.astype(bf16).reshape(2, CQ * seq_len, seq_len)
-    w_qkv = jnp.pad(w_qkv.reshape(D, 6, DH), ((0, 0), (0, 0), (0, HP - DH))).reshape(D, 6 * HP)
-    w_o = lax.all_gather(w_out, FS, axis=0, tiled=True)
-    w_in = to_columns(jnp.concatenate([spread_columns(w, BLK) for w in (w_gate, w_up)], axis=2))
-    w_dn = down_rows(w_down, chip)
     valid = (jnp.arange(seq_len) < length).astype(f32)
     dy = cotangent.astype(f32) * valid[:, None]
-    dy_rows = gather_slow(dy.astype(bf16)).reshape(CHIPS * seq_len, D)
-
+
+    gains = jnp.concatenate([gain_attn[None], gain_ffn[None], jnp.zeros((6, D), f32)], axis=0)
+    xn, qkv, scores, weights, outs, heads, hmid, hn_rows, w_in, w_dn, dy_rows = run_front(
+        group_lengths, mix, x_all, layer_input, gains, w_qkv, toep, gain_pair, w_out_all, w_gate, w_up, w_down, dy.astype(bf16)
+    )
+    xn_rows, hn_rows, dy_rows = (rows.reshape(CHIPS * seq_len, D) for rows in (xn, hn_rows, dy_rows))
+    w_in, w_dn, w_o = w_in.reshape(D, 2 * BLK), w_dn.reshape(BLK, D), w_out_all.reshape(D, D)
+    heads = jnp.transpose(heads, (1, 0, 2)).reshape(seq_len, D)
     input_float = layer_input.astype(f32)
     input_scale = rms(input_float)
-    x_rows = x_all.reshape(CHIPS * seq_len, D).astype(f32)
-    xn_rows = (x_rows * rms(x_rows) * gain_attn).astype(bf16)
-    qkv = dot(xn_rows, w_qkv).astype(bf16).reshape(CHIPS, seq_len, 6 * HP)
-    heads_pad, scores, weights, outs = run_forward(group_lengths, mix, qkv, toep, gain_pair)
-    heads_sent = heads_pad.reshape(CHIPS, seq_len, 2, HP)[..., :DH].reshape(CHIPS, seq_len, 2 * DH)
-    heads = jnp.transpose(exchange_chips(heads_sent), (1, 0, 2)).reshape(seq_len, D)
-    hmid = input_float + dot(heads, w_o)
     hmid_scale = rms(hmid)
-    hn_rows = gather_chips((hmid * hmid_scale * gain_ffn).astype(bf16), 2).reshape(CHIPS * seq_len, D)
     both = dot(hn_rows, w_in)
     gate, up = both[:, :BLK], both[:, BLK:]
     sig = jax.nn.sigmoid(gate)
@@ -1216,9 +1511,9 @@
     dqkv, theta_sums, mixer_sums, gain_sums, grad_out = run_back(
         group_lengths, mix, qkv, toep, gain_pair, scores, weights, outs, jnp.transpose(dheads, (1, 0, 2)), dattn, strips
     )
-    dqkv_rows = dqkv.reshape(CHIPS * seq_len, 6 * HP)
+    dqkv_rows = dqkv.reshape(CHIPS * seq_len, 6 * DH)
     dxn_parts = dot_nt(dqkv_rows, w_qkv).astype(bf16).reshape(CHIPS, seq_len, D)
-    grad_qkv = dot_tn(xn_rows, dqkv_rows).astype(bf16).reshape(D, 6, HP)[..., :DH]
+    grad_qkv = dot_tn(xn_rows, dqkv_rows).astype(bf16)
     dxn, qkv_sums, out_sums = share(
         dxn_parts,
         grad_qkv.reshape(ROW_TILES, 2, CHIPS, 2, part, 6 * DH),

time: 686 us -> 613 us (0.89)
  waiting for transfers between devices: 146 us -> 28.8 us
  Pallas kernels: 260 us -> 366 us
  starting transfers between devices: 51 us -> 22.5 us
  between operations: 16.6 us -> 2.74 us
  local copies, waits for them, and re-layouts: 94 us -> 83.1 us
    pallas_call x3 -> x2, Pallas kernels: 78.8 us -> 176 us  [the longest x1 109 us: run_front(): pl.pallas_call(forward_body, in_specs=[SMEM, SMEM] + [VMEM] * 7 + [ANYS]...]
    ppermute x6 -> x3, waiting for transfers between devices: 94.4 us -> 28.8 us  [swap(): return lax.ppermute(values, axis, [(0, 1), (1, 0)])]
    all_to_all x2 -> x0, waiting for transfers between devices: 51.2 us -> none  [the longest x1 51.2 us: to_columns(): lax.all_to_all(sent, ('g', 'a', 'b'), split_axis=0, concat_axis=0, tiled=...]
    reshape x5 -> x0, local copies, waits for them, and re-layouts: 15.5 us -> none  [the longest x2 5.28 us: spread_columns(): blocks = weight.reshape(rows, 2, CHIPS // 2, width)]
    all_to_all x2 -> x0, starting transfers between devices: 13.4 us -> none  [the longest x1 9.55 us: gather_slow(): lax.all_to_all(jnp.broadcast_to(rows[None], (CHIPS,) + rows.shape), CHIP,...]
    all_to_all x4 -> x3, starting transfers between devices: 28 us -> 19.8 us  [exchange_chips(): return lax.all_to_all(parts, CHIP, split_axis=0, concat_axis=0, tiled=True)]
    pallas_call x1, Pallas kernels: 46 us -> 54.1 us  [run_back(): pl.pallas_call(back_body, in_specs=[SMEM, SMEM] + [VMEM] * 9, out_specs=[...]
    reduce_sum x11, local copies, waits for them, and re-layouts: 0.79 us -> 7.72 us  [body_fast(): jnp.sum(jnp.where(taps[tap][None, :, None, :], theta_sums, 0.0), axis=(1,...]
  transfers between devices with their start and end apart: 13 -> 6, of which waited for: 4 -> 1; matrix products, arithmetic and copies ran while one was open for 18% -> 19% of each run, Pallas kernels for 22% -> 22%
where the time goes in v4:
time: 613 us; the launch traced here: 604 us
  Pallas kernels  366 us (60%)
  local copies, waits for them, and re-layouts  83.1 us (14%)
  matrix products  66.9 us (11%)
  other arithmetic  33.7 us (5%)
  waiting for transfers between devices  28.8 us (5%)
  starting transfers between devices  22.5 us (4%)
    pallas_call x1, Pallas kernels, run_front(): pl.pallas_call(forward_body, in_specs=[SMEM, SMEM] + [VMEM] * 7 + [ANYS]...  109 us
    pallas_call x1, Pallas kernels, dispatch(): pl.pallas_call(dispatch_body, in_specs=[ANYS] * 4, out_specs=[ANYS] * 4,...  67.2 us
    pallas_call x1, Pallas kernels, to_slots(): pl.pallas_call(to_slots_body, in_specs=[ANYS] * 2, out_specs=[ANYS] * 2,...  57.3 us
    pallas_call x1, Pallas kernels, run_back(): pl.pallas_call(back_body, in_specs=[SMEM, SMEM] + [VMEM] * 9, out_specs=[...  54.1 us
    pallas_call x1, Pallas kernels, share(): pl.pallas_call(share_body, in_specs=[VMEM] * 3, out_specs=[VMEM] * 3, out...  46.5 us
    pallas_call x1, Pallas kernels, scatter_chips(): pl.pallas_call(scatter_body, in_specs=[vmem], out_specs=vmem, out_shape=j...  32.1 us
    ppermute x3, waiting for transfers between devices, swap(): return lax.ppermute(values, axis, [(0, 1), (1, 0)])  28.8 us
    all_to_all x3, starting transfers between devices, exchange_chips(): return lax.all_to_all(parts, CHIP, split_axis=0, concat_axis=0, tiled=True)  19.8 us
  transfers between devices with their start and end apart: 6, of which 1 were waited for; matrix products, arithmetic and copies ran while one was open for 19% of the time, Pallas kernels for 22%

profile of v4, /device:TPU:11, one launch (start us, length us, event | category | flops | bytes accessed | tf_op | source)
XLA Modules:
  0.0 604.2 jit_solution(776207722886210624)
XLA Ops:
  7.2 67.2 %dispatch.1 = (bf16[8,128,1536]{2,1,0:T(8,128)(2,1)}, f32[32,8,128]{2,1,0:T(8,128)}, bf16[16,96,576]{2,1,0:T(8,128)(2,1)}, bf16[16,96,1536]{2,1,0:T(8,128)(2,1)}) custom-call(bf16[128,1536]{1,0:T(8,128)(2,1)} %x_ref.3, f32[8,128]{1,0:T(8,128)} %maximum_bitcast_fusion.1.vec_ref, bf16[8,96,576]{2,1,0:T(8,128)(2,1)} %maximum_bitcast_fusion.blocks_ref, ...), custom_call_target="tpu_custom_call" | custom-call | tf_op jit(solution)/shard_map/dispatch/pallas_call | solution.py:978
  82.0 3.7 select_convert_fusion.toep_ref
  85.7 109.0 %front.1 = (bf16[8,128,1536]{2,1,0:T(8,128)(2,1)}, bf16[8,128,768]{2,1,0:T(8,128)(2,1)}, bf16[8,2,128,128]{3,2,1,0:T(8,128)(2,1)}, f32[8,2,128,128]{3,2,1,0:T(8,...) custom-call(s32[8]{0:T(128)} %convert_element_type.132.len_ref, ...), custom_call_target="tpu_custom_call" | custom-call | tf_op jit(solution)/shard_map/front/pallas_call | solution.py:1187
  196.8 6.2 %all-to-all-start.1 = ((bf16[8,128,192]{1,2,0:T(8,128)(2,1)}), bf16[8,128,192]{1,2,0:T(8,128)(2,1)}, u32[]{:S(2)}, u32[]{:S(2)}) async-start(bf16[8,128,192]{1,2,0:T(8,128)(2,1)} %bitcast.32), calls=%async_computation.1 | async-start | bytes 786432 | tf_op jit(solution)/shard_map/all_to_all | solution.py:459
  203.0 6.6 %fusion.63 = f32[1024,1024]{0,1:T(8,128)S(1)} fusion(bf16[1024,1536]{1,0:T(8,128)(2,1)} %bitcast.260, bf16[1536,1024]{1,0:T(8,128)(2,1)} %bitcast.325), kind=kOutput, calls=%fused_computation.165 | convolution fusion | flops 3221225472 | bytes 10485760 | tf_op jit(solution)/shard_map/dot_general | solution.py:40
  209.6 4.2 multiply_convert_fusion.1
  216.1 5.2 convolution_convert_fusion.2
  221.3 4.8 all-to-all-start
  226.1 2.9 copy.127
  228.9 4.2 fusion.65
  235.8 2.4 collective-permute-start.1
  238.2 2.8 copy.125
  243.5 3.5 fusion.64
  247.0 2.7 copy-done.19
  251.8 5.0 convolution_convert_fusion.3
  259.0 32.1 %scatter_chips.1 = f32[128,1536]{1,0:T(8,128)S(1)} custom-call(bf16[8,128,1536]{2,1,0:T(8,128)(2,1)S(1)} %bitcast.243), custom_call_target="tpu_custom_call" | custom-call | tf_op jit(solution)/shard_map/scatter_chips/pallas_call | solution.py:440
  305.2 2.9 fusion.15
  309.9 8.8 %all-to-all-start.2 = ((bf16[8,9,32,512]{3,2,1,0:T(8,128)(2,1)}), bf16[8,9,32,512]{3,2,1,0:T(8,128)(2,1)}, u32[]{:S(2)}, u32[]{:S(2)}) async-start(bf16[8,9,32,512]{3,2,1,0:T(8,128)(2,1)} %pad_maximum_fusion), calls=%async_computation.2 | async-start | bytes 4718592 | tf_op jit(solution)/shard_map/all_to_all | solution.py:459
  318.7 2.4 convert_reduce_fusion
  322.4 4.1 convolution_convert_fusion.4
  330.7 54.1 %attention_back.1 = (bf16[8,128,576]{2,1,0:T(8,128)(2,1)S(1)}, f32[2,128,768]{2,1,0:T(8,128)S(1)}, f32[8,128]{1,0:T(8,128)S(1)}, f32[1,256]{1,0:T(1,128)S(1)}, bf16[192,1536]{1,0:T(8,128)(2,1)S(1)}) custom-call(s32[8]{0:T(128)S(1)} %copy-done.11, f32[4]{0:T(128)S(1)} %copy-done.12, bf16[8,128,768]{2,1,0:T(8,128)(2,1)S(1)} %copy-done.2, ...), custom_call_target="tpu_custom_call" | custom-call | tf_op jit(solution)/shard_map/attention_back/pallas_call | solution.py:1295
  387.6 3.3 bitcast_convert_fusion
  390.9 3.3 copy.123
  394.3 2.6 select_reduce_fusion
  405.7 4.6 convolution_convert_fusion.1
  410.3 46.5 %share_gradients.1 = (f32[128,1536]{1,0:T(8,128)S(1)}, bf16[3,3,16,1536]{3,2,1,0:T(8,128)(2,1)S(1)}, bf16[3,16,1536]{2,1,0:T(8,128)(2,1)S(1)}) custom-call(bf16[8,128,1536]{2,1,0:T(8,128)(2,1)S(1)} %bitcast.244, bf16[3,2,8,2,16,576]{5,4,3,2,1,0:T(8,128)(2,1)S(1)} %bitcast.242, bf16[3,2,2,16,1536]{4,3,2,1,0:T(8,128)(2,1)S(1)} %bitcast.247), custom_call_target="tpu_custom_call" | custom-call | tf_op jit(solution)/shard_map/share_gradients/pallas_call | solution.py:1378
  481.4 2.3 fusion.31
  483.7 28.8 %collective-permute-done.2 = bf16[72,16,512]{2,1,0:T(8,128)(2,1)} collective-permute-done((bf16[72,16,512]{2,1,0:T(8,128)(2,1)}, bf16[72,16,512]{2,1,0:T(8,128)(2,1)}, u32[]{:S(2)}, u32[]{:S(2)}) %collective-permute-start.2) | collective-permute-done | bytes 1179680 | tf_op jit(solution)/shard_map/ppermute | solution.py:467
  516.2 2.3 reshape.413.slots_ref
  518.5 57.3 %to_slots.1 = (bf16[32,64,512]{2,1,0:T(8,128)(2,1)}, f32[32,8,128]{2,1,0:T(8,128)}) custom-call(bf16[32,64,512]{2,1,0:T(8,128)(2,1)} %reshape.413.slots_ref, f32[32,8,128]{2,1,0:T(8,128)} %reshape.418.vec_ref), custom_call_target="tpu_custom_call" | custom-call | tf_op jit(solution)/shard_map/to_slots/pallas_call | solution.py:1429
  577.8 12.1 %fusion = (f32[4,512,512]{2,1,0:T(8,128)}, f32[4,512,512]{2,1,0:T(8,128)}) fusion(f32[4,512,512]{2,1,0:T(8,128)} %param.37, f32[4,512,512]{2,1,0:T(8,128)} %param.36, f32[4,512,512]{2,1,0:T(8,128)} %param.34, bf16[4,512,512]{2,1,0:T(8,128)(2,1)S(1)} %bitcast.255, f32[4,512,512]{2,1,0:T(8,128)} %param.33), kind=kOutput, calls=%fused_computation.4 | convolution fusion | flops 2156920832 | bytes 27262976 | tf_op jit(solution)/shard_map/saj,sjb->sab/dot_general | solution.py:1575
  589.8 13.5 %fusion.60 = (bf16[4,512,512]{2,1,0:T(8,128)(2,1)}, f32[4,512,512]{2,1,0:T(8,128)}) fusion(f32[4,512,512]{2,1,0:T(8,128)} %param.35, f32[4,512,512]{2,1,0:T(8,128)} %param.34, f32[4,512,512]{2,1,0:T(8,128)} %get-tuple-element.95, f32[4,512,512]{2,1,0:T(8,128)} %get-tuple-element.94, f32[4,512,512]{2,1,0:T(8,128)} %param.33), kind=kOutput, calls=%fused_computation.164 | convolution fusion | flops 2159017984 | bytes 27262976 | tf_op jit(solution)/shard_map/sib,sjb->sij/dot_general | solution.py:1580
  (315 shorter events, 89.9 us)
Async XLA Ops:
  7.2 72.8 %copy-start.24 = (bf16[128,1536]{1,0:T(8,128)(2,1)S(1)}, bf16[128,1536]{1,0:T(8,128)(2,1)}, u32[]{:S(2)}) copy-start(bf16[128,1536]{1,0:T(8,128)(2,1)} %param.23) | copy-start | bytes 1179652
  76.7 118.0 %copy-start.54 = (f32[128]{0:T(128)}, f32[128]{0:T(128)S(1)}, u32[]{:S(2)}) copy-start(f32[128]{0:T(128)S(1)} %compare_convert_fusion) | copy-start | bytes 1540
  196.8 24.5 %all-to-all-start.1 = ((bf16[8,128,192]{1,2,0:T(8,128)(2,1)}), bf16[8,128,192]{1,2,0:T(8,128)(2,1)}, u32[]{:S(2)}, u32[]{:S(2)}) async-start(bf16[8,128,192]{1,2,0:T(8,128)(2,1)} %bitcast.32), calls=%async_computation.1 | async-start | bytes 786432 | tf_op jit(solution)/shard_map/all_to_all | solution.py:459
  203.0 6.6 %copy-start.21 = (bf16[8,128,1536]{2,1,0:T(8,128)(2,1)S(1)}, bf16[8,128,1536]{2,1,0:T(8,128)(2,1)}, u32[]{:S(2)}) copy-start(bf16[8,128,1536]{2,1,0:T(8,128)(2,1)} %get-tuple-element.47) | copy-start | bytes 9437188
  203.0 6.6 %copy-start.59 = (bf16[2,256,1536]{2,1,0:T(8,128)(2,1)S(1)}, bf16[2,256,1536]{2,1,0:T(8,128)(2,1)}, u32[]{:S(2)}) copy-start(bf16[2,256,1536]{2,1,0:T(8,128)(2,1)} %get-tuple-element.42) | copy-start | bytes 4718596
  221.3 88.6 %all-to-all-start = ((bf16[8,128,1536]{2,1,0:T(8,128)(2,1)}), bf16[8,128,1536]{2,1,0:T(8,128)(2,1)}, u32[]{:S(2)}, u32[]{:S(2)}) async-start(bf16[8,128,1536]{2,1,0:T(8,128)(2,1)} %convolution_convert_fusion.2), calls=%async_computation | async-start | bytes 6291456 | tf_op jit(solution)/shard_map/all_to_all | solution.py:459
  228.9 9.3 %copy-start.20 = (bf16[8,128,1536]{2,1,0:T(8,128)(2,1)S(1)}, bf16[8,128,1536]{2,1,0:T(8,128)(2,1)}, u32[]{:S(2)}) copy-start(bf16[8,128,1536]{2,1,0:T(8,128)(2,1)} %get-tuple-element.40) | copy-start | bytes 9437188
  235.8 67.5 %collective-permute-start.1 = (bf16[8,32,3,512]{3,1,2,0:T(8,128)(2,1)}, bf16[8,32,3,512]{3,1,2,0:T(8,128)(2,1)}, u32[]{:S(2)}, u32[]{:S(2)}) collective-permute-start(bf16[8,32,3,512]{3,1,2,0:T(8,128)(2,1)} %fusion.34), channel_id=1, source_target_pairs={{0,2},{2,0},{1,3},{3,1},{4,6},{6,4},{5,7},{7,5},{8,10},{10,8},{9,1... | collective-permute-start | bytes 2359304 | tf_op jit(solution)/shard_map/ppermute | solution.py:467
  243.5 7.5 %copy-start.58 = (bf16[16,96,1024]{2,1,0:T(8,128)(2,1)S(1)}, bf16[16,96,1024]{2,1,0:T(8,128)(2,1)}, u32[]{:S(2)}) copy-start(bf16[16,96,1024]{2,1,0:T(8,128)(2,1)} %get-tuple-element.41) | copy-start | bytes 9437188
  251.1 5.8 copy-start.16
  251.1 54.1 %collective-permute-start = (bf16[3,8,32,2,512]{4,2,3,1,0:T(8,128)(2,1)}, bf16[3,8,32,2,512]{4,2,3,1,0:T(8,128)(2,1)}, u32[]{:S(2)}, u32[]{:S(2)}) collective-permute-start(bf16[3,8,32,2,512]{4,2,3,1,0:T(8,128)(2,1)} %fusion.14), channel_id=1, source_target_pairs={{0,2},{2,0},{1,3},{3,1},{4,6},{6,4},{5,7},{7,5},{8,10},{10,8},{9,1... | collective-permute-start | bytes 4718600 | tf_op jit(solution)/shard_map/ppermute | solution.py:467
  256.9 34.3 %copy-start.49 = (pred[128,128]{0,1:T(32,128)(4,1)S(1)}, pred[128,128]{0,1:T(32,128)(4,1)}, u32[]{:S(2)}) copy-start(pred[128,128]{0,1:T(32,128)(4,1)} %constant.175) | copy-start | bytes 49156
  256.9 35.1 %copy-start.48 = (pred[128,128]{0,1:T(32,128)(4,1)S(1)}, pred[128,128]{0,1:T(32,128)(4,1)}, u32[]{:S(2)}) copy-start(pred[128,128]{0,1:T(32,128)(4,1)} %constant.173) | copy-start | bytes 49156
  257.0 35.8 %copy-start.47 = (pred[128,128]{0,1:T(32,128)(4,1)S(1)}, pred[128,128]{0,1:T(32,128)(4,1)}, u32[]{:S(2)}) copy-start(pred[128,128]{0,1:T(32,128)(4,1)} %constant.171) | copy-start | bytes 49156
  258.9 34.8 %copy-start.46 = (pred[128,128]{0,1:T(32,128)(4,1)S(1)}, pred[128,128]{0,1:T(32,128)(4,1)}, u32[]{:S(2)}) copy-start(pred[128,128]{0,1:T(32,128)(4,1)} %constant.169) | copy-start | bytes 49156
  258.9 35.6 %copy-start.45 = (pred[128,128]{0,1:T(32,128)(4,1)S(1)}, pred[128,128]{0,1:T(32,128)(4,1)}, u32[]{:S(2)}) copy-start(pred[128,128]{0,1:T(32,128)(4,1)} %constant.167) | copy-start | bytes 49156
  258.9 36.5 %copy-start.44 = (pred[128,128]{0,1:T(32,128)(4,1)S(1)}, pred[128,128]{0,1:T(32,128)(4,1)}, u32[]{:S(2)}) copy-start(pred[128,128]{0,1:T(32,128)(4,1)} %constant.165) | copy-start | bytes 49156
  258.9 37.3 %copy-start.43 = (pred[128,128]{0,1:T(32,128)(4,1)S(1)}, pred[128,128]{0,1:T(32,128)(4,1)}, u32[]{:S(2)}) copy-start(pred[128,128]{0,1:T(32,128)(4,1)} %constant.163) | copy-start | bytes 49156
  258.9 38.1 %copy-start.42 = (pred[128,128]{0,1:T(32,128)(4,1)S(1)}, pred[128,128]{0,1:T(32,128)(4,1)}, u32[]{:S(2)}) copy-start(pred[128,128]{0,1:T(32,128)(4,1)} %constant.161) | copy-start | bytes 49156
  259.0 39.0 %copy-start.41 = (pred[128,128]{0,1:T(32,128)(4,1)S(1)}, pred[128,128]{0,1:T(32,128)(4,1)}, u32[]{:S(2)}) copy-start(pred[128,128]{0,1:T(32,128)(4,1)} %constant.159) | copy-start | bytes 49156
  291.1 7.7 %copy-start.40 = (pred[128,128]{0,1:T(32,128)(4,1)S(1)}, pred[128,128]{0,1:T(32,128)(4,1)}, u32[]{:S(2)}) copy-start(pred[128,128]{0,1:T(32,128)(4,1)} %constant.157) | copy-start | bytes 49156
  291.1 8.5 %copy-start.39 = (pred[128,128]{0,1:T(32,128)(4,1)S(1)}, pred[128,128]{0,1:T(32,128)(4,1)}, u32[]{:S(2)}) copy-start(pred[128,128]{0,1:T(32,128)(4,1)} %constant.155) | copy-start | bytes 49156
  291.1 9.3 %copy-start.14 = (bf16[128,1536]{1,0:T(8,128)(2,1)S(1)}, bf16[128,1536]{1,0:T(8,128)(2,1)}, u32[]{:S(2)}) copy-start(bf16[128,1536]{1,0:T(8,128)(2,1)} %x_ref.3) | copy-start | bytes 1179652
  309.9 147.1 %all-to-all-start.2 = ((bf16[8,9,32,512]{3,2,1,0:T(8,128)(2,1)}), bf16[8,9,32,512]{3,2,1,0:T(8,128)(2,1)}, u32[]{:S(2)}, u32[]{:S(2)}) async-start(bf16[8,9,32,512]{3,2,1,0:T(8,128)(2,1)} %pad_maximum_fusion), calls=%async_computation.2 | async-start | bytes 4718592 | tf_op jit(solution)/shard_map/all_to_all | solution.py:459
  330.7 56.9 %copy-start.57 = (bf16[8,128,1536]{2,1,0:T(8,128)(2,1)S(1)}, bf16[8,128,1536]{2,1,0:T(8,128)(2,1)}, u32[]{:S(2)}) copy-start(bf16[8,128,1536]{2,1,0:T(8,128)(2,1)} %get-tuple-element.50) | copy-start | bytes 9437188
  405.7 4.6 copy-start.8
  461.0 51.5 %collective-permute-start.2 = (bf16[72,16,512]{2,1,0:T(8,128)(2,1)}, bf16[72,16,512]{2,1,0:T(8,128)(2,1)}, u32[]{:S(2)}, u32[]{:S(2)}) collective-permute-start(bf16[72,16,512]{2,1,0:T(8,128)(2,1)} %fusion.17), channel_id=1, source_target_pairs={{0,16},{16,0},{1,17},{17,1},{2,18},{18,2},{3,19},{19,3},{4,20},{20... | collective-permute-start | bytes 3538952 | tf_op jit(solution)/shard_map/ppermute | solution.py:467
  461.3 12.0 %copy-start.15 = (bf16[128,1536]{1,0:T(8,128)(2,1)S(1)}, bf16[128,1536]{1,0:T(8,128)(2,1)}, u32[]{:S(2)}) copy-start(bf16[128,1536]{1,0:T(8,128)(2,1)} %x_ref.3) | copy-start | bytes 1179652
  465.6 47.0 %copy-start.18 = (bf16[8,3,32,512]{3,2,1,0:T(8,128)(2,1)S(1)}, bf16[8,3,32,512]{3,2,1,0:T(8,128)(2,1)}, u32[]{:S(2)}) copy-start(bf16[8,3,32,512]{3,2,1,0:T(8,128)(2,1)} %copy-done.17) | copy-start | bytes 2359300
  589.8 13.5 %copy-start.51 = (f32[356]{0:T(512)S(1)}, f32[356]{0:T(512)}, u32[]{:S(2)}) copy-start(f32[356]{0:T(512)} %param.38) | copy-start | bytes 4276
  589.8 13.5 %copy-start.52 = (f32[356]{0:T(512)S(1)}, f32[356]{0:T(512)}, u32[]{:S(2)}) copy-start(f32[356]{0:T(512)} %param.40) | copy-start | bytes 4276
  589.8 13.5 %copy-start.53 = (f32[356]{0:T(512)S(1)}, f32[356]{0:T(512)}, u32[]{:S(2)}) copy-start(f32[356]{0:T(512)} %param.39) | copy-start | bytes 4276
  (35 other events, 87.6 us)

commit v5 on v4

--- a/solution.py
+++ b/solution.py
@@ -1198,35 +1198,138 @@
     )(lengths, mix, x_all, x, gains, w_qkv, toep, gain, w_o, w_gate, w_up, w_down, dy)
 
 
-def back_body(
-    len_ref, mix_ref, qkv_ref, toep_ref, gain_ref, s_ref, p_ref, o_ref, sent_ref, dattn_ref, strips_ref,
-    dqkv_ref, theta_ref, mixer_ref, gain_grad_ref, go_ref,
-    pad_ref, grads_ref, all_ref, own_sem, send, recv, *hops,
+def middle_body(
+    len_ref, mix_ref, hn_ref, w_in_ref, w_dn_ref, dy_ref, dy_own_ref, hmid_ref, gain_ffn_ref, wo_ref,
+    qkv_ref, toep_ref, gain_ref, s_ref, p_ref, o_ref, strips_ref,
+    layer_ref, dhmid_ref, gain_ffn_grad_ref, dqkv_ref, theta_ref, mixer_ref, gain_grad_ref, go_ref, tiles_ref,
+    pad_ref, inner_ref, dboth_ref, parts_ref, dattn_ref, all_ref, grads_ref, sent_ref, strips_in, gin_ref, gd_ref,
+    half_in, half_d, in_gu, in_d, near2, in22, in32, local_sems, strip_send, strip_recv, head_send, head_recv,
+    core_send, core_recv, gu_send, gu_recv, d_send, d_recv, *rest,
 ):
-    seqs, rows = qkv_ref.shape[:2]
+    scatter_args, scatter2_sems, side = rest[:11], rest[11:17], rest[17:]
+    seqs, rows, _ = hn_ref.shape
+    g, a, b, c, y = (lax.axis_index(axis) for axis in ALL)
     me = chip_index()
-    own = pltpu.make_async_copy(sent_ref.at[me], grads_ref.at[me], own_sem)
-    own.start()
-    barrier = pltpu.get_barrier_semaphore()
-    for mask in range(1, 8):
-        pl.semaphore_signal(barrier, inc=1, device_id=chip_at(mask))
-    pl.semaphore_wait(barrier, 7)
-    sent = []
+    strip_local = pltpu.make_async_copy(strips_ref.at[me], strips_in.at[me], local_sems.at[0])
+    strip_local.start()
+    greet_all()
+    strips_sent = []
     for mask in (7, 6, 5, 3, 4, 2, 1):
         to = flipped(me, [axis for axis in BITS if mask & BITS[axis]])
-        sent.append(push(sent_ref.at[to], grads_ref.at[me], send.at[mask], recv.at[mask], chip_at(mask)))
-    gather = SideGather(dattn_ref, all_ref, *hops)
+        strips_sent.append(push(strips_ref.at[to], strips_in.at[me], strip_send.at[mask], strip_recv.at[mask], chip_at(mask)))
+
+    def hidden(at, carry):
+        two = pl.ds(at * 2, 2)
+        both = dot(hn_ref[two].reshape(2 * rows, D), w_in_ref[...])
+        gate, up = both[:, :BLK], both[:, BLK:]
+        dinner = dot_nt(dy_ref[two].reshape(2 * rows, D), w_dn_ref[...])
+        sig = jax.nn.sigmoid(gate)
+        silu = gate * sig
+        inner_ref[two] = (silu * up).astype(bf16).reshape(2, rows, BLK)
+        dgate = (dinner * up * (sig * (1.0 + gate * (1.0 - sig)))).astype(bf16)
+        dup = (dinner * silu).astype(bf16)
+        dboth_ref[two, :, 0:BLK] = dgate.reshape(2, rows, BLK)
+        dboth_ref[two, :, BLK:] = dup.reshape(2, rows, BLK)
+        back = dot_nt(dgate, w_in_ref[:, 0:BLK]) + dot_nt(dup, w_in_ref[:, BLK:])
+        parts_ref[two] = back.astype(bf16).reshape(2, rows, D)
+        return carry
+
+    lax.fori_loop(0, seqs // 2, hidden, 0)
+    scatter = Scatter(parts_ref, *scatter_args)
+    scatter.start()
+
+    def down_grad(col, carry):
+        cols = pl.ds(pl.multiple_of(col * BLK, BLK), BLK)
+        made = dot_tn(inner_ref[...].reshape(seqs * rows, BLK), dy_ref[:, :, cols].reshape(seqs * rows, BLK))
+        gd_ref[:, :, :, :, cols] = made.astype(bf16).reshape(2, CHIPS, 2, BLK // 32, BLK)
+        return carry
+
+    lax.fori_loop(0, ROW_TILES, down_grad, 0)
+    to_core = [push(gd_ref.at[1 - c], half_d, core_send.at[0], core_recv.at[0], across("c"))]
+    scatter.onward()
+
+    def in_grad(row, carry):
+        values = hn_ref[:, :, pl.ds(pl.multiple_of(row * BLK, BLK), BLK)].reshape(seqs * rows, BLK)
+        for which in range(2):
+            cols = slice(which * BLK, (which + 1) * BLK)
+            made = dot_tn(values, dboth_ref[:, :, cols].reshape(seqs * rows, BLK))
+            gin_ref[row, :, :, :, :, cols] = made.astype(bf16).reshape(2, CHIPS, 2, BLK // 32, BLK)
+        return carry
+
+    lax.fori_loop(0, ROW_TILES, in_grad, 0)
+    to_core.append(push(gin_ref.at[:, 1 - c], half_in, core_send.at[1], core_recv.at[1], across("c")))
+    scatter.last()
+    half = rows // 2
+    gain_sum = jnp.zeros((1, D), f32)
+    for part in range(2):
+        here = pl.ds(part * half, half)
+        grad = scatter.finish(part)
+        values = hmid_ref[here]
+        scale = rms(values)
+        unit = values * scale
+        inside = grad * gain_ffn_ref[...]
+        gain_sum += jnp.sum(grad * unit, axis=0, keepdims=True)
+        dhmid = scale * (inside - unit * jnp.mean(inside * unit, axis=-1, keepdims=True)) + dy_own_ref[here].astype(f32)
+        dhmid_ref[here] = dhmid
+        dattn_ref[here] = dhmid.astype(bf16)
+    gain_ffn_grad_ref[...] = gain_sum
+
+    def grad_copy(to):
+        return pltpu.make_async_remote_copy(
+            src_ref=sent_ref.at[to], dst_ref=grads_ref.at[me], send_sem=head_send.at[to], recv_sem=head_recv.at[me],
+            device_id={"y": lax.div(to, 4), "a": lax.rem(lax.div(to, 2), 2), "b": lax.rem(to, 2)},
+        )
+
+    def send_grad(step, carry):
+        to = lax.rem(me + step, seqs)
+        sent_ref[to] = dot_nt(dattn_ref[...], wo_ref[to]).astype(bf16)
+
+        @pl.when(step > 0)
+        def _():
+            grad_copy(to).start()
+
+        return carry
+
+    lax.fori_loop(0, seqs, send_grad, 0)
+    grads_ref[me] = sent_ref[me]
+    gather = SideGather(dattn_ref, all_ref, *side)
     gather.start()
+
+    slot = g * CHIPS + me
+    to_core[0].wait_recv()
+    half_d[...] = (half_d[...].astype(f32) + gd_ref[c].astype(f32)).astype(bf16)
+    tiles_sent = []
+    order = (15, 14, 13, 11, 12, 10, 9, 8, 7, 6, 5, 3, 4, 2, 1)
+    for mask in order:
+        to = flipped(me, [axis for axis in BITS if mask & BITS[axis]])
+        tiles_sent.append(
+            push(half_d.at[to, other_bit("g", mask & 8)], in_d.at[slot], d_send.at[mask], d_recv.at[mask], wide_at(mask))
+        )
+    in_d[slot] = half_d[me, g]
+    to_core[1].wait_recv()
+    for row in range(ROW_TILES):
+        half_in[row] = (half_in[row].astype(f32) + gin_ref[row, c].astype(f32)).astype(bf16)
+    for mask in order:
+        to = flipped(me, [axis for axis in BITS if mask & BITS[axis]])
+        tiles_sent.append(
+            push(half_in.at[:, to, other_bit("g", mask & 8)], in_gu.at[slot], gu_send.at[mask], gu_recv.at[mask], wide_at(mask))
+        )
+    in_gu[slot] = half_in[:, me, g]
+
     pad_ref[rows : rows + 8, :] = jnp.zeros((8, rows), f32)
     theta_ref[...] = jnp.zeros_like(theta_ref)
     mixer_ref[...] = jnp.zeros_like(mixer_ref)
     gain_grad_ref[...] = jnp.zeros_like(gain_grad_ref)
-    own.wait()
-    for copy in sent:
-        copy.wait_recv()
     query_at = lax.broadcasted_iota(jnp.int32, (rows, rows), 0)
     key_at = lax.broadcasted_iota(jnp.int32, (rows, rows), 1)
     blank = jnp.zeros((rows, HP - DH), f32)
+
+    def grad_arrived(step, carry):
+        source = lax.rem(me + step, seqs)
+        pltpu.make_async_copy(sent_ref.at[source], grads_ref.at[source], head_recv.at[source]).wait()
+        return carry
+
+    lax.fori_loop(1, seqs, grad_arrived, 0)
 
     def one(seq, carry):
         keep = (key_at <= query_at) & (key_at < len_ref[seq])
@@ -1273,15 +1376,59 @@
 
     lax.fori_loop(0, 4, one, 0)
     gather.onward()
+    scatter.drain()
+
+    def outputs(at, carry):
+        two = pl.ds(at * 2, 2)
+        made = dot(inner_ref[two].reshape(2 * rows, BLK), w_dn_ref[...])
+        parts_ref[two] = made.astype(bf16).reshape(2, rows, D)
+        return carry
+
+    lax.fori_loop(0, seqs // 2, outputs, 0)
+    scatter2 = Scatter(parts_ref, near2, in22, in32, *scatter_args[3:5], *scatter2_sems)
+    scatter2.start()
     lax.fori_loop(4, seqs, one, 0)
+    scatter2.onward()
     gather.last()
     gather.finish()
-    strips = strips_ref[...]
-    for col in range(ROW_TILES):
-        at = slice(col * BLK, (col + 1) * BLK)
-        go_ref[:, at] = dot_tn(strips, all_ref[:, :, at].reshape(seqs * rows, BLK)).astype(bf16)
+    strip_local.wait()
+    for copy in strips_sent:
+        copy.wait_recv()
+    strips = strips_in[...].reshape(seqs * rows, 2 * DH)
+
+    def out_grad(col, carry):
+        cols = pl.ds(pl.multiple_of(col * BLK, BLK), BLK)
+        go_ref[:, cols] = dot_tn(strips, all_ref[:, :, cols].reshape(seqs * rows, BLK)).astype(bf16)
+        return carry
+
+    lax.fori_loop(0, ROW_TILES, out_grad, 0)
+    scatter2.last()
+    for part in range(2):
+        here = pl.ds(part * half, half)
+        layer_ref[here] = (hmid_ref[here] + scatter2.finish(part)).astype(bf16)
+    for copy in tiles_sent:
+        copy.wait_recv()
+
+    def sum_tiles(chip, carry):
+        for row in range(ROW_TILES):
+            made = (in_gu[chip, row].astype(f32) + in_gu[CHIPS + chip, row].astype(f32)).astype(bf16)
+            tiles_ref[row * FF_TILES + chip] = made[:, :BLK]
+            tiles_ref[(ROW_TILES + row) * FF_TILES + chip] = made[:, BLK:]
+        made = (in_d[chip].astype(f32) + in_d[CHIPS + chip].astype(f32)).astype(bf16)
+        for col in range(ROW_TILES):
+            tiles_ref[2 * ROW_TILES * FF_TILES + chip * ROW_TILES + col] = made[:, col * BLK : (col + 1) * BLK]
+        return carry
+
+    lax.fori_loop(0, CHIPS, sum_tiles, 0)
+
+    def grad_left(step, carry):
+        grad_copy(lax.rem(me + step, seqs)).wait_send()
+        return carry
+
+    lax.fori_loop(1, seqs, grad_left, 0)
     gather.drain()
-    for copy in sent:
+    scatter2.drain()
+    for copy in strips_sent + to_core + tiles_sent:
         copy.wait_send()
 
 
@@ -1289,27 +1436,37 @@
     return {axis: 1 - lax.axis_index(axis) for axis in BITS if mask & BITS[axis]}
 
 
-def run_back(lengths, mix, qkv, toep, gain, scores, weights, outs, sent, dattn, strips):
-    seqs, rows, _ = qkv.shape
+def run_middle(
+    lengths, mix, hn, w_in, w_dn, dy, dy_own, hmid, gain_ffn, w_o, qkv, toep, gain, scores, weights, outs, strips
+):
+    seqs, rows, _ = hn.shape
     dma = pltpu.SemaphoreType.DMA
+    part = BLK // 32
+    shapes = [
+        ((rows, D), bf16), ((rows, D), f32), ((1, D), f32), ((seqs, rows, 6 * DH), bf16), ((2, rows, CQ * rows), f32),
+        ((8, rows), f32), ((1, 2 * HP), f32), ((2 * DH, D), bf16), ((9 * CHIPS, part, BLK), bf16),
+    ]
+    three = pltpu.VMEM((3, rows, D), bf16)
+    one = pltpu.VMEM((rows, D), bf16)
+    every = pltpu.VMEM((CHIPS, rows, D), bf16)
+    heads = pltpu.VMEM((CHIPS, rows, 2 * DH), bf16)
     return pl.pallas_call(
-        back_body,
-        in_specs=[SMEM, SMEM] + [VMEM] * 9,
-        out_specs=[VMEM] * 5,
-        out_shape=[
-            jax.ShapeDtypeStruct((seqs, rows, 6 * DH), bf16),
-            jax.ShapeDtypeStruct((2, rows, CQ * rows), f32),
-            jax.ShapeDtypeStruct((8, rows), f32),
-            jax.ShapeDtypeStruct((1, 2 * HP), f32),
-            jax.ShapeDtypeStruct((2 * DH, D), bf16),
-        ],
+        middle_body,
+        in_specs=[SMEM, SMEM] + [VMEM] * 15,
+        out_specs=[VMEM] * len(shapes),
+        out_shape=[jax.ShapeDtypeStruct(*shape) for shape in shapes],
         scratch_shapes=[
-            pltpu.VMEM((rows + 8, rows), f32), pltpu.VMEM((seqs, rows, 2 * DH), bf16),
-            pltpu.VMEM((CHIPS, rows, D), bf16), dma, dma((8,)), dma((8,)),
-        ] + side_sems(),
-        name="attention_back",
-        compiler_params=pltpu.CompilerParams(collective_id=4, has_side_effects=True, vmem_limit_bytes=32 * 2**20),
-    )(lengths, mix, qkv, toep, gain, scores, weights, outs, sent, dattn, strips)
+            pltpu.VMEM((rows + 8, rows), f32), pltpu.VMEM((seqs, rows, BLK), bf16), pltpu.VMEM((seqs, rows, 2 * BLK), bf16),
+            every, one, every, heads, heads, heads,
+            pltpu.VMEM((ROW_TILES, 2, CHIPS, 2, part, 2 * BLK), bf16), pltpu.VMEM((2, CHIPS, 2, part, D), bf16),
+            pltpu.VMEM((ROW_TILES, CHIPS, 2, part, 2 * BLK), bf16), pltpu.VMEM((CHIPS, 2, part, D), bf16),
+            pltpu.VMEM((2 * CHIPS, ROW_TILES, part, 2 * BLK), bf16), pltpu.VMEM((2 * CHIPS, part, D), bf16),
+            three, one, three, dma((1,)),
+        ] + [dma((8,))] * 4 + [dma((2,))] * 2 + [dma((16,))] * 4
+        + scatter_scratch(rows, D) + [dma((3,))] * 2 + [dma((3, 2))] * 4 + side_sems(),
+        name="middle",
+        compiler_params=pltpu.CompilerParams(collective_id=3, has_side_effects=True, vmem_limit_bytes=61 * 2**20),
+    )(lengths, mix, hn, w_in, w_dn, dy, dy_own, hmid, gain_ffn, w_o, qkv, toep, gain, scores, weights, outs, strips)
 
 
 def share_body(
@@ -1481,35 +1638,18 @@
     xn, qkv, scores, weights, outs, heads, hmid, hn_rows, w_in, w_dn, dy_rows = run_front(
         group_lengths, mix, x_all, layer_input, gains, w_qkv, toep, gain_pair, w_out_all, w_gate, w_up, w_down, dy.astype(bf16)
     )
-    xn_rows, hn_rows, dy_rows = (rows.reshape(CHIPS * seq_len, D) for rows in (xn, hn_rows, dy_rows))
-    w_in, w_dn, w_o = w_in.reshape(D, 2 * BLK), w_dn.reshape(BLK, D), w_out_all.reshape(D, D)
-    heads = jnp.transpose(heads, (1, 0, 2)).reshape(seq_len, D)
+    xn_rows = xn.reshape(CHIPS * seq_len, D)
+    w_in, w_dn = w_in.reshape(D, 2 * BLK), w_dn.reshape(BLK, D)
+    strip = BLK // (2 * CHIPS)
+    part = strip // 2
+    heads = jnp.transpose(heads, (1, 0, 2)).reshape(seq_len, 2 * ROW_TILES, CHIPS, strip)
+    strips = jnp.transpose(heads, (2, 0, 1, 3)).reshape(CHIPS, seq_len, 2 * ROW_TILES * strip)
     input_float = layer_input.astype(f32)
     input_scale = rms(input_float)
-    hmid_scale = rms(hmid)
-    both = dot(hn_rows, w_in)
-    gate, up = both[:, :BLK], both[:, BLK:]
-    sig = jax.nn.sigmoid(gate)
-    silu = gate * sig
-    inner = (silu * up).astype(bf16)
-
-    strip = BLK // (2 * CHIPS)
-    part = strip // 2
-    dinner = dot_nt(dy_rows, w_dn)
-    dgate = (dinner * up * (sig * (1.0 + gate * (1.0 - sig)))).astype(bf16)
-    dup = (dinner * silu).astype(bf16)
-    dboth = jnp.concatenate([dgate, dup], axis=1)
-    dhn = scatter_chips(dot_nt(dboth, w_in).astype(bf16).reshape(CHIPS, seq_len, D), 3)
-    ffn = scatter_slow(dot(inner, w_dn).reshape(CHIPS, seq_len, D))
-    layer_output = (hmid + ffn).astype(bf16)
-    dhmid, grad_gain_ffn = norm_backward(hmid, hmid_scale, gain_ffn, dhn)
-    dhmid = dhmid + dy
-    dattn = dhmid.astype(bf16)
-    dheads = dot_nt(dattn, w_o).astype(bf16).reshape(seq_len, CHIPS, 2 * DH)
-    strips = jnp.transpose(heads.reshape(seq_len, 2 * ROW_TILES, CHIPS, strip), (2, 0, 1, 3))
-    strips = exchange_chips(strips.reshape(CHIPS, seq_len, 2 * ROW_TILES * strip)).reshape(CHIPS * seq_len, -1)
-    dqkv, theta_sums, mixer_sums, gain_sums, grad_out = run_back(
-        group_lengths, mix, qkv, toep, gain_pair, scores, weights, outs, jnp.transpose(dheads, (1, 0, 2)), dattn, strips
+
+    layer_output, dhmid, grad_gain_ffn, dqkv, theta_sums, mixer_sums, gain_sums, grad_out, ffn_sums = run_middle(
+        group_lengths, mix, hn_rows, w_in, w_dn, dy_rows, dy.astype(bf16), hmid, gain_ffn.reshape(1, D),
+        w_out_all.reshape(CHIPS, 2 * DH, D), qkv, toep, gain_pair, scores, weights, outs, strips,
     )
     dqkv_rows = dqkv.reshape(CHIPS * seq_len, 6 * DH)
     dxn_parts = dot_nt(dqkv_rows, w_qkv).astype(bf16).reshape(CHIPS, seq_len, D)
@@ -1534,7 +1674,7 @@
             lax.dynamic_update_slice_in_dim(
                 jnp.zeros((D,), f32), gain_sums.reshape(2, HP)[:, :DH].reshape(-1), chip * 2 * DH, 0
             ),
-            grad_gain_ffn,
+            grad_gain_ffn.reshape(-1),
             lax.dynamic_update_slice_in_dim(
                 jnp.zeros((H * CQ * CK,), f32), grad_theta.reshape(-1), chip * 2 * CQ * CK, 0
             ),
@@ -1543,15 +1683,6 @@
     )
     pieces = jnp.pad(vector_grad.reshape(fs_size, 1, own_vec), ((0, 0), (0, 0), (0, 1024 - own_vec)))
     pieces = jnp.broadcast_to(pieces, (fs_size, reps, 1024)).reshape(devices, 8, 128)
-
-    grad_in = dot_tn(hn_rows, dboth).reshape(ROW_TILES, 2, CHIPS, strip, 2, BLK)
-    grad_down = dot_tn(inner, dy_rows).reshape(2, CHIPS, strip, ROW_TILES, BLK)
-    grad_in = jnp.transpose(half_for_core(grad_in, 1), (1, 3, 0, 2, 4)).reshape(CHIPS, 2 * ROW_TILES, strip, BLK)
-    grad_down = jnp.transpose(half_for_core(grad_down, 0), (0, 2, 1, 3))
-    ffn_tiles = exchange_chips(jnp.concatenate([grad_in, grad_down], axis=1).astype(bf16))
-    gate_tiles = jnp.transpose(ffn_tiles[:, : 2 * ROW_TILES], (1, 0, 2, 3)).reshape(-1, strip, BLK)
-    down_tiles = ffn_tiles[:, 2 * ROW_TILES :].reshape(-1, strip, BLK)
-    ffn_sums = sum_groups(jnp.concatenate([gate_tiles, down_tiles], axis=0))
 
     own_slots = basis_left.shape[0]
     slot_total = own_slots * devices

time: 613 us -> 493 us (0.80)
  local copies, waits for them, and re-layouts: 83.1 us -> 25.2 us
  Pallas kernels: 366 us -> 407 us
  matrix products: 66.9 us -> 36.2 us
  waiting for transfers between devices: 28.8 us -> 0 us
  starting transfers between devices: 22.5 us -> 0 us
  other arithmetic: 33.7 us -> 12.6 us
    pallas_call x2 -> x1, Pallas kernels: 86.3 us -> 132 us  [run_middle(): pl.pallas_call(middle_body, in_specs=[SMEM, SMEM] + [VMEM] * 15, out_spec...]
    ppermute x3 -> x0, waiting for transfers between devices: 28.8 us -> none  [swap(): return lax.ppermute(values, axis, [(0, 1), (1, 0)])]
    all_to_all x3 -> x0, starting transfers between devices: 19.8 us -> none  [exchange_chips(): return lax.all_to_all(parts, CHIP, split_axis=0, concat_axis=0, tiled=True)]
    unnamed x155 -> x96, local copies, waits for them, and re-layouts: 17.7 us -> 2.75 us
    dot_general x4 -> x1, matrix products: 17.9 us -> 4.65 us  [dot_nt(): lax.dot_general(left, right, (((1,), (1,)), ((), ())), preferred_element_...]
    dot_general x3 -> x1, matrix products: 12.5 us -> 0.74 us  [dot(): return jnp.dot(left, right, preferred_element_type=f32)]
    dot_general x3 -> x0, local copies, waits for them, and re-layouts: 7.98 us -> none  [the longest x2 5.71 us: dot_tn(): lax.dot_general(left, right, (((0,), (0,)), ((), ())), preferred_element_...]
    reduce_sum x11, local copies, waits for them, and re-layouts: 7.72 us -> 0.11 us  [body_fast(): jnp.sum(jnp.where(taps[tap][None, :, None, :], theta_sums, 0.0), axis=(1,...]
  transfers between devices with their start and end apart: 6 -> 0, of which waited for: 1 -> 0; matrix products, arithmetic and copies ran while one was open for 19% -> 0% of each run, Pallas kernels for 22% -> 0%
where the time goes in v5:
time: 493 us; the launch traced here: 484 us
  Pallas kernels  407 us (83%)
  matrix products  36.2 us (7%)
  local copies, waits for them, and re-layouts  25.2 us (5%)
  other arithmetic  12.6 us (3%)
    pallas_call x1, Pallas kernels, run_middle(): pl.pallas_call(middle_body, in_specs=[SMEM, SMEM] + [VMEM] * 15, out_spec...  132 us
    pallas_call x1, Pallas kernels, run_front(): pl.pallas_call(forward_body, in_specs=[SMEM, SMEM] + [VMEM] * 7 + [ANYS]...  109 us
    pallas_call x1, Pallas kernels, dispatch(): pl.pallas_call(dispatch_body, in_specs=[ANYS] * 4, out_specs=[ANYS] * 4,...  67.1 us
    pallas_call x1, Pallas kernels, to_slots(): pl.pallas_call(to_slots_body, in_specs=[ANYS] * 2, out_specs=[ANYS] * 2,...  53.6 us
    pallas_call x1, Pallas kernels, share(): pl.pallas_call(share_body, in_specs=[VMEM] * 3, out_specs=[VMEM] * 3, out...  45.3 us
    dot_general x1, matrix products, body_fast(): jnp.einsum('sib,sjb->sij', turned.astype(bf16), right_low, preferred_elem...  13.6 us
    dot_general x1, matrix products, body_fast(): jnp.einsum('saj,sjb->sab', rotated.astype(bf16), right_low, preferred_ele...  12.1 us

profile of v5, /device:TPU:11, one launch (start us, length us, event | category | flops | bytes accessed | tf_op | source)
XLA Modules:
  0.0 483.6 jit_solution(3585411424061332244)
XLA Ops:
  1.4 0.7 convert_element_type.73
  2.0 0.7 maximum_bitcast_fusion.1.vec_ref
  2.7 1.3 reshape.346
  4.1 1.3 reshape.347
  5.9 1.3 maximum_bitcast_fusion.blocks_ref
  7.2 67.1 %dispatch.1 = (bf16[8,128,1536]{2,1,0:T(8,128)(2,1)}, f32[32,8,128]{2,1,0:T(8,128)}, bf16[16,96,576]{2,1,0:T(8,128)(2,1)}, bf16[16,96,1536]{2,1,0:T(8,128)(2,1)}) custom-call(bf16[128,1536]{1,0:T(8,128)(2,1)} %x_ref.3, f32[8,128]{1,0:T(8,128)} %maximum_bitcast_fusion.1.vec_ref, bf16[8,96,576]{2,1,0:T(8,128)(2,1)} %maximum_bitcast_fusion.blocks_ref, ...), custom_call_target="tpu_custom_call" | custom-call | tf_op jit(solution)/shard_map/dispatch/pallas_call | solution.py:978
  74.3 1.0 reshape.349
  77.1 3.7 select_convert_fusion.toep_ref
  81.4 0.7 slice.110
  83.3 0.6 convert_element_type.78.len_ref
  84.0 0.7 maximum_maximum_fusion.gains_ref
  84.7 0.9 multiply_convert_fusion.dy_ref.dy_own_ref
  85.6 109.0 %front.1 = (bf16[8,128,1536]{2,1,0:T(8,128)(2,1)}, bf16[8,128,768]{2,1,0:T(8,128)(2,1)}, bf16[8,2,128,128]{3,2,1,0:T(8,128)(2,1)}, f32[8,2,128,128]{3,2,1,0:T(8,...) custom-call(s32[8]{0:T(128)} %convert_element_type.78.len_ref, ...), custom_call_target="tpu_custom_call" | custom-call | tf_op jit(solution)/shard_map/front/pallas_call | solution.py:1187
  194.6 1.3 copy.99
  195.9 1.0 copy.101.strips_ref
  197.0 132.0 %middle.1 = (bf16[128,1536]{1,0:T(8,128)(2,1)}, f32[128,1536]{1,0:T(8,128)}, f32[1,1536]{1,0:T(1,128)}, bf16[8,128,576]{2,1,0:T(8,128)(2,1)}, f32[2,128,768]{2,1...) custom-call(s32[8]{0:T(128)} %convert_element_type.78.len_ref, ...), custom_call_target="tpu_custom_call" | custom-call | tf_op jit(solution)/shard_map/middle/pallas_call | solution.py:1453
  331.8 1.0 select_reduce_fusion
  334.5 5.1 %bitcast_convert_fusion = bf16[1536,576]{0,1:T(8,128)(2,1)} fusion(bf16[8,128,1536]{2,1,0:T(8,128)(2,1)} %get-tuple-element.55, bf16[8,128,576]{2,1,0:T(8,128)(2,1)S(1)} %copy-done.28), kind=kOutput, calls=%fused_computation.7 | convolution fusion | flops 1812824064 | bytes 6094848 | tf_op jit(solution)/shard_map/dot_general | solution.py:48
  339.7 2.8 copy.103
  342.5 4.6 convolution_convert_fusion.1
  347.2 45.3 %share_gradients.1 = (f32[128,1536]{1,0:T(8,128)S(1)}, bf16[3,3,16,1536]{3,2,1,0:T(8,128)(2,1)S(1)}, bf16[3,16,1536]{2,1,0:T(8,128)(2,1)S(1)}) custom-call(bf16[8,128,1536]{2,1,0:T(8,128)(2,1)S(1)} %bitcast.168, bf16[3,2,8,2,16,576]{5,4,3,2,1,0:T(8,128)(2,1)S(1)} %bitcast.167, bf16[3,2,2,16,1536]{4,3,2,1,0:T(8,128)(2,1)S(1)} %bitcast.169), custom_call_target="tpu_custom_call" | custom-call | tf_op jit(solution)/shard_map/share_gradients/pallas_call | solution.py:1535
  394.0 0.8 reshape.371.vec_ref
  395.7 0.7 copy.142
  396.4 0.7 convolution_convert_fusion
  397.1 2.3 reshape.365.slots_ref
  399.5 53.6 %to_slots.1 = (bf16[32,64,512]{2,1,0:T(8,128)(2,1)}, f32[32,8,128]{2,1,0:T(8,128)}) custom-call(bf16[32,64,512]{2,1,0:T(8,128)(2,1)} %reshape.365.slots_ref, f32[32,8,128]{2,1,0:T(8,128)} %reshape.371.vec_ref), custom_call_target="tpu_custom_call" | custom-call | tf_op jit(solution)/shard_map/to_slots/pallas_call | solution.py:1586
  453.0 1.8 copy.117
  454.9 12.1 %fusion = (f32[4,512,512]{2,1,0:T(8,128)}, f32[4,512,512]{2,1,0:T(8,128)}) fusion(f32[4,512,512]{2,1,0:T(8,128)} %param.37, f32[4,512,512]{2,1,0:T(8,128)} %param.36, f32[4,512,512]{2,1,0:T(8,128)} %param.34, bf16[4,512,512]{2,1,0:T(8,128)(2,1)S(1)} %bitcast.171, f32[4,512,512]{2,1,0:T(8,128)} %param.33), kind=kOutput, calls=%fused_computation.3 | convolution fusion | flops 2156920832 | bytes 27262976 | tf_op jit(solution)/shard_map/saj,sjb->sab/dot_general | solution.py:1706
  467.0 13.6 %fusion.49 = (bf16[4,512,512]{2,1,0:T(8,128)(2,1)}, f32[4,512,512]{2,1,0:T(8,128)}) fusion(f32[4,512,512]{2,1,0:T(8,128)} %param.35, f32[4,512,512]{2,1,0:T(8,128)} %param.34, f32[4,512,512]{2,1,0:T(8,128)} %get-tuple-element.128, f32[4,512,512]{2,1,0:T(8,128)} %get-tuple-element.129, f32[4,512,512]{2,1,0:T(8,128)} %param.33), kind=kOutput, calls=%fused_computation.126 | convolution fusion | flops 2159017984 | bytes 27262976 | tf_op jit(solution)/shard_map/sib,sjb->sij/dot_general | solution.py:1711
  480.6 0.6 fusion.43
  481.2 1.2 fusion.24
  482.4 0.7 copy.180
  (214 shorter events, 10.7 us)
Async XLA Ops:
  0.6 4.9 %copy-start.8 = (bf16[96,1536]{1,0:T(8,128)(2,1)S(1)}, bf16[96,1536]{1,0:T(8,128)(2,1)}, u32[]{:S(2)}) copy-start(bf16[96,1536]{1,0:T(8,128)(2,1)} %param.26) | copy-start | bytes 884740
  74.3 10.4 %copy-start.7 = (bf16[128,1536]{1,0:T(8,128)(2,1)S(1)}, bf16[128,1536]{1,0:T(8,128)(2,1)}, u32[]{:S(2)}) copy-start(bf16[128,1536]{1,0:T(8,128)(2,1)} %param.23) | copy-start | bytes 1179652
  83.9 110.7 %copy-start.10 = (f32[1,1536]{1,0:T(1,128)}, f32[1,1536]{1,0:T(1,128)S(1)}, u32[]{:S(2)}) copy-start(f32[1,1536]{1,0:T(1,128)S(1)} %broadcast_in_dim.416.gain_ffn_ref) | copy-start | bytes 18436
  196.9 132.1 %copy-start.21 = (pred[128,128]{0,1:T(32,128)(4,1)S(1)}, pred[128,128]{0,1:T(32,128)(4,1)}, u32[]{:S(2)}) copy-start(pred[128,128]{0,1:T(32,128)(4,1)} %constant.137) | copy-start | bytes 49156
  196.9 132.4 %copy-start.20 = (pred[128,128]{0,1:T(32,128)(4,1)S(1)}, pred[128,128]{0,1:T(32,128)(4,1)}, u32[]{:S(2)}) copy-start(pred[128,128]{0,1:T(32,128)(4,1)} %constant.139) | copy-start | bytes 49156
  196.9 132.6 %copy-start.19 = (pred[128,128]{0,1:T(32,128)(4,1)S(1)}, pred[128,128]{0,1:T(32,128)(4,1)}, u32[]{:S(2)}) copy-start(pred[128,128]{0,1:T(32,128)(4,1)} %constant.141) | copy-start | bytes 49156
  196.9 132.9 %copy-start.18 = (pred[128,128]{0,1:T(32,128)(4,1)S(1)}, pred[128,128]{0,1:T(32,128)(4,1)}, u32[]{:S(2)}) copy-start(pred[128,128]{0,1:T(32,128)(4,1)} %constant.143) | copy-start | bytes 49156
  196.9 133.1 %copy-start.17 = (pred[128,128]{0,1:T(32,128)(4,1)S(1)}, pred[128,128]{0,1:T(32,128)(4,1)}, u32[]{:S(2)}) copy-start(pred[128,128]{0,1:T(32,128)(4,1)} %constant.145) | copy-start | bytes 49156
  196.9 133.4 %copy-start.16 = (pred[128,128]{0,1:T(32,128)(4,1)S(1)}, pred[128,128]{0,1:T(32,128)(4,1)}, u32[]{:S(2)}) copy-start(pred[128,128]{0,1:T(32,128)(4,1)} %constant.147) | copy-start | bytes 49156
  196.9 133.6 %copy-start.15 = (pred[128,128]{0,1:T(32,128)(4,1)S(1)}, pred[128,128]{0,1:T(32,128)(4,1)}, u32[]{:S(2)}) copy-start(pred[128,128]{0,1:T(32,128)(4,1)} %constant.149) | copy-start | bytes 49156
  197.0 133.8 %copy-start.14 = (pred[128,128]{0,1:T(32,128)(4,1)S(1)}, pred[128,128]{0,1:T(32,128)(4,1)}, u32[]{:S(2)}) copy-start(pred[128,128]{0,1:T(32,128)(4,1)} %constant.151) | copy-start | bytes 49156
  197.0 134.1 %copy-start.13 = (pred[128,128]{0,1:T(32,128)(4,1)S(1)}, pred[128,128]{0,1:T(32,128)(4,1)}, u32[]{:S(2)}) copy-start(pred[128,128]{0,1:T(32,128)(4,1)} %constant.153) | copy-start | bytes 49156
  197.0 134.3 %copy-start.12 = (pred[128,128]{0,1:T(32,128)(4,1)S(1)}, pred[128,128]{0,1:T(32,128)(4,1)}, u32[]{:S(2)}) copy-start(pred[128,128]{0,1:T(32,128)(4,1)} %constant.155) | copy-start | bytes 49156
  329.0 2.6 copy-start.11
  329.0 2.8 copy-start.4
  329.0 5.5 %copy-start.28 = (bf16[8,128,576]{2,1,0:T(8,128)(2,1)S(1)}, bf16[8,128,576]{2,1,0:T(8,128)(2,1)}, u32[]{:S(2)}) copy-start(bf16[8,128,576]{2,1,0:T(8,128)(2,1)} %get-tuple-element.54) | copy-start | bytes 3538948
  339.7 2.8 copy-start.29
  342.5 4.7 copy-start
  347.2 45.3 %copy-start.1 = (bf16[128,1536]{1,0:T(8,128)(2,1)S(1)}, bf16[128,1536]{1,0:T(8,128)(2,1)}, u32[]{:S(2)}) copy-start(bf16[128,1536]{1,0:T(8,128)(2,1)} %x_ref.3) | copy-start | bytes 1179652
  347.2 45.8 %copy-start.27 = (f32[1,256]{1,0:T(1,128)S(1)}, f32[1,256]{1,0:T(1,128)}, u32[]{:S(2)}) copy-start(f32[1,256]{1,0:T(1,128)} %get-tuple-element.62) | copy-start | bytes 3076
  347.2 46.1 %copy-start.26 = (f32[8,128]{1,0:T(8,128)S(1)}, f32[8,128]{1,0:T(8,128)}, u32[]{:S(2)}) copy-start(f32[8,128]{1,0:T(8,128)} %get-tuple-element.65) | copy-start | bytes 12292
  347.2 46.5 %copy-start.22 = (f32[1,1536]{1,0:T(1,128)S(1)}, f32[1,1536]{1,0:T(1,128)}, u32[]{:S(2)}) copy-start(f32[1,1536]{1,0:T(1,128)} %get-tuple-element.63) | copy-start | bytes 18436
  393.0 2.6 copy-start.3
  394.9 1.5 copy-start.30
  466.9 13.6 %copy-start.9 = (f32[32,8,128]{2,1,0:T(8,128)S(1)}, f32[32,8,128]{2,1,0:T(8,128)}, u32[]{:S(2)}) copy-start(f32[32,8,128]{2,1,0:T(8,128)} %get-tuple-element.67) | copy-start | bytes 393220
  466.9 13.7 %copy-start.23 = (f32[356]{0:T(512)S(1)}, f32[356]{0:T(512)}, u32[]{:S(2)}) copy-start(f32[356]{0:T(512)} %param.38) | copy-start | bytes 4276
  466.9 13.7 %copy-start.24 = (f32[356]{0:T(512)S(1)}, f32[356]{0:T(512)}, u32[]{:S(2)}) copy-start(f32[356]{0:T(512)} %param.40) | copy-start | bytes 4276
  466.9 13.7 %copy-start.25 = (f32[356]{0:T(512)S(1)}, f32[356]{0:T(512)}, u32[]{:S(2)}) copy-start(f32[356]{0:T(512)} %param.39) | copy-start | bytes 4276
  466.9 14.3 %copy-start.2 = (bf16[128,1536]{1,0:T(8,128)(2,1)S(1)}, bf16[128,1536]{1,0:T(8,128)(2,1)}, u32[]{:S(2)}) copy-start(bf16[128,1536]{1,0:T(8,128)(2,1)} %x_ref.3) | copy-start | bytes 1179652
  467.0 14.3 %copy-start.5 = (f32[128,1536]{1,0:T(8,128)S(1)}, f32[128,1536]{1,0:T(8,128)}, u32[]{:S(2)}) copy-start(f32[128,1536]{1,0:T(8,128)} %get-tuple-element.58) | copy-start | bytes 2359300
  480.6 1.9 copy-start.6

commit v6 on v5

--- a/solution.py
+++ b/solution.py
@@ -875,6 +875,71 @@
             copy.wait_send()
 
 
+class SideScatter:
+    def __init__(self, parts, near, in1, in2, acc2, acc3, send1, recv1, send2, recv2, send3, recv3):
+        self.parts, self.near, self.in1, self.in2, self.acc2, self.acc3 = parts, near, in1, in2, acc2, acc3
+        self.sems = ((send1, recv1), (send2, recv2), (send3, recv3))
+        self.me = chip_index()
+        half = parts.shape[1] // 2
+        self.low, self.high = pl.ds(0, half), pl.ds(half, half)
+
+    def start(self):
+        send, recv = self.sems[0]
+        far, side = flipped(self.me, ("a", "b", "y")), flipped(self.me, ("b", "y"))
+        self.first = [
+            push(self.parts.at[block, rows], self.in1.at[at], send.at[at], recv.at[at], across(axis))
+            for at, (block, rows, axis) in enumerate(
+                ((far, self.high, "y"), (far, self.low, "b"), (side, self.low, "b"), (side, self.high, "y"))
+            )
+        ]
+
+    def add(self, at, axes, rows, acc):
+        self.first[at].wait_recv()
+        block = flipped(self.me, axes)
+        acc[...] = self.parts[block]
+        acc[rows] = (self.parts[block, rows].astype(f32) + self.in1[at].astype(f32)).astype(bf16)
+        return acc
+
+    def onward(self):
+        send, recv = self.sems[1]
+        third_send, third_recv = self.sems[2]
+        self.second = [
+            push(self.add(0, ("a", "b"), self.high, self.acc2.at[0]), self.in2.at[0], send.at[0], recv.at[0], across("b")),
+            push(self.add(1, ("a", "y"), self.low, self.acc2.at[1]), self.in2.at[1], send.at[1], recv.at[1], across("y")),
+        ]
+        self.third = [
+            push(self.add(at, (axis,), rows, self.acc3.at[to]), self.near.at[to], third_send.at[to], third_recv.at[to], across(axis))
+            for at, axis, rows, to in ((3, "b", self.high, 1), (2, "y", self.low, 2))
+        ]
+
+    def last(self):
+        send, recv = self.sems[2]
+        for copy in self.second:
+            copy.wait_recv()
+        self.acc3[0] = (
+            self.parts[flipped(self.me, ("a",))].astype(f32) + (self.in2[0].astype(f32) + self.in2[1].astype(f32))
+        ).astype(bf16)
+        self.third.append(push(self.acc3.at[0], self.near.at[0], send.at[0], recv.at[0], across("a")))
+
+    def finish(self):
+        for copy in self.third:
+            copy.wait_recv()
+        return (self.parts[self.me].astype(f32) + self.near[0].astype(f32)) + (
+            self.near[1].astype(f32) + self.near[2].astype(f32)
+        )
+
+    def drain(self):
+        for copy in self.first + self.second + self.third:
+            copy.wait_send()
+
+
+def side_scatter_scratch(rows, width):
+    dma = pltpu.SemaphoreType.DMA
+    return [
+        pltpu.VMEM(dims + (width,), bf16) for dims in ((3, rows), (4, rows // 2), (2, rows), (2, rows), (3, rows))
+    ] + [dma((4,))] * 2 + [dma((2,))] * 2 + [dma((3,))] * 2
+
+
 def scatter_scratch(rows, width):
     dma = pltpu.SemaphoreType.DMA
     three = pltpu.VMEM((3, rows, width), bf16)
@@ -884,171 +949,200 @@
 VMEM = pl.BlockSpec(memory_space=pltpu.VMEM)
 
 
-def dispatch_body(
-    x_ref, vec_ref, blocks_ref, w_out_ref, out_ref, vecs_ref, wq_ref, wo_ref,
-    vec_send, vec_recv, vec_local, w_local, o_local, w_send, w_recv, core_send, core_recv,
-    o_send, o_recv, o_side_send, o_side_recv, o_core_send, o_core_recv, *hops,
-):
+def vectors_body(vec_ref, vecs_ref, send, recv, local_sem):
     devices = lax.axis_size(ALL)
     me = device_index()
-    g, a, b, c, y = (lax.axis_index(axis) for axis in ALL)
-    mine = ((g * 2 + a) * 2 + b) * 2 + c
-    local = pltpu.make_async_copy(vec_ref, vecs_ref.at[me], vec_local)
+    local = pltpu.make_async_copy(vec_ref, vecs_ref.at[me], local_sem)
     local.start()
-    own = pltpu.make_async_copy(blocks_ref.at[chip_index()], wq_ref.at[mine], w_local)
-    own.start()
-    own_out = pltpu.make_async_copy(w_out_ref, wo_ref.at[mine], o_local)
-    own_out.start()
     greet_all()
-    gather = Gather(x_ref, out_ref, *hops)
-    gather.start()
 
     def push_vec(step, carry):
         pltpu.make_async_remote_copy(
-            src_ref=vec_ref, dst_ref=vecs_ref.at[me], send_sem=vec_send, recv_sem=vec_recv,
+            src_ref=vec_ref, dst_ref=vecs_ref.at[me], send_sem=send, recv_sem=recv,
             device_id=device_at(lax.rem(me + step, devices)),
         ).start()
         return carry
 
     lax.fori_loop(1, devices, push_vec, 0)
-    sent, relayed = [], []
-    for mask in (4, 6, 5, 7, 2, 1, 3):
-        block = (y * 2 + other_bit("a", mask & 2)) * 2 + other_bit("b", mask & 1)
-        sent.append(push(blocks_ref.at[block], wq_ref.at[mine], w_send.at[mask], w_recv.at[mask], group_at(mask)))
-    half = pl.ds(pl.multiple_of(y * 48, 16), 48)
-    shard = {mask: source_at(mask) for mask in range(8)}
-    lines = {
-        mask: push(w_out_ref.at[half], wo_ref.at[mine, half], o_send.at[mask], o_recv.at[mask], group_at(mask))
-        for mask in (2, 4, 6)
-    }
-    lines[1] = push(w_out_ref.at[half], wo_ref.at[mine, half], o_send.at[1], o_recv.at[1], across("b"))
-    o_core = [push(w_out_ref, wo_ref.at[mine], o_core_send.at[0], o_core_recv.at[0], across("c"))]
-    own.wait()
-    relayed.append(push(wq_ref.at[mine], wq_ref.at[mine], core_send.at[0], core_recv.at[0], across("c")))
-    gather.onward()
-    o_side = {}
-
-    def to_side(mask):
-        lines[mask].wait_recv()
-        piece = wo_ref.at[shard[mask], half]
-        o_side[mask] = push(piece, piece, o_side_send.at[mask], o_side_recv.at[mask], across("y"))
-
-    def relay(mask):
-        sent[(4, 6, 5, 7, 2, 1, 3).index(mask)].wait_recv()
-        block = wq_ref.at[shard[mask]]
-        relayed.append(push(block, block, core_send.at[mask], core_recv.at[mask], across("c")))
-
-    for mask in (2, 4, 6):
-        lines[mask].wait_recv()
-        piece = wo_ref.at[shard[mask], half]
-        lines[mask + 1] = push(piece, piece, o_send.at[mask + 1], o_recv.at[mask + 1], across("b"))
-        o_side[mask] = push(piece, piece, o_side_send.at[mask], o_side_recv.at[mask], across("y"))
-    to_side(1)
-    relay(4)
-    relay(6)
-    gather.last()
-    for mask in (3, 5, 7):
-        to_side(mask)
-    for mask in (5, 7, 2, 1, 3):
-        relay(mask)
-    for mask in (2, 4, 6, 1, 3, 5, 7):
-        o_side[mask].wait_recv()
-        block = wo_ref.at[shard[mask]]
-        o_core.append(push(block, block, o_core_send.at[mask], o_core_recv.at[mask], across("c")))
-    gather.finish()
-    for copy in relayed + o_core:
-        copy.wait_recv()
     others = vecs_ref.at[pl.ds(0, devices - 1)]
-    pltpu.make_async_copy(others, others, vec_recv).wait()
-    pltpu.make_async_copy(others, others, vec_send).wait()
+    pltpu.make_async_copy(others, others, recv).wait()
+    pltpu.make_async_copy(others, others, send).wait()
     local.wait()
-    own_out.wait()
-    gather.drain()
-    for copy in sent + relayed + list(lines.values()) + list(o_side.values()) + o_core:
-        copy.wait_send()
+
+
+def gather_vectors(vec):
+    return pl.pallas_call(
+        vectors_body,
+        in_specs=[VMEM],
+        out_specs=VMEM,
+        out_shape=jax.ShapeDtypeStruct((lax.axis_size(ALL),) + vec.shape, vec.dtype),
+        scratch_shapes=[pltpu.SemaphoreType.DMA] * 3,
+        name="gather_vectors",
+        compiler_params=pltpu.CompilerParams(collective_id=1, has_side_effects=True),
+    )(vec)
 
 
 def source_at(mask):
     return ((other_bit("g", mask & 4) * 2 + other_bit("a", mask & 2)) * 2 + other_bit("b", mask & 1)) * 2 + lax.axis_index("c")
 
 
-def dispatch(rows, vec, blocks, w_out):
-    count, width = rows.shape
-    dma = pltpu.SemaphoreType.DMA
-    return pl.pallas_call(
-        dispatch_body,
-        in_specs=[ANYS] * 4,
-        out_specs=[ANYS] * 4,
-        out_shape=[
-            jax.ShapeDtypeStruct((CHIPS, count, width), rows.dtype),
-            jax.ShapeDtypeStruct((lax.axis_size(ALL),) + vec.shape, vec.dtype),
-            jax.ShapeDtypeStruct((16,) + blocks.shape[1:], blocks.dtype),
-            jax.ShapeDtypeStruct((16,) + w_out.shape, w_out.dtype),
-        ],
-        scratch_shapes=[dma] * 5 + [dma((8,))] * 10 + hop_sems(),
-        name="dispatch",
-        compiler_params=pltpu.CompilerParams(collective_id=1, has_side_effects=True),
-    )(rows, vec, blocks, w_out)
-
-
-def forward_body(
-    len_ref, mix_ref, x_all_ref, x_ref, gains_ref, wq_ref, toep_ref, gain_ref, wo_ref, w_gate_ref, w_up_ref, w_down_ref, dy_ref,
-    xn_ref, qkv_ref, s_ref, p_ref, o_ref, heads_ref, hmid_ref, hn_all_ref, w_in_ref, w_dn_ref, dy_all_ref,
-    pad_ref, out_heads, hn_ref, local_sems, w_send, w_recv, u_send, u_recv, core_send, core_recv,
-    d_send, d_recv, head_send, head_recv, *hops,
+def front_body(
+    len_ref, mix_ref, x_ref, gains_ref, toep_ref, gain_ref, blocks_ref, w_out_ref, w_gate_ref, w_up_ref, w_down_ref, dy_ref,
+    xn_ref, qkv_ref, s_ref, p_ref, o_ref, heads_ref, hmid_ref, wq_ref, wo_ref, hn_all_ref, w_in_ref, w_dn_ref, dy_all_ref,
+    x_all_ref, pad_ref, out_heads, hn_ref, passing, local_sems, q_send, q_recv, q_core_send, q_core_recv,
+    o_send, o_recv, o_side_send, o_side_recv, o_core_send, o_core_recv, d_send, d_recv,
+    w_send, w_recv, u_send, u_recv, core_send, core_recv, head_send, head_recv, *hops,
 ):
     seqs, rows, _ = x_all_ref.shape
     g, a, b, c, y = (lax.axis_index(axis) for axis in ALL)
     me = chip_index()
     mine = source_at(0)
+    shard = {mask: source_at(mask) for mask in range(8)}
     low, high = pl.ds(0, BLK), pl.ds(BLK, BLK)
+    order = (4, 6, 5, 7, 2, 1, 3)
 
     def columns(chip):
         return pl.ds(pl.multiple_of(chip * BLK, BLK), BLK)
 
-    greet_all()
+    def block_to(mask):
+        return (y * 2 + other_bit("a", mask & 2)) * 2 + other_bit("b", mask & 1)
+
     local = [
-        pltpu.make_async_copy(w_gate_ref.at[:, columns(me)], w_in_ref.at[mine, :, low], local_sems.at[0]),
-        pltpu.make_async_copy(w_up_ref.at[:, columns(me)], w_in_ref.at[mine, :, high], local_sems.at[1]),
+        pltpu.make_async_copy(blocks_ref.at[me], wq_ref.at[mine], local_sems.at[0]),
+        pltpu.make_async_copy(w_out_ref, wo_ref.at[mine], local_sems.at[1]),
+        pltpu.make_async_copy(w_gate_ref.at[:, columns(me)], w_in_ref.at[mine, :, low], local_sems.at[2]),
+        pltpu.make_async_copy(w_up_ref.at[:, columns(me)], w_in_ref.at[mine, :, high], local_sems.at[3]),
     ]
+    down_local = pltpu.make_async_copy(w_down_ref, w_dn_ref.at[c], local_sems.at[4])
     for copy in local:
         copy.start()
-    gate, up, relayed = {}, {}, []
-    order = (4, 6, 5, 7, 2, 1, 3)
-    for mask in order:
-        to = (y * 2 + other_bit("a", mask & 2)) * 2 + other_bit("b", mask & 1)
-        gate[mask] = push(
-            w_gate_ref.at[:, columns(to)], w_in_ref.at[mine, :, low], w_send.at[mask], w_recv.at[mask], group_at(mask)
-        )
-        up[mask] = push(
-            w_up_ref.at[:, columns(to)], w_in_ref.at[mine, :, high], u_send.at[mask], u_recv.at[mask], group_at(mask)
-        )
-
-    def down_to_group():
-        return pltpu.make_async_remote_copy(
-            src_ref=w_down_ref, dst_ref=w_dn_ref.at[c], send_sem=d_send.at[0], recv_sem=d_recv.at[0], device_id=across("g")
-        )
-
-    def down_to_core():
-        return pltpu.make_async_remote_copy(
-            src_ref=w_dn_ref.at[c], dst_ref=w_dn_ref.at[c], send_sem=d_send.at[1], recv_sem=d_recv.at[1], device_id=across("c")
-        )
-
-    down_local = pltpu.make_async_copy(w_down_ref, w_dn_ref.at[c], local_sems.at[2])
 
     @pl.when(g == y)
     def _():
         down_local.start()
-        down_to_group().start()
-
-    side = SideGather(dy_ref, dy_all_ref, *hops[:7])
-    side.start()
+
+    greet_all()
+    sent, relayed = {}, []
+    first = Gather(x_ref, x_all_ref, *hops[:7])
+    side = SideGather(dy_ref, dy_all_ref, *hops[7:14])
+    gather = Gather(hn_ref, hn_all_ref, *hops[14:])
+
+    first.start()
+    for mask in order:
+        sent[mask] = push(blocks_ref.at[block_to(mask)], wq_ref.at[mine], q_send.at[mask], q_recv.at[mask], group_at(mask))
+
+    def relay_qkv(mask):
+        sent[mask].wait_recv()
+        block = wq_ref.at[shard[mask]]
+        relayed.append(push(block, block, q_core_send.at[mask], q_core_recv.at[mask], across("c")))
+
+    half = pl.ds(pl.multiple_of(y * 48, 16), 48)
+    lines, o_side, o_core = {}, {}, []
+
+    def start_lines():
+        for mask in (2, 4, 6):
+            lines[mask] = push(w_out_ref.at[half], wo_ref.at[mine, half], o_send.at[mask], o_recv.at[mask], group_at(mask))
+        lines[1] = push(w_out_ref.at[half], wo_ref.at[mine, half], o_send.at[1], o_recv.at[1], across("b"))
+        o_core.append(push(w_out_ref, wo_ref.at[mine], o_core_send.at[0], o_core_recv.at[0], across("c")))
+
+    def to_side(mask):
+        lines[mask].wait_recv()
+        piece = wo_ref.at[shard[mask], half]
+        o_side[mask] = push(piece, piece, o_side_send.at[mask], o_side_recv.at[mask], across("y"))
+        if mask in (2, 4, 6):
+            lines[mask + 1] = push(piece, piece, o_send.at[mask + 1], o_recv.at[mask + 1], across("b"))
+
+    def out_to_core():
+        for mask in (2, 4, 6, 1, 3, 5, 7):
+            o_side[mask].wait_recv()
+            block = wo_ref.at[shard[mask]]
+            o_core.append(push(block, block, o_core_send.at[mask], o_core_recv.at[mask], across("c")))
+
+    count = w_down_ref.shape[0] // 2
+    upper, lower = pl.ds(0, count), pl.ds(count, count)
+
+    def down_copy(src, dst, at, axis):
+        return pltpu.make_async_remote_copy(
+            src_ref=src, dst_ref=dst, send_sem=d_send.at[at], recv_sem=d_recv.at[at], device_id=across(axis)
+        )
+
+    def down_direct():
+        return down_copy(w_down_ref.at[upper], w_dn_ref.at[c, upper], 0, "g")
+
+    def down_around():
+        return down_copy(w_down_ref.at[lower], passing, 1, "g")
+
+    def down_over():
+        return down_copy(passing, w_dn_ref.at[c, lower], 2, "y")
+
+    def down_to_core():
+        return down_copy(w_dn_ref.at[c], w_dn_ref.at[c], 3, "c")
+
+    def down_start():
+        @pl.when(g == y)
+        def _():
+            down_direct().start()
+
+        @pl.when(g != y)
+        def _():
+            down_around().start()
+
+    def down_pass():
+        @pl.when(g == y)
+        def _():
+            down_around().wait_recv()
+            down_over().start()
+
+    def down_last():
+        @pl.when(g == y)
+        def _():
+            down_local.wait()
+            down_to_core().start()
+            down_direct().wait_send()
+            down_over().wait_send()
+
+        @pl.when(g != y)
+        def _():
+            down_direct().wait_recv()
+            down_over().wait_recv()
+            down_to_core().start()
+            down_around().wait_send()
+
+    gate, up = {}, {}
+
+    def send_columns(masks):
+        for mask in masks:
+            to = columns(block_to(mask))
+            gate[mask] = push(w_gate_ref.at[:, to], w_in_ref.at[mine, :, low], w_send.at[mask], w_recv.at[mask], group_at(mask))
+            up[mask] = push(w_up_ref.at[:, to], w_in_ref.at[mine, :, high], u_send.at[mask], u_recv.at[mask], group_at(mask))
 
     def relay(mask):
         gate[mask].wait_recv()
         up[mask].wait_recv()
-        block = w_in_ref.at[source_at(mask)]
+        block = w_in_ref.at[shard[mask]]
         relayed.append(push(block, block, core_send.at[mask], core_recv.at[mask], across("c")))
+
+    start_lines()
+    local[0].wait()
+    relayed.append(push(wq_ref.at[mine], wq_ref.at[mine], q_core_send.at[0], q_core_recv.at[0], across("c")))
+    first.onward()
+    down_start()
+    for mask in (2, 4, 6):
+        to_side(mask)
+    to_side(1)
+    relay_qkv(4)
+    relay_qkv(6)
+    first.last()
+    send_columns((4, 6, 5, 7))
+    for mask in (5, 7, 2, 1, 3):
+        relay_qkv(mask)
+    side.start()
+    first.finish()
+    for copy in relayed:
+        copy.wait_recv()
+    send_columns((2, 1, 3))
+    qkv_relayed = relayed[:]
+    del relayed[:]
 
     pad_ref[0:8, :] = jnp.zeros((8, rows), f32)
     blank = jnp.zeros((rows, HP - DH), bf16)
@@ -1058,7 +1152,7 @@
         values = x_all_ref[pl.ds(at * batch, batch)].astype(f32).reshape(batch * rows, D)
         normed = (values * rms(values) * gains_ref[0:1, :]).astype(bf16)
         xn_ref[pl.ds(at * batch, batch)] = normed.reshape(batch, rows, D)
-        made = dot(normed, wq_ref[...]).astype(bf16)
+        made = dot(normed, wq_ref[...].reshape(D, 6 * DH)).astype(bf16)
         for seq in range(batch):
             for piece in range(6):
                 qkv_ref[at * batch + seq, :, piece * HP : (piece + 1) * HP] = jnp.concatenate(
@@ -1066,8 +1160,13 @@
                 )
         return carry
 
-    lax.fori_loop(0, seqs // batch, project, 0)
-    for copy in local:
+    project(0, 0)
+    for mask in (3, 5, 7):
+        to_side(mask)
+    down_pass()
+    project(1, 0)
+    side.onward()
+    for copy in local[1:]:
         copy.wait()
     relayed.append(push(w_in_ref.at[mine], w_in_ref.at[mine], core_send.at[0], core_recv.at[0], across("c")))
     query_at = lax.broadcasted_iota(jnp.int32, (rows, rows), 0)
@@ -1113,10 +1212,11 @@
         return carry
 
     lax.fori_loop(0, 4, attend, 0)
-    side.onward()
+    out_to_core()
     lax.fori_loop(4, seqs, attend, 0)
     heads_ref[me] = out_heads[me]
-    side.last()
+    for copy in o_core:
+        copy.wait_recv()
 
     def head_arrived(step, carry):
         source = lax.rem(me + step, seqs)
@@ -1137,28 +1237,17 @@
     lax.fori_loop(0, ROW_TILES, project_out, 0)
     hmid = hmid_ref[...]
     hn_ref[...] = (hmid * rms(hmid) * gains_ref[1:2, :]).astype(bf16)
-    gather = Gather(hn_ref, hn_all_ref, *hops[7:])
     gather.start()
-    for mask in (2, 1, 3):
+    side.last()
+    for mask in (4, 6):
         relay(mask)
     gather.onward()
-    for mask in (4, 6):
+    for mask in (5, 7, 2):
         relay(mask)
     gather.last()
-    for mask in (5, 7):
+    for mask in (1, 3):
         relay(mask)
-
-    @pl.when(g == y)
-    def _():
-        down_local.wait()
-        down_to_core().start()
-        down_to_group().wait_send()
-
-    @pl.when(g != y)
-    def _():
-        down_to_group().wait_recv()
-        down_to_core().start()
-
+    down_last()
     down_to_core().wait()
     side.finish()
     gather.finish()
@@ -1170,59 +1259,80 @@
         return carry
 
     lax.fori_loop(1, seqs, head_left, 0)
+    first.drain()
     side.drain()
     gather.drain()
-    for copy in relayed + list(gate.values()) + list(up.values()):
+    for copies in (sent, lines, o_side, gate, up):
+        for copy in copies.values():
+            copy.wait_send()
+    for copy in qkv_relayed + relayed + o_core:
         copy.wait_send()
 
 
-def run_front(lengths, mix, x_all, x, gains, w_qkv, toep, gain, w_o, w_gate, w_up, w_down, dy):
-    seqs, rows, _ = x_all.shape
+def run_front(lengths, mix, x, gains, toep, gain, blocks, w_out, w_gate, w_up, w_down, dy):
+    rows = x.shape[0]
     dma = pltpu.SemaphoreType.DMA
     shapes = [
-        ((seqs, rows, D), bf16), ((seqs, rows, 6 * HP), bf16), ((seqs, 2, rows, rows), bf16), ((seqs, 2, rows, rows), f32),
-        ((seqs, rows, 2 * HP), f32), ((CHIPS, rows, 2 * DH), bf16), ((rows, D), f32), ((CHIPS, rows, D), bf16),
+        ((CHIPS, rows, D), bf16), ((CHIPS, rows, 6 * HP), bf16), ((CHIPS, 2, rows, rows), bf16), ((CHIPS, 2, rows, rows), f32),
+        ((CHIPS, rows, 2 * HP), f32), ((CHIPS, rows, 2 * DH), bf16), ((rows, D), f32),
+        ((16,) + blocks.shape[1:], bf16), ((16,) + w_out.shape, bf16), ((CHIPS, rows, D), bf16),
         ((16, w_gate.shape[0], 2 * BLK), bf16), ((2,) + w_down.shape, bf16), ((CHIPS, rows, D), bf16),
     ]
     return pl.pallas_call(
-        forward_body,
-        in_specs=[SMEM, SMEM] + [VMEM] * 7 + [ANYS] * 4,
-        out_specs=[VMEM] * 7 + [ANYS] * 4,
+        front_body,
+        in_specs=[SMEM, SMEM] + [VMEM] * 4 + [ANYS] * 6,
+        out_specs=[VMEM] * 9 + [ANYS] * 4,
         out_shape=[jax.ShapeDtypeStruct(*shape) for shape in shapes],
         scratch_shapes=[
-            pltpu.VMEM((rows + 8, rows), f32), pltpu.VMEM((seqs, rows, 2 * DH), bf16), pltpu.VMEM((rows, D), bf16),
-            dma((3,)),
-        ] + [dma((8,))] * 6 + [dma((2,))] * 2 + [dma((8,))] * 2 + side_sems() + hop_sems(),
+            pltpu.VMEM((CHIPS, rows, D), bf16), pltpu.VMEM((rows + 8, rows), f32), pltpu.VMEM((CHIPS, rows, 2 * DH), bf16),
+            pltpu.VMEM((rows, D), bf16), pltpu.VMEM((w_down.shape[0] // 2, D), bf16), dma((5,)),
+        ] + [dma((8,))] * 10 + [dma((4,))] * 2 + [dma((8,))] * 8 + hop_sems() + side_sems() + hop_sems(),
         name="front",
         compiler_params=pltpu.CompilerParams(collective_id=2, has_side_effects=True, vmem_limit_bytes=56 * 2**20),
-    )(lengths, mix, x_all, x, gains, w_qkv, toep, gain, w_o, w_gate, w_up, w_down, dy)
+    )(lengths, mix, x, gains, toep, gain, blocks, w_out, w_gate, w_up, w_down, dy)
 
 
 def middle_body(
-    len_ref, mix_ref, hn_ref, w_in_ref, w_dn_ref, dy_ref, dy_own_ref, hmid_ref, gain_ffn_ref, wo_ref,
+    len_ref, mix_ref, hn_ref, dy_ref, xn_ref, w_in_ref, w_dn_ref, wq_ref, dy_own_ref, hmid_ref, gain_ffn_ref, wo_ref,
     qkv_ref, toep_ref, gain_ref, s_ref, p_ref, o_ref, strips_ref,
-    layer_ref, dhmid_ref, gain_ffn_grad_ref, dqkv_ref, theta_ref, mixer_ref, gain_grad_ref, go_ref, tiles_ref,
-    pad_ref, inner_ref, dboth_ref, parts_ref, dattn_ref, all_ref, grads_ref, sent_ref, strips_in, gin_ref, gd_ref,
-    half_in, half_d, in_gu, in_d, near2, in22, in32, local_sems, strip_send, strip_recv, head_send, head_recv,
-    core_send, core_recv, gu_send, gu_recv, d_send, d_recv, *rest,
+    inner_ref, dhmid_ref, dxn_ref, gain_ffn_grad_ref, theta_ref, mixer_ref, gain_grad_ref, tiles_ref,
+    theta_sums, pad_ref, first_ref, second_ref, dboth_ref, parts_ref, dattn_ref, grads_ref, sent_ref, strips_in, gin_ref, gd_ref,
+    half_in, half_d, near_in, near_d, dqkv_ref, gq_ref, go_ref, core_q, core_o, in_q, in_o,
+    near3, in23, in33, local_sems, load_sems, strip_send, strip_recv, head_send, head_recv,
+    core_send, core_recv, near_send, near_recv, gu_send, gu_recv, q_send, q_recv, *rest,
 ):
-    scatter_args, scatter2_sems, side = rest[:11], rest[11:17], rest[17:]
+    scatter_args, scatter3_sems, side = rest[:11], rest[11:17], rest[17:]
     seqs, rows, _ = hn_ref.shape
     g, a, b, c, y = (lax.axis_index(axis) for axis in ALL)
     me = chip_index()
+    pairs = [(1 - y) * 2 + 1 - a, (1 - y) * 2 + a, y * 2 + 1 - a, y * 2 + a]
+    loads = []
+    for at, pair in enumerate(pairs):
+        two = pl.ds(pair * 2, 2)
+        loads.append(
+            [
+                pltpu.make_async_copy(hn_ref.at[two], first_ref.at[two], load_sems.at[at]),
+                pltpu.make_async_copy(dy_ref.at[two], second_ref.at[two], load_sems.at[4 + at]),
+            ]
+        )
+    for copies in loads:
+        for copy in copies:
+            copy.start()
     strip_local = pltpu.make_async_copy(strips_ref.at[me], strips_in.at[me], local_sems.at[0])
     strip_local.start()
     greet_all()
-    strips_sent = []
-    for mask in (7, 6, 5, 3, 4, 2, 1):
-        to = flipped(me, [axis for axis in BITS if mask & BITS[axis]])
-        strips_sent.append(push(strips_ref.at[to], strips_in.at[me], strip_send.at[mask], strip_recv.at[mask], chip_at(mask)))
-
-    def hidden(at, carry):
-        two = pl.ds(at * 2, 2)
-        both = dot(hn_ref[two].reshape(2 * rows, D), w_in_ref[...])
+    chips = (7, 6, 5, 3, 4, 2, 1)
+    to_chip = {mask: flipped(me, [axis for axis in BITS if mask & BITS[axis]]) for mask in chips}
+    strips_sent = [
+        push(strips_ref.at[to_chip[mask]], strips_in.at[me], strip_send.at[mask], strip_recv.at[mask], chip_at(mask))
+        for mask in chips
+    ]
+
+    def hidden(pair):
+        two = pl.ds(pair * 2, 2)
+        both = dot(first_ref[two].reshape(2 * rows, D), w_in_ref[...])
         gate, up = both[:, :BLK], both[:, BLK:]
-        dinner = dot_nt(dy_ref[two].reshape(2 * rows, D), w_dn_ref[...])
+        dinner = dot_nt(second_ref[two].reshape(2 * rows, D), w_dn_ref[...])
         sig = jax.nn.sigmoid(gate)
         silu = gate * sig
         inner_ref[two] = (silu * up).astype(bf16).reshape(2, rows, BLK)
@@ -1232,33 +1342,77 @@
         dboth_ref[two, :, BLK:] = dup.reshape(2, rows, BLK)
         back = dot_nt(dgate, w_in_ref[:, 0:BLK]) + dot_nt(dup, w_in_ref[:, BLK:])
         parts_ref[two] = back.astype(bf16).reshape(2, rows, D)
-        return carry
-
-    lax.fori_loop(0, seqs // 2, hidden, 0)
+
+    def wait_load(at):
+        for copy in loads[at]:
+            copy.wait()
+
+    wait_load(0)
+    hidden(pairs[0])
     scatter = Scatter(parts_ref, *scatter_args)
     scatter.start()
+    wait_load(1)
+    wait_load(2)
+
+    def two_more(step, carry):
+        hidden((1 - y) * 2 + a + step * ((2 * y - 1) * 2 + 1 - a - a))
+        return carry
+
+    lax.fori_loop(0, 2, two_more, 0)
+    scatter.onward()
+    wait_load(3)
+    hidden(pairs[3])
 
     def down_grad(col, carry):
         cols = pl.ds(pl.multiple_of(col * BLK, BLK), BLK)
-        made = dot_tn(inner_ref[...].reshape(seqs * rows, BLK), dy_ref[:, :, cols].reshape(seqs * rows, BLK))
+        made = dot_tn(inner_ref[...].reshape(seqs * rows, BLK), second_ref[:, :, cols].reshape(seqs * rows, BLK))
         gd_ref[:, :, :, :, cols] = made.astype(bf16).reshape(2, CHIPS, 2, BLK // 32, BLK)
         return carry
 
     lax.fori_loop(0, ROW_TILES, down_grad, 0)
     to_core = [push(gd_ref.at[1 - c], half_d, core_send.at[0], core_recv.at[0], across("c"))]
-    scatter.onward()
 
     def in_grad(row, carry):
-        values = hn_ref[:, :, pl.ds(pl.multiple_of(row * BLK, BLK), BLK)].reshape(seqs * rows, BLK)
+        values = first_ref[:, :, pl.ds(pl.multiple_of(row * BLK, BLK), BLK)].reshape(seqs * rows, BLK)
         for which in range(2):
             cols = slice(which * BLK, (which + 1) * BLK)
             made = dot_tn(values, dboth_ref[:, :, cols].reshape(seqs * rows, BLK))
             gin_ref[row, :, :, :, :, cols] = made.astype(bf16).reshape(2, CHIPS, 2, BLK // 32, BLK)
         return carry
 
-    lax.fori_loop(0, ROW_TILES, in_grad, 0)
-    to_core.append(push(gin_ref.at[:, 1 - c], half_in, core_send.at[1], core_recv.at[1], across("c")))
+    def in_to_core(row):
+        to_core.append(push(gin_ref.at[row, 1 - c], half_in.at[row], core_send.at[1 + row], core_recv.at[1 + row], across("c")))
+
+    in_grad(0, 0)
+    in_to_core(0)
+    to_core[0].wait_recv()
+
+    def core_down(chip, carry):
+        half_d[chip] = (half_d[chip].astype(f32) + gd_ref[c, chip].astype(f32)).astype(bf16)
+        return carry
+
+    lax.fori_loop(0, CHIPS, core_down, 0)
+    to_near = [push(half_d.at[:, 1 - g], near_d, near_send.at[0], near_recv.at[0], across("g"))]
     scatter.last()
+    lax.fori_loop(1, ROW_TILES, in_grad, 0)
+    in_to_core(1)
+    in_to_core(2)
+    xn_load = pltpu.make_async_copy(xn_ref, first_ref, load_sems.at[8])
+    xn_load.start()
+
+    def core_rows(row):
+        to_core[1 + row].wait_recv()
+
+        def core_chip(chip, carry):
+            half_in[row, chip] = (half_in[row, chip].astype(f32) + gin_ref[row, c, chip].astype(f32)).astype(bf16)
+            return carry
+
+        lax.fori_loop(0, CHIPS, core_chip, 0)
+        to_near.append(push(half_in.at[row, :, 1 - g], near_in.at[row], near_send.at[1 + row], near_recv.at[1 + row], across("g")))
+
+    core_rows(0)
+    core_rows(1)
+    core_rows(2)
     half = rows // 2
     gain_sum = jnp.zeros((1, D), f32)
     for part in range(2):
@@ -1292,32 +1446,11 @@
 
     lax.fori_loop(0, seqs, send_grad, 0)
     grads_ref[me] = sent_ref[me]
-    gather = SideGather(dattn_ref, all_ref, *side)
+    gather = SideGather(dattn_ref, second_ref, *side)
     gather.start()
 
-    slot = g * CHIPS + me
-    to_core[0].wait_recv()
-    half_d[...] = (half_d[...].astype(f32) + gd_ref[c].astype(f32)).astype(bf16)
-    tiles_sent = []
-    order = (15, 14, 13, 11, 12, 10, 9, 8, 7, 6, 5, 3, 4, 2, 1)
-    for mask in order:
-        to = flipped(me, [axis for axis in BITS if mask & BITS[axis]])
-        tiles_sent.append(
-            push(half_d.at[to, other_bit("g", mask & 8)], in_d.at[slot], d_send.at[mask], d_recv.at[mask], wide_at(mask))
-        )
-    in_d[slot] = half_d[me, g]
-    to_core[1].wait_recv()
-    for row in range(ROW_TILES):
-        half_in[row] = (half_in[row].astype(f32) + gin_ref[row, c].astype(f32)).astype(bf16)
-    for mask in order:
-        to = flipped(me, [axis for axis in BITS if mask & BITS[axis]])
-        tiles_sent.append(
-            push(half_in.at[:, to, other_bit("g", mask & 8)], in_gu.at[slot], gu_send.at[mask], gu_recv.at[mask], wide_at(mask))
-        )
-    in_gu[slot] = half_in[:, me, g]
-
     pad_ref[rows : rows + 8, :] = jnp.zeros((8, rows), f32)
-    theta_ref[...] = jnp.zeros_like(theta_ref)
+    theta_sums[...] = jnp.zeros_like(theta_sums)
     mixer_ref[...] = jnp.zeros_like(mixer_ref)
     gain_grad_ref[...] = jnp.zeros_like(gain_grad_ref)
     query_at = lax.broadcasted_iota(jnp.int32, (rows, rows), 0)
@@ -1360,7 +1493,7 @@
             weight = weights[head]
             grad_conv = weight * (grad_weight - jnp.sum(weight * grad_weight, axis=-1, keepdims=True))
             wide = shifted_up(pad_ref, grad_conv).astype(bf16)
-            theta_ref[head] += dot_tn(s_ref[seq, head], wide)
+            theta_sums[head] += dot_tn(s_ref[seq, head], wide)
             grad_scores = jnp.zeros((rows, rows), f32)
             for lag in range(CQ):
                 grad_scores += dot_nt(
@@ -1374,151 +1507,149 @@
         dqkv_ref[seq] = jnp.concatenate([part[:, :DH] for part in made], axis=1).astype(bf16)
         return carry
 
-    lax.fori_loop(0, 4, one, 0)
+    lax.fori_loop(0, seqs, one, 0)
     gather.onward()
     scatter.drain()
-
-    def outputs(at, carry):
+    tiles_sent = []
+
+    tap_at = query_at - key_at + CK // 2
+
+    def taps(at, carry):
+        lag = lax.rem(at, CQ)
+        values = theta_sums[lax.div(at, CQ), :, pl.ds(pl.multiple_of(lag * rows, rows), rows)]
+        for tap in range(CK):
+            theta_ref[pl.ds(at * CK + tap, 1), :] = jnp.sum(
+                jnp.where(tap_at == tap, values, 0.0), axis=0, keepdims=True
+            )
+        return carry
+
+    xn_load.wait()
+    all_rows = seqs * rows
+
+    def qkv_grad(row, carry):
+        cols = pl.ds(pl.multiple_of(row * BLK, BLK), BLK)
+        made = dot_tn(first_ref[:, :, cols].reshape(all_rows, BLK), dqkv_ref[...].reshape(all_rows, 6 * DH))
+        gq_ref[row] = made.astype(bf16).reshape(2, CHIPS, 2, BLK // 32, 6 * DH)
+        return carry
+
+    lax.fori_loop(0, ROW_TILES, qkv_grad, 0)
+    to_core.append(push(gq_ref.at[:, 1 - c], core_q, core_send.at[4], core_recv.at[4], across("c")))
+
+    def input_part(at, carry):
         two = pl.ds(at * 2, 2)
-        made = dot(inner_ref[two].reshape(2 * rows, BLK), w_dn_ref[...])
+        made = dot_nt(dqkv_ref[two].reshape(2 * rows, 6 * DH), wq_ref[...])
         parts_ref[two] = made.astype(bf16).reshape(2, rows, D)
         return carry
 
-    lax.fori_loop(0, seqs // 2, outputs, 0)
-    scatter2 = Scatter(parts_ref, near2, in22, in32, *scatter_args[3:5], *scatter2_sems)
-    scatter2.start()
-    lax.fori_loop(4, seqs, one, 0)
-    scatter2.onward()
+    lax.fori_loop(0, seqs // 2, input_part, 0)
+    scatter3 = Scatter(parts_ref, near3, in23, in33, *scatter_args[3:5], *scatter3_sems)
+    scatter3.start()
+    lax.fori_loop(0, 2 * CQ, taps, 0)
+    to_core[4].wait_recv()
+
+    def core_chip_q(chip, carry):
+        for row in range(ROW_TILES):
+            core_q[row, chip] = (core_q[row, chip].astype(f32) + gq_ref[row, c, chip].astype(f32)).astype(bf16)
+        return carry
+
+    lax.fori_loop(0, CHIPS, core_chip_q, 0)
+    slot = g * CHIPS + me
+    order = (15, 14, 13, 11, 12, 10, 9, 8, 7, 6, 5, 3, 4, 2, 1)
+    for mask in order:
+        to = flipped(me, [axis for axis in BITS if mask & BITS[axis]])
+        tiles_sent.append(
+            push(core_q.at[:, to, other_bit("g", mask & 8)], in_q.at[slot], q_send.at[mask], q_recv.at[mask], wide_at(mask))
+        )
+    in_q[slot] = core_q[:, me, g]
     gather.last()
+    to_near[0].wait_recv()
+
+    def near_down(chip, carry):
+        half_d[chip, g] = (half_d[chip, g].astype(f32) + near_d[chip].astype(f32)).astype(bf16)
+        return carry
+
+    lax.fori_loop(0, CHIPS, near_down, 0)
+    base = 4 * ROW_TILES**2
+
+    def spread(ref, cols, tile, which):
+        for mask in chips:
+            at = which * CHIPS + mask
+            tiles_sent.append(
+                push(ref.at[to_chip[mask], g, :, cols], tiles_ref.at[tile], gu_send.at[at], gu_recv.at[at], chip_at(mask))
+            )
+        tiles_ref[tile] = ref[me, g, :, cols]
+
+    for col in range(ROW_TILES):
+        spread(half_d, pl.ds(col * BLK, BLK), base + 2 * ROW_TILES * FF_TILES + me * ROW_TILES + col, 6 + col)
+    scatter3.onward()
     gather.finish()
     strip_local.wait()
     for copy in strips_sent:
         copy.wait_recv()
-    strips = strips_in[...].reshape(seqs * rows, 2 * DH)
 
     def out_grad(col, carry):
         cols = pl.ds(pl.multiple_of(col * BLK, BLK), BLK)
-        go_ref[:, cols] = dot_tn(strips, all_ref[:, :, cols].reshape(seqs * rows, BLK)).astype(bf16)
+        made = dot_tn(strips_in[...].reshape(all_rows, 2 * DH), second_ref[:, :, cols].reshape(all_rows, BLK))
+        go_ref[:, :, :, :, cols] = made.astype(bf16).reshape(ROW_TILES, 2, 2, BLK // 32, BLK)
         return carry
 
     lax.fori_loop(0, ROW_TILES, out_grad, 0)
-    scatter2.last()
-    for part in range(2):
-        here = pl.ds(part * half, half)
-        layer_ref[here] = (hmid_ref[here] + scatter2.finish(part)).astype(bf16)
+    to_core.append(push(go_ref.at[:, 1 - c], core_o, core_send.at[5], core_recv.at[5], across("c")))
+
+    def near_rows(row):
+        to_near[1 + row].wait_recv()
+
+        def near_chip(chip, carry):
+            half_in[row, chip, g] = (half_in[row, chip, g].astype(f32) + near_in[row, chip].astype(f32)).astype(bf16)
+            return carry
+
+        lax.fori_loop(0, CHIPS, near_chip, 0)
+        for which in range(2):
+            spread(
+                half_in.at[row], pl.ds(which * BLK, BLK), base + (which * ROW_TILES + row) * FF_TILES + me, 2 * row + which
+            )
+
+    near_rows(0)
+    to_core[5].wait_recv()
+    core_o[...] = (core_o[...].astype(f32) + go_ref[:, c].astype(f32)).astype(bf16)
+    to_near.append(push(core_o.at[:, 1 - g], in_o, near_send.at[4], near_recv.at[4], across("g")))
+    scatter3.last()
+    near_rows(1)
+    near_rows(2)
+    dxn_ref[0:half] = scatter3.finish(0)
+    dxn_ref[half:] = scatter3.finish(1)
+
+    def three_tiles(at, values):
+        for col in range(ROW_TILES):
+            tiles_ref[at + col] = values[:, col * BLK : (col + 1) * BLK].astype(bf16)
+
+    to_near[4].wait_recv()
+    for row in range(ROW_TILES):
+        three_tiles(3 * ROW_TILES**2 + row * ROW_TILES, in_o[row].astype(f32) + core_o[row, g].astype(f32))
     for copy in tiles_sent:
-        copy.wait_recv()
-
-    def sum_tiles(chip, carry):
-        for row in range(ROW_TILES):
-            made = (in_gu[chip, row].astype(f32) + in_gu[CHIPS + chip, row].astype(f32)).astype(bf16)
-            tiles_ref[row * FF_TILES + chip] = made[:, :BLK]
-            tiles_ref[(ROW_TILES + row) * FF_TILES + chip] = made[:, BLK:]
-        made = (in_d[chip].astype(f32) + in_d[CHIPS + chip].astype(f32)).astype(bf16)
-        for col in range(ROW_TILES):
-            tiles_ref[2 * ROW_TILES * FF_TILES + chip * ROW_TILES + col] = made[:, col * BLK : (col + 1) * BLK]
-        return carry
-
-    lax.fori_loop(0, CHIPS, sum_tiles, 0)
-
-    def grad_left(step, carry):
-        grad_copy(lax.rem(me + step, seqs)).wait_send()
-        return carry
-
-    lax.fori_loop(1, seqs, grad_left, 0)
-    gather.drain()
-    scatter2.drain()
-    for copy in strips_sent + to_core + tiles_sent:
-        copy.wait_send()
-
-
-def chip_at(mask):
-    return {axis: 1 - lax.axis_index(axis) for axis in BITS if mask & BITS[axis]}
-
-
-def run_middle(
-    lengths, mix, hn, w_in, w_dn, dy, dy_own, hmid, gain_ffn, w_o, qkv, toep, gain, scores, weights, outs, strips
-):
-    seqs, rows, _ = hn.shape
-    dma = pltpu.SemaphoreType.DMA
-    part = BLK // 32
-    shapes = [
-        ((rows, D), bf16), ((rows, D), f32), ((1, D), f32), ((seqs, rows, 6 * DH), bf16), ((2, rows, CQ * rows), f32),
-        ((8, rows), f32), ((1, 2 * HP), f32), ((2 * DH, D), bf16), ((9 * CHIPS, part, BLK), bf16),
-    ]
-    three = pltpu.VMEM((3, rows, D), bf16)
-    one = pltpu.VMEM((rows, D), bf16)
-    every = pltpu.VMEM((CHIPS, rows, D), bf16)
-    heads = pltpu.VMEM((CHIPS, rows, 2 * DH), bf16)
-    return pl.pallas_call(
-        middle_body,
-        in_specs=[SMEM, SMEM] + [VMEM] * 15,
-        out_specs=[VMEM] * len(shapes),
-        out_shape=[jax.ShapeDtypeStruct(*shape) for shape in shapes],
-        scratch_shapes=[
-            pltpu.VMEM((rows + 8, rows), f32), pltpu.VMEM((seqs, rows, BLK), bf16), pltpu.VMEM((seqs, rows, 2 * BLK), bf16),
-            every, one, every, heads, heads, heads,
-            pltpu.VMEM((ROW_TILES, 2, CHIPS, 2, part, 2 * BLK), bf16), pltpu.VMEM((2, CHIPS, 2, part, D), bf16),
-            pltpu.VMEM((ROW_TILES, CHIPS, 2, part, 2 * BLK), bf16), pltpu.VMEM((CHIPS, 2, part, D), bf16),
-            pltpu.VMEM((2 * CHIPS, ROW_TILES, part, 2 * BLK), bf16), pltpu.VMEM((2 * CHIPS, part, D), bf16),
-            three, one, three, dma((1,)),
-        ] + [dma((8,))] * 4 + [dma((2,))] * 2 + [dma((16,))] * 4
-        + scatter_scratch(rows, D) + [dma((3,))] * 2 + [dma((3, 2))] * 4 + side_sems(),
-        name="middle",
-        compiler_params=pltpu.CompilerParams(collective_id=3, has_side_effects=True, vmem_limit_bytes=61 * 2**20),
-    )(lengths, mix, hn, w_in, w_dn, dy, dy_own, hmid, gain_ffn, w_o, qkv, toep, gain, scores, weights, outs, strips)
-
-
-def share_body(
-    parts_ref, gq_ref, go_ref, dxn_ref, qkv_ref, out_ref,
-    core_q, core_o, in_q, in_o, core_send, core_recv, send, recv, go_send, go_recv, *scatter_args,
-):
-    g, a, b, c, y = (lax.axis_index(axis) for axis in ALL)
-    me = chip_index()
-    barrier = pltpu.get_barrier_semaphore()
-    pl.semaphore_signal(barrier, inc=1, device_id=across("c"))
-    for mask in range(1, 16):
-        pl.semaphore_signal(barrier, inc=1, device_id=wide_at(mask))
-    pl.semaphore_wait(barrier, 16)
-    to_core = [
-        push(gq_ref.at[:, 1 - c], core_q, core_send.at[0], core_recv.at[0], across("c")),
-        push(go_ref.at[:, 1 - c], core_o, core_send.at[1], core_recv.at[1], across("c")),
-    ]
-    scatter = Scatter(parts_ref, *scatter_args)
-    scatter.start()
-    to_core[0].wait_recv()
-    for row in range(ROW_TILES):
-        core_q[row] = (core_q[row].astype(f32) + gq_ref[row, c].astype(f32)).astype(bf16)
-    slot = g * CHIPS + me
-    sent = []
-    for mask in (15, 14, 13, 11, 12, 10, 9, 8, 7, 6, 5, 3, 4, 2, 1):
-        to = flipped(me, [axis for axis in BITS if mask & BITS[axis]])
-        sent.append(
-            push(
-                core_q.at[:, to, other_bit("g", mask & 8)], in_q.at[slot], send.at[mask], recv.at[mask], wide_at(mask)
-            )
-        )
-    to_core[1].wait_recv()
-    core_o[...] = (core_o[...].astype(f32) + go_ref[:, c].astype(f32)).astype(bf16)
-    to_group = push(core_o.at[:, 1 - g], in_o, go_send, go_recv, across("g"))
-    in_q[slot] = core_q[:, me, g]
-    scatter.onward()
-    scatter.last()
-    dxn_ref[0 : dxn_ref.shape[0] // 2] = scatter.finish(0)
-    dxn_ref[dxn_ref.shape[0] // 2 :] = scatter.finish(1)
-    to_group.wait_recv()
-    out_ref[...] = (in_o[...].astype(f32) + core_o[:, g].astype(f32)).astype(bf16)
-    for copy in sent:
         copy.wait_recv()
     for row in range(ROW_TILES):
         sums = [in_q[chip, row].astype(f32) + in_q[CHIPS + chip, row].astype(f32) for chip in range(CHIPS)]
         for which in range(3):
-            qkv_ref[which, row] = jnp.concatenate(
-                [part[:, which * 2 * DH : (which + 1) * 2 * DH] for part in sums], axis=1
-            ).astype(bf16)
-    scatter.drain()
-    for copy in to_core + sent + [to_group]:
+            three_tiles(
+                which * ROW_TILES**2 + row * ROW_TILES,
+                jnp.concatenate([part[:, which * 2 * DH : (which + 1) * 2 * DH] for part in sums], axis=1),
+            )
+    tiles_ref[tiles_ref.shape[0] - 1] = jnp.zeros(tiles_ref.shape[1:], bf16)
+
+    def grad_left(step, carry):
+        grad_copy(lax.rem(me + step, seqs)).wait_send()
+        return carry
+
+    lax.fori_loop(1, seqs, grad_left, 0)
+    gather.drain()
+    scatter3.drain()
+    for copy in strips_sent + to_core + to_near + tiles_sent:
         copy.wait_send()
+
+
+def chip_at(mask):
+    return {axis: 1 - lax.axis_index(axis) for axis in BITS if mask & BITS[axis]}
 
 
 def wide_at(mask):
@@ -1528,36 +1659,69 @@
     return at
 
 
-def share(parts, gq, go):
-    _, rows, width = parts.shape
+def run_middle(
+    lengths, mix, hn, dy, xn, w_in, w_dn, w_qkv, dy_own, hmid, gain_ffn, w_o, qkv, toep, gain, scores, weights, outs, strips
+):
+    seqs, rows, _ = hn.shape
     dma = pltpu.SemaphoreType.DMA
-    part = gq.shape[-2]
+    part = BLK // 32
+    tiles = 4 * ROW_TILES**2 + 3 * ROW_TILES * FF_TILES
+    shapes = [
+        ((seqs, rows, BLK), bf16), ((rows, D), f32), ((rows, D), f32), ((1, D), f32), ((2 * CQ * CK, rows), f32),
+        ((8, rows), f32), ((1, 2 * HP), f32), ((tiles + 1, part, BLK), bf16),
+    ]
+
+    def low(*dims):
+        return pltpu.VMEM(dims, bf16)
+
+    every, heads = low(CHIPS, rows, D), low(CHIPS, rows, 2 * DH)
     return pl.pallas_call(
-        share_body,
-        in_specs=[VMEM] * 3,
-        out_specs=[VMEM] * 3,
-        out_shape=[
-            jax.ShapeDtypeStruct((rows, width), f32),
-            jax.ShapeDtypeStruct((3, ROW_TILES, part, D), bf16),
-            jax.ShapeDtypeStruct((ROW_TILES, part, D), bf16),
-        ],
+        middle_body,
+        in_specs=[SMEM] * 2 + [ANYS] * 3 + [VMEM] * 14,
+        out_specs=[VMEM] * len(shapes),
+        out_shape=[jax.ShapeDtypeStruct(*shape) for shape in shapes],
         scratch_shapes=[
-            pltpu.VMEM((ROW_TILES, CHIPS, 2, part, 6 * DH), bf16), pltpu.VMEM((ROW_TILES, 2, part, D), bf16),
-            pltpu.VMEM((2 * CHIPS, ROW_TILES, part, 6 * DH), bf16), pltpu.VMEM((ROW_TILES, part, D), bf16),
-            dma((2,)), dma((2,)), dma((16,)), dma((16,)), dma, dma,
-        ] + scatter_scratch(rows, width),
-        name="share_gradients",
-        compiler_params=pltpu.CompilerParams(collective_id=5, has_side_effects=True, vmem_limit_bytes=40 * 2**20),
-    )(parts, gq, go)
-
-
-def to_slots_body(slots_ref, vec_ref, out_ref, vecs_ref, local_sems, send, recv, vec_send, vec_recv):
+            pltpu.VMEM((2, rows, CQ * rows), f32), pltpu.VMEM((rows + 8, rows), f32), every, every, low(seqs, rows, 2 * BLK), every, low(rows, D), heads, heads, heads,
+            low(ROW_TILES, 2, CHIPS, 2, part, 2 * BLK), low(2, CHIPS, 2, part, D),
+            low(ROW_TILES, CHIPS, 2, part, 2 * BLK), low(CHIPS, 2, part, D),
+            low(ROW_TILES, CHIPS, part, 2 * BLK), low(CHIPS, part, D),
+            low(seqs, rows, 6 * DH), low(ROW_TILES, 2, CHIPS, 2, part, 6 * DH), low(ROW_TILES, 2, 2, part, D),
+            low(ROW_TILES, CHIPS, 2, part, 6 * DH), low(ROW_TILES, 2, part, D),
+            low(2 * CHIPS, ROW_TILES, part, 6 * DH), low(ROW_TILES, part, D),
+            low(3, rows, D), low(rows, D), low(3, rows, D), dma((1,)), dma((9,)),
+        ] + [dma((8,))] * 4 + [dma((6,))] * 2 + [dma((5,))] * 2 + [dma((9 * CHIPS,))] * 2 + [dma((16,))] * 2
+        + scatter_scratch(rows, D) + [dma((3,))] * 2 + [dma((3, 2))] * 4 + side_sems(),
+        name="middle",
+        compiler_params=pltpu.CompilerParams(collective_id=3, has_side_effects=True, vmem_limit_bytes=63 * 2**20),
+    )(
+        lengths, mix, hn, dy, xn, w_in, w_dn, w_qkv, dy_own, hmid, gain_ffn, w_o,
+        qkv, toep, gain, scores, weights, outs, strips,
+    )
+
+
+def to_slots_body(
+    pick_ref, tiles_ref, vec_ref, inner_ref, w_dn_ref, hmid_ref, out_ref, vecs_ref, layer_ref,
+    slots_ref, parts_ref, local_sems, send, recv, vec_send, vec_recv, *scatter_args,
+):
     devices = lax.axis_size(ALL)
+    own_slots, side = out_ref.shape[:2]
+    part = slots_ref.shape[1]
+
+    def fill(at, carry):
+        slots_ref[at] = tiles_ref[pick_ref[at]]
+        return carry
+
+    lax.fori_loop(0, slots_ref.shape[0], fill, 0)
     me = device_index()
-    local = [
-        pltpu.make_async_copy(slots_ref.at[me], out_ref.at[me], local_sems.at[0]),
-        pltpu.make_async_copy(vec_ref.at[me], vecs_ref.at[me], local_sems.at[1]),
-    ]
+    place = (lax.axis_index("c") * CHIPS + chip_index()) * 2 + lax.axis_index("g")
+    rows = pl.ds(pl.multiple_of(place * part, part), part)
+    local = [pltpu.make_async_copy(vec_ref.at[me], vecs_ref.at[me], local_sems.at[0])]
+    for slot in range(own_slots):
+        local.append(
+            pltpu.make_async_copy(
+                slots_ref.at[me * own_slots + slot], out_ref.at[slot, rows], local_sems.at[1 + slot]
+            )
+        )
     for copy in local:
         copy.start()
     greet_all()
@@ -1567,31 +1731,86 @@
         pltpu.make_async_remote_copy(
             src_ref=vec_ref.at[to], dst_ref=vecs_ref.at[me], send_sem=vec_send, recv_sem=vec_recv, device_id=device_at(to)
         ).start()
-        pltpu.make_async_remote_copy(
-            src_ref=slots_ref.at[to], dst_ref=out_ref.at[me], send_sem=send, recv_sem=recv, device_id=device_at(to)
-        ).start()
+        for slot in range(own_slots):
+            pltpu.make_async_remote_copy(
+                src_ref=slots_ref.at[to * own_slots + slot], dst_ref=out_ref.at[slot, rows],
+                send_sem=send, recv_sem=recv, device_id=device_at(to),
+            ).start()
         return carry
 
     lax.fori_loop(1, devices, push_all, 0)
-    for ref, one, two in ((vecs_ref, vec_send, vec_recv), (out_ref, send, recv)):
-        others = ref.at[pl.ds(0, devices - 1)]
-        pltpu.make_async_copy(others, others, two).wait()
-        pltpu.make_async_copy(others, others, one).wait()
+
+    seqs, length = inner_ref.shape[:2]
+
+    def outputs(at, carry):
+        two = pl.ds(at * 2, 2)
+        made = dot(inner_ref[two].reshape(2 * length, BLK), w_dn_ref[...])
+        parts_ref[two] = made.astype(bf16).reshape(2, length, D)
+        return carry
+
+    lax.fori_loop(0, seqs // 2, outputs, 0)
+    scatter = SideScatter(parts_ref, *scatter_args)
+    scatter.start()
+    scatter.onward()
+    scatter.last()
+    layer_ref[...] = (hmid_ref[...] + scatter.finish()).astype(bf16)
+    scatter.drain()
+    others = vecs_ref.at[pl.ds(0, devices - 1)]
+    pltpu.make_async_copy(others, others, vec_recv).wait()
+    pltpu.make_async_copy(others, others, vec_send).wait()
+    others = out_ref.at[:, pl.ds(0, side - part)]
+    pltpu.make_async_copy(others, others, recv).wait()
+    pltpu.make_async_copy(others, others, send).wait()
     for copy in local:
         copy.wait()
 
 
-def to_slots(slots, vecs):
+def to_slots(pick, tiles, vecs, inner, w_dn, hmid, own_slots):
+    rows = hmid.shape[0]
     dma = pltpu.SemaphoreType.DMA
     return pl.pallas_call(
         to_slots_body,
-        in_specs=[ANYS] * 2,
-        out_specs=[ANYS] * 2,
-        out_shape=[jax.ShapeDtypeStruct(slots.shape, slots.dtype), jax.ShapeDtypeStruct(vecs.shape, vecs.dtype)],
-        scratch_shapes=[dma((2,))] + [dma] * 4,
+        in_specs=[SMEM, VMEM, ANYS] + [VMEM] * 3,
+        out_specs=[ANYS] * 2 + [VMEM],
+        out_shape=[
+            jax.ShapeDtypeStruct((own_slots, BLK, BLK), bf16), jax.ShapeDtypeStruct(vecs.shape, vecs.dtype),
+            jax.ShapeDtypeStruct(hmid.shape, bf16),
+        ],
+        scratch_shapes=[
+            pltpu.VMEM((pick.shape[0],) + tiles.shape[1:], bf16), pltpu.VMEM((CHIPS, rows, D), bf16), dma((1 + own_slots,)),
+        ] + [dma] * 4 + side_scatter_scratch(rows, D),
         name="to_slots",
-        compiler_params=pltpu.CompilerParams(collective_id=6, has_side_effects=True),
-    )(slots, vecs)
+        compiler_params=pltpu.CompilerParams(collective_id=6, has_side_effects=True, vmem_limit_bytes=32 * 2**20),
+    )(pick, tiles, vecs, inner, w_dn, hmid)
+
+
+def update_body(grad_ref, left_ref, right_ref, master_ref, first_ref, second_ref, first_out, second_out, master_out, copy_out):
+    left, right = left_ref[0].astype(bf16), right_ref[0].astype(bf16)
+    rotated = dot(dot_tn(left, grad_ref[0]).astype(bf16), right)
+    first = beta_first * first_ref[0] + (1.0 - beta_first) * rotated
+    second = beta_second * second_ref[0] + (1.0 - beta_second) * rotated * rotated
+    first_out[0] = first
+    second_out[0] = second
+    direction = (first / (jnp.sqrt(second) + eps_adam)).astype(bf16)
+    turned = dot_nt(dot(left, direction).astype(bf16), right)
+    master = master_ref[0]
+    master = master - rate_block * (turned + decay_block * master)
+    master_out[0] = master
+    copy_out[0] = master.astype(bf16)
+
+
+def update(grad, left, right, master, first, second):
+    spec = pl.BlockSpec((1, BLK, BLK), lambda slot: (slot, 0, 0))
+    return pl.pallas_call(
+        update_body,
+        grid=(grad.shape[0],),
+        in_specs=[spec] * 6,
+        out_specs=[spec] * 4,
+        out_shape=[jax.ShapeDtypeStruct(grad.shape, kind) for kind in (f32, f32, f32, bf16)],
+        name="update",
+        compiler_params=pltpu.CompilerParams(vmem_limit_bytes=40 * 2**20),
+        cost_estimate=pl.CostEstimate(flops=43 * 10**8, bytes_accessed=36 * 2**20, transcendentals=10**6),
+    )(grad, left, right, master, first, second)
 
 
 def body_fast(
@@ -1608,8 +1827,7 @@
         [vec_copy.astype(f32), jnp.zeros((1023 - own_vec,), f32), length.astype(f32).reshape(1)]
     ).reshape(8, 128)
     blocks = jnp.concatenate([w.reshape(-1, CHIPS, 2 * DH) for w in (w_query, w_key, w_value)], axis=2)
-    x_all, small_all, w_qkv, w_out_all = dispatch(layer_input, small, jnp.transpose(blocks, (1, 0, 2)), w_out)
-    w_qkv = w_qkv.reshape(D, 6 * DH)
+    small_all = gather_vectors(small)
     small_all = small_all.reshape(fs_size, reps, 1024)
     vector = small_all[:, 0, :own_vec].reshape(-1)
     group_lengths = small_all[:, :, 1023].reshape(-1, 2, 2, 2, reps)
@@ -1635,10 +1853,11 @@
     dy = cotangent.astype(f32) * valid[:, None]
 
     gains = jnp.concatenate([gain_attn[None], gain_ffn[None], jnp.zeros((6, D), f32)], axis=0)
-    xn, qkv, scores, weights, outs, heads, hmid, hn_rows, w_in, w_dn, dy_rows = run_front(
-        group_lengths, mix, x_all, layer_input, gains, w_qkv, toep, gain_pair, w_out_all, w_gate, w_up, w_down, dy.astype(bf16)
+    xn, qkv, scores, weights, outs, heads, hmid, w_qkv, w_out_all, hn_rows, w_in, w_dn, dy_rows = run_front(
+        group_lengths, mix, layer_input, gains, toep, gain_pair, jnp.transpose(blocks, (1, 0, 2)),
+        w_out, w_gate, w_up, w_down, dy.astype(bf16),
     )
-    xn_rows = xn.reshape(CHIPS * seq_len, D)
+    w_qkv = w_qkv.reshape(D, 6 * DH)
     w_in, w_dn = w_in.reshape(D, 2 * BLK), w_dn.reshape(BLK, D)
     strip = BLK // (2 * CHIPS)
     part = strip // 2
@@ -1647,26 +1866,18 @@
     input_float = layer_input.astype(f32)
     input_scale = rms(input_float)
 
-    layer_output, dhmid, grad_gain_ffn, dqkv, theta_sums, mixer_sums, gain_sums, grad_out, ffn_sums = run_middle(
-        group_lengths, mix, hn_rows, w_in, w_dn, dy_rows, dy.astype(bf16), hmid, gain_ffn.reshape(1, D),
+    own_slots = basis_left.shape[0]
+    matches = jnp.arange(own_slots * devices)[:, None] == owners[None, :]
+    tile_count = owners.shape[0]
+    pick = jnp.min(jnp.where(matches, jnp.arange(tile_count, dtype=jnp.int32)[None, :], tile_count), axis=1)
+    inner, dhmid, dxn, grad_gain_ffn, theta_sums, mixer_sums, gain_sums, tiles = run_middle(
+        group_lengths, mix, hn_rows, dy_rows, xn, w_in, w_dn, w_qkv, dy.astype(bf16), hmid, gain_ffn.reshape(1, D),
         w_out_all.reshape(CHIPS, 2 * DH, D), qkv, toep, gain_pair, scores, weights, outs, strips,
-    )
-    dqkv_rows = dqkv.reshape(CHIPS * seq_len, 6 * DH)
-    dxn_parts = dot_nt(dqkv_rows, w_qkv).astype(bf16).reshape(CHIPS, seq_len, D)
-    grad_qkv = dot_tn(xn_rows, dqkv_rows).astype(bf16)
-    dxn, qkv_sums, out_sums = share(
-        dxn_parts,
-        grad_qkv.reshape(ROW_TILES, 2, CHIPS, 2, part, 6 * DH),
-        grad_out.reshape(ROW_TILES, 2, 2, part, D),
     )
     dinput, grad_gain_attn = norm_backward(input_float, input_scale, gain_attn, dxn)
     input_grad = dinput + dhmid
 
-    taps = jnp.asarray(band())
-    theta_sums = theta_sums.reshape(2, seq_len, CQ, seq_len)
-    grad_theta = jnp.stack(
-        [jnp.sum(jnp.where(taps[tap][None, :, None, :], theta_sums, 0.0), axis=(1, 3)) for tap in range(CK)], axis=2
-    )
+    grad_theta = jnp.sum(theta_sums, axis=1)
     grad_mixer = jnp.sum(mixer_sums[:4], axis=1)
     vector_grad = jnp.concatenate(
         [
@@ -1684,37 +1895,18 @@
     pieces = jnp.pad(vector_grad.reshape(fs_size, 1, own_vec), ((0, 0), (0, 0), (0, 1024 - own_vec)))
     pieces = jnp.broadcast_to(pieces, (fs_size, reps, 1024)).reshape(devices, 8, 128)
 
-    own_slots = basis_left.shape[0]
-    slot_total = own_slots * devices
-    sums = jnp.concatenate(
-        [
-            jnp.transpose(qkv_sums.reshape(3, ROW_TILES, part, ROW_TILES, BLK), (0, 1, 3, 2, 4)).reshape(-1, part, BLK),
-            jnp.transpose(out_sums.reshape(ROW_TILES, part, ROW_TILES, BLK), (0, 2, 1, 3)).reshape(-1, part, BLK),
-            ffn_sums,
-        ],
-        axis=0,
+    own_grad, pieces, layer_output = to_slots(
+        pick, tiles, pieces, inner, w_dn, hmid, own_slots
     )
-    matches = (jnp.arange(slot_total)[:, None] == owners[None, :]).astype(bf16)
-    slots = dot(matches, sums.reshape(sums.shape[0], -1)).astype(bf16)
-    slots, pieces = to_slots(slots.reshape(devices, own_slots * part, BLK), pieces)
     vector_total = jnp.sum(pieces, axis=0).reshape(1024)[:own_vec]
-    slots = slots.reshape(2, 2, 2, 2, 2, own_slots, part, BLK)
-    own_grad = jnp.transpose(slots, (5, 3, 4, 1, 2, 0, 6, 7)).reshape(own_slots, BLK, BLK)
-
-    left_low, right_low = basis_left.astype(bf16), basis_right.astype(bf16)
-    rotated = jnp.einsum("sia,sij->saj", left_low, own_grad, preferred_element_type=f32)
-    rotated = jnp.einsum("saj,sjb->sab", rotated.astype(bf16), right_low, preferred_element_type=f32)
-    first_new = beta_first * block_first + (1.0 - beta_first) * rotated
-    second_new = beta_second * block_second + (1.0 - beta_second) * rotated * rotated
-    direction = (first_new / (jnp.sqrt(second_new) + eps_adam)).astype(bf16)
-    turned = jnp.einsum("sia,sab->sib", left_low, direction, preferred_element_type=f32)
-    turned = jnp.einsum("sib,sjb->sij", turned.astype(bf16), right_low, preferred_element_type=f32)
-    master_new = block_master - rate_block * (turned + decay_block * block_master)
+    first_new, second_new, master_new, copy_new = update(
+        own_grad, basis_left, basis_right, block_master, block_first, block_second
+    )
     vec_first_new = beta_first * vec_first + (1.0 - beta_first) * vector_total
     vec_second_new = beta_second * vec_second + (1.0 - beta_second) * vector_total * vector_total
     vec_master_new = vec_master - rate_vector * vec_first_new / (jnp.sqrt(vec_second_new) + eps_adam)
     return (
-        layer_output, input_grad, first_new, second_new, master_new, master_new.astype(bf16),
+        layer_output, input_grad, first_new, second_new, master_new, copy_new,
         vec_first_new, vec_second_new, vec_master_new, vec_master_new.astype(bf16),
     )
 

time: 493 us -> 424 us (0.86)
  matrix products: 36.2 us -> 0 us
  Pallas kernels: 407 us -> 385 us
  local copies, waits for them, and re-layouts: 25.2 us -> 16.7 us
    dot_general x5 -> x0, matrix products: 36.2 us -> none  [the longest x1 13.6 us: body_fast(): jnp.einsum('sib,sjb->sij', turned.astype(bf16), right_low, preferred_elem...]
    pallas_call x5, Pallas kernels: 407 us -> 385 us  [the longest x1 151 us: run_front(): pl.pallas_call(front_body, in_specs=[SMEM, SMEM] + [VMEM] * 4 + [ANYS] *...]
where the time goes in v6:
time: 424 us; the launch traced here: 419 us
  Pallas kernels  385 us (91%)
  local copies, waits for them, and re-layouts  16.7 us (4%)
  other arithmetic  15.4 us (4%)
    pallas_call x1, Pallas kernels, run_front(): pl.pallas_call(front_body, in_specs=[SMEM, SMEM] + [VMEM] * 4 + [ANYS] *...  151 us
    pallas_call x1, Pallas kernels, run_middle(): pl.pallas_call(middle_body, in_specs=[SMEM] * 2 + [ANYS] * 3 + [VMEM] * 1...  149 us
    pallas_call x1, Pallas kernels, to_slots(): pl.pallas_call(to_slots_body, in_specs=[SMEM, VMEM, ANYS] + [VMEM] * 3, o...  61.8 us
    pallas_call x1, Pallas kernels, update(): pl.pallas_call(update_body, grid=(grad.shape[0],), in_specs=[spec] * 6, o...  12 us
    pallas_call x1, Pallas kernels, gather_vectors(): pl.pallas_call(vectors_body, in_specs=[VMEM], out_specs=VMEM, out_shape=j...  10.5 us

profile of v6, /device:TPU:11, one launch (start us, length us, event | category | flops | bytes accessed | tf_op | source)
XLA Modules:
  0.0 418.7 jit_solution(4163527938498464481)
XLA Ops:
  1.4 0.7 convert_element_type.43
  2.0 0.7 maximum_bitcast_fusion.1.vec_ref
  2.7 10.5 %gather_vectors.1 = f32[32,8,128]{2,1,0:T(8,128)} custom-call(f32[8,128]{1,0:T(8,128)} %maximum_bitcast_fusion.1.vec_ref), custom_call_target="tpu_custom_call" | custom-call | tf_op jit(solution)/shard_map/gather_vectors/pallas_call | solution.py:974
  13.2 1.0 reshape.275
  16.0 3.7 select_convert_fusion.toep_ref
  19.8 0.6 pad.8
  20.4 0.7 slice.68
  21.1 0.6 reshape.276.mix_ref
  22.2 0.6 convert_element_type.48.len_ref
  23.0 0.7 maximum_maximum_fusion.gains_ref
  23.7 0.9 multiply_convert_fusion.dy_ref.dy_own_ref
  25.0 0.3 reshape.281
  25.4 0.3 reshape.282
  25.8 1.3 maximum_bitcast_fusion.blocks_ref
  27.1 151.2 %front.1 = (bf16[8,128,1536]{2,1,0:T(8,128)(2,1)}, bf16[8,128,768]{2,1,0:T(8,128)(2,1)}, bf16[8,2,128,128]{3,2,1,0:T(8,128)(2,1)}, f32[8,2,128,128]{3,2,1,0:T(8,...) custom-call(s32[8]{0:T(128)} %convert_element_type.48.len_ref, ...), custom_call_target="tpu_custom_call" | custom-call | tf_op jit(solution)/shard_map/front/pallas_call | solution.py:1281
  178.3 1.3 copy.70
  179.6 1.0 copy.72.strips_ref
  180.6 149.0 %middle.1 = (bf16[8,128,512]{2,1,0:T(8,128)(2,1)}, f32[128,1536]{1,0:T(8,128)}, f32[128,1536]{1,0:T(8,128)}, f32[1,1536]{1,0:T(1,128)}, f32[132,128]{1,0:T(8,128...) custom-call(s32[8]{0:T(128)} %convert_element_type.48.len_ref, f32[4]{0:T(128)} %reshape.276.mix_ref, ...), custom_call_target="tpu_custom_call" | custom-call | tf_op jit(solution)/shard_map/middle/pallas_call | solution.py:1678
  329.7 1.1 reduce_sum.56
  331.1 0.8 reshape.290
  332.0 0.8 slice_reduce_fusion
  333.1 1.2 fusion.8
  334.2 1.6 fusion.4
  335.8 0.7 reduce.11
  337.0 1.6 copy-done.4
  338.7 1.2 copy-done.5
  339.9 61.8 %to_slots.1 = (bf16[4,512,512]{2,1,0:T(8,128)(2,1)S(1)}, f32[32,8,128]{2,1,0:T(8,128)S(1)}, bf16[128,1536]{1,0:T(8,128)(2,1)S(1)}) custom-call(s32[128]{0:T(128)S(1)} %select_reduce_fusion.pick_ref, bf16[109,16,512]{2,1,0:T(8,128)(2,1)S(1)} %copy-done.4, f32[32,8,128]{2,1,0:T(8,128)S(1)} %reshape.293.vec_ref, bf16[8,128,512]{2,1,0:T(8,128)(2,1)S(1)} %copy-done.5, ...), custom_call_target="tpu_custom_call" | custom-call | tf_op jit(solution)/shard_map/to_slots/pallas_call | solution.py:1771
  401.8 2.2 copy-done.2
  404.0 12.0 %update.1 = (f32[4,512,512]{2,1,0:T(8,128)}, f32[4,512,512]{2,1,0:T(8,128)}, f32[4,512,512]{2,1,0:T(8,128)}, bf16[4,512,512]{2,1,0:T(8,128)(2,1)}) custom-call(bf16[4,512,512]{2,1,0:T(8,128)(2,1)S(1)} %get-tuple-element.60.grad_ref, f32[4,512,512]{2,1,0:T(8,128)S(1)} %copy-done.1, f32[4,512,512]{2,1,0:T(8,128)S(1)} %copy-done.2, f32[4,512,512]{2,1,0:T(8,128)} %master_ref.1, ...), custom_call_target="tpu_custom_call" | custom-call | flops 4300000256 | bytes 37748736 | tf_op jit(solution)/shard_map/update/pallas_call | solution.py:1804
  416.1 1.2 fusion.7
  417.3 0.6 fusion.21
  417.9 0.7 copy.114
  (116 shorter events, 4.1 us)
Async XLA Ops:
  0.6 23.0 %copy-start.9 = (bf16[128,1536]{1,0:T(8,128)(2,1)S(1)}, bf16[128,1536]{1,0:T(8,128)(2,1)}, u32[]{:S(2)}) copy-start(bf16[128,1536]{1,0:T(8,128)(2,1)} %param.22) | copy-start | bytes 1179652
  13.2 11.3 %copy-start.10 = (bf16[96,1536]{1,0:T(8,128)(2,1)S(1)}, bf16[96,1536]{1,0:T(8,128)(2,1)}, u32[]{:S(2)}) copy-start(bf16[96,1536]{1,0:T(8,128)(2,1)} %param.23) | copy-start | bytes 884740
  15.6 9.3 %copy-start.11 = (bf16[96,1536]{1,0:T(8,128)(2,1)S(1)}, bf16[96,1536]{1,0:T(8,128)(2,1)}, u32[]{:S(2)}) copy-start(bf16[96,1536]{1,0:T(8,128)(2,1)} %param.24) | copy-start | bytes 884740
  16.0 9.3 %copy-start.12 = (bf16[96,1536]{1,0:T(8,128)(2,1)S(1)}, bf16[96,1536]{1,0:T(8,128)(2,1)}, u32[]{:S(2)}) copy-start(bf16[96,1536]{1,0:T(8,128)(2,1)} %param.25) | copy-start | bytes 884740
  22.9 4.2 %copy-start.13 = (f32[1,1536]{1,0:T(1,128)}, f32[1,1536]{1,0:T(1,128)S(1)}, u32[]{:S(2)}) copy-start(f32[1,1536]{1,0:T(1,128)S(1)} %broadcast_in_dim.293.gain_ffn_ref) | copy-start | bytes 18436
  180.6 156.3 %copy-start.17 = (s32[108]{0:T(128)S(1)}, s32[108]{0:T(128)}, u32[]{:S(2)}) copy-start(s32[108]{0:T(128)} %param.31) | copy-start | bytes 1300
  180.6 156.4 %copy-start.3 = (f32[128,1536]{1,0:T(8,128)S(1)}, f32[128,1536]{1,0:T(8,128)}, u32[]{:S(2)}) copy-start(f32[128,1536]{1,0:T(8,128)} %get-tuple-element.44.hmid_ref) | copy-start | bytes 2359300
  329.7 7.4 %copy-start = (bf16[2,256,1536]{2,1,0:T(8,128)(2,1)S(1)}, bf16[2,256,1536]{2,1,0:T(8,128)(2,1)}, u32[]{:S(2)}) copy-start(bf16[2,256,1536]{2,1,0:T(8,128)(2,1)} %get-tuple-element.42) | copy-start | bytes 4718596
  336.9 64.9 %copy-start.1 = (f32[4,512,512]{2,1,0:T(8,128)S(1)}, f32[4,512,512]{2,1,0:T(8,128)}, u32[]{:S(2)}) copy-start(f32[4,512,512]{2,1,0:T(8,128)} %left_ref.1) | copy-start | bytes 12582916
  337.0 1.6 copy-start.4
  338.6 1.3 copy-start.5
  401.8 2.2 copy-start.2
  404.0 12.1 %copy-start.6 = (bf16[128,1536]{1,0:T(8,128)(2,1)S(1)}, bf16[128,1536]{1,0:T(8,128)(2,1)}, u32[]{:S(2)}) copy-start(bf16[128,1536]{1,0:T(8,128)(2,1)} %x_ref.1) | copy-start | bytes 1179652
  404.0 12.1 %copy-start.7 = (f32[128,1536]{1,0:T(8,128)S(1)}, f32[128,1536]{1,0:T(8,128)}, u32[]{:S(2)}) copy-start(f32[128,1536]{1,0:T(8,128)} %get-tuple-element.52) | copy-start | bytes 2359300
  404.0 12.1 %copy-start.8 = (f32[128,1536]{1,0:T(8,128)S(1)}, f32[128,1536]{1,0:T(8,128)}, u32[]{:S(2)}) copy-start(f32[128,1536]{1,0:T(8,128)} %get-tuple-element.59) | copy-start | bytes 2359300
  404.0 13.3 %copy-start.14 = (f32[356]{0:T(512)S(1)}, f32[356]{0:T(512)}, u32[]{:S(2)}) copy-start(f32[356]{0:T(512)} %param.37) | copy-start | bytes 4276
  404.0 13.3 %copy-start.15 = (f32[356]{0:T(512)S(1)}, f32[356]{0:T(512)}, u32[]{:S(2)}) copy-start(f32[356]{0:T(512)} %param.39) | copy-start | bytes 4276
  404.0 13.3 %copy-start.16 = (f32[356]{0:T(512)S(1)}, f32[356]{0:T(512)}, u32[]{:S(2)}) copy-start(f32[356]{0:T(512)} %param.38) | copy-start | bytes 4276

commit v7 on v6

--- a/solution.py
+++ b/solution.py
@@ -1,3 +1,4 @@
+import functools
 import math
 
 import jax
@@ -949,37 +950,34 @@
 VMEM = pl.BlockSpec(memory_space=pltpu.VMEM)
 
 
-def vectors_body(vec_ref, vecs_ref, send, recv, local_sem):
-    devices = lax.axis_size(ALL)
-    me = device_index()
-    local = pltpu.make_async_copy(vec_ref, vecs_ref.at[me], local_sem)
-    local.start()
-    greet_all()
-
-    def push_vec(step, carry):
-        pltpu.make_async_remote_copy(
-            src_ref=vec_ref, dst_ref=vecs_ref.at[me], send_sem=send, recv_sem=recv,
-            device_id=device_at(lax.rem(me + step, devices)),
-        ).start()
-        return carry
-
-    lax.fori_loop(1, devices, push_vec, 0)
-    others = vecs_ref.at[pl.ds(0, devices - 1)]
-    pltpu.make_async_copy(others, others, recv).wait()
-    pltpu.make_async_copy(others, others, send).wait()
-    local.wait()
-
-
-def gather_vectors(vec):
-    return pl.pallas_call(
-        vectors_body,
-        in_specs=[VMEM],
-        out_specs=VMEM,
-        out_shape=jax.ShapeDtypeStruct((lax.axis_size(ALL),) + vec.shape, vec.dtype),
-        scratch_shapes=[pltpu.SemaphoreType.DMA] * 3,
-        name="gather_vectors",
-        compiler_params=pltpu.CompilerParams(collective_id=1, has_side_effects=True),
-    )(vec)
+HEAD_ROW, FFN_ROW, THETA_ROW, MIX_ROW, VEC_ROWS = 12, 28, 40, 56, 64
+SHARD_ROWS = 16
+
+
+def vector_row(at):
+    for begin, row, width in (
+        (3 * D + H * CQ * CK, MIX_ROW, 4), (3 * D, THETA_ROW, CQ * CK), (2 * D, FFN_ROW, 128), (D, HEAD_ROW, DH), (0, 0, 128)
+    ):
+        if at >= begin:
+            return row + (at - begin) // width
+
+
+def vector_rows(own_vec, shards):
+    return [min(vector_row(shard * own_vec), VEC_ROWS - SHARD_ROWS) // 8 * 8 for shard in range(shards)]
+
+
+def rows_of_vector(flat):
+    conv_end = 3 * D + H * CQ * CK
+    return jnp.concatenate(
+        [
+            flat[:D].reshape(-1, 128),
+            jnp.pad(flat[D : 2 * D].reshape(H, DH), ((0, 0), (0, 128 - DH))),
+            flat[2 * D : 3 * D].reshape(-1, 128),
+            jnp.pad(flat[3 * D : conv_end].reshape(H, CQ * CK), ((0, 0), (0, 128 - CQ * CK))),
+            jnp.pad(flat[conv_end : conv_end + 2 * H].reshape(CHIPS, 4), ((0, 0), (0, 124))),
+        ],
+        axis=0,
+    )
 
 
 def source_at(mask):
@@ -987,9 +985,9 @@
 
 
 def front_body(
-    len_ref, mix_ref, x_ref, gains_ref, toep_ref, gain_ref, blocks_ref, w_out_ref, w_gate_ref, w_up_ref, w_down_ref, dy_ref,
-    xn_ref, qkv_ref, s_ref, p_ref, o_ref, heads_ref, hmid_ref, wq_ref, wo_ref, hn_all_ref, w_in_ref, w_dn_ref, dy_all_ref,
-    x_all_ref, pad_ref, out_heads, hn_ref, passing, local_sems, q_send, q_recv, q_core_send, q_core_recv,
+    first_rows, length_ref, vec_ref, x_ref, w_query_ref, w_key_ref, w_value_ref, cot_ref,
+    w_out_ref, w_gate_ref, w_up_ref, w_down_ref, dy_ref, len_ref, mix_ref, gains_ref, toep_ref, gain_ref, xn_ref, qkv_ref, s_ref, p_ref, o_ref, heads_ref, hmid_ref, wq_ref, wo_ref, hn_all_ref, w_in_ref, w_dn_ref, dy_all_ref,
+    blocks_ref, own_len_ref, vecs_ref, full_ref, x_all_ref, pad_ref, out_heads, hn_ref, passing, vec_send, vec_recv, len_send, len_recv, local_sems, q_send, q_recv, q_core_send, q_core_recv,
     o_send, o_recv, o_side_send, o_side_recv, o_core_send, o_core_recv, d_send, d_recv,
     w_send, w_recv, u_send, u_recv, core_send, core_recv, head_send, head_recv, *hops,
 ):
@@ -1008,13 +1006,17 @@
         return (y * 2 + other_bit("a", mask & 2)) * 2 + other_bit("b", mask & 1)
 
     local = [
-        pltpu.make_async_copy(blocks_ref.at[me], wq_ref.at[mine], local_sems.at[0]),
         pltpu.make_async_copy(w_out_ref, wo_ref.at[mine], local_sems.at[1]),
         pltpu.make_async_copy(w_gate_ref.at[:, columns(me)], w_in_ref.at[mine, :, low], local_sems.at[2]),
         pltpu.make_async_copy(w_up_ref.at[:, columns(me)], w_in_ref.at[mine, :, high], local_sems.at[3]),
     ]
     down_local = pltpu.make_async_copy(w_down_ref, w_dn_ref.at[c], local_sems.at[4])
-    for copy in local:
+    own_len_ref[...] = jnp.full(own_len_ref.shape, length_ref[0].astype(f32), f32)
+    own_small = [
+        pltpu.make_async_copy(vec_ref, vecs_ref.at[mine], local_sems.at[5]),
+        pltpu.make_async_copy(own_len_ref, len_ref.at[me], local_sems.at[6]),
+    ]
+    for copy in local + own_small:
         copy.start()
 
     @pl.when(g == y)
@@ -1027,7 +1029,29 @@
     side = SideGather(dy_ref, dy_all_ref, *hops[7:14])
     gather = Gather(hn_ref, hn_all_ref, *hops[14:])
 
+    def push_vec(step, carry):
+        to = lax.rem(mine + step, 16)
+        pltpu.make_async_remote_copy(
+            src_ref=vec_ref, dst_ref=vecs_ref.at[mine], send_sem=vec_send, recv_sem=vec_recv,
+            device_id={
+                "g": lax.div(to, 8), "a": lax.rem(lax.div(to, 4), 2), "b": lax.rem(lax.div(to, 2), 2), "c": lax.rem(to, 2)
+            },
+        ).start()
+        return carry
+
+    lax.fori_loop(1, 16, push_vec, 0)
+    lengths_sent = [
+        push(own_len_ref, len_ref.at[me], len_send.at[mask], len_recv.at[mask], chip_at(mask)) for mask in range(1, 8)
+    ]
+
     first.start()
+    for chip in range(CHIPS):
+        cols = slice(chip * 2 * DH, (chip + 1) * 2 * DH)
+        blocks_ref[chip] = jnp.concatenate([w_query_ref[:, cols], w_key_ref[:, cols], w_value_ref[:, cols]], axis=1)
+    wq_ref[mine] = blocks_ref[me]
+    valid = lax.broadcasted_iota(jnp.int32, cot_ref.shape, 0) < length_ref[0]
+    dy_ref[...] = jnp.where(valid, cot_ref[...].astype(f32), 0.0).astype(bf16)
+
     for mask in order:
         sent[mask] = push(blocks_ref.at[block_to(mask)], wq_ref.at[mine], q_send.at[mask], q_recv.at[mask], group_at(mask))
 
@@ -1052,8 +1076,8 @@
         if mask in (2, 4, 6):
             lines[mask + 1] = push(piece, piece, o_send.at[mask + 1], o_recv.at[mask + 1], across("b"))
 
-    def out_to_core():
-        for mask in (2, 4, 6, 1, 3, 5, 7):
+    def out_to_core(masks):
+        for mask in masks:
             o_side[mask].wait_recv()
             block = wo_ref.at[shard[mask]]
             o_core.append(push(block, block, o_core_send.at[mask], o_core_recv.at[mask], across("c")))
@@ -1122,25 +1146,47 @@
         block = w_in_ref.at[shard[mask]]
         relayed.append(push(block, block, core_send.at[mask], core_recv.at[mask], across("c")))
 
-    start_lines()
-    local[0].wait()
+    side.start()
     relayed.append(push(wq_ref.at[mine], wq_ref.at[mine], q_core_send.at[0], q_core_recv.at[0], across("c")))
     first.onward()
+    start_lines()
+
+    for copy in own_small:
+        copy.wait()
+    others = vecs_ref.at[pl.ds(0, 15)]
+    pltpu.make_async_copy(others, others, vec_recv).wait()
+    full_ref[...] = jnp.zeros_like(full_ref)
+    for at, row in enumerate(first_rows):
+        full_ref[row : row + SHARD_ROWS, :] += vecs_ref[at]
+    gains_ref[...] = jnp.zeros_like(gains_ref)
+    for row in range(D // 128):
+        gains_ref[0:1, row * 128 : (row + 1) * 128] = full_ref[row : row + 1, :]
+        gains_ref[1:2, row * 128 : (row + 1) * 128] = full_ref[FFN_ROW + row : FFN_ROW + row + 1, :]
+    mix_ref[...] = full_ref[pl.ds(MIX_ROW + me, 1), :]
+    query_at = lax.broadcasted_iota(jnp.int32, (rows, rows), 0)
+    key_at = lax.broadcasted_iota(jnp.int32, (rows, rows), 1)
+    key_float = key_at.astype(f32)
+    tap_at = query_at - key_at + CK // 2
+    for head in range(2):
+        gain_ref[:, head * HP : (head + 1) * HP] = full_ref[pl.ds(HEAD_ROW + 2 * me + head, 1), :]
+        theta = full_ref[pl.ds(THETA_ROW + 2 * me + head, 1), :]
+        for lag in range(CQ):
+            band_values = jnp.zeros((rows, rows), f32)
+            for tap in range(CK):
+                at = lag * CK + tap
+                band_values = jnp.where(tap_at == tap, theta[:, at : at + 1], band_values)
+            toep_ref[head, lag * rows : (lag + 1) * rows, :] = band_values.astype(bf16)
+
+    side.onward()
+    first.last()
+    side.last()
     down_start()
-    for mask in (2, 4, 6):
-        to_side(mask)
-    to_side(1)
-    relay_qkv(4)
-    relay_qkv(6)
-    first.last()
-    send_columns((4, 6, 5, 7))
-    for mask in (5, 7, 2, 1, 3):
+    for mask in order:
         relay_qkv(mask)
-    side.start()
+    send_columns((2, 1, 3, 4, 6, 5, 7))
     first.finish()
-    for copy in relayed:
+    for copy in relayed + lengths_sent:
         copy.wait_recv()
-    send_columns((2, 1, 3))
     qkv_relayed = relayed[:]
     del relayed[:]
 
@@ -1161,16 +1207,12 @@
         return carry
 
     project(0, 0)
-    for mask in (3, 5, 7):
+    for mask in (2, 4, 6, 1):
         to_side(mask)
-    down_pass()
     project(1, 0)
-    side.onward()
-    for copy in local[1:]:
+    for copy in local:
         copy.wait()
     relayed.append(push(w_in_ref.at[mine], w_in_ref.at[mine], core_send.at[0], core_recv.at[0], across("c")))
-    query_at = lax.broadcasted_iota(jnp.int32, (rows, rows), 0)
-    key_at = lax.broadcasted_iota(jnp.int32, (rows, rows), 1)
 
     def head_copy(seq):
         return pltpu.make_async_remote_copy(
@@ -1180,7 +1222,7 @@
 
     def attend(step, carry):
         seq = lax.rem(me + step, seqs)
-        keep = (key_at <= query_at) & (key_at < len_ref[seq])
+        keep = (key_at <= query_at) & (key_float < len_ref[seq, 0:1, :])
         weights, made = [], []
         for head in range(2):
             query = qkv_ref[seq, :, head * HP : (head + 1) * HP]
@@ -1197,7 +1239,7 @@
             p_ref[seq, head] = weight
             weights.append(weight)
         for head in range(2):
-            mixed = mix_ref[2 * head] * weights[0] + mix_ref[2 * head + 1] * weights[1]
+            mixed = mix_ref[:, 2 * head : 2 * head + 1] * weights[0] + mix_ref[:, 2 * head + 1 : 2 * head + 2] * weights[1]
             value = qkv_ref[seq, :, (4 + head) * HP : (5 + head) * HP]
             out = dot(mixed.astype(bf16), value)
             o_ref[seq, :, head * HP : (head + 1) * HP] = out
@@ -1211,9 +1253,14 @@
 
         return carry
 
-    lax.fori_loop(0, 4, attend, 0)
-    out_to_core()
-    lax.fori_loop(4, seqs, attend, 0)
+    lax.fori_loop(0, 3, attend, 0)
+    for mask in (3, 5, 7):
+        to_side(mask)
+    down_pass()
+    lax.fori_loop(3, 6, attend, 0)
+    out_to_core((2, 4, 6))
+    lax.fori_loop(6, seqs, attend, 0)
+    out_to_core((1, 3, 5, 7))
     heads_ref[me] = out_heads[me]
     for copy in o_core:
         copy.wait_recv()
@@ -1238,7 +1285,6 @@
     hmid = hmid_ref[...]
     hn_ref[...] = (hmid * rms(hmid) * gains_ref[1:2, :]).astype(bf16)
     gather.start()
-    side.last()
     for mask in (4, 6):
         relay(mask)
     gather.onward()
@@ -1265,31 +1311,33 @@
     for copies in (sent, lines, o_side, gate, up):
         for copy in copies.values():
             copy.wait_send()
-    for copy in qkv_relayed + relayed + o_core:
+    pltpu.make_async_copy(others, others, vec_send).wait()
+    for copy in qkv_relayed + relayed + o_core + lengths_sent:
         copy.wait_send()
 
 
-def run_front(lengths, mix, x, gains, toep, gain, blocks, w_out, w_gate, w_up, w_down, dy):
+def run_front(first_rows, length, vec, x, w_query, w_key, w_value, cotangent, w_out, w_gate, w_up, w_down):
     rows = x.shape[0]
     dma = pltpu.SemaphoreType.DMA
     shapes = [
+        (x.shape, bf16), ((CHIPS, 8, 128), f32), ((1, 128), f32), ((8, D), f32), ((2, CQ * rows, rows), bf16), ((1, 2 * HP), f32),
         ((CHIPS, rows, D), bf16), ((CHIPS, rows, 6 * HP), bf16), ((CHIPS, 2, rows, rows), bf16), ((CHIPS, 2, rows, rows), f32),
         ((CHIPS, rows, 2 * HP), f32), ((CHIPS, rows, 2 * DH), bf16), ((rows, D), f32),
-        ((16,) + blocks.shape[1:], bf16), ((16,) + w_out.shape, bf16), ((CHIPS, rows, D), bf16),
+        ((16, w_query.shape[0], 6 * DH), bf16), ((16,) + w_out.shape, bf16), ((CHIPS, rows, D), bf16),
         ((16, w_gate.shape[0], 2 * BLK), bf16), ((2,) + w_down.shape, bf16), ((CHIPS, rows, D), bf16),
     ]
     return pl.pallas_call(
-        front_body,
-        in_specs=[SMEM, SMEM] + [VMEM] * 4 + [ANYS] * 6,
-        out_specs=[VMEM] * 9 + [ANYS] * 4,
+        functools.partial(front_body, first_rows),
+        in_specs=[SMEM] + [VMEM] * 6 + [ANYS] * 4,
+        out_specs=[VMEM] * 15 + [ANYS] * 4,
         out_shape=[jax.ShapeDtypeStruct(*shape) for shape in shapes],
         scratch_shapes=[
-            pltpu.VMEM((CHIPS, rows, D), bf16), pltpu.VMEM((rows + 8, rows), f32), pltpu.VMEM((CHIPS, rows, 2 * DH), bf16),
-            pltpu.VMEM((rows, D), bf16), pltpu.VMEM((w_down.shape[0] // 2, D), bf16), dma((5,)),
+            pltpu.VMEM((CHIPS, w_query.shape[0], 6 * DH), bf16), pltpu.VMEM((8, 128), f32), pltpu.VMEM((16,) + vec.shape, f32), pltpu.VMEM((VEC_ROWS, 128), f32), pltpu.VMEM((CHIPS, rows, D), bf16), pltpu.VMEM((rows + 8, rows), f32), pltpu.VMEM((CHIPS, rows, 2 * DH), bf16),
+            pltpu.VMEM((rows, D), bf16), pltpu.VMEM((w_down.shape[0] // 2, D), bf16), dma, dma, dma((8,)), dma((8,)), dma((7,)),
         ] + [dma((8,))] * 10 + [dma((4,))] * 2 + [dma((8,))] * 8 + hop_sems() + side_sems() + hop_sems(),
         name="front",
         compiler_params=pltpu.CompilerParams(collective_id=2, has_side_effects=True, vmem_limit_bytes=56 * 2**20),
-    )(lengths, mix, x, gains, toep, gain, blocks, w_out, w_gate, w_up, w_down, dy)
+    )(length, vec, x, w_query, w_key, w_value, cotangent, w_out, w_gate, w_up, w_down)
 
 
 def middle_body(
@@ -1819,44 +1867,22 @@
 ):
     chip = chip_index()
     seq_len = layer_input.shape[0]
-    length = lengths[0]
     own_vec = vec_copy.shape[0]
     devices, fs_size, reps = lax.axis_size(ALL), lax.axis_size(FS), lax.axis_size("y")
 
-    small = jnp.concatenate(
-        [vec_copy.astype(f32), jnp.zeros((1023 - own_vec,), f32), length.astype(f32).reshape(1)]
-    ).reshape(8, 128)
-    blocks = jnp.concatenate([w.reshape(-1, CHIPS, 2 * DH) for w in (w_query, w_key, w_value)], axis=2)
-    small_all = gather_vectors(small)
-    small_all = small_all.reshape(fs_size, reps, 1024)
-    vector = small_all[:, 0, :own_vec].reshape(-1)
-    group_lengths = small_all[:, :, 1023].reshape(-1, 2, 2, 2, reps)
-    group_lengths = lax.dynamic_index_in_dim(group_lengths, lax.axis_index("g"), 0, keepdims=False)
-    group_lengths = lax.dynamic_index_in_dim(group_lengths, lax.axis_index("c"), 2, keepdims=False)
-    group_lengths = jnp.transpose(group_lengths, (2, 0, 1)).reshape(CHIPS).astype(jnp.int32)
-    gain_attn, gain_head, gain_ffn = vector[:D], vector[D : 2 * D], vector[2 * D : 3 * D]
-    conv_end = 3 * D + H * CQ * CK
-    theta = lax.dynamic_slice_in_dim(vector[3 * D : conv_end].reshape(H, CQ, CK), chip * 2, 2, 0)
-    mixer = lax.dynamic_slice_in_dim(vector[conv_end : conv_end + 2 * H].reshape(H, 2), chip * 2, 2, 0)
-    mix = mixer.reshape(4)
-    gain_pair = jnp.pad(
-        lax.dynamic_slice_in_dim(gain_head.reshape(H, DH), chip * 2, 2, 0), ((0, 0), (0, HP - DH))
-    ).reshape(1, 2 * HP)
-    toep = jnp.zeros((2, CQ, seq_len, seq_len), f32)
-    offset = (
-        jnp.arange(seq_len, dtype=jnp.int32)[:, None] - jnp.arange(seq_len, dtype=jnp.int32)[None, :] + CK // 2
+    fs_index = ((lax.axis_index("g") * 2 + lax.axis_index("a")) * 2 + lax.axis_index("b")) * 2 + lax.axis_index("c")
+    first_rows = vector_rows(own_vec, fs_size)
+    flat = lax.dynamic_update_slice_in_dim(jnp.zeros((fs_size * own_vec,), f32), vec_copy.astype(f32), fs_index * own_vec, 0)
+    first = lax.dynamic_index_in_dim(jnp.array(first_rows, jnp.int32), fs_index, 0, keepdims=False)
+    vec = lax.dynamic_slice_in_dim(rows_of_vector(flat), first, SHARD_ROWS, 0)
+
+    (
+        dy, group_lengths, mix, gains, toep, gain_pair, xn, qkv, scores, weights, outs, heads, hmid, w_qkv, w_out_all,
+        hn_rows, w_in, w_dn, dy_rows,
+    ) = run_front(
+        first_rows, lengths, vec, layer_input, w_query, w_key, w_value, cotangent, w_out, w_gate, w_up, w_down
     )
-    for tap in range(CK):
-        toep = jnp.where(offset[None, None] == tap, theta[:, :, tap][:, :, None, None], toep)
-    toep = toep.astype(bf16).reshape(2, CQ * seq_len, seq_len)
-    valid = (jnp.arange(seq_len) < length).astype(f32)
-    dy = cotangent.astype(f32) * valid[:, None]
-
-    gains = jnp.concatenate([gain_attn[None], gain_ffn[None], jnp.zeros((6, D), f32)], axis=0)
-    xn, qkv, scores, weights, outs, heads, hmid, w_qkv, w_out_all, hn_rows, w_in, w_dn, dy_rows = run_front(
-        group_lengths, mix, layer_input, gains, toep, gain_pair, jnp.transpose(blocks, (1, 0, 2)),
-        w_out, w_gate, w_up, w_down, dy.astype(bf16),
-    )
+    gain_attn = gains[0]
     w_qkv = w_qkv.reshape(D, 6 * DH)
     w_in, w_dn = w_in.reshape(D, 2 * BLK), w_dn.reshape(BLK, D)
     strip = BLK // (2 * CHIPS)
@@ -1871,7 +1897,7 @@
     tile_count = owners.shape[0]
     pick = jnp.min(jnp.where(matches, jnp.arange(tile_count, dtype=jnp.int32)[None, :], tile_count), axis=1)
     inner, dhmid, dxn, grad_gain_ffn, theta_sums, mixer_sums, gain_sums, tiles = run_middle(
-        group_lengths, mix, hn_rows, dy_rows, xn, w_in, w_dn, w_qkv, dy.astype(bf16), hmid, gain_ffn.reshape(1, D),
+        group_lengths[:, 0, 0].astype(jnp.int32), mix[0, :4], hn_rows, dy_rows, xn, w_in, w_dn, w_qkv, dy, hmid, gains[1:2],
         w_out_all.reshape(CHIPS, 2 * DH, D), qkv, toep, gain_pair, scores, weights, outs, strips,
     )
     dinput, grad_gain_attn = norm_backward(input_float, input_scale, gain_attn, dxn)

time: 424 us -> 397 us (0.936)
  Pallas kernels: 385 us -> 364 us
  other arithmetic: 15.4 us -> 9.58 us
    pallas_call x2 -> x1, Pallas kernels: 162 us -> 141 us  [run_front(): pl.pallas_call(functools.partial(front_body, first_rows), in_specs=[SMEM]...]
where the time goes in v7:
time: 397 us; the launch traced here: 392 us
  Pallas kernels  364 us (92%)
  local copies, waits for them, and re-layouts  15 us (4%)
  other arithmetic  9.58 us (2%)
    pallas_call x1, Pallas kernels, run_middle(): pl.pallas_call(middle_body, in_specs=[SMEM] * 2 + [ANYS] * 3 + [VMEM] * 1...  149 us
    pallas_call x1, Pallas kernels, run_front(): pl.pallas_call(functools.partial(front_body, first_rows), in_specs=[SMEM]...  141 us
    pallas_call x1, Pallas kernels, to_slots(): pl.pallas_call(to_slots_body, in_specs=[SMEM, VMEM, ANYS] + [VMEM] * 3, o...  61.5 us
    pallas_call x1, Pallas kernels, update(): pl.pallas_call(update_body, grid=(grad.shape[0],), in_specs=[spec] * 6, o...  12 us

profile of v7, /device:TPU:11, one launch (start us, length us, event | category | flops | bytes accessed | tf_op | source)
XLA Modules:
  0.0 391.9 jit_solution(16975319369085886446)
XLA Ops:
  0.7 0.8 convert_dynamic-update-slice_fusion
  1.6 0.1 reshape.96
  1.8 0.2 concatenate.6
  2.1 1.2 dynamic_slice.7
  5.2 0.6 constant_dynamic-slice_fusion.vec_ref
  6.5 141.3 %front.1 = (bf16[128,1536]{1,0:T(8,128)(2,1)}, f32[8,8,128]{2,1,0:T(8,128)}, f32[1,128]{1,0:T(1,128)}, f32[8,1536]{1,0:T(8,128)}, bf16[2,768,128]{2,1,0:T(8,128)...) custom-call(s32[1]{0:T(128)S(6)} %copy.42.length_ref, ...), custom_call_target="tpu_custom_call" | custom-call | tf_op jit(solution)/shard_map/front/pallas_call | solution.py:1329
  147.9 1.3 copy.34
  149.2 1.0 copy.36.strips_ref
  150.2 1.5 slice_reduce_fusion
  151.7 1.5 convert_reduce_fusion.len_ref
  153.2 1.1 slice_bitcast_fusion.2.mix_ref
  154.3 149.0 %middle.1 = (bf16[8,128,512]{2,1,0:T(8,128)(2,1)}, f32[128,1536]{1,0:T(8,128)}, f32[128,1536]{1,0:T(8,128)}, f32[1,1536]{1,0:T(1,128)}, f32[132,128]{1,0:T(8,128...) custom-call(s32[8]{0:T(128)} %convert_reduce_fusion.len_ref, f32[4]{0:T(128)} %slice_bitcast_fusion.2.mix_ref, ...), custom_call_target="tpu_custom_call" | custom-call | tf_op jit(solution)/shard_map/middle/pallas_call | solution.py:1726
  303.4 1.1 reduce_sum.56
  304.5 0.3 dynamic_update_slice.14
  304.8 0.7 reshape.105
  305.5 0.2 dynamic_update_slice.13
  305.6 0.8 slice_reduce_fusion.1
  306.4 0.2 dynamic_update_slice.15
  306.7 1.2 fusion.8
  307.8 1.6 fusion.4
  309.4 0.7 reduce.1
  310.2 0.1 reshape.107
  310.4 0.1 reshape.108.vec_ref
  310.5 0.1 select_reduce_fusion.pick_ref
  310.6 1.6 copy-done.4
  312.3 1.2 copy-done.5
  313.5 61.5 %to_slots.1 = (bf16[4,512,512]{2,1,0:T(8,128)(2,1)S(1)}, f32[32,8,128]{2,1,0:T(8,128)S(1)}, bf16[128,1536]{1,0:T(8,128)(2,1)S(1)}) custom-call(s32[128]{0:T(128)S(1)} %select_reduce_fusion.pick_ref, bf16[109,16,512]{2,1,0:T(8,128)(2,1)S(1)} %copy-done.4, f32[32,8,128]{2,1,0:T(8,128)S(1)} %reshape.108.vec_ref, bf16[8,128,512]{2,1,0:T(8,128)(2,1)S(1)} %copy-done.5, ...), custom_call_target="tpu_custom_call" | custom-call | tf_op jit(solution)/shard_map/to_slots/pallas_call | solution.py:1819
  375.1 2.2 copy-done.2
  377.3 12.0 %update.1 = (f32[4,512,512]{2,1,0:T(8,128)}, f32[4,512,512]{2,1,0:T(8,128)}, f32[4,512,512]{2,1,0:T(8,128)}, bf16[4,512,512]{2,1,0:T(8,128)(2,1)}) custom-call(bf16[4,512,512]{2,1,0:T(8,128)(2,1)S(1)} %get-tuple-element.72.grad_ref, f32[4,512,512]{2,1,0:T(8,128)S(1)} %copy-done.1, f32[4,512,512]{2,1,0:T(8,128)S(1)} %copy-done.2, f32[4,512,512]{2,1,0:T(8,128)} %master_ref.1, ...), custom_call_target="tpu_custom_call" | custom-call | flops 4300000256 | bytes 37748736 | tf_op jit(solution)/shard_map/update/pallas_call | solution.py:1852
  389.3 1.2 fusion.7
  390.6 0.6 fusion.10
  391.2 0.7 copy.43
  (42 shorter events, 0.5 us)
Async XLA Ops:
  154.3 156.2 %copy-start.12 = (s32[108]{0:T(128)S(1)}, s32[108]{0:T(128)}, u32[]{:S(2)}) copy-start(s32[108]{0:T(128)} %param.32) | copy-start | bytes 1300
  154.3 156.3 %copy-start.3 = (f32[128,1536]{1,0:T(8,128)S(1)}, f32[128,1536]{1,0:T(8,128)}, u32[]{:S(2)}) copy-start(f32[128,1536]{1,0:T(8,128)} %get-tuple-element.53.hmid_ref) | copy-start | bytes 2359300
  303.3 7.3 %copy-start = (bf16[2,256,1536]{2,1,0:T(8,128)(2,1)S(1)}, bf16[2,256,1536]{2,1,0:T(8,128)(2,1)}, u32[]{:S(2)}) copy-start(bf16[2,256,1536]{2,1,0:T(8,128)(2,1)} %get-tuple-element.50) | copy-start | bytes 4718596
  310.5 64.5 %copy-start.1 = (f32[4,512,512]{2,1,0:T(8,128)S(1)}, f32[4,512,512]{2,1,0:T(8,128)}, u32[]{:S(2)}) copy-start(f32[4,512,512]{2,1,0:T(8,128)} %left_ref.1) | copy-start | bytes 12582916
  310.6 1.6 copy-start.4
  312.3 1.3 copy-start.5
  375.0 2.2 copy-start.2
  377.2 12.1 %copy-start.6 = (bf16[128,1536]{1,0:T(8,128)(2,1)S(1)}, bf16[128,1536]{1,0:T(8,128)(2,1)}, u32[]{:S(2)}) copy-start(bf16[128,1536]{1,0:T(8,128)(2,1)} %x_ref.1) | copy-start | bytes 1179652
  377.2 12.1 %copy-start.7 = (f32[128,1536]{1,0:T(8,128)S(1)}, f32[128,1536]{1,0:T(8,128)}, u32[]{:S(2)}) copy-start(f32[128,1536]{1,0:T(8,128)} %get-tuple-element.64) | copy-start | bytes 2359300
  377.2 12.1 %copy-start.8 = (f32[128,1536]{1,0:T(8,128)S(1)}, f32[128,1536]{1,0:T(8,128)}, u32[]{:S(2)}) copy-start(f32[128,1536]{1,0:T(8,128)} %get-tuple-element.71) | copy-start | bytes 2359300
  377.2 13.3 %copy-start.9 = (f32[356]{0:T(512)S(1)}, f32[356]{0:T(512)}, u32[]{:S(2)}) copy-start(f32[356]{0:T(512)} %param.38) | copy-start | bytes 4276
  377.2 13.3 %copy-start.10 = (f32[356]{0:T(512)S(1)}, f32[356]{0:T(512)}, u32[]{:S(2)}) copy-start(f32[356]{0:T(512)} %param.40) | copy-start | bytes 4276
  377.3 13.3 %copy-start.11 = (f32[356]{0:T(512)S(1)}, f32[356]{0:T(512)}, u32[]{:S(2)}) copy-start(f32[356]{0:T(512)} %param.39) | copy-start | bytes 4276

commit v8 on v7

--- a/solution.py
+++ b/solution.py
@@ -986,7 +986,9 @@
 
 def front_body(
     first_rows, length_ref, vec_ref, x_ref, w_query_ref, w_key_ref, w_value_ref, cot_ref,
-    w_out_ref, w_gate_ref, w_up_ref, w_down_ref, dy_ref, len_ref, mix_ref, gains_ref, toep_ref, gain_ref, xn_ref, qkv_ref, s_ref, p_ref, o_ref, heads_ref, hmid_ref, wq_ref, wo_ref, hn_all_ref, w_in_ref, w_dn_ref, dy_all_ref,
+    w_out_ref, w_gate_ref, w_up_ref, w_down_ref, dy_ref, len_ref, mix_ref, gains_ref, toep_ref, gain_ref, heads_ref, hmid_ref,
+    xn_out, qkv_out, s_out, p_out, o_out, wq_out, wo_out, hn_all_ref, w_in_ref, w_dn_ref, dy_all_ref,
+    xn_ref, qkv_ref, s_ref, p_ref, o_ref, wq_ref, wo_ref, leave_sems,
     blocks_ref, own_len_ref, vecs_ref, full_ref, x_all_ref, pad_ref, out_heads, hn_ref, passing, vec_send, vec_recv, len_send, len_recv, local_sems, q_send, q_recv, q_core_send, q_core_recv,
     o_send, o_recv, o_side_send, o_side_recv, o_core_send, o_core_recv, d_send, d_recv,
     w_send, w_recv, u_send, u_recv, core_send, core_recv, head_send, head_recv, *hops,
@@ -1024,6 +1026,13 @@
         down_local.start()
 
     greet_all()
+    leaving = []
+
+    def leave(src, dst):
+        copy = pltpu.make_async_copy(src, dst, leave_sems.at[len(leaving)])
+        copy.start()
+        leaving.append(copy)
+
     sent, relayed = {}, []
     first = Gather(x_ref, x_all_ref, *hops[:7])
     side = SideGather(dy_ref, dy_all_ref, *hops[7:14])
@@ -1162,7 +1171,10 @@
     for row in range(D // 128):
         gains_ref[0:1, row * 128 : (row + 1) * 128] = full_ref[row : row + 1, :]
         gains_ref[1:2, row * 128 : (row + 1) * 128] = full_ref[FFN_ROW + row : FFN_ROW + row + 1, :]
-    mix_ref[...] = full_ref[pl.ds(MIX_ROW + me, 1), :]
+    mix_ref[...] = jnp.zeros_like(mix_ref)
+    mix_row = full_ref[pl.ds(MIX_ROW + me, 1), :]
+    for at in range(4):
+        mix_ref[at : at + 1, :] = jnp.broadcast_to(mix_row[:, at : at + 1], (1, 128))
     query_at = lax.broadcasted_iota(jnp.int32, (rows, rows), 0)
     key_at = lax.broadcasted_iota(jnp.int32, (rows, rows), 1)
     key_float = key_at.astype(f32)
@@ -1210,6 +1222,9 @@
     for mask in (2, 4, 6, 1):
         to_side(mask)
     project(1, 0)
+    leave(xn_ref, xn_out)
+    leave(qkv_ref, qkv_out)
+    leave(wq_ref, wq_out)
     for copy in local:
         copy.wait()
     relayed.append(push(w_in_ref.at[mine], w_in_ref.at[mine], core_send.at[0], core_recv.at[0], across("c")))
@@ -1239,7 +1254,7 @@
             p_ref[seq, head] = weight
             weights.append(weight)
         for head in range(2):
-            mixed = mix_ref[:, 2 * head : 2 * head + 1] * weights[0] + mix_ref[:, 2 * head + 1 : 2 * head + 2] * weights[1]
+            mixed = mix_ref[2 * head : 2 * head + 1, :] * weights[0] + mix_ref[2 * head + 1 : 2 * head + 2, :] * weights[1]
             value = qkv_ref[seq, :, (4 + head) * HP : (5 + head) * HP]
             out = dot(mixed.astype(bf16), value)
             o_ref[seq, :, head * HP : (head + 1) * HP] = out
@@ -1262,8 +1277,12 @@
     lax.fori_loop(6, seqs, attend, 0)
     out_to_core((1, 3, 5, 7))
     heads_ref[me] = out_heads[me]
+    leave(s_ref, s_out)
+    leave(p_ref, p_out)
+    leave(o_ref, o_out)
     for copy in o_core:
         copy.wait_recv()
+    leave(wo_ref, wo_out)
 
     def head_arrived(step, carry):
         source = lax.rem(me + step, seqs)
@@ -1299,6 +1318,8 @@
     gather.finish()
     for copy in relayed:
         copy.wait_recv()
+    for copy in leaving:
+        copy.wait()
 
     def head_left(step, carry):
         head_copy(lax.rem(me + step, seqs)).wait_send()
@@ -1319,19 +1340,24 @@
 def run_front(first_rows, length, vec, x, w_query, w_key, w_value, cotangent, w_out, w_gate, w_up, w_down):
     rows = x.shape[0]
     dma = pltpu.SemaphoreType.DMA
-    shapes = [
-        (x.shape, bf16), ((CHIPS, 8, 128), f32), ((1, 128), f32), ((8, D), f32), ((2, CQ * rows, rows), bf16), ((1, 2 * HP), f32),
+    small = [
+        (x.shape, bf16), ((CHIPS, 8, 128), f32), ((8, 128), f32), ((8, D), f32), ((2, CQ * rows, rows), bf16), ((1, 2 * HP), f32),
+        ((CHIPS, rows, 2 * DH), bf16), ((rows, D), f32),
+    ]
+    large = [
         ((CHIPS, rows, D), bf16), ((CHIPS, rows, 6 * HP), bf16), ((CHIPS, 2, rows, rows), bf16), ((CHIPS, 2, rows, rows), f32),
-        ((CHIPS, rows, 2 * HP), f32), ((CHIPS, rows, 2 * DH), bf16), ((rows, D), f32),
-        ((16, w_query.shape[0], 6 * DH), bf16), ((16,) + w_out.shape, bf16), ((CHIPS, rows, D), bf16),
-        ((16, w_gate.shape[0], 2 * BLK), bf16), ((2,) + w_down.shape, bf16), ((CHIPS, rows, D), bf16),
+        ((CHIPS, rows, 2 * HP), f32), ((16, w_query.shape[0], 6 * DH), bf16), ((16,) + w_out.shape, bf16),
+    ]
+    gathered = [
+        ((CHIPS, rows, D), bf16), ((16, w_gate.shape[0], 2 * BLK), bf16), ((2,) + w_down.shape, bf16), ((CHIPS, rows, D), bf16),
     ]
     return pl.pallas_call(
         functools.partial(front_body, first_rows),
         in_specs=[SMEM] + [VMEM] * 6 + [ANYS] * 4,
-        out_specs=[VMEM] * 15 + [ANYS] * 4,
-        out_shape=[jax.ShapeDtypeStruct(*shape) for shape in shapes],
-        scratch_shapes=[
+        out_specs=[VMEM] * len(small) + [ANYS] * (len(large) + len(gathered)),
+        out_shape=[jax.ShapeDtypeStruct(*shape) for shape in small + large + gathered],
+        scratch_shapes=[pltpu.VMEM(*shape) for shape in large] + [
+            dma((len(large),)),
             pltpu.VMEM((CHIPS, w_query.shape[0], 6 * DH), bf16), pltpu.VMEM((8, 128), f32), pltpu.VMEM((16,) + vec.shape, f32), pltpu.VMEM((VEC_ROWS, 128), f32), pltpu.VMEM((CHIPS, rows, D), bf16), pltpu.VMEM((rows + 8, rows), f32), pltpu.VMEM((CHIPS, rows, 2 * DH), bf16),
             pltpu.VMEM((rows, D), bf16), pltpu.VMEM((w_down.shape[0] // 2, D), bf16), dma, dma, dma((8,)), dma((8,)), dma((7,)),
         ] + [dma((8,))] * 10 + [dma((4,))] * 2 + [dma((8,))] * 8 + hop_sems() + side_sems() + hop_sems(),
@@ -1341,9 +1367,10 @@
 
 
 def middle_body(
-    len_ref, mix_ref, hn_ref, dy_ref, xn_ref, w_in_ref, w_dn_ref, wq_ref, dy_own_ref, hmid_ref, gain_ffn_ref, wo_ref,
-    qkv_ref, toep_ref, gain_ref, s_ref, p_ref, o_ref, strips_ref,
+    len_ref, mix_ref, hn_ref, dy_ref, xn_ref, w_in_hbm, w_dn_hbm, wq_hbm, dy_own_ref, hmid_ref, gains_ref, wo_hbm,
+    qkv_hbm, toep_ref, gain_ref, s_hbm, p_hbm, o_hbm, strips_ref,
     inner_ref, dhmid_ref, dxn_ref, gain_ffn_grad_ref, theta_ref, mixer_ref, gain_grad_ref, tiles_ref,
+    w_in_ref, w_dn_ref, wq_ref, wo_ref, qkv_ref, s_ref, p_ref, o_ref, enter_sems,
     theta_sums, pad_ref, first_ref, second_ref, dboth_ref, parts_ref, dattn_ref, grads_ref, sent_ref, strips_in, gin_ref, gd_ref,
     half_in, half_d, near_in, near_d, dqkv_ref, gq_ref, go_ref, core_q, core_o, in_q, in_o,
     near3, in23, in33, local_sems, load_sems, strip_send, strip_recv, head_send, head_recv,
@@ -1363,9 +1390,21 @@
                 pltpu.make_async_copy(dy_ref.at[two], second_ref.at[two], load_sems.at[4 + at]),
             ]
         )
+    enter = [
+        pltpu.make_async_copy(src, dst, enter_sems.at[at])
+        for at, (src, dst) in enumerate(
+            (
+                (w_in_hbm, w_in_ref), (w_dn_hbm, w_dn_ref), (wo_hbm, wo_ref), (qkv_hbm, qkv_ref), (s_hbm, s_ref),
+                (p_hbm, p_ref), (o_hbm, o_ref), (wq_hbm, wq_ref),
+            )
+        )
+    ]
+    enter[0].start()
     for copies in loads:
         for copy in copies:
             copy.start()
+    for copy in enter[1:]:
+        copy.start()
     strip_local = pltpu.make_async_copy(strips_ref.at[me], strips_in.at[me], local_sems.at[0])
     strip_local.start()
     greet_all()
@@ -1396,6 +1435,8 @@
             copy.wait()
 
     wait_load(0)
+    enter[0].wait()
+    enter[1].wait()
     hidden(pairs[0])
     scatter = Scatter(parts_ref, *scatter_args)
     scatter.start()
@@ -1469,12 +1510,15 @@
         values = hmid_ref[here]
         scale = rms(values)
         unit = values * scale
-        inside = grad * gain_ffn_ref[...]
+        inside = grad * gains_ref[1:2, :]
         gain_sum += jnp.sum(grad * unit, axis=0, keepdims=True)
         dhmid = scale * (inside - unit * jnp.mean(inside * unit, axis=-1, keepdims=True)) + dy_own_ref[here].astype(f32)
         dhmid_ref[here] = dhmid
         dattn_ref[here] = dhmid.astype(bf16)
     gain_ffn_grad_ref[...] = gain_sum
+
+    for copy in enter[2:]:
+        copy.wait()
 
     def grad_copy(to):
         return pltpu.make_async_remote_copy(
@@ -1503,6 +1547,7 @@
     gain_grad_ref[...] = jnp.zeros_like(gain_grad_ref)
     query_at = lax.broadcasted_iota(jnp.int32, (rows, rows), 0)
     key_at = lax.broadcasted_iota(jnp.int32, (rows, rows), 1)
+    key_float = key_at.astype(f32)
     blank = jnp.zeros((rows, HP - DH), f32)
 
     def grad_arrived(step, carry):
@@ -1513,7 +1558,7 @@
     lax.fori_loop(1, seqs, grad_arrived, 0)
 
     def one(seq, carry):
-        keep = (key_at <= query_at) & (key_at < len_ref[seq])
+        keep = (key_at <= query_at) & (key_float < len_ref[seq, 0:1, :])
         weights = [p_ref[seq, 0], p_ref[seq, 1]]
         grad_mixed, made = [], [None] * 6
         grads = grads_ref[seq].astype(f32)
@@ -1528,7 +1573,9 @@
             grad_out = scale * (inner - unit * (jnp.sum(inner * unit, axis=-1, keepdims=True) * (1.0 / DH)))
             grad_out = grad_out.astype(bf16)
             value = qkv_ref[seq, :, (4 + head) * HP : (5 + head) * HP]
-            mixed = (mix_ref[2 * head] * weights[0] + mix_ref[2 * head + 1] * weights[1]).astype(bf16)
+            mixed = (
+                mix_ref[2 * head : 2 * head + 1, :] * weights[0] + mix_ref[2 * head + 1 : 2 * head + 2, :] * weights[1]
+            ).astype(bf16)
             made[4 + head] = dot_tn(mixed, grad_out)
             back = dot_nt(grad_out, value)
             grad_mixed.append(back)
@@ -1537,7 +1584,7 @@
                     back * weights[source], axis=0, keepdims=True
                 )
         for head in range(2):
-            grad_weight = mix_ref[head] * grad_mixed[0] + mix_ref[2 + head] * grad_mixed[1]
+            grad_weight = mix_ref[head : head + 1, :] * grad_mixed[0] + mix_ref[2 + head : 3 + head, :] * grad_mixed[1]
             weight = weights[head]
             grad_conv = weight * (grad_weight - jnp.sum(weight * grad_weight, axis=-1, keepdims=True))
             wide = shifted_up(pad_ref, grad_conv).astype(bf16)
@@ -1555,8 +1602,9 @@
         dqkv_ref[seq] = jnp.concatenate([part[:, :DH] for part in made], axis=1).astype(bf16)
         return carry
 
-    lax.fori_loop(0, seqs, one, 0)
+    lax.fori_loop(0, 4, one, 0)
     gather.onward()
+    lax.fori_loop(4, seqs, one, 0)
     scatter.drain()
     tiles_sent = []
 
@@ -1725,10 +1773,11 @@
     every, heads = low(CHIPS, rows, D), low(CHIPS, rows, 2 * DH)
     return pl.pallas_call(
         middle_body,
-        in_specs=[SMEM] * 2 + [ANYS] * 3 + [VMEM] * 14,
+        in_specs=[VMEM] * 2 + [ANYS] * 6 + [VMEM] * 3 + [ANYS] * 2 + [VMEM] * 2 + [ANYS] * 3 + [VMEM],
         out_specs=[VMEM] * len(shapes),
         out_shape=[jax.ShapeDtypeStruct(*shape) for shape in shapes],
-        scratch_shapes=[
+        scratch_shapes=[pltpu.VMEM(a.shape, a.dtype) for a in (w_in, w_dn, w_qkv, w_o, qkv, scores, weights, outs)] + [
+            dma((8,)),
             pltpu.VMEM((2, rows, CQ * rows), f32), pltpu.VMEM((rows + 8, rows), f32), every, every, low(seqs, rows, 2 * BLK), every, low(rows, D), heads, heads, heads,
             low(ROW_TILES, 2, CHIPS, 2, part, 2 * BLK), low(2, CHIPS, 2, part, D),
             low(ROW_TILES, CHIPS, 2, part, 2 * BLK), low(CHIPS, 2, part, D),
@@ -1748,12 +1797,18 @@
 
 
 def to_slots_body(
-    pick_ref, tiles_ref, vec_ref, inner_ref, w_dn_ref, hmid_ref, out_ref, vecs_ref, layer_ref,
-    slots_ref, parts_ref, local_sems, send, recv, vec_send, vec_recv, *scatter_args,
+    pick_ref, tiles_ref, vec_ref, inner_hbm, w_dn_hbm, hmid_hbm, out_ref, vecs_ref, layer_ref,
+    inner_ref, w_dn_ref, hmid_ref, enter_sems, slots_ref, parts_ref, local_sems, send, recv, vec_send, vec_recv, *scatter_args,
 ):
     devices = lax.axis_size(ALL)
     own_slots, side = out_ref.shape[:2]
     part = slots_ref.shape[1]
+    enter = [
+        pltpu.make_async_copy(src, dst, enter_sems.at[at])
+        for at, (src, dst) in enumerate(((inner_hbm, inner_ref), (w_dn_hbm, w_dn_ref), (hmid_hbm, hmid_ref)))
+    ]
+    for copy in enter:
+        copy.start()
 
     def fill(at, carry):
         slots_ref[at] = tiles_ref[pick_ref[at]]
@@ -1779,16 +1834,17 @@
         pltpu.make_async_remote_copy(
             src_ref=vec_ref.at[to], dst_ref=vecs_ref.at[me], send_sem=vec_send, recv_sem=vec_recv, device_id=device_at(to)
         ).start()
-        for slot in range(own_slots):
-            pltpu.make_async_remote_copy(
-                src_ref=slots_ref.at[to * own_slots + slot], dst_ref=out_ref.at[slot, rows],
-                send_sem=send, recv_sem=recv, device_id=device_at(to),
-            ).start()
+        pltpu.make_async_remote_copy(
+            src_ref=slots_ref.at[pl.ds(to * own_slots, own_slots)], dst_ref=out_ref.at[:, rows],
+            send_sem=send, recv_sem=recv, device_id=device_at(to),
+        ).start()
         return carry
 
     lax.fori_loop(1, devices, push_all, 0)
 
     seqs, length = inner_ref.shape[:2]
+    for copy in enter:
+        copy.wait()
 
     def outputs(at, carry):
         two = pl.ds(at * 2, 2)
@@ -1818,17 +1874,17 @@
     dma = pltpu.SemaphoreType.DMA
     return pl.pallas_call(
         to_slots_body,
-        in_specs=[SMEM, VMEM, ANYS] + [VMEM] * 3,
+        in_specs=[SMEM, VMEM] + [ANYS] * 4,
         out_specs=[ANYS] * 2 + [VMEM],
         out_shape=[
             jax.ShapeDtypeStruct((own_slots, BLK, BLK), bf16), jax.ShapeDtypeStruct(vecs.shape, vecs.dtype),
             jax.ShapeDtypeStruct(hmid.shape, bf16),
         ],
-        scratch_shapes=[
-            pltpu.VMEM((pick.shape[0],) + tiles.shape[1:], bf16), pltpu.VMEM((CHIPS, rows, D), bf16), dma((1 + own_slots,)),
+        scratch_shapes=[pltpu.VMEM(a.shape, a.dtype) for a in (inner, w_dn, hmid)] + [
+            dma((3,)), pltpu.VMEM((pick.shape[0],) + tiles.shape[1:], bf16), pltpu.VMEM((CHIPS, rows, D), bf16), dma((1 + own_slots,)),
         ] + [dma] * 4 + side_scatter_scratch(rows, D),
         name="to_slots",
-        compiler_params=pltpu.CompilerParams(collective_id=6, has_side_effects=True, vmem_limit_bytes=32 * 2**20),
+        compiler_params=pltpu.CompilerParams(collective_id=6, has_side_effects=True, vmem_limit_bytes=60 * 2**20),
     )(pick, tiles, vecs, inner, w_dn, hmid)
 
 
@@ -1856,7 +1912,7 @@
         out_specs=[spec] * 4,
         out_shape=[jax.ShapeDtypeStruct(grad.shape, kind) for kind in (f32, f32, f32, bf16)],
         name="update",
-        compiler_params=pltpu.CompilerParams(vmem_limit_bytes=40 * 2**20),
+        compiler_params=pltpu.CompilerParams(vmem_limit_bytes=60 * 2**20),
         cost_estimate=pl.CostEstimate(flops=43 * 10**8, bytes_accessed=36 * 2**20, transcendentals=10**6),
     )(grad, left, right, master, first, second)
 
@@ -1877,7 +1933,7 @@
     vec = lax.dynamic_slice_in_dim(rows_of_vector(flat), first, SHARD_ROWS, 0)
 
     (
-        dy, group_lengths, mix, gains, toep, gain_pair, xn, qkv, scores, weights, outs, heads, hmid, w_qkv, w_out_all,
+        dy, group_lengths, mix, gains, toep, gain_pair, heads, hmid, xn, qkv, scores, weights, outs, w_qkv, w_out_all,
         hn_rows, w_in, w_dn, dy_rows,
     ) = run_front(
         first_rows, lengths, vec, layer_input, w_query, w_key, w_value, cotangent, w_out, w_gate, w_up, w_down
@@ -1897,7 +1953,7 @@
     tile_count = owners.shape[0]
     pick = jnp.min(jnp.where(matches, jnp.arange(tile_count, dtype=jnp.int32)[None, :], tile_count), axis=1)
     inner, dhmid, dxn, grad_gain_ffn, theta_sums, mixer_sums, gain_sums, tiles = run_middle(
-        group_lengths[:, 0, 0].astype(jnp.int32), mix[0, :4], hn_rows, dy_rows, xn, w_in, w_dn, w_qkv, dy, hmid, gains[1:2],
+        group_lengths, mix, hn_rows, dy_rows, xn, w_in, w_dn, w_qkv, dy, hmid, gains,
         w_out_all.reshape(CHIPS, 2 * DH, D), qkv, toep, gain_pair, scores, weights, outs, strips,
     )
     dinput, grad_gain_attn = norm_backward(input_float, input_scale, gain_attn, dxn)

time: 397 us -> 379 us (0.955)
  Pallas kernels: 364 us -> 354 us
  local copies, waits for them, and re-layouts: 15 us -> 8.8 us
    pallas_call x2, Pallas kernels: 210 us -> 203 us  [the longest x1 140 us: run_middle(): pl.pallas_call(middle_body, in_specs=[VMEM] * 2 + [ANYS] * 6 + [VMEM] * 3...]
    unnamed x27 -> x19, local copies, waits for them, and re-layouts: 5.85 us -> 0.79 us
    pallas_call x1, Pallas kernels: 141 us -> 137 us  [run_front(): pl.pallas_call(functools.partial(front_body, first_rows), in_specs=[SMEM]...]
where the time goes in v8:
time: 379 us; the launch traced here: 374 us
  Pallas kernels  354 us (93%)
  local copies, waits for them, and re-layouts  8.8 us (2%)
  other arithmetic  7.35 us (2%)
    pallas_call x1, Pallas kernels, run_middle(): pl.pallas_call(middle_body, in_specs=[VMEM] * 2 + [ANYS] * 6 + [VMEM] * 3...  140 us
    pallas_call x1, Pallas kernels, run_front(): pl.pallas_call(functools.partial(front_body, first_rows), in_specs=[SMEM]...  137 us
    pallas_call x1, Pallas kernels, to_slots(): pl.pallas_call(to_slots_body, in_specs=[SMEM, VMEM] + [ANYS] * 4, out_spe...  62.7 us
    pallas_call x1, Pallas kernels, update(): pl.pallas_call(update_body, grid=(grad.shape[0],), in_specs=[spec] * 6, o...  14.1 us

profile of v8, /device:TPU:11, one launch (start us, length us, event | category | flops | bytes accessed | tf_op | source)
XLA Modules:
  0.0 373.6 jit_solution(6654470269154889284)
XLA Ops:
  0.7 0.8 convert_dynamic-update-slice_fusion
  1.5 0.1 reshape.93
  1.6 0.1 reshape.95
  1.7 0.1 slice.48
  1.7 0.1 reshape.96
  1.8 0.2 concatenate.6
  2.1 1.2 dynamic_slice.7
  5.2 0.6 constant_dynamic-slice_fusion.vec_ref
  6.5 137.2 %front.1 = (bf16[128,1536]{1,0:T(8,128)(2,1)}, f32[8,8,128]{2,1,0:T(8,128)}, f32[8,128]{1,0:T(8,128)}, f32[8,1536]{1,0:T(8,128)}, bf16[2,768,128]{2,1,0:T(8,128)...) custom-call(s32[1]{0:T(128)S(6)} %copy.42.length_ref, ...), custom_call_target="tpu_custom_call" | custom-call | tf_op jit(solution)/shard_map/front/pallas_call | solution.py:1354
  143.7 1.3 copy.34
  145.1 1.0 copy.36.strips_ref
  146.1 140.0 %middle.1 = (bf16[8,128,512]{2,1,0:T(8,128)(2,1)}, f32[128,1536]{1,0:T(8,128)}, f32[128,1536]{1,0:T(8,128)}, f32[1,1536]{1,0:T(1,128)}, f32[132,128]{1,0:T(8,128...) custom-call(f32[8,8,128]{2,1,0:T(8,128)} %get-tuple-element.44.len_ref, ...), custom_call_target="tpu_custom_call" | custom-call | tf_op jit(solution)/shard_map/middle/pallas_call | solution.py:1774
  286.1 1.0 reduce_sum.56
  287.1 0.3 dynamic_update_slice.14
  287.4 0.7 reshape.104
  288.2 0.2 dynamic_update_slice.13
  288.3 0.8 slice_reduce_fusion.1
  289.1 0.2 dynamic_update_slice.15
  289.4 0.8 slice_reduce_fusion
  290.2 0.2 fusion.8
  290.4 1.5 fusion.4
  291.8 0.7 reduce
  292.5 0.1 concatenate.7
  292.6 0.1 reshape.106
  292.8 0.8 reshape.107.vec_ref
  293.6 0.6 select_reduce_fusion.pick_ref
  294.2 62.7 %to_slots.1 = (bf16[4,512,512]{2,1,0:T(8,128)(2,1)}, f32[32,8,128]{2,1,0:T(8,128)}, bf16[128,1536]{1,0:T(8,128)(2,1)}) custom-call(s32[128]{0:T(128)} %select_reduce_fusion.pick_ref, bf16[109,16,512]{2,1,0:T(8,128)(2,1)} %get-tuple-element.63.tiles_ref, f32[32,8,128]{2,1,0:T(8,128)} %reshape.107.vec_ref, bf16[8,128,512]{2,1,0:T(8,128)(2,1)} %get-tuple-element.69.inner_hbm, ...), custom_call_target="tpu_custom_call" | custom-call | tf_op jit(solution)/shard_map/to_slots/pallas_call | solution.py:1875
  356.9 0.0 copy-start.5
  356.9 14.1 %update.1 = (f32[4,512,512]{2,1,0:T(8,128)}, f32[4,512,512]{2,1,0:T(8,128)}, f32[4,512,512]{2,1,0:T(8,128)}, bf16[4,512,512]{2,1,0:T(8,128)(2,1)}) custom-call(bf16[4,512,512]{2,1,0:T(8,128)(2,1)} %get-tuple-element.72.grad_ref, f32[4,512,512]{2,1,0:T(8,128)} %left_ref.1, f32[4,512,512]{2,1,0:T(8,128)} %right_ref.1, f32[4,512,512]{2,1,0:T(8,128)} %master_ref.1, ...), custom_call_target="tpu_custom_call" | custom-call | flops 4300000256 | bytes 37748736 | tf_op jit(solution)/shard_map/update/pallas_call | solution.py:1908
  371.0 1.2 fusion.7
  372.3 0.6 fusion.10
  372.9 0.7 copy.43
  (32 shorter events, 0.2 us)
Async XLA Ops:
  146.1 144.1 %copy-start = (bf16[128,1536]{1,0:T(8,128)(2,1)S(1)}, bf16[128,1536]{1,0:T(8,128)(2,1)}, u32[]{:S(2)}) copy-start(bf16[128,1536]{1,0:T(8,128)(2,1)} %x_ref.1) | copy-start | bytes 1179652
  146.1 147.5 %copy-start.8 = (s32[108]{0:T(128)S(1)}, s32[108]{0:T(128)}, u32[]{:S(2)}) copy-start(s32[108]{0:T(128)} %param.32) | copy-start | bytes 1300
  356.9 14.2 %copy-start.1 = (f32[128,1536]{1,0:T(8,128)S(1)}, f32[128,1536]{1,0:T(8,128)}, u32[]{:S(2)}) copy-start(f32[128,1536]{1,0:T(8,128)} %get-tuple-element.64) | copy-start | bytes 2359300
  356.9 14.2 %copy-start.2 = (f32[128,1536]{1,0:T(8,128)S(1)}, f32[128,1536]{1,0:T(8,128)}, u32[]{:S(2)}) copy-start(f32[128,1536]{1,0:T(8,128)} %get-tuple-element.71) | copy-start | bytes 2359300
  356.9 15.3 %copy-start.4 = (f32[32,8,128]{2,1,0:T(8,128)S(1)}, f32[32,8,128]{2,1,0:T(8,128)}, u32[]{:S(2)}) copy-start(f32[32,8,128]{2,1,0:T(8,128)} %get-tuple-element.77) | copy-start | bytes 393220
  356.9 15.4 %copy-start.5 = (f32[356]{0:T(512)S(1)}, f32[356]{0:T(512)}, u32[]{:S(2)}) copy-start(f32[356]{0:T(512)} %param.38) | copy-start | bytes 4276
  356.9 15.4 %copy-start.6 = (f32[356]{0:T(512)S(1)}, f32[356]{0:T(512)}, u32[]{:S(2)}) copy-start(f32[356]{0:T(512)} %param.40) | copy-start | bytes 4276
  356.9 15.4 %copy-start.7 = (f32[356]{0:T(512)S(1)}, f32[356]{0:T(512)}, u32[]{:S(2)}) copy-start(f32[356]{0:T(512)} %param.39) | copy-start | bytes 4276
  371.0 1.9 copy-start.3

commit v9 on v8

--- a/solution.py
+++ b/solution.py
@@ -986,9 +986,9 @@
 
 def front_body(
     first_rows, length_ref, vec_ref, x_ref, w_query_ref, w_key_ref, w_value_ref, cot_ref,
-    w_out_ref, w_gate_ref, w_up_ref, w_down_ref, dy_ref, len_ref, mix_ref, gains_ref, toep_ref, gain_ref, heads_ref, hmid_ref,
+    w_out_ref, w_gate_ref, w_up_ref, w_down_ref, dy_ref, len_ref, mix_ref, gains_ref, toep_ref, gain_ref, strips_ref, hmid_ref,
     xn_out, qkv_out, s_out, p_out, o_out, wq_out, wo_out, hn_all_ref, w_in_ref, w_dn_ref, dy_all_ref,
-    xn_ref, qkv_ref, s_ref, p_ref, o_ref, wq_ref, wo_ref, leave_sems,
+    xn_ref, qkv_ref, s_ref, p_ref, o_ref, wq_ref, wo_ref, heads_ref, leave_sems,
     blocks_ref, own_len_ref, vecs_ref, full_ref, x_all_ref, pad_ref, out_heads, hn_ref, passing, vec_send, vec_recv, len_send, len_recv, local_sems, q_send, q_recv, q_core_send, q_core_recv,
     o_send, o_recv, o_side_send, o_side_recv, o_core_send, o_core_recv, d_send, d_recv,
     w_send, w_recv, u_send, u_recv, core_send, core_recv, head_send, head_recv, *hops,
@@ -1304,6 +1304,14 @@
     hmid = hmid_ref[...]
     hn_ref[...] = (hmid * rms(hmid) * gains_ref[1:2, :]).astype(bf16)
     gather.start()
+    width = BLK // (2 * CHIPS)
+    for chip in range(CHIPS):
+        pieces = []
+        for at in range(2 * ROW_TILES):
+            begin = at * (BLK // 2) + chip * width
+            source, begin = begin // (2 * DH), begin % (2 * DH)
+            pieces.append(heads_ref[source, :, begin : begin + width])
+        strips_ref[chip] = jnp.concatenate(pieces, axis=1)
     for mask in (4, 6):
         relay(mask)
     gather.onward()
@@ -1357,7 +1365,7 @@
         out_specs=[VMEM] * len(small) + [ANYS] * (len(large) + len(gathered)),
         out_shape=[jax.ShapeDtypeStruct(*shape) for shape in small + large + gathered],
         scratch_shapes=[pltpu.VMEM(*shape) for shape in large] + [
-            dma((len(large),)),
+            pltpu.VMEM((CHIPS, rows, 2 * DH), bf16), dma((len(large),)),
             pltpu.VMEM((CHIPS, w_query.shape[0], 6 * DH), bf16), pltpu.VMEM((8, 128), f32), pltpu.VMEM((16,) + vec.shape, f32), pltpu.VMEM((VEC_ROWS, 128), f32), pltpu.VMEM((CHIPS, rows, D), bf16), pltpu.VMEM((rows + 8, rows), f32), pltpu.VMEM((CHIPS, rows, 2 * DH), bf16),
             pltpu.VMEM((rows, D), bf16), pltpu.VMEM((w_down.shape[0] // 2, D), bf16), dma, dma, dma((8,)), dma((8,)), dma((7,)),
         ] + [dma((8,))] * 10 + [dma((4,))] * 2 + [dma((8,))] * 8 + hop_sems() + side_sems() + hop_sems(),
@@ -1929,11 +1937,14 @@
     fs_index = ((lax.axis_index("g") * 2 + lax.axis_index("a")) * 2 + lax.axis_index("b")) * 2 + lax.axis_index("c")
     first_rows = vector_rows(own_vec, fs_size)
     flat = lax.dynamic_update_slice_in_dim(jnp.zeros((fs_size * own_vec,), f32), vec_copy.astype(f32), fs_index * own_vec, 0)
-    first = lax.dynamic_index_in_dim(jnp.array(first_rows, jnp.int32), fs_index, 0, keepdims=False)
+    first = sum(
+        (first_rows[at] - first_rows[at - 1]) * (fs_index >= at).astype(jnp.int32)
+        for at in range(1, fs_size) if first_rows[at] != first_rows[at - 1]
+    )
     vec = lax.dynamic_slice_in_dim(rows_of_vector(flat), first, SHARD_ROWS, 0)
 
     (
-        dy, group_lengths, mix, gains, toep, gain_pair, heads, hmid, xn, qkv, scores, weights, outs, w_qkv, w_out_all,
+        dy, group_lengths, mix, gains, toep, gain_pair, strips, hmid, xn, qkv, scores, weights, outs, w_qkv, w_out_all,
         hn_rows, w_in, w_dn, dy_rows,
     ) = run_front(
         first_rows, lengths, vec, layer_input, w_query, w_key, w_value, cotangent, w_out, w_gate, w_up, w_down
@@ -1941,10 +1952,6 @@
     gain_attn = gains[0]
     w_qkv = w_qkv.reshape(D, 6 * DH)
     w_in, w_dn = w_in.reshape(D, 2 * BLK), w_dn.reshape(BLK, D)
-    strip = BLK // (2 * CHIPS)
-    part = strip // 2
-    heads = jnp.transpose(heads, (1, 0, 2)).reshape(seq_len, 2 * ROW_TILES, CHIPS, strip)
-    strips = jnp.transpose(heads, (2, 0, 1, 3)).reshape(CHIPS, seq_len, 2 * ROW_TILES * strip)
     input_float = layer_input.astype(f32)
     input_scale = rms(input_float)
 

time: 379 us -> 373 us (0.984)
  no operation moved by 1% of the time
where the time goes in v9:
time: 373 us; the launch traced here: 368 us
  Pallas kernels  354 us (95%)
  other arithmetic  7.35 us (2%)
  local copies, waits for them, and re-layouts  5.24 us (1%)
    pallas_call x1, Pallas kernels, run_middle(): pl.pallas_call(middle_body, in_specs=[VMEM] * 2 + [ANYS] * 6 + [VMEM] * 3...  140 us
    pallas_call x1, Pallas kernels, run_front(): pl.pallas_call(functools.partial(front_body, first_rows), in_specs=[SMEM]...  137 us
    pallas_call x1, Pallas kernels, to_slots(): pl.pallas_call(to_slots_body, in_specs=[SMEM, VMEM] + [ANYS] * 4, out_spe...  62.7 us
    pallas_call x1, Pallas kernels, update(): pl.pallas_call(update_body, grid=(grad.shape[0],), in_specs=[spec] * 6, o...  14.1 us

profile of v9, /device:TPU:11, one launch (start us, length us, event | category | flops | bytes accessed | tf_op | source)
XLA Modules:
  0.0 368.2 jit_solution(923316748522889456)
XLA Ops:
  0.7 0.8 convert_dynamic-update-slice_fusion
  1.5 0.1 reshape.87
  1.6 0.1 reshape.89
  1.7 0.1 slice.48
  1.8 0.1 reshape.90
  1.9 0.2 concatenate.6
  2.1 0.6 constant_dynamic-slice_fusion.vec_ref
  3.3 137.2 %front.1 = (bf16[128,1536]{1,0:T(8,128)(2,1)}, f32[8,8,128]{2,1,0:T(8,128)}, f32[8,128]{1,0:T(8,128)}, f32[8,1536]{1,0:T(8,128)}, bf16[2,768,128]{2,1,0:T(8,128)...) custom-call(s32[1]{0:T(128)S(6)} %copy.35.length_ref, ...), custom_call_target="tpu_custom_call" | custom-call | tf_op jit(solution)/shard_map/front/pallas_call | solution.py:1362
  140.6 0.0 copy-start
  140.6 0.0 copy-start.8
  140.6 140.1 %middle.1 = (bf16[8,128,512]{2,1,0:T(8,128)(2,1)}, f32[128,1536]{1,0:T(8,128)}, f32[128,1536]{1,0:T(8,128)}, f32[1,1536]{1,0:T(1,128)}, f32[132,128]{1,0:T(8,128...) custom-call(f32[8,8,128]{2,1,0:T(8,128)} %get-tuple-element.44.len_ref, ...), custom_call_target="tpu_custom_call" | custom-call | tf_op jit(solution)/shard_map/middle/pallas_call | solution.py:1782
  280.7 1.0 reduce_sum.56
  281.7 0.3 dynamic_update_slice.14
  282.0 0.8 reshape.96
  282.8 0.2 dynamic_update_slice.13
  282.9 0.8 slice_reduce_fusion.1
  283.7 0.2 dynamic_update_slice.15
  284.0 0.8 slice_reduce_fusion
  284.8 0.2 fusion.8
  285.0 1.5 fusion.4
  286.4 0.7 reduce
  287.1 0.1 concatenate.7
  287.2 0.1 reshape.98
  287.4 0.8 reshape.99.vec_ref
  288.2 0.6 select_reduce_fusion.pick_ref
  288.8 62.7 %to_slots.1 = (bf16[4,512,512]{2,1,0:T(8,128)(2,1)}, f32[32,8,128]{2,1,0:T(8,128)}, bf16[128,1536]{1,0:T(8,128)(2,1)}) custom-call(s32[128]{0:T(128)} %select_reduce_fusion.pick_ref, bf16[109,16,512]{2,1,0:T(8,128)(2,1)} %get-tuple-element.63.tiles_ref, f32[32,8,128]{2,1,0:T(8,128)} %reshape.99.vec_ref, bf16[8,128,512]{2,1,0:T(8,128)(2,1)} %get-tuple-element.69.inner_hbm, ...), custom_call_target="tpu_custom_call" | custom-call | tf_op jit(solution)/shard_map/to_slots/pallas_call | solution.py:1883
  351.5 0.0 copy-start.5
  351.5 0.0 copy-start.6
  351.5 14.1 %update.1 = (f32[4,512,512]{2,1,0:T(8,128)}, f32[4,512,512]{2,1,0:T(8,128)}, f32[4,512,512]{2,1,0:T(8,128)}, bf16[4,512,512]{2,1,0:T(8,128)(2,1)}) custom-call(bf16[4,512,512]{2,1,0:T(8,128)(2,1)} %get-tuple-element.72.grad_ref, f32[4,512,512]{2,1,0:T(8,128)} %left_ref.1, f32[4,512,512]{2,1,0:T(8,128)} %right_ref.1, f32[4,512,512]{2,1,0:T(8,128)} %master_ref.1, ...), custom_call_target="tpu_custom_call" | custom-call | flops 4300000256 | bytes 37748736 | tf_op jit(solution)/shard_map/update/pallas_call | solution.py:1916
  365.6 1.2 fusion.7
  366.8 0.6 fusion.10
  367.5 0.7 copy.36
  (28 shorter events, 0.2 us)
Async XLA Ops:
  140.6 144.2 %copy-start = (bf16[128,1536]{1,0:T(8,128)(2,1)S(1)}, bf16[128,1536]{1,0:T(8,128)(2,1)}, u32[]{:S(2)}) copy-start(bf16[128,1536]{1,0:T(8,128)(2,1)} %x_ref.1) | copy-start | bytes 1179652
  140.6 147.6 %copy-start.8 = (s32[108]{0:T(128)S(1)}, s32[108]{0:T(128)}, u32[]{:S(2)}) copy-start(s32[108]{0:T(128)} %param.31) | copy-start | bytes 1300
  351.4 14.2 %copy-start.1 = (f32[128,1536]{1,0:T(8,128)S(1)}, f32[128,1536]{1,0:T(8,128)}, u32[]{:S(2)}) copy-start(f32[128,1536]{1,0:T(8,128)} %get-tuple-element.64) | copy-start | bytes 2359300
  351.4 14.2 %copy-start.2 = (f32[128,1536]{1,0:T(8,128)S(1)}, f32[128,1536]{1,0:T(8,128)}, u32[]{:S(2)}) copy-start(f32[128,1536]{1,0:T(8,128)} %get-tuple-element.71) | copy-start | bytes 2359300
  351.4 15.3 %copy-start.4 = (f32[32,8,128]{2,1,0:T(8,128)S(1)}, f32[32,8,128]{2,1,0:T(8,128)}, u32[]{:S(2)}) copy-start(f32[32,8,128]{2,1,0:T(8,128)} %get-tuple-element.77) | copy-start | bytes 393220
  351.5 15.4 %copy-start.5 = (f32[356]{0:T(512)S(1)}, f32[356]{0:T(512)}, u32[]{:S(2)}) copy-start(f32[356]{0:T(512)} %param.37) | copy-start | bytes 4276
  351.5 15.4 %copy-start.6 = (f32[356]{0:T(512)S(1)}, f32[356]{0:T(512)}, u32[]{:S(2)}) copy-start(f32[356]{0:T(512)} %param.39) | copy-start | bytes 4276
  351.5 15.4 %copy-start.7 = (f32[356]{0:T(512)S(1)}, f32[356]{0:T(512)}, u32[]{:S(2)}) copy-start(f32[356]{0:T(512)} %param.38) | copy-start | bytes 4276
  365.6 1.9 copy-start.3

commit v10 on v9

--- a/solution.py
+++ b/solution.py
@@ -1848,7 +1848,8 @@
         ).start()
         return carry
 
-    lax.fori_loop(1, devices, push_all, 0)
+    lax.fori_loop(devices // 4, devices, push_all, 0)
+    lax.fori_loop(1, devices // 4, push_all, 0)
 
     seqs, length = inner_ref.shape[:2]
     for copy in enter:

time: 373 us -> 372 us (level)
  no operation moved by 1% of the time
where the time goes in v10:
time: 372 us; the launch traced here: 367 us
  Pallas kernels  352 us (95%)
  other arithmetic  7.35 us (2%)
  local copies, waits for them, and re-layouts  5.24 us (1%)
    pallas_call x1, Pallas kernels, run_middle(): pl.pallas_call(middle_body, in_specs=[VMEM] * 2 + [ANYS] * 6 + [VMEM] * 3...  140 us
    pallas_call x1, Pallas kernels, run_front(): pl.pallas_call(functools.partial(front_body, first_rows), in_specs=[SMEM]...  137 us
    pallas_call x1, Pallas kernels, to_slots(): pl.pallas_call(to_slots_body, in_specs=[SMEM, VMEM] + [ANYS] * 4, out_spe...  61 us
    pallas_call x1, Pallas kernels, update(): pl.pallas_call(update_body, grid=(grad.shape[0],), in_specs=[spec] * 6, o...  14.1 us

profile of v10, /device:TPU:11, one launch (start us, length us, event | category | flops | bytes accessed | tf_op | source)
XLA Modules:
  0.0 366.6 jit_solution(12589938701182653955)
XLA Ops:
  0.7 0.8 convert_dynamic-update-slice_fusion
  1.5 0.1 reshape.87
  1.6 0.1 reshape.89
  1.7 0.1 slice.48
  1.8 0.1 reshape.90
  1.9 0.2 concatenate.6
  2.1 0.6 constant_dynamic-slice_fusion.vec_ref
  3.3 137.2 %front.1 = (bf16[128,1536]{1,0:T(8,128)(2,1)}, f32[8,8,128]{2,1,0:T(8,128)}, f32[8,128]{1,0:T(8,128)}, f32[8,1536]{1,0:T(8,128)}, bf16[2,768,128]{2,1,0:T(8,128)...) custom-call(s32[1]{0:T(128)S(6)} %copy.35.length_ref, ...), custom_call_target="tpu_custom_call" | custom-call | tf_op jit(solution)/shard_map/front/pallas_call | solution.py:1362
  140.6 0.0 copy-start
  140.6 0.0 copy-start.8
  140.6 140.1 %middle.1 = (bf16[8,128,512]{2,1,0:T(8,128)(2,1)}, f32[128,1536]{1,0:T(8,128)}, f32[128,1536]{1,0:T(8,128)}, f32[1,1536]{1,0:T(1,128)}, f32[132,128]{1,0:T(8,128...) custom-call(f32[8,8,128]{2,1,0:T(8,128)} %get-tuple-element.44.len_ref, ...), custom_call_target="tpu_custom_call" | custom-call | tf_op jit(solution)/shard_map/middle/pallas_call | solution.py:1782
  280.7 1.0 reduce_sum.56
  281.7 0.3 dynamic_update_slice.14
  282.0 0.8 reshape.96
  282.8 0.2 dynamic_update_slice.13
  282.9 0.8 slice_reduce_fusion.1
  283.7 0.2 dynamic_update_slice.15
  284.0 0.8 slice_reduce_fusion
  284.8 0.2 fusion.8
  285.0 1.5 fusion.4
  286.4 0.7 reduce
  287.1 0.1 concatenate.7
  287.2 0.1 reshape.98
  287.4 0.8 reshape.99.vec_ref
  288.2 0.6 select_reduce_fusion.pick_ref
  288.8 61.0 %to_slots.1 = (bf16[4,512,512]{2,1,0:T(8,128)(2,1)}, f32[32,8,128]{2,1,0:T(8,128)}, bf16[128,1536]{1,0:T(8,128)(2,1)}) custom-call(s32[128]{0:T(128)} %select_reduce_fusion.pick_ref, bf16[109,16,512]{2,1,0:T(8,128)(2,1)} %get-tuple-element.63.tiles_ref, f32[32,8,128]{2,1,0:T(8,128)} %reshape.99.vec_ref, bf16[8,128,512]{2,1,0:T(8,128)(2,1)} %get-tuple-element.69.inner_hbm, ...), custom_call_target="tpu_custom_call" | custom-call | tf_op jit(solution)/shard_map/to_slots/pallas_call | solution.py:1884
  349.9 0.0 copy-start.6
  349.9 0.0 copy-start.7
  349.9 14.1 %update.1 = (f32[4,512,512]{2,1,0:T(8,128)}, f32[4,512,512]{2,1,0:T(8,128)}, f32[4,512,512]{2,1,0:T(8,128)}, bf16[4,512,512]{2,1,0:T(8,128)(2,1)}) custom-call(bf16[4,512,512]{2,1,0:T(8,128)(2,1)} %get-tuple-element.72.grad_ref, f32[4,512,512]{2,1,0:T(8,128)} %left_ref.1, f32[4,512,512]{2,1,0:T(8,128)} %right_ref.1, f32[4,512,512]{2,1,0:T(8,128)} %master_ref.1, ...), custom_call_target="tpu_custom_call" | custom-call | flops 4300000256 | bytes 37748736 | tf_op jit(solution)/shard_map/update/pallas_call | solution.py:1917
  364.0 1.2 fusion.7
  365.2 0.6 fusion.10
  365.8 0.7 copy.36
  (28 shorter events, 0.2 us)
Async XLA Ops:
  140.6 144.2 %copy-start = (bf16[128,1536]{1,0:T(8,128)(2,1)S(1)}, bf16[128,1536]{1,0:T(8,128)(2,1)}, u32[]{:S(2)}) copy-start(bf16[128,1536]{1,0:T(8,128)(2,1)} %x_ref.1) | copy-start | bytes 1179652
  140.6 147.6 %copy-start.8 = (s32[108]{0:T(128)S(1)}, s32[108]{0:T(128)}, u32[]{:S(2)}) copy-start(s32[108]{0:T(128)} %param.31) | copy-start | bytes 1300
  349.8 14.2 %copy-start.1 = (f32[128,1536]{1,0:T(8,128)S(1)}, f32[128,1536]{1,0:T(8,128)}, u32[]{:S(2)}) copy-start(f32[128,1536]{1,0:T(8,128)} %get-tuple-element.64) | copy-start | bytes 2359300
  349.8 14.2 %copy-start.2 = (f32[128,1536]{1,0:T(8,128)S(1)}, f32[128,1536]{1,0:T(8,128)}, u32[]{:S(2)}) copy-start(f32[128,1536]{1,0:T(8,128)} %get-tuple-element.71) | copy-start | bytes 2359300
  349.8 15.3 %copy-start.4 = (f32[32,8,128]{2,1,0:T(8,128)S(1)}, f32[32,8,128]{2,1,0:T(8,128)}, u32[]{:S(2)}) copy-start(f32[32,8,128]{2,1,0:T(8,128)} %get-tuple-element.77) | copy-start | bytes 393220
  349.8 15.4 %copy-start.5 = (f32[356]{0:T(512)S(1)}, f32[356]{0:T(512)}, u32[]{:S(2)}) copy-start(f32[356]{0:T(512)} %param.37) | copy-start | bytes 4276
  349.9 15.4 %copy-start.6 = (f32[356]{0:T(512)S(1)}, f32[356]{0:T(512)}, u32[]{:S(2)}) copy-start(f32[356]{0:T(512)} %param.39) | copy-start | bytes 4276
  349.9 15.4 %copy-start.7 = (f32[356]{0:T(512)S(1)}, f32[356]{0:T(512)}, u32[]{:S(2)}) copy-start(f32[356]{0:T(512)} %param.38) | copy-start | bytes 4276
  364.0 1.9 copy-start.3

commit v11 on v10

--- a/solution.py
+++ b/solution.py
@@ -1377,7 +1377,7 @@
 def middle_body(
     len_ref, mix_ref, hn_ref, dy_ref, xn_ref, w_in_hbm, w_dn_hbm, wq_hbm, dy_own_ref, hmid_ref, gains_ref, wo_hbm,
     qkv_hbm, toep_ref, gain_ref, s_hbm, p_hbm, o_hbm, strips_ref,
-    inner_ref, dhmid_ref, dxn_ref, gain_ffn_grad_ref, theta_ref, mixer_ref, gain_grad_ref, tiles_ref,
+    inner_ref, dhmid_ref, dxn_ref, gain_ffn_grad_ref, theta_ref, gain_grad_ref, tiles_ref,
     w_in_ref, w_dn_ref, wq_ref, wo_ref, qkv_ref, s_ref, p_ref, o_ref, enter_sems,
     theta_sums, pad_ref, first_ref, second_ref, dboth_ref, parts_ref, dattn_ref, grads_ref, sent_ref, strips_in, gin_ref, gd_ref,
     half_in, half_d, near_in, near_d, dqkv_ref, gq_ref, go_ref, core_q, core_o, in_q, in_o,
@@ -1551,7 +1551,9 @@
 
     pad_ref[rows : rows + 8, :] = jnp.zeros((8, rows), f32)
     theta_sums[...] = jnp.zeros_like(theta_sums)
-    mixer_ref[...] = jnp.zeros_like(mixer_ref)
+    taps_end = 2 * CQ * CK
+    mixer_ref = theta_ref.at[pl.ds(taps_end + 4, 8)]
+    theta_ref[taps_end:, :] = jnp.zeros((theta_ref.shape[0] - taps_end, rows), f32)
     gain_grad_ref[...] = jnp.zeros_like(gain_grad_ref)
     query_at = lax.broadcasted_iota(jnp.int32, (rows, rows), 0)
     key_at = lax.broadcasted_iota(jnp.int32, (rows, rows), 1)
@@ -1771,8 +1773,8 @@
     part = BLK // 32
     tiles = 4 * ROW_TILES**2 + 3 * ROW_TILES * FF_TILES
     shapes = [
-        ((seqs, rows, BLK), bf16), ((rows, D), f32), ((rows, D), f32), ((1, D), f32), ((2 * CQ * CK, rows), f32),
-        ((8, rows), f32), ((1, 2 * HP), f32), ((tiles + 1, part, BLK), bf16),
+        ((seqs, rows, BLK), bf16), ((rows, D), f32), ((rows, D), f32), ((1, D), f32), ((2 * CQ * CK + 12, rows), f32),
+        ((1, 2 * HP), f32), ((tiles + 1, part, BLK), bf16),
     ]
 
     def low(*dims):
@@ -1960,15 +1962,16 @@
     matches = jnp.arange(own_slots * devices)[:, None] == owners[None, :]
     tile_count = owners.shape[0]
     pick = jnp.min(jnp.where(matches, jnp.arange(tile_count, dtype=jnp.int32)[None, :], tile_count), axis=1)
-    inner, dhmid, dxn, grad_gain_ffn, theta_sums, mixer_sums, gain_sums, tiles = run_middle(
+    inner, dhmid, dxn, grad_gain_ffn, theta_sums, gain_sums, tiles = run_middle(
         group_lengths, mix, hn_rows, dy_rows, xn, w_in, w_dn, w_qkv, dy, hmid, gains,
         w_out_all.reshape(CHIPS, 2 * DH, D), qkv, toep, gain_pair, scores, weights, outs, strips,
     )
     dinput, grad_gain_attn = norm_backward(input_float, input_scale, gain_attn, dxn)
     input_grad = dinput + dhmid
 
-    grad_theta = jnp.sum(theta_sums, axis=1)
-    grad_mixer = jnp.sum(mixer_sums[:4], axis=1)
+    tap_sums = jnp.sum(theta_sums, axis=1)
+    grad_theta = tap_sums[: 2 * CQ * CK]
+    grad_mixer = tap_sums[2 * CQ * CK + 4 : 2 * CQ * CK + 8]
     vector_grad = jnp.concatenate(
         [
             grad_gain_attn,

time: 372 us -> 371 us (level)
  no operation moved by 1% of the time
where the time goes in v11:
time: 371 us; the launch traced here: 366 us
  Pallas kernels  352 us (95%)
  other arithmetic  6.57 us (2%)
  local copies, waits for them, and re-layouts  5 us (1%)
    pallas_call x1, Pallas kernels, run_middle(): pl.pallas_call(middle_body, in_specs=[VMEM] * 2 + [ANYS] * 6 + [VMEM] * 3...  140 us
    pallas_call x1, Pallas kernels, run_front(): pl.pallas_call(functools.partial(front_body, first_rows), in_specs=[SMEM]...  137 us
    pallas_call x1, Pallas kernels, to_slots(): pl.pallas_call(to_slots_body, in_specs=[SMEM, VMEM] + [ANYS] * 4, out_spe...  61 us
    pallas_call x1, Pallas kernels, update(): pl.pallas_call(update_body, grid=(grad.shape[0],), in_specs=[spec] * 6, o...  14.1 us

profile of v11, /device:TPU:11, one launch (start us, length us, event | category | flops | bytes accessed | tf_op | source)
XLA Modules:
  0.0 365.6 jit_solution(7037479964471391882)
XLA Ops:
  0.7 0.8 convert_dynamic-update-slice_fusion
  1.5 0.1 reshape.87
  1.6 0.1 reshape.89
  1.7 0.1 slice.52
  1.8 0.1 reshape.90
  1.9 0.2 concatenate.6
  2.1 0.6 constant_dynamic-slice_fusion.vec_ref
  3.3 137.2 %front.1 = (bf16[128,1536]{1,0:T(8,128)(2,1)}, f32[8,8,128]{2,1,0:T(8,128)}, f32[8,128]{1,0:T(8,128)}, f32[8,1536]{1,0:T(8,128)}, bf16[2,768,128]{2,1,0:T(8,128)...) custom-call(s32[1]{0:T(128)S(6)} %copy.35.length_ref, ...), custom_call_target="tpu_custom_call" | custom-call | tf_op jit(solution)/shard_map/front/pallas_call | solution.py:1362
  140.6 0.0 copy-start
  140.6 0.0 copy-start.8
  140.6 140.1 %middle.1 = (bf16[8,128,512]{2,1,0:T(8,128)(2,1)}, f32[128,1536]{1,0:T(8,128)}, f32[128,1536]{1,0:T(8,128)}, f32[1,1536]{1,0:T(1,128)}, f32[144,128]{1,0:T(8,128...) custom-call(f32[8,8,128]{2,1,0:T(8,128)} %get-tuple-element.43.len_ref, f32[8,128]{1,0:T(8,128)} %get-tuple-element.44.mix_ref, ...), custom_call_target="tpu_custom_call" | custom-call | tf_op jit(solution)/shard_map/middle/pallas_call | solution.py:1784
  280.7 1.0 reduce_sum.47
  281.7 0.1 slice_dynamic-update-slice_fusion
  281.9 0.8 reshape.96
  282.6 0.2 dynamic_update_slice.13
  282.8 0.2 slice_dynamic-update-slice_fusion.1
  283.0 0.8 slice_reduce_fusion
  283.8 0.2 fusion.8
  284.0 1.5 fusion.4
  285.4 0.7 reduce
  286.1 0.1 concatenate.7
  286.2 0.1 reshape.98
  286.4 0.8 reshape.99.vec_ref
  287.1 0.6 select_reduce_fusion.pick_ref
  287.8 61.0 %to_slots.1 = (bf16[4,512,512]{2,1,0:T(8,128)(2,1)}, f32[32,8,128]{2,1,0:T(8,128)}, bf16[128,1536]{1,0:T(8,128)(2,1)}) custom-call(s32[128]{0:T(128)} %select_reduce_fusion.pick_ref, bf16[109,16,512]{2,1,0:T(8,128)(2,1)} %get-tuple-element.62.tiles_ref, f32[32,8,128]{2,1,0:T(8,128)} %reshape.99.vec_ref, bf16[8,128,512]{2,1,0:T(8,128)(2,1)} %get-tuple-element.67.inner_hbm, ...), custom_call_target="tpu_custom_call" | custom-call | tf_op jit(solution)/shard_map/to_slots/pallas_call | solution.py:1886
  348.8 0.0 copy-start.5
  348.9 0.0 copy-start.6
  348.9 0.0 copy-start.7
  348.9 14.1 %update.1 = (f32[4,512,512]{2,1,0:T(8,128)}, f32[4,512,512]{2,1,0:T(8,128)}, f32[4,512,512]{2,1,0:T(8,128)}, bf16[4,512,512]{2,1,0:T(8,128)(2,1)}) custom-call(bf16[4,512,512]{2,1,0:T(8,128)(2,1)} %get-tuple-element.70.grad_ref, f32[4,512,512]{2,1,0:T(8,128)} %left_ref.1, f32[4,512,512]{2,1,0:T(8,128)} %right_ref.1, f32[4,512,512]{2,1,0:T(8,128)} %master_ref.1, ...), custom_call_target="tpu_custom_call" | custom-call | flops 4300000256 | bytes 37748736 | tf_op jit(solution)/shard_map/update/pallas_call | solution.py:1919
  363.0 1.2 fusion.7
  364.2 0.6 fusion.10
  364.8 0.7 copy.36
  (27 shorter events, 0.2 us)
Async XLA Ops:
  140.6 143.2 %copy-start = (bf16[128,1536]{1,0:T(8,128)(2,1)S(1)}, bf16[128,1536]{1,0:T(8,128)(2,1)}, u32[]{:S(2)}) copy-start(bf16[128,1536]{1,0:T(8,128)(2,1)} %x_ref.1) | copy-start | bytes 1179652
  140.6 146.6 %copy-start.8 = (s32[108]{0:T(128)S(1)}, s32[108]{0:T(128)}, u32[]{:S(2)}) copy-start(s32[108]{0:T(128)} %param.31) | copy-start | bytes 1300
  348.8 14.1 %copy-start.1 = (f32[128,1536]{1,0:T(8,128)S(1)}, f32[128,1536]{1,0:T(8,128)}, u32[]{:S(2)}) copy-start(f32[128,1536]{1,0:T(8,128)} %get-tuple-element.63) | copy-start | bytes 2359300
  348.8 14.1 %copy-start.2 = (f32[128,1536]{1,0:T(8,128)S(1)}, f32[128,1536]{1,0:T(8,128)}, u32[]{:S(2)}) copy-start(f32[128,1536]{1,0:T(8,128)} %get-tuple-element.69) | copy-start | bytes 2359300
  348.8 15.3 %copy-start.4 = (f32[32,8,128]{2,1,0:T(8,128)S(1)}, f32[32,8,128]{2,1,0:T(8,128)}, u32[]{:S(2)}) copy-start(f32[32,8,128]{2,1,0:T(8,128)} %get-tuple-element.75) | copy-start | bytes 393220
  348.8 15.3 %copy-start.5 = (f32[356]{0:T(512)S(1)}, f32[356]{0:T(512)}, u32[]{:S(2)}) copy-start(f32[356]{0:T(512)} %param.37) | copy-start | bytes 4276
  348.9 15.3 %copy-start.6 = (f32[356]{0:T(512)S(1)}, f32[356]{0:T(512)}, u32[]{:S(2)}) copy-start(f32[356]{0:T(512)} %param.39) | copy-start | bytes 4276
  348.9 15.3 %copy-start.7 = (f32[356]{0:T(512)S(1)}, f32[356]{0:T(512)}, u32[]{:S(2)}) copy-start(f32[356]{0:T(512)} %param.38) | copy-start | bytes 4276
  362.9 1.9 copy-start.3
